TPU v7x, 32 devices: a whole 2x2x4 slice. The times are simulated.
32 devices in a mesh: dp: 8 (over z, x), seq: 4 (over y, core).
Axes of the slice: x: 2, y: 2, z: 4, core: 2. Of those that a mesh axis runs over, the one named last changes fastest.
Arguments:
- tokens: bfloat16 [8, 512, 8192], P('dp', 'seq'), may hold values from -6 to 6
- gain: float32 [8192], replicated, may hold values from 0.25 to 1.75
- w_t: bfloat16 [512, 8192], P('dp', 'seq'), may hold values from -0.0625 to 0.0625
- grad_values: bfloat16 [8, 512, 512], P('dp', 'seq'), may hold values from -6 to 6
- owner: int32 [512], replicated, may hold values from 0 to 7, as said below
- master: float32 [8, 128, 8192], P('dp', None, 'seq'), may hold values from -0.0625 to 0.0625
- moment1: float32 [8, 128, 8192], P('dp', None, 'seq'), may hold values from -0.024 to 0.024
- moment2: float32 [8, 128, 8192], P('dp', None, 'seq'), may hold values from 1e-06 to 4e-05
Outputs:
- values: bfloat16 [8, 512, 512], P('dp', 'seq')
- grad_x: bfloat16 [8, 512, 8192], P('dp', 'seq')
- new_master: float32 [8, 128, 8192], P('dp', None, 'seq')
- new_moment1: float32 [8, 128, 8192], P('dp', None, 'seq')
- new_moment2: float32 [8, 128, 8192], P('dp', None, 'seq')
Inputs may be any that keep to these rules, and one draw needn't show every extreme that they name: `owner`: each index of dp owns at most 128 rows and some own exactly 128; some may own none.
All inputs are finite; a program needn't handle non-finite values.
Results may differ from a plain program's by a relative error of at most 0.012.
Values may be sent and summed in bfloat16 or wider, within the bound.
No kernel may reach another device: no remote copies, remote signals or barrier semaphores. Data moves between devices by JAX's collectives and lax.ppermute only.
A program may use at most 128 MiB of HBM per device.

v0:
```python
import jax
import jax.numpy as jnp
from jax import lax
from jax.sharding import PartitionSpec as P

beta_one = 0.9
beta_two = 0.95
learn_rate = 0.001
adam_eps = 1e-08
bias_one = 1.0 - 0.9**10
bias_two = 1.0 - 0.95**10


def on_device(tokens, gain, w_t, grad_values, owner, master, moment1, moment2):
    tok_float = tokens[0].astype(jnp.float32)
    inv_rms = lax.rsqrt(jnp.mean(tok_float * tok_float, axis=-1, keepdims=True) + 1e-05)
    scaled = tok_float * inv_rms
    normed = (scaled * gain).astype(jnp.bfloat16)
    value_grad = grad_values[0]
    normed_cols = lax.all_to_all(normed, "seq", split_axis=1, concat_axis=0, tiled=True)
    grads_all = lax.all_gather(value_grad, "seq", axis=0, tiled=True)
    grad_block = lax.dot_general(
        grads_all, normed_cols, (((0,), (0,)), ((), ())), preferred_element_type=jnp.float32
    )
    groups = lax.axis_size("dp")
    col_block = lax.all_gather(w_t, "dp", axis=0, tiled=True)
    full_weight = lax.all_gather(col_block, "seq", axis=1, tiled=True)
    values = lax.dot_general(
        normed, full_weight, (((1,), (1,)), ((), ())), preferred_element_type=jnp.float32
    ).astype(jnp.bfloat16)
    grad_normed = jnp.dot(value_grad, full_weight, preferred_element_type=jnp.float32).astype(
        jnp.bfloat16
    )
    weighted = gain[None, :] * grad_normed.astype(jnp.float32)
    grad_x = (
        inv_rms * (weighted - scaled * jnp.mean(weighted * scaled, axis=-1, keepdims=True))
    ).astype(jnp.bfloat16)
    own_index = lax.axis_index("dp")
    slot_count = master.shape[1]
    token_total = normed_cols.shape[0] * groups
    onehot = (owner[:, None] == jnp.arange(groups, dtype=jnp.int32)[None, :]).astype(jnp.int32)
    prior_count = jnp.cumsum(onehot, axis=0) - onehot
    slot_row = jnp.sum(prior_count * onehot, axis=1)
    select_all = (
        (owner[None, None, :] == jnp.arange(groups, dtype=jnp.int32)[:, None, None])
        & (slot_row[None, None, :] == jnp.arange(slot_count, dtype=jnp.int32)[None, :, None])
    ).astype(jnp.float32)
    select_mine = lax.dynamic_index_in_dim(select_all, own_index, 0, keepdims=False)
    occupied = jnp.sum(select_mine, axis=-1, keepdims=True)
    summed = lax.psum(grad_block, "dp")
    slot_grad = jnp.dot(select_mine, summed, precision=lax.Precision.HIGHEST)
    slot_grad = slot_grad / token_total
    new_moment1 = (beta_one * moment1[0] + (1.0 - beta_one) * slot_grad) * occupied
    new_moment2 = (beta_two * moment2[0] + (1.0 - beta_two) * slot_grad * slot_grad) * occupied
    step_dir = new_moment1 / bias_one / (jnp.sqrt(new_moment2 / bias_two) + adam_eps)
    new_master = (master[0] - learn_rate * step_dir) * occupied
    return (values[None], grad_x[None], new_master[None], new_moment1[None], new_moment2[None])


def solution(mesh):
    placed = (
        P("dp", "seq", None),
        P(),
        P("dp", "seq"),
        P("dp", "seq", None),
        P(),
        P("dp", None, "seq"),
        P("dp", None, "seq"),
        P("dp", None, "seq"),
    )
    return jax.shard_map(
        on_device,
        mesh=mesh,
        in_specs=placed,
        out_specs=(
            P("dp", "seq", None),
            P("dp", "seq", None),
            P("dp", None, "seq"),
            P("dp", None, "seq"),
            P("dp", None, "seq"),
        ),
        check_vma=False,
    )
```

profile of v0, /device:TPU:0, one launch (start us, length us, event | category | flops | bytes accessed | tf_op | source)
XLA Modules:
  0.0 299.3 jit_solution(5601828714796782724)
XLA Ops:
  7.2 0.0 copy-start
  7.2 0.0 copy-start.5
  7.2 0.0 all-gather.4.cloned.1.call-start
  7.2 0.7 all-gather.4.cloned.1.call-update
  7.9 6.0 %reshape.109 = f32[128,4,2048]{2,1,0:T(4,128)} reshape(bf16[1,128,8192]{2,1,0:T(8,128)(2,1)} %param.8) | data formatting | bytes 6291456 | tf_op jit(solution)/shard_map/convert_element_type | solution.py:15
  13.9 0.0 copy-done.5
  13.9 0.0 copy-done
  13.9 0.5 fusion.2
  14.4 0.0 copy-start.4
  14.5 5.9 %fusion.4 = bf16[128,4,2048]{2,0,1:T(8,128)(2,1)} fusion(f32[128,4,2048]{2,1,0:T(4,128)} %reshape.109, f32[4,2048]{1,0:T(4,128)S(1)} %mul.132, f32[128]{0:T(128)S(1)} %add_rsqrt_fusion), kind=kLoop, calls=%fused_computation.8 | loop fusion | flops 3145728 | bytes 6324736 | tf_op jit(solution)/shard_map/convert_element_type | solution.py:18
  20.3 4.5 %all-to-all-start = ((bf16[128,4,2048]{2,0,1:T(8,128)(2,1)}), bf16[128,4,2048]{2,0,1:T(8,128)(2,1)}, u32[]{:S(2)}, u32[]{:S(2)}) async-start(bf16[128,4,2048]{2,0,1:T(8,128)(2,1)} %fusion.4), calls=%async_computation | async-start | bytes 4194304 | tf_op jit(solution)/shard_map/all_to_all | solution.py:20
  24.8 0.0 all-reduce.2.cloned.1.call-start
  24.9 0.0 copy-done.4
  24.9 29.9 %all-gather = bf16[1,512,512]{2,1,0:T(8,128)(2,1)S(1)} all-gather(bf16[1,128,512]{2,1,0:T(8,128)(2,1)S(1)} %copy-done.4), channel_id=2, replica_groups=mesh['dp'=8,'seq'=4] {'seq'}, dimensions={1}, use_global_device_ids=true | all-gather | bytes 655360 | tf_op jit(solution)/shard_map/all_gather | solution.py:21
  54.7 0.0 all-to-all-done
  54.7 4.9 %convolution_bitcast_fusion = f32[512,2048]{0,1:T(8,128)} fusion(bf16[512,2048]{1,0:T(8,128)(2,1)} %bitcast.11, bf16[1,512,512]{2,1,0:T(8,128)(2,1)S(1)} %all-gather), kind=kOutput, calls=%fused_computation.12 | convolution fusion | flops 1073741824 | bytes 6815744 | tf_op jit(solution)/shard_map/dot_general | solution.py:22
  59.6 0.0 copy-start.6
  59.6 0.0 copy-start.2
  59.6 0.0 all-reduce.2.cloned.1.call-update
  59.6 0.2 all-gather.6.cloned.1.call-start
  59.9 2.3 all-gather.4.cloned.1.call-done
  62.2 0.0 all-gather.6.cloned.1.call-update
  62.2 0.0 copy-done.6
  62.2 1.1 reduce-window.6
  63.4 0.2 slice_reduce_fusion
  63.6 0.1 fusion.22
  63.8 0.2 broadcast_and_fusion
  64.0 0.0 copy-start.3
  64.0 0.8 copy-done.3
  64.8 0.1 convert_reduce_fusion
  64.9 155.8 %all-reduce.2.cloned.1.call-done = f32[512,2048]{0,1:T(8,128)} async-done(((f32[512,2048]{0,1:T(8,128)}), f32[512,2048]{0,1:T(8,128)}) %all-reduce.2.cloned.1.call-update) | async-done | bytes 4194320 | tf_op jit(solution)/shard_map/psum | solution.py:50
  220.7 0.0 copy-done.2
  220.7 7.5 %fusion.25 = (f32[1,128,2048]{2,1,0:T(8,128)}, f32[1,128,2048]{2,1,0:T(8,128)}, f32[1,128,2048]{2,1,0:T(8,128)}) fusion(f32[128]{0:T(128)S(1)} %convert_reduce_fusion, f32[1,128,2048]{2,1,0:T(8,128)S(1)} %copy-done.2, f32[1,128,2048]{2,1,0:T(8,128)} %param.14, f32[1,128,2048]{2,1,0:T(8,128)} %param.13, f32[512,2048]{0,1:T(8,128)} %all-reduce.2.cloned.1.call-done, ...), kind=kOutput, calls=%fused_computation.46 | convolution fusion | flops 1615069184 | bytes 10551812 | tf_op jit(solution)/shard_map/dot_general | solution.py:51
  228.2 51.4 %all-gather.6.cloned.1.call-done = bf16[512,8192]{1,0:T(8,128)(2,1)} async-done(((bf16[512,2048]{1,0:T(8,128)(2,1)}), bf16[512,8192]{1,0:T(8,128)(2,1)}) %all-gather.6.cloned.1.call-update) | async-done | bytes 8388624 | tf_op jit(solution)/shard_map/all_gather | solution.py:27
  279.6 5.4 %multiply_reduce_fusion = (f32[128]{0:T(128)S(1)}, f32[128,8192]{1,0:T(8,128)S(1)}) fusion(bf16[1,128,8192]{2,1,0:T(8,128)(2,1)S(1)} %copy-done, f32[128]{0:T(128)S(1)} %add_rsqrt_fusion, bf16[512,8192]{1,0:T(8,128)(2,1)} %all-gather.6.cloned.1.call-done, bf16[1,128,512]{2,1,0:T(8,128)(2,1)S(1)} %copy-done.4, f32[8192]{0:T(1024)S(1)} %copy-done.5), kind=kOutput, calls=%fused_computation.10 | convolution fusion | flops 1081081728 | bytes 14844928 | tf_op jit(solution)/shard_map/dot_general | solution.py:31
  285.0 0.0 copy-start.1
  285.0 2.3 fusion.6
  287.3 1.9 copy-done.1
  289.1 3.6 %fusion.10 = bf16[1,128,512]{2,1,0:T(8,128)(2,1)} fusion(bf16[512,8192]{1,0:T(8,128)(2,1)S(1)} %copy-done.1, bf16[1,128,8192]{2,1,0:T(8,128)(2,1)S(1)} %copy-done, f32[8192]{0:T(1024)S(1)} %copy-done.5, f32[128]{0:T(128)S(1)} %add_rsqrt_fusion), kind=kOutput, calls=%fused_computation.18 | convolution fusion | flops 1078001664 | bytes 10650112 | tf_op jit(solution)/shard_map/dot_general | solution.py:28
  (8 shorter events, 0.1 us)
Async XLA Ops:
  7.2 6.8 %copy-start = (bf16[1,128,8192]{2,1,0:T(8,128)(2,1)S(1)}, bf16[1,128,8192]{2,1,0:T(8,128)(2,1)}, u32[]{:S(2)}) copy-start(bf16[1,128,8192]{2,1,0:T(8,128)(2,1)} %param.8) | copy-start | bytes 6291460
  7.2 6.7 %copy-start.5 = (f32[8192]{0:T(1024)S(1)}, f32[8192]{0:T(1024)}, u32[]{:S(2)}) copy-start(f32[8192]{0:T(1024)} %param.9) | copy-start | bytes 98308
  7.2 55.0 %all-gather.4.cloned.1.call-start = ((), (), s32[]{:S(2)}) async-start(), calls=%async_computation.1 | async-start | bytes 2359296 | tf_op jit(solution)/shard_map/all_gather | solution.py:26
  14.4 10.4 %copy-start.4 = (bf16[1,128,512]{2,1,0:T(8,128)(2,1)S(1)}, bf16[1,128,512]{2,1,0:T(8,128)(2,1)}, u32[]{:S(2)}) copy-start(bf16[1,128,512]{2,1,0:T(8,128)(2,1)} %param.11) | copy-start | bytes 393220
  20.3 34.4 %all-to-all-start = ((bf16[128,4,2048]{2,0,1:T(8,128)(2,1)}), bf16[128,4,2048]{2,0,1:T(8,128)(2,1)}, u32[]{:S(2)}, u32[]{:S(2)}) async-start(bf16[128,4,2048]{2,0,1:T(8,128)(2,1)} %fusion.4), calls=%async_computation | async-start | bytes 4194304 | tf_op jit(solution)/shard_map/all_to_all | solution.py:20
  24.8 195.9 %all-reduce.2.cloned.1.call-start = ((), (), s32[]{:S(2)}) async-start(), calls=%async_computation.3 | async-start | bytes 8388608 | tf_op jit(solution)/shard_map/psum | solution.py:50
  59.6 2.6 copy-start.6
  59.6 161.1 %copy-start.2 = (f32[1,128,2048]{2,1,0:T(8,128)S(1)}, f32[1,128,2048]{2,1,0:T(8,128)}, u32[]{:S(2)}) copy-start(f32[1,128,2048]{2,1,0:T(8,128)} %param.15) | copy-start | bytes 3145732
  59.6 219.9 %all-gather.6.cloned.1.call-start = ((), (), s32[]{:S(2)}) async-start(), calls=%async_computation.2 | async-start | bytes 10485760 | tf_op jit(solution)/shard_map/all_gather | solution.py:27
  64.0 0.8 copy-start.3
  285.0 4.1 %copy-start.1 = (bf16[512,8192]{1,0:T(8,128)(2,1)S(1)}, bf16[512,8192]{1,0:T(8,128)(2,1)}, u32[]{:S(2)}) copy-start(bf16[512,8192]{1,0:T(8,128)(2,1)} %all-gather.6.cloned.1.call-done) | copy-start | bytes 25165828
Sparse Core Ops, SparseCore 0:
  10.1 51.9 all-gather.3
  65.8 154.7 all-reduce.1
  222.3 57.2 all-gather.5
where the time goes:
time: 300 us; the launch traced here: 299 us
  waiting for transfers between devices  210 us (70%)
  blocking collectives  29.9 us (10%)
  matrix products  21.4 us (7%)
  between operations  13.9 us (5%)
  other arithmetic  10.3 us (3%)
  local copies, waits for them, and re-layouts  8.92 us (3%)
  starting transfers between devices  4.78 us (2%)
    psum x1, waiting for transfers between devices, on_device(): summed = lax.psum(grad_block, 'dp')  156 us
    all_gather x1, waiting for transfers between devices, on_device(): full_weight = lax.all_gather(col_block, 'seq', axis=1, tiled=True)  51.4 us
    all_gather x1, blocking collectives, on_device(): grads_all = lax.all_gather(value_grad, 'seq', axis=0, tiled=True)  29.9 us
    dot_general x1, matrix products, on_device(): slot_grad = jnp.dot(select_mine, summed, precision=lax.Precision.HIGHEST)  7.52 us
  transfers between devices with their start and end apart: 4, of which 3 were waited for; matrix products, arithmetic and copies ran while one was open for 9% of the time, Pallas kernels for 0%

commit v1 on v0

v1 whole, which is shorter than its diff:
```python
import functools

import jax
import jax.numpy as jnp
from jax import lax
from jax.experimental import pallas as pl
from jax.experimental.pallas import tpu as pltpu
from jax.sharding import PartitionSpec as P

beta_one = 0.9
beta_two = 0.95
learn_rate = 0.001
adam_eps = 1e-08
bias_one = 1.0 - 0.9**10
bias_two = 1.0 - 0.95**10
norm_eps = 1e-05

bf16 = jnp.bfloat16
f32 = jnp.float32


def norm_kernel(offs, tok_ref, gain_ref, *out_refs):
    width = out_refs[0].shape[-1]
    tok = tok_ref[...].astype(f32)
    inv_rms = lax.rsqrt(jnp.mean(tok * tok, axis=-1, keepdims=True) + norm_eps)
    for k, out_ref in enumerate(out_refs):
        for j in range(2):
            cols = pl.ds(pl.multiple_of(offs[2 * k + j] * width, width), width)
            scaled = tok_ref[:, cols].astype(f32) * inv_rms
            out_ref[j] = (scaled * gain_ref[:, cols]).astype(bf16)


def norm_blocks(offs, tokens, gain, chips, width):
    rows, model = tokens.shape
    step = min(rows, 32)
    return pl.pallas_call(
        norm_kernel,
        grid_spec=pltpu.PrefetchScalarGridSpec(
            num_scalar_prefetch=1,
            grid=(rows // step,),
            in_specs=[
                pl.BlockSpec((step, model), lambda i, offs: (i, 0)),
                pl.BlockSpec((1, model), lambda i, offs: (0, 0)),
            ],
            out_specs=[pl.BlockSpec((2, step, width), lambda i, offs: (0, i, 0))] * chips,
        ),
        out_shape=[jax.ShapeDtypeStruct((2, rows, width), bf16)] * chips,
        compiler_params=pltpu.CompilerParams(vmem_limit_bytes=24 * 1024 * 1024),
        name="norm_blocks",
    )(offs, tokens, gain)


def grad_x_kernel(offs, tok_ref, gain_ref, *refs):
    grad_refs, out_ref = refs[:-1], refs[-1]
    model = tok_ref.shape[-1]
    width = grad_refs[0].shape[-1]
    tok = tok_ref[...].astype(f32)
    inv_rms = lax.rsqrt(jnp.mean(tok * tok, axis=-1, keepdims=True) + norm_eps)
    total = jnp.zeros((tok.shape[0], 1), f32)
    for k, grad_ref in enumerate(grad_refs):
        for j in range(2):
            cols = pl.ds(pl.multiple_of(offs[2 * k + j] * width, width), width)
            weighted = gain_ref[:, cols] * grad_ref[j].astype(f32)
            scaled = tok_ref[:, cols].astype(f32) * inv_rms
            total += jnp.sum(weighted * scaled, axis=-1, keepdims=True)
    mean = total / model
    for k, grad_ref in enumerate(grad_refs):
        for j in range(2):
            cols = pl.ds(pl.multiple_of(offs[2 * k + j] * width, width), width)
            weighted = gain_ref[:, cols] * grad_ref[j].astype(f32)
            scaled = tok_ref[:, cols].astype(f32) * inv_rms
            out_ref[:, cols] = (inv_rms * (weighted - scaled * mean)).astype(bf16)


def grad_x_blocks(offs, tokens, gain, grads):
    rows, model = tokens.shape
    width = grads[0].shape[-1]
    step = min(rows, 32)
    return pl.pallas_call(
        grad_x_kernel,
        grid_spec=pltpu.PrefetchScalarGridSpec(
            num_scalar_prefetch=1,
            grid=(rows // step,),
            in_specs=[
                pl.BlockSpec((step, model), lambda i, offs: (i, 0)),
                pl.BlockSpec((1, model), lambda i, offs: (0, 0)),
            ]
            + [pl.BlockSpec((2, step, width), lambda i, offs: (0, i, 0))] * len(grads),
            out_specs=pl.BlockSpec((step, model), lambda i, offs: (i, 0)),
        ),
        out_shape=jax.ShapeDtypeStruct((rows, model), bf16),
        compiler_params=pltpu.CompilerParams(vmem_limit_bytes=24 * 1024 * 1024),
        name="grad_x_blocks",
    )(offs, tokens, gain, *grads)


def on_device(groups, seqs, tokens, gain, w_t, grad_values, owner, master, moment1, moment2):
    planes = groups // 2
    chips = seqs
    tokens, value_grad = tokens[0], grad_values[0]
    rows, model = tokens.shape
    feats = owner.shape[0]
    slots = master.shape[1]
    width = model // (2 * seqs)
    share = w_t.shape[0]

    own_dp = lax.axis_index("dp")
    own_seq = lax.axis_index("seq")
    own_x, own_z = own_dp % 2, own_dp // 2
    own_core = own_seq % 2

    def permute(value, target):
        pairs = []
        for dp in range(groups):
            for seq in range(seqs):
                to = target(dp, seq)
                if to is not None:
                    pairs.append((dp * seqs + seq, to[0] * seqs + to[1]))
        return lax.ppermute(value, ("dp", "seq"), pairs)

    def to_chip(value, k):
        return permute(value, lambda dp, seq: (dp ^ (k & 1), seq ^ (k >> 1 << 1)))

    def to_core(value):
        return permute(value, lambda dp, seq: (dp, seq ^ 1))

    def to_x(value):
        return permute(value, lambda dp, seq: (dp ^ 1, seq))

    def to_plane(value, turn):
        return permute(value, lambda dp, seq: ((dp + 2 * turn) % groups, seq))

    offs = jnp.stack(
        [
            ((own_seq ^ (k >> 1 << 1)) ^ j) * 2 + (own_x ^ (k & 1))
            for k in range(chips)
            for j in range(2)
        ]
    ).astype(jnp.int32)
    gain_row = gain[None, :]

    grads = [value_grad] + [to_chip(value_grad, k) for k in range(1, chips)]
    grads_core = jnp.concatenate(grads, axis=0)
    grads_other = to_core(grads_core)

    halves = w_t.reshape(share, 2, width)
    w_keep = lax.dynamic_index_in_dim(halves, own_x, 1, keepdims=False)
    w_got = to_x(lax.dynamic_index_in_dim(halves, 1 - own_x, 1, keepdims=False))
    first = own_x == 0
    w_plane = jnp.concatenate(
        [jnp.where(first, w_keep, w_got), jnp.where(first, w_got, w_keep)], axis=0
    )
    w_own = jnp.zeros((planes, 2 * share, width), bf16)
    w_own = lax.dynamic_update_index_in_dim(w_own, w_plane, own_z, 0)
    for turn in range(1, planes):
        w_own = lax.dynamic_update_index_in_dim(
            w_own, to_plane(w_plane, turn), (own_z - turn) % planes, 0
        )
    w_own = w_own.reshape(feats, width)
    w_other = to_core(w_own)

    normed = norm_blocks(offs, tokens, gain_row, chips, width)
    normed = [normed[0]] + [to_chip(normed[k], k) for k in range(1, chips)]
    cols_own = jnp.concatenate([n[0] for n in normed], axis=0)
    cols_other = jnp.concatenate([n[1] for n in normed], axis=0)
    cols_far = to_core(cols_other)

    index = jnp.arange(feats, dtype=jnp.int32)
    same = (owner[:, None] == owner[None, :]) & (index[None, :] < index[:, None])
    slot = owner * slots + jnp.sum(same.astype(jnp.int32), axis=1)
    select = (slot[:, None] == jnp.arange(groups * slots, dtype=jnp.int32)[None, :]).astype(bf16)
    count = jnp.sum((owner == own_dp).astype(jnp.int32))
    occupied = (jnp.arange(slots, dtype=jnp.int32) < count).astype(f32)[:, None]
    grads_sel = jnp.dot(
        jnp.concatenate([grads_core, grads_other], axis=0), select, preferred_element_type=f32
    ).astype(bf16)
    partial = lax.dot_general(
        grads_sel,
        jnp.concatenate([cols_own, cols_far], axis=0),
        (((0,), (0,)), ((), ())),
        preferred_element_type=f32,
    ).astype(bf16)
    partial = partial.reshape(planes, 2 * slots, width)

    def block(at):
        return lax.dynamic_index_in_dim(partial, jnp.clip(at, 0, planes - 1), 0, keepdims=False)

    right = left = None
    for step in range(1, planes):
        send_right = block(planes - step + own_z)
        send_left = block(step + own_z - planes)
        if right is not None:
            send_right = (send_right.astype(f32) + right.astype(f32)).astype(bf16)
            send_left = (send_left.astype(f32) + left.astype(f32)).astype(bf16)
        right = permute(
            send_right, lambda dp, seq: (dp + 2, seq) if dp // 2 < min(step, planes - 1) else None
        )
        left = permute(
            send_left,
            lambda dp, seq: (dp - 2, seq) if planes - 1 - dp // 2 < min(step, planes - 1) else None,
        )
    mine = block(own_z).astype(f32) + right.astype(f32) + left.astype(f32)
    mine = mine.reshape(2, slots, width)
    kept = lax.dynamic_index_in_dim(mine, own_x, 0, keepdims=False)
    got = to_x(lax.dynamic_index_in_dim(mine, 1 - own_x, 0, keepdims=False).astype(bf16)).astype(f32)

    grad_blocks = [
        jnp.dot(grads_core, w, preferred_element_type=f32).astype(bf16).reshape(chips, rows, width)
        for w in (w_own, w_other)
    ]
    grad_blocks = jnp.stack(grad_blocks, axis=1)
    grad_home = [grad_blocks[0]] + [to_chip(grad_blocks[k], k) for k in range(1, chips)]
    grad_x = grad_x_blocks(offs, tokens, gain_row, grad_home)

    dims = (((1,), (1,)), ((), ()))
    value_part = lax.dot_general(cols_own, w_own, dims, preferred_element_type=f32)
    value_part += lax.dot_general(cols_other, w_other, dims, preferred_element_type=f32)
    value_part = value_part.reshape(chips, rows, feats)
    values = value_part[0]
    for k in range(1, chips):
        values += to_chip(value_part[k].astype(bf16), k).astype(f32)
    values = values.astype(bf16)

    token_total = rows * seqs * groups
    slot_grad = jnp.concatenate([jnp.where(first, kept, got), jnp.where(first, got, kept)], axis=1)
    slot_grad = slot_grad / token_total
    new_moment1 = (beta_one * moment1[0] + (1.0 - beta_one) * slot_grad) * occupied
    new_moment2 = (beta_two * moment2[0] + (1.0 - beta_two) * slot_grad * slot_grad) * occupied
    step_dir = new_moment1 / bias_one / (jnp.sqrt(new_moment2 / bias_two) + adam_eps)
    new_master = (master[0] - learn_rate * step_dir) * occupied
    return (values[None], grad_x[None], new_master[None], new_moment1[None], new_moment2[None])


def solution(mesh):
    placed = (
        P("dp", "seq", None),
        P(),
        P("dp", "seq"),
        P("dp", "seq", None),
        P(),
        P("dp", None, "seq"),
        P("dp", None, "seq"),
        P("dp", None, "seq"),
    )
    return jax.shard_map(
        functools.partial(on_device, mesh.shape["dp"], mesh.shape["seq"]),
        mesh=mesh,
        in_specs=placed,
        out_specs=(
            P("dp", "seq", None),
            P("dp", "seq", None),
            P("dp", None, "seq"),
            P("dp", None, "seq"),
            P("dp", None, "seq"),
        ),
        check_vma=False,
    )
```

time: 300 us -> 143 us (0.48)
  the two profiles are of different devices: /device:TPU:0 before, /device:TPU:16 now
where the time goes in v1:
time: 143 us
  waiting for transfers between devices  53.9 us (38%)
  starting transfers between devices  33.3 us (23%)
  local copies, waits for them, and re-layouts  23.2 us (16%)
  matrix products  13.6 us (10%)
  other arithmetic  11.5 us (8%)
  Pallas kernels  6.14 us (4%)
    ppermute x26, waiting for transfers between devices, permute(): return lax.ppermute(value, ('dp', 'seq'), pairs)  53.9 us
    ppermute x26, starting transfers between devices, permute(): return lax.ppermute(value, ('dp', 'seq'), pairs)  33.3 us
    unnamed x37, local copies, waits for them, and re-layouts  10.3 us
    dot_general x1, matrix products, on_device(): lax.dot_general(grads_sel, jnp.concatenate([cols_own, cols_far], axis=0),...  5.51 us
    dynamic_update_slice x3, local copies, waits for them, and re-layouts, on_device(): lax.dynamic_update_index_in_dim(w_own, to_plane(w_plane, turn), (own_z -...  5.01 us
    pallas_call x1, Pallas kernels, grad_x_blocks(): pl.pallas_call(grad_x_kernel, grid_spec=pltpu.PrefetchScalarGridSpec(num_...  4.27 us
    dot_general x2, matrix products, on_device(): jnp.dot(grads_core, w, preferred_element_type=f32).astype(bf16)  4.18 us
    squeeze x4, local copies, waits for them, and re-layouts, on_device(): cols_own = jnp.concatenate([n[0] for n in normed], axis=0)  2.95 us
  transfers between devices with their start and end apart: 26, of which 7 were waited for; matrix products, arithmetic and copies ran while one was open for 30% of the time, Pallas kernels for 4%

profile of v1, /device:TPU:16, one launch (start us, length us, event | category | flops | bytes accessed | tf_op | source)
XLA Modules:
  0.0 142.8 jit_solution(16464758037475440714)
XLA Ops:
  0.6 2.5 %collective-permute-start.13 = (bf16[128,512]{1,0:T(8,128)(2,1)}, bf16[128,512]{1,0:T(8,128)(2,1)S(1)}, u32[]{:S(2)}, u32[]{:S(2)}) collective-permute-start(bf16[128,512]{1,0:T(8,128)(2,1)} %bitcast.114), channel_id=1, source_target_pairs={{0,6},{1,7},{2,4},{3,5},{4,2},{5,3},{6,0},{7,1},{8,14},{9,15},{10,... | collective-permute-start | bytes 393224 | tf_op jit(solution)/shard_map/ppermute | solution.py:119
  4.2 1.1 reshape.175
  6.6 1.5 %collective-permute-start.3 = (bf16[64,1024]{1,0:T(8,128)(2,1)}, bf16[64,1024]{1,0:T(8,128)(2,1)}, u32[]{:S(2)}, u32[]{:S(2)}) collective-permute-start(bf16[64,1024]{1,0:T(8,128)(2,1)} %bitcast.99), channel_id=1, source_target_pairs={{0,4},{1,5},{2,6},{3,7},{4,0},{5,1},{6,2},{7,3},{8,12},{9,13},{10,... | collective-permute-start | bytes 393224 | tf_op jit(solution)/shard_map/ppermute | solution.py:119
  8.2 1.6 %copy-done = bf16[1,128,8192]{2,1,0:T(8,128)(2,1)S(1)} copy-done((bf16[1,128,8192]{2,1,0:T(8,128)(2,1)S(1)}, bf16[1,128,8192]{2,1,0:T(8,128)(2,1)}, u32[]{:S(2)}) %copy-start) | copy-done | bytes 2097176
  9.8 1.9 %norm_blocks.1 = (bf16[2,128,1024]{2,1,0:T(8,128)(2,1)S(1)}, bf16[2,128,1024]{2,1,0:T(8,128)(2,1)S(1)}, bf16[2,128,1024]{2,1,0:T(8,128)(2,1)S(1)}, bf16[2,128,1024]{2,1,0:T(8,128)(2,1)S(1)}) custom-call(s32[8]{0:T(128)S(1)} %stack.38.offs, bf16[128,8192]{1,0:T(8,128)(2,1)S(1)} %bitcast.100, f32[1,8192]{1,0:T(1,128)S(1)} %bitcast.102), custom_call_target="tpu_custom_call" | custom-call | tf_op jit(solution)/shard_map/norm_blocks/pallas_call | solution.py:36
  11.7 1.6 %collective-permute-start.2 = (bf16[2,128,1024]{2,1,0:T(8,128)(2,1)S(1)}, bf16[2,128,1024]{2,1,0:T(8,128)(2,1)S(1)}, u32[]{:S(2)}, u32[]{:S(2)}) collective-permute-start(bf16[2,128,1024]{2,1,0:T(8,128)(2,1)S(1)} %get-tuple-element.12), channel_id=1, source_target_pairs={{0,6},{1,7},{2,4},{3,5},{4,2},{5,3},{6,0},{7,1},{8,14},{9,15},{10,... | collective-permute-start | bytes 1572872 | tf_op jit(solution)/shard_map/ppermute | solution.py:119
  13.2 0.8 slice_bitcast_fusion.7
  16.9 1.0 bitcast_select_fusion.1
  18.6 1.5 %collective-permute-start = (bf16[2,128,1024]{2,1,0:T(8,128)(2,1)S(1)}, bf16[2,128,1024]{2,1,0:T(8,128)(2,1)S(1)}, u32[]{:S(2)}, u32[]{:S(2)}) collective-permute-start(bf16[2,128,1024]{2,1,0:T(8,128)(2,1)S(1)} %get-tuple-element.10), channel_id=1, source_target_pairs={{0,4},{1,5},{2,6},{3,7},{4,0},{5,1},{6,2},{7,3},{8,12},{9,13},{10,... | collective-permute-start | bytes 1572872 | tf_op jit(solution)/shard_map/ppermute | solution.py:119
  20.1 1.6 %constant_dynamic-update-slice_fusion.3 = bf16[1024,512]{1,0:T(8,128)(2,1)} fusion(bf16[1024,512]{1,0:T(8,128)(2,1)} %constant_dynamic-update-slice_fusion.4, bf16[128,512]{1,0:T(8,128)(2,1)} %collective-permute-done.11), kind=kLoop, calls=%fused_computation.81 | loop fusion | bytes 262144
  21.7 1.6 %collective-permute-start.4 = (bf16[128,1024]{1,0:T(8,128)(2,1)}, bf16[128,1024]{1,0:T(8,128)(2,1)}, u32[]{:S(2)}, u32[]{:S(2)}) collective-permute-start(bf16[128,1024]{1,0:T(8,128)(2,1)} %pad_maximum_fusion.4), channel_id=1, source_target_pairs={{0,8},{1,9},{2,10},{3,11},{4,12},{5,13},{6,14},{7,15},{8,16},{9,17... | collective-permute-start | bytes 786440 | tf_op jit(solution)/shard_map/ppermute | solution.py:119
  23.6 1.0 pad_maximum_fusion.3
  24.6 1.6 %constant_dynamic-update-slice_fusion.2 = bf16[1024,512]{1,0:T(8,128)(2,1)} fusion(bf16[1024,512]{1,0:T(8,128)(2,1)} %constant_dynamic-update-slice_fusion.3, bf16[128,512]{1,0:T(8,128)(2,1)} %collective-permute-done.12), kind=kLoop, calls=%fused_computation.80 | loop fusion | bytes 262144
  26.1 1.4 collective-permute-done.2
  28.0 0.7 slice_bitcast_fusion.3
  28.7 7.7 %collective-permute-done.1 = bf16[2,128,1024]{2,1,0:T(8,128)(2,1)S(1)} collective-permute-done((bf16[2,128,1024]{2,1,0:T(8,128)(2,1)S(1)}, bf16[2,128,1024]{2,1,0:T(8,128)(2,1)S(1)}, u32[]{:S(2)}, u32[]{:S(2)}) %collective-permute-start.1) | collective-permute-done | bytes 524320 | tf_op jit(solution)/shard_map/ppermute | solution.py:119
  36.6 0.7 slice_bitcast_fusion.4
  38.6 1.1 broadcast_in_dim.36
  42.6 1.1 constant_dynamic-update-slice_fusion.5
  43.9 5.5 %fusion.3 = bf16[1024,1024]{1,0:T(8,128)(2,1)S(1)} fusion(bf16[1024,1024]{1,0:T(8,128)(2,1)} %constant_dynamic-update-slice_fusion.5, bf16[1024,512]{1,0:T(8,128)(2,1)} %copy-done.13, s32[512]{0:T(512)S(1)} %get-tuple-element.41), kind=kOutput, calls=%fused_computation.10 | convolution fusion | flops 3223846912 | bytes 5244928 | tf_op jit(solution)/shard_map/dot_general | solution.py:177
  49.4 0.9 dynamic-slice_bitcast_fusion.1
  51.0 1.7 %bitcast_dynamic-update-slice_fusion.2 = bf16[4,128,1024]{2,1,0:T(8,128)(2,1)} fusion(bf16[4,128,1024]{2,1,0:T(8,128)(2,1)} %bitcast_dynamic-update-slice_fusion.3, s32[]{:T(128)S(6)} %select_n.87, bf16[128,1024]{1,0:T(8,128)(2,1)} %collective-permute-done.4), kind=kLoop, calls=%fused_computation.70 | loop fusion | bytes 524292 | tf_op jit(solution)/shard_map/jit(dynamic_update_index_in_dim)/dynamic_update_slice | solution.py:156
  52.7 1.7 %bitcast_dynamic-update-slice_fusion.1 = bf16[4,128,1024]{2,1,0:T(8,128)(2,1)} fusion(bf16[4,128,1024]{2,1,0:T(8,128)(2,1)} %bitcast_dynamic-update-slice_fusion.2, s32[]{:T(128)S(6)} %select_n.89, bf16[128,1024]{1,0:T(8,128)(2,1)} %collective-permute-done.5), kind=kLoop, calls=%fused_computation.69 | loop fusion | bytes 524292 | tf_op jit(solution)/shard_map/jit(dynamic_update_index_in_dim)/dynamic_update_slice | solution.py:156
  54.3 1.7 %bitcast_dynamic-update-slice_fusion = bf16[4,128,1024]{2,1,0:T(8,128)(2,1)} fusion(bf16[4,128,1024]{2,1,0:T(8,128)(2,1)} %bitcast_dynamic-update-slice_fusion.1, s32[]{:T(128)S(6)} %select_n.91, bf16[128,1024]{1,0:T(8,128)(2,1)} %collective-permute-done.6), kind=kLoop, calls=%fused_computation.68 | loop fusion | bytes 524292 | tf_op jit(solution)/shard_map/jit(dynamic_update_index_in_dim)/dynamic_update_slice | solution.py:156
  56.1 1.3 collective-permute-start.22
  57.4 1.0 fusion.15
  58.4 1.3 collective-permute-start.20
  59.7 2.1 %convolution_convert_fusion.1 = bf16[512,1024]{1,0:T(8,128)(2,1)S(1)} fusion(bf16[512,1024]{1,0:T(8,128)(2,1)} %bitcast.18, bf16[128,512]{1,0:T(8,128)(2,1)S(1)} %collective-permute-done.13, bf16[128,512]{1,0:T(8,128)(2,1)} %collective-permute-done.12, bf16[128,512]{1,0:T(8,128)(2,1)} %collective-permute-done.11, bf16[128,512]{1,0:T(8,128)(2,1)S(1)} %bitcast.118), kind=kOutput, calls=%fused_computation.12 | convolution fusion | flops 539492352 | bytes 2621440 | tf_op jit(solution)/shard_map/dot_general | solution.py:208
  61.8 10.7 %collective-permute-done.22 = bf16[256,1024]{1,0:T(8,128)(2,1)} collective-permute-done((bf16[256,1024]{1,0:T(8,128)(2,1)}, bf16[256,1024]{1,0:T(8,128)(2,1)}, u32[]{:S(2)}, u32[]{:S(2)}) %collective-permute-start.22) | collective-permute-done | bytes 524320 | tf_op jit(solution)/shard_map/ppermute | solution.py:119
  72.6 8.6 %collective-permute-done.20 = bf16[256,1024]{1,0:T(8,128)(2,1)} collective-permute-done((bf16[256,1024]{1,0:T(8,128)(2,1)}, bf16[256,1024]{1,0:T(8,128)(2,1)}, u32[]{:S(2)}, u32[]{:S(2)}) %collective-permute-start.20) | collective-permute-done | bytes 524320 | tf_op jit(solution)/shard_map/ppermute | solution.py:119
  81.1 1.6 %fusion.16 = (bf16[256,1024]{1,0:T(8,128)(2,1)S(1)}, bf16[256,1024]{1,0:T(8,128)(2,1)S(1)}) fusion(bf16[256,1024]{1,0:T(8,128)(2,1)} %collective-permute-done.20, bf16[4,256,1024]{2,1,0:T(8,128)(2,1)S(1)} %bitcast.106, s32[]{:T(128)S(6)} %min.23, bf16[256,1024]{1,0:T(8,128)(2,1)} %collective-permute-done.22, s32[]{:T(128)S(6)} %min.27), kind=kLoop, calls=%fused_computation.30 | loop fusion | flops 2097152 | bytes 3145736 | tf_op jit(solution)/shard_map/convert_element_type | solution.py:193
  82.8 3.8 %collective-permute-start.23 = (bf16[256,1024]{1,0:T(8,128)(2,1)S(1)}, bf16[256,1024]{1,0:T(8,128)(2,1)S(1)}, u32[]{:S(2)}, u32[]{:S(2)}) collective-permute-start(bf16[256,1024]{1,0:T(8,128)(2,1)S(1)} %get-tuple-element.17), channel_id=1, source_target_pairs={{16,8},{17,9},{18,10},{19,11},{20,12},{21,13},{22,14},{23,15},{24,... | collective-permute-start | bytes 1572872 | tf_op jit(solution)/shard_map/ppermute | solution.py:119
  86.6 2.0 %fusion.36 = f32[512,512]{1,0:T(8,128)S(1)} fusion(bf16[512,1024]{1,0:T(8,128)(2,1)} %collective-permute-done.7, bf16[128,1024]{1,0:T(8,128)(2,1)S(1)} %get-tuple-element.36, bf16[128,1024]{1,0:T(8,128)(2,1)S(1)} %get-tuple-element.34, bf16[128,1024]{1,0:T(8,128)(2,1)S(1)} %get-tuple-element.32, bf16[128,1024]{1,0:T(8,128)(2,1)S(1)} %get-tuple-element.30), kind=kOutput, calls=%fused_computation.94 | convolution fusion | flops 541065216 | bytes 3145728 | tf_op jit(solution)/shard_map/dot_general | solution.py:217
  88.6 2.0 %fusion.38 = (bf16[512,512]{1,0:T(8,128)(2,1)S(1)}, f32[512,512]{1,0:T(8,128)S(1)}) fusion(f32[512,512]{1,0:T(8,128)S(1)} %fusion.36, bf16[512,1024]{1,0:T(8,128)(2,1)} %bitcast.18, bf16[128,1024]{1,0:T(8,128)(2,1)S(1)} %copy-done.8, bf16[128,1024]{1,0:T(8,128)(2,1)S(1)} %copy-done.9, bf16[128,1024]{1,0:T(8,128)(2,1)S(1)} %copy-done.10, ...), kind=kOutput, calls=%fused_computation.96 | convolution fusion | flops 541589504 | bytes 4718592 | tf_op jit(solution)/shard_map/dot_general | solution.py:216
  90.6 2.2 %collective-permute-start.21 = (bf16[256,1024]{1,0:T(8,128)(2,1)S(1)}, bf16[256,1024]{1,0:T(8,128)(2,1)S(1)}, u32[]{:S(2)}, u32[]{:S(2)}) collective-permute-start(bf16[256,1024]{1,0:T(8,128)(2,1)S(1)} %get-tuple-element.16), channel_id=1, source_target_pairs={{0,8},{1,9},{2,10},{3,11},{4,12},{5,13},{6,14},{7,15},{8,16},{9,17... | collective-permute-start | bytes 1572872 | tf_op jit(solution)/shard_map/ppermute | solution.py:119
  92.8 4.5 %collective-permute-done.23 = bf16[256,1024]{1,0:T(8,128)(2,1)S(1)} collective-permute-done((bf16[256,1024]{1,0:T(8,128)(2,1)S(1)}, bf16[256,1024]{1,0:T(8,128)(2,1)S(1)}, u32[]{:S(2)}, u32[]{:S(2)}) %collective-permute-start.23) | collective-permute-done | bytes 524320 | tf_op jit(solution)/shard_map/ppermute | solution.py:119
  97.5 3.5 %collective-permute-start.24 = (bf16[256,1024]{1,0:T(8,128)(2,1)S(1)}, bf16[256,1024]{1,0:T(8,128)(2,1)S(1)}, u32[]{:S(2)}, u32[]{:S(2)}) collective-permute-start(bf16[256,1024]{1,0:T(8,128)(2,1)S(1)} %fusion.14), channel_id=1, source_target_pairs={{8,0},{9,1},{10,2},{11,3},{12,4},{13,5},{14,6},{15,7},{16,8},{17,9... | collective-permute-start | bytes 1572872 | tf_op jit(solution)/shard_map/ppermute | solution.py:119
  101.1 1.6 %collective-permute-start.10 = (bf16[128,512]{1,0:T(8,128)(2,1)S(1)}, bf16[128,512]{1,0:T(8,128)(2,1)S(1)}, u32[]{:S(2)}, u32[]{:S(2)}) collective-permute-start(bf16[128,512]{1,0:T(8,128)(2,1)S(1)} %get-tuple-element.27), channel_id=1, source_target_pairs={{0,6},{1,7},{2,4},{3,5},{4,2},{5,3},{6,0},{7,1},{8,14},{9,15},{10,... | collective-permute-start | bytes 393224 | tf_op jit(solution)/shard_map/ppermute | solution.py:119
  103.2 2.1 %convolution_convert_fusion = bf16[512,1024]{1,0:T(8,128)(2,1)S(1)} fusion(bf16[512,1024]{1,0:T(8,128)(2,1)} %collective-permute-done.7, bf16[128,512]{1,0:T(8,128)(2,1)S(1)} %collective-permute-done.13, bf16[128,512]{1,0:T(8,128)(2,1)} %collective-permute-done.12, bf16[128,512]{1,0:T(8,128)(2,1)} %collective-permute-done.11, bf16[128,512]{1,0:T(8,128)(2,1)S(1)} %bitcast.119), kind=kOutput, calls=%fused_computation.11 | convolution fusion | flops 539492352 | bytes 2621440 | tf_op jit(solution)/shard_map/dot_general | solution.py:208
  105.5 1.5 %collective-permute-start.14 = (bf16[2,128,1024]{2,1,0:T(8,128)(2,1)S(1)}, bf16[2,128,1024]{2,1,0:T(8,128)(2,1)S(1)}, u32[]{:S(2)}, u32[]{:S(2)}) collective-permute-start(bf16[2,128,1024]{2,1,0:T(8,128)(2,1)S(1)} %get-tuple-element.22), channel_id=1, source_target_pairs={{0,4},{1,5},{2,6},{3,7},{4,0},{5,1},{6,2},{7,3},{8,12},{9,13},{10,... | collective-permute-start | bytes 1572872 | tf_op jit(solution)/shard_map/ppermute | solution.py:119
  107.0 1.5 %collective-permute-start.15 = (bf16[2,128,1024]{2,1,0:T(8,128)(2,1)S(1)}, bf16[2,128,1024]{2,1,0:T(8,128)(2,1)S(1)}, u32[]{:S(2)}, u32[]{:S(2)}) collective-permute-start(bf16[2,128,1024]{2,1,0:T(8,128)(2,1)S(1)} %get-tuple-element.23), channel_id=1, source_target_pairs={{0,2},{1,3},{2,0},{3,1},{4,6},{5,7},{6,4},{7,5},{8,10},{9,11},{10,... | collective-permute-start | bytes 1572872 | tf_op jit(solution)/shard_map/ppermute | solution.py:119
  108.5 2.4 %collective-permute-done.24 = bf16[256,1024]{1,0:T(8,128)(2,1)S(1)} collective-permute-done((bf16[256,1024]{1,0:T(8,128)(2,1)S(1)}, bf16[256,1024]{1,0:T(8,128)(2,1)S(1)}, u32[]{:S(2)}, u32[]{:S(2)}) %collective-permute-start.24) | collective-permute-done | bytes 524320 | tf_op jit(solution)/shard_map/ppermute | solution.py:119
  111.0 1.5 %collective-permute-start.16 = (bf16[2,128,1024]{2,1,0:T(8,128)(2,1)S(1)}, bf16[2,128,1024]{2,1,0:T(8,128)(2,1)S(1)}, u32[]{:S(2)}, u32[]{:S(2)}) collective-permute-start(bf16[2,128,1024]{2,1,0:T(8,128)(2,1)S(1)} %get-tuple-element.20), channel_id=1, source_target_pairs={{0,6},{1,7},{2,4},{3,5},{4,2},{5,3},{6,0},{7,1},{8,14},{9,15},{10,... | collective-permute-start | bytes 1572872 | tf_op jit(solution)/shard_map/ppermute | solution.py:119
  112.8 1.5 %collective-permute-start.8 = (bf16[128,512]{1,0:T(8,128)(2,1)S(1)}, bf16[128,512]{1,0:T(8,128)(2,1)S(1)}, u32[]{:S(2)}, u32[]{:S(2)}) collective-permute-start(bf16[128,512]{1,0:T(8,128)(2,1)S(1)} %get-tuple-element.26), channel_id=1, source_target_pairs={{0,4},{1,5},{2,6},{3,7},{4,0},{5,1},{6,2},{7,3},{8,12},{9,13},{10,... | collective-permute-start | bytes 393224 | tf_op jit(solution)/shard_map/ppermute | solution.py:119
  115.7 18.6 %collective-permute-done.8 = bf16[128,512]{1,0:T(8,128)(2,1)S(1)} collective-permute-done((bf16[128,512]{1,0:T(8,128)(2,1)S(1)}, bf16[128,512]{1,0:T(8,128)(2,1)S(1)}, u32[]{:S(2)}, u32[]{:S(2)}) %collective-permute-start.8) | collective-permute-done | bytes 131104 | tf_op jit(solution)/shard_map/ppermute | solution.py:119
  135.1 4.3 %grad_x_blocks.1 = bf16[128,8192]{1,0:T(8,128)(2,1)} custom-call(s32[8]{0:T(128)S(1)} %stack.38.offs, bf16[128,8192]{1,0:T(8,128)(2,1)S(1)} %bitcast.101, f32[1,8192]{1,0:T(1,128)S(1)} %bitcast.103, bf16[2,128,1024]{2,1,0:T(8,128)(2,1)S(1)} %get-tuple-element.21.refs_0_, bf16[2,128,1024]{2,1,0:T(8,128)(2,1)S(1)} %collective-permute-done.14.refs_1_, ...), custom_call_target="tpu_custom_call" | custom-call | tf_op jit(solution)/shard_map/grad_x_blocks/pallas_call | solution.py:79
  139.5 1.1 copy-done.3
  140.5 2.3 %subtract_multiply_fusion = (f32[1,128,2048]{2,1,0:T(8,128)}, f32[1,128,2048]{2,1,0:T(8,128)}, f32[1,128,2048]{2,1,0:T(8,128)}) fusion(f32[1,128,2048]{2,1,0:T(8,128)S(1)} %copy-done.3, f32[128]{0:T(128)S(1)} %compare_convert_fusion, f32[1,128,1024]{2,1,0:T(8,128)S(1)} %get-tuple-element.25, f32[1,128,1024]{2,1,0:T(8,128)S(1)} %get-tuple-element.24, ...), kind=kLoop, calls=%fused_computation.33 | loop fusion | flops 4718592 | bytes 7340544 | tf_op jit(solution)/shard_map/mul | solution.py:230
  (80 shorter events, 15.5 us)
Async XLA Ops:
  0.6 7.6 %copy-start.2 = (f32[8192]{0:T(1024)S(1)}, f32[8192]{0:T(1024)}, u32[]{:S(2)}) copy-start(f32[8192]{0:T(1024)} %param.9) | copy-start | bytes 98308
  0.6 21.0 %collective-permute-start.13 = (bf16[128,512]{1,0:T(8,128)(2,1)}, bf16[128,512]{1,0:T(8,128)(2,1)S(1)}, u32[]{:S(2)}, u32[]{:S(2)}) collective-permute-start(bf16[128,512]{1,0:T(8,128)(2,1)} %bitcast.114), channel_id=1, source_target_pairs={{0,6},{1,7},{2,4},{3,5},{4,2},{5,3},{6,0},{7,1},{8,14},{9,15},{10,... | collective-permute-start | bytes 393224 | tf_op jit(solution)/shard_map/ppermute | solution.py:119
  3.2 20.1 %collective-permute-start.12 = (bf16[128,512]{1,0:T(8,128)(2,1)}, bf16[128,512]{1,0:T(8,128)(2,1)}, u32[]{:S(2)}, u32[]{:S(2)}) collective-permute-start(bf16[128,512]{1,0:T(8,128)(2,1)} %bitcast.115), channel_id=1, source_target_pairs={{0,2},{1,3},{2,0},{3,1},{4,6},{5,7},{6,4},{7,5},{8,10},{9,11},{10,... | collective-permute-start | bytes 393224 | tf_op jit(solution)/shard_map/ppermute | solution.py:119
  3.7 14.9 %collective-permute-start.11 = (bf16[128,512]{1,0:T(8,128)(2,1)}, bf16[128,512]{1,0:T(8,128)(2,1)}, u32[]{:S(2)}, u32[]{:S(2)}) collective-permute-start(bf16[128,512]{1,0:T(8,128)(2,1)} %bitcast.116), channel_id=1, source_target_pairs={{0,4},{1,5},{2,6},{3,7},{4,0},{5,1},{6,2},{7,3},{8,12},{9,13},{10,... | collective-permute-start | bytes 393224 | tf_op jit(solution)/shard_map/ppermute | solution.py:119
  5.9 8.8 %copy-start.6 = (bf16[1,128,512]{2,1,0:T(8,128)(2,1)S(1)}, bf16[1,128,512]{2,1,0:T(8,128)(2,1)}, u32[]{:S(2)}) copy-start(bf16[1,128,512]{2,1,0:T(8,128)(2,1)} %param.11) | copy-start | bytes 393220
  6.6 8.8 %copy-start.11 = (s32[512]{0:T(512)S(1)}, s32[512]{0:T(512)}, u32[]{:S(2)}) copy-start(s32[512]{0:T(512)} %param.12) | copy-start | bytes 6148
  6.6 9.8 %collective-permute-start.3 = (bf16[64,1024]{1,0:T(8,128)(2,1)}, bf16[64,1024]{1,0:T(8,128)(2,1)}, u32[]{:S(2)}, u32[]{:S(2)}) collective-permute-start(bf16[64,1024]{1,0:T(8,128)(2,1)} %bitcast.99), channel_id=1, source_target_pairs={{0,4},{1,5},{2,6},{3,7},{4,0},{5,1},{6,2},{7,3},{8,12},{9,13},{10,... | collective-permute-start | bytes 393224 | tf_op jit(solution)/shard_map/ppermute | solution.py:119
  8.2 1.6 %copy-start = (bf16[1,128,8192]{2,1,0:T(8,128)(2,1)S(1)}, bf16[1,128,8192]{2,1,0:T(8,128)(2,1)}, u32[]{:S(2)}) copy-start(bf16[1,128,8192]{2,1,0:T(8,128)(2,1)} %param.8) | copy-start | bytes 6291460
  11.7 15.9 %collective-permute-start.2 = (bf16[2,128,1024]{2,1,0:T(8,128)(2,1)S(1)}, bf16[2,128,1024]{2,1,0:T(8,128)(2,1)S(1)}, u32[]{:S(2)}, u32[]{:S(2)}) collective-permute-start(bf16[2,128,1024]{2,1,0:T(8,128)(2,1)S(1)} %get-tuple-element.12), channel_id=1, source_target_pairs={{0,6},{1,7},{2,4},{3,5},{4,2},{5,3},{6,0},{7,1},{8,14},{9,15},{10,... | collective-permute-start | bytes 1572872 | tf_op jit(solution)/shard_map/ppermute | solution.py:119
  16.4 20.0 %collective-permute-start.1 = (bf16[2,128,1024]{2,1,0:T(8,128)(2,1)S(1)}, bf16[2,128,1024]{2,1,0:T(8,128)(2,1)S(1)}, u32[]{:S(2)}, u32[]{:S(2)}) collective-permute-start(bf16[2,128,1024]{2,1,0:T(8,128)(2,1)S(1)} %get-tuple-element.11), channel_id=1, source_target_pairs={{0,2},{1,3},{2,0},{3,1},{4,6},{5,7},{6,4},{7,5},{8,10},{9,11},{10,... | collective-permute-start | bytes 1572872 | tf_op jit(solution)/shard_map/ppermute | solution.py:119
  18.6 18.7 %collective-permute-start = (bf16[2,128,1024]{2,1,0:T(8,128)(2,1)S(1)}, bf16[2,128,1024]{2,1,0:T(8,128)(2,1)S(1)}, u32[]{:S(2)}, u32[]{:S(2)}) collective-permute-start(bf16[2,128,1024]{2,1,0:T(8,128)(2,1)S(1)} %get-tuple-element.10), channel_id=1, source_target_pairs={{0,4},{1,5},{2,6},{3,7},{4,0},{5,1},{6,2},{7,3},{8,12},{9,13},{10,... | collective-permute-start | bytes 1572872 | tf_op jit(solution)/shard_map/ppermute | solution.py:119
  21.7 29.3 %collective-permute-start.4 = (bf16[128,1024]{1,0:T(8,128)(2,1)}, bf16[128,1024]{1,0:T(8,128)(2,1)}, u32[]{:S(2)}, u32[]{:S(2)}) collective-permute-start(bf16[128,1024]{1,0:T(8,128)(2,1)} %pad_maximum_fusion.4), channel_id=1, source_target_pairs={{0,8},{1,9},{2,10},{3,11},{4,12},{5,13},{6,14},{7,15},{8,16},{9,17... | collective-permute-start | bytes 786440 | tf_op jit(solution)/shard_map/ppermute | solution.py:119
  23.2 29.4 %collective-permute-start.5 = (bf16[128,1024]{1,0:T(8,128)(2,1)}, bf16[128,1024]{1,0:T(8,128)(2,1)}, u32[]{:S(2)}, u32[]{:S(2)}) collective-permute-start(bf16[128,1024]{1,0:T(8,128)(2,1)} %pad_maximum_fusion.4), channel_id=1, source_target_pairs={{0,16},{1,17},{2,18},{3,19},{4,20},{5,21},{6,22},{7,23},{8,24},{9,... | collective-permute-start | bytes 786440 | tf_op jit(solution)/shard_map/ppermute | solution.py:119
  27.6 26.8 %collective-permute-start.6 = (bf16[128,1024]{1,0:T(8,128)(2,1)}, bf16[128,1024]{1,0:T(8,128)(2,1)}, u32[]{:S(2)}, u32[]{:S(2)}) collective-permute-start(bf16[128,1024]{1,0:T(8,128)(2,1)} %pad_maximum_fusion.4), channel_id=1, source_target_pairs={{0,24},{1,25},{2,26},{3,27},{4,28},{5,29},{6,30},{7,31},{8,0},{9,1... | collective-permute-start | bytes 786440 | tf_op jit(solution)/shard_map/ppermute | solution.py:119
  28.7 9.8 %copy-start.12 = (bf16[1024,512]{1,0:T(8,128)(2,1)S(1)}, bf16[1024,512]{1,0:T(8,128)(2,1)}, u32[]{:S(2)}) copy-start(bf16[1024,512]{1,0:T(8,128)(2,1)} %constant_dynamic-update-slice_fusion.2) | copy-start | bytes 3145732
  36.4 6.1 %collective-permute-start.17 = (bf16[512,512]{1,0:T(8,128)(2,1)S(1)}, bf16[512,512]{1,0:T(8,128)(2,1)S(1)}, u32[]{:S(2)}, u32[]{:S(2)}) collective-permute-start(bf16[512,512]{1,0:T(8,128)(2,1)S(1)} %pad_maximum_fusion.3), channel_id=1, source_target_pairs={{0,1},{1,0},{2,3},{3,2},{4,5},{5,4},{6,7},{7,6},{8,9},{9,8},{10,11... | collective-permute-start | bytes 1572872 | tf_op jit(solution)/shard_map/ppermute | solution.py:119
  38.1 4.5 %collective-permute-start.18 = (bf16[512,1024]{1,0:T(8,128)(2,1)S(1)}, bf16[512,1024]{1,0:T(8,128)(2,1)S(1)}, u32[]{:S(2)}, u32[]{:S(2)}) collective-permute-start(bf16[512,1024]{1,0:T(8,128)(2,1)S(1)} %pad_maximum_fusion), channel_id=1, source_target_pairs={{0,1},{1,0},{2,3},{3,2},{4,5},{5,4},{6,7},{7,6},{8,9},{9,8},{10,11... | collective-permute-start | bytes 3145736 | tf_op jit(solution)/shard_map/ppermute | solution.py:119
  42.6 1.3 copy-start.13
  50.3 7.1 %collective-permute-start.19 = (bf16[256,1024]{1,0:T(8,128)(2,1)S(1)}, bf16[256,1024]{1,0:T(8,128)(2,1)S(1)}, u32[]{:S(2)}, u32[]{:S(2)}) collective-permute-start(bf16[256,1024]{1,0:T(8,128)(2,1)S(1)} %get-tuple-element.18), channel_id=1, source_target_pairs={{0,8},{1,9},{2,10},{3,11},{4,12},{5,13},{6,14},{7,15}} | collective-permute-start | bytes 1572872 | tf_op jit(solution)/shard_map/ppermute | solution.py:119
  56.0 30.6 %collective-permute-start.7 = (bf16[512,1024]{1,0:T(8,128)(2,1)}, bf16[512,1024]{1,0:T(8,128)(2,1)}, u32[]{:S(2)}, u32[]{:S(2)}) collective-permute-start(bf16[512,1024]{1,0:T(8,128)(2,1)} %bitcast.18), channel_id=1, source_target_pairs={{0,1},{1,0},{2,3},{3,2},{4,5},{5,4},{6,7},{7,6},{8,9},{9,8},{10,11... | collective-permute-start | bytes 3145736 | tf_op jit(solution)/shard_map/ppermute | solution.py:119
  56.1 16.4 %collective-permute-start.22 = (bf16[256,1024]{1,0:T(8,128)(2,1)}, bf16[256,1024]{1,0:T(8,128)(2,1)}, u32[]{:S(2)}, u32[]{:S(2)}) collective-permute-start(bf16[256,1024]{1,0:T(8,128)(2,1)} %get-tuple-element.19), channel_id=1, source_target_pairs={{24,16},{25,17},{26,18},{27,19},{28,20},{29,21},{30,22},{31,23}} | collective-permute-start | bytes 1572872 | tf_op jit(solution)/shard_map/ppermute | solution.py:119
  58.4 22.7 %collective-permute-start.20 = (bf16[256,1024]{1,0:T(8,128)(2,1)}, bf16[256,1024]{1,0:T(8,128)(2,1)}, u32[]{:S(2)}, u32[]{:S(2)}) collective-permute-start(bf16[256,1024]{1,0:T(8,128)(2,1)} %fusion.15), channel_id=1, source_target_pairs={{0,8},{1,9},{2,10},{3,11},{4,12},{5,13},{6,14},{7,15},{8,16},{9,17... | collective-permute-start | bytes 1572872 | tf_op jit(solution)/shard_map/ppermute | solution.py:119
  82.7 5.8 %copy-start.7 = (bf16[128,1024]{1,0:T(8,128)(2,1)S(1)}, bf16[128,1024]{1,0:T(8,128)(2,1)}, u32[]{:S(2)}) copy-start(bf16[128,1024]{1,0:T(8,128)(2,1)} %get-tuple-element.29) | copy-start | bytes 786436
  82.8 5.8 %copy-start.8 = (bf16[128,1024]{1,0:T(8,128)(2,1)S(1)}, bf16[128,1024]{1,0:T(8,128)(2,1)}, u32[]{:S(2)}) copy-start(bf16[128,1024]{1,0:T(8,128)(2,1)} %get-tuple-element.35) | copy-start | bytes 786436
  82.8 5.8 %copy-start.9 = (bf16[128,1024]{1,0:T(8,128)(2,1)S(1)}, bf16[128,1024]{1,0:T(8,128)(2,1)}, u32[]{:S(2)}) copy-start(bf16[128,1024]{1,0:T(8,128)(2,1)} %get-tuple-element.33) | copy-start | bytes 786436
  82.8 5.8 %copy-start.10 = (bf16[128,1024]{1,0:T(8,128)(2,1)S(1)}, bf16[128,1024]{1,0:T(8,128)(2,1)}, u32[]{:S(2)}) copy-start(bf16[128,1024]{1,0:T(8,128)(2,1)} %get-tuple-element.31) | copy-start | bytes 786436
  82.8 14.5 %collective-permute-start.23 = (bf16[256,1024]{1,0:T(8,128)(2,1)S(1)}, bf16[256,1024]{1,0:T(8,128)(2,1)S(1)}, u32[]{:S(2)}, u32[]{:S(2)}) collective-permute-start(bf16[256,1024]{1,0:T(8,128)(2,1)S(1)} %get-tuple-element.17), channel_id=1, source_target_pairs={{16,8},{17,9},{18,10},{19,11},{20,12},{21,13},{22,14},{23,15},{24,... | collective-permute-start | bytes 1572872 | tf_op jit(solution)/shard_map/ppermute | solution.py:119
  90.6 16.4 %collective-permute-start.21 = (bf16[256,1024]{1,0:T(8,128)(2,1)S(1)}, bf16[256,1024]{1,0:T(8,128)(2,1)S(1)}, u32[]{:S(2)}, u32[]{:S(2)}) collective-permute-start(bf16[256,1024]{1,0:T(8,128)(2,1)S(1)} %get-tuple-element.16), channel_id=1, source_target_pairs={{0,8},{1,9},{2,10},{3,11},{4,12},{5,13},{6,14},{7,15},{8,16},{9,17... | collective-permute-start | bytes 1572872 | tf_op jit(solution)/shard_map/ppermute | solution.py:119
  97.5 13.5 %collective-permute-start.24 = (bf16[256,1024]{1,0:T(8,128)(2,1)S(1)}, bf16[256,1024]{1,0:T(8,128)(2,1)S(1)}, u32[]{:S(2)}, u32[]{:S(2)}) collective-permute-start(bf16[256,1024]{1,0:T(8,128)(2,1)S(1)} %fusion.14), channel_id=1, source_target_pairs={{8,0},{9,1},{10,2},{11,3},{12,4},{13,5},{14,6},{15,7},{16,8},{17,9... | collective-permute-start | bytes 1572872 | tf_op jit(solution)/shard_map/ppermute | solution.py:119
  101.1 11.7 %collective-permute-start.10 = (bf16[128,512]{1,0:T(8,128)(2,1)S(1)}, bf16[128,512]{1,0:T(8,128)(2,1)S(1)}, u32[]{:S(2)}, u32[]{:S(2)}) collective-permute-start(bf16[128,512]{1,0:T(8,128)(2,1)S(1)} %get-tuple-element.27), channel_id=1, source_target_pairs={{0,6},{1,7},{2,4},{3,5},{4,2},{5,3},{6,0},{7,1},{8,14},{9,15},{10,... | collective-permute-start | bytes 393224 | tf_op jit(solution)/shard_map/ppermute | solution.py:119
  102.7 11.7 %collective-permute-start.9 = (bf16[128,512]{1,0:T(8,128)(2,1)S(1)}, bf16[128,512]{1,0:T(8,128)(2,1)S(1)}, u32[]{:S(2)}, u32[]{:S(2)}) collective-permute-start(bf16[128,512]{1,0:T(8,128)(2,1)S(1)} %get-tuple-element.28), channel_id=1, source_target_pairs={{0,2},{1,3},{2,0},{3,1},{4,6},{5,7},{6,4},{7,5},{8,10},{9,11},{10,... | collective-permute-start | bytes 393224 | tf_op jit(solution)/shard_map/ppermute | solution.py:119
  105.5 29.6 %copy-start.1 = (bf16[1,128,8192]{2,1,0:T(8,128)(2,1)S(1)}, bf16[1,128,8192]{2,1,0:T(8,128)(2,1)}, u32[]{:S(2)}) copy-start(bf16[1,128,8192]{2,1,0:T(8,128)(2,1)} %param.8) | copy-start | bytes 6291460
  105.5 29.5 %collective-permute-start.14 = (bf16[2,128,1024]{2,1,0:T(8,128)(2,1)S(1)}, bf16[2,128,1024]{2,1,0:T(8,128)(2,1)S(1)}, u32[]{:S(2)}, u32[]{:S(2)}) collective-permute-start(bf16[2,128,1024]{2,1,0:T(8,128)(2,1)S(1)} %get-tuple-element.22), channel_id=1, source_target_pairs={{0,4},{1,5},{2,6},{3,7},{4,0},{5,1},{6,2},{7,3},{8,12},{9,13},{10,... | collective-permute-start | bytes 1572872 | tf_op jit(solution)/shard_map/ppermute | solution.py:119
  107.0 28.0 %collective-permute-start.15 = (bf16[2,128,1024]{2,1,0:T(8,128)(2,1)S(1)}, bf16[2,128,1024]{2,1,0:T(8,128)(2,1)S(1)}, u32[]{:S(2)}, u32[]{:S(2)}) collective-permute-start(bf16[2,128,1024]{2,1,0:T(8,128)(2,1)S(1)} %get-tuple-element.23), channel_id=1, source_target_pairs={{0,2},{1,3},{2,0},{3,1},{4,6},{5,7},{6,4},{7,5},{8,10},{9,11},{10,... | collective-permute-start | bytes 1572872 | tf_op jit(solution)/shard_map/ppermute | solution.py:119
  111.0 24.1 %collective-permute-start.16 = (bf16[2,128,1024]{2,1,0:T(8,128)(2,1)S(1)}, bf16[2,128,1024]{2,1,0:T(8,128)(2,1)S(1)}, u32[]{:S(2)}, u32[]{:S(2)}) collective-permute-start(bf16[2,128,1024]{2,1,0:T(8,128)(2,1)S(1)} %get-tuple-element.20), channel_id=1, source_target_pairs={{0,6},{1,7},{2,4},{3,5},{4,2},{5,3},{6,0},{7,1},{8,14},{9,15},{10,... | collective-permute-start | bytes 1572872 | tf_op jit(solution)/shard_map/ppermute | solution.py:119
  112.8 21.5 %collective-permute-start.8 = (bf16[128,512]{1,0:T(8,128)(2,1)S(1)}, bf16[128,512]{1,0:T(8,128)(2,1)S(1)}, u32[]{:S(2)}, u32[]{:S(2)}) collective-permute-start(bf16[128,512]{1,0:T(8,128)(2,1)S(1)} %get-tuple-element.26), channel_id=1, source_target_pairs={{0,4},{1,5},{2,6},{3,7},{4,0},{5,1},{6,2},{7,3},{8,12},{9,13},{10,... | collective-permute-start | bytes 393224 | tf_op jit(solution)/shard_map/ppermute | solution.py:119
  114.3 25.0 %collective-permute-start.25 = (bf16[128,1024]{1,0:T(8,128)(2,1)S(1)}, bf16[128,1024]{1,0:T(8,128)(2,1)S(1)}, u32[]{:S(2)}, u32[]{:S(2)}) collective-permute-start(bf16[128,1024]{1,0:T(8,128)(2,1)S(1)} %fusion.30), channel_id=1, source_target_pairs={{0,4},{1,5},{2,6},{3,7},{4,0},{5,1},{6,2},{7,3},{8,12},{9,13},{10,... | collective-permute-start | bytes 786440 | tf_op jit(solution)/shard_map/ppermute | solution.py:119
  135.0 4.4 %copy-start.4 = (f32[1,128,2048]{2,1,0:T(8,128)S(1)}, f32[1,128,2048]{2,1,0:T(8,128)}, u32[]{:S(2)}) copy-start(f32[1,128,2048]{2,1,0:T(8,128)} %param.14) | copy-start | bytes 3145732
  135.0 4.4 %copy-start.5 = (f32[1,128,2048]{2,1,0:T(8,128)S(1)}, f32[1,128,2048]{2,1,0:T(8,128)}, u32[]{:S(2)}) copy-start(f32[1,128,2048]{2,1,0:T(8,128)} %param.15) | copy-start | bytes 3145732
  139.3 1.2 copy-start.3

commit v2 on v0

v2 whole, which is shorter than its diff:
```python
import functools

import jax
import jax.numpy as jnp
from jax import lax
from jax.experimental import pallas as pl
from jax.experimental.pallas import tpu as pltpu
from jax.sharding import PartitionSpec as P

beta_one = 0.9
beta_two = 0.95
learn_rate = 0.001
adam_eps = 1e-08
bias_one = 1.0 - 0.9**10
bias_two = 1.0 - 0.95**10
norm_eps = 1e-05

bf16 = jnp.bfloat16
f32 = jnp.float32


def cost(flops, moved):
    return pl.CostEstimate(flops=flops, bytes_accessed=moved, transcendentals=0)


def limit(mib):
    return pltpu.CompilerParams(vmem_limit_bytes=mib * 1024 * 1024)


def column_block(k, j, width):
    seq = lax.axis_index("seq") ^ (k >> 1 << 1) ^ j
    x = (lax.axis_index("dp") % 2) ^ (k & 1)
    return pl.ds(pl.multiple_of((seq * 2 + x) * width, width), width)


def norm_kernel(tok_ref, gain_ref, *out_refs):
    width = out_refs[0].shape[-1]
    tok = tok_ref[...].astype(f32)
    inv_rms = lax.rsqrt(jnp.mean(tok * tok, axis=-1, keepdims=True) + norm_eps)
    for k, out_ref in enumerate(out_refs):
        for j in range(2):
            cols = column_block(k, j, width)
            scaled = tok_ref[:, cols].astype(f32) * inv_rms
            out_ref[j] = (scaled * gain_ref[:, cols]).astype(bf16)


def norm_blocks(tokens, gain, chips, width):
    rows, model = tokens.shape
    step = min(rows, 32)
    return pl.pallas_call(
        norm_kernel,
        grid=(rows // step,),
        in_specs=[
            pl.BlockSpec((step, model), lambda i: (i, 0)),
            pl.BlockSpec((1, model), lambda i: (0, 0)),
        ],
        out_specs=[pl.BlockSpec((2, step, width), lambda i: (0, i, 0))] * chips,
        out_shape=[jax.ShapeDtypeStruct((2, rows, width), bf16)] * chips,
        compiler_params=limit(24),
        cost_estimate=cost(8 * rows * model, 4 * rows * model),
        name="norm_blocks",
    )(tokens, gain)


def grad_x_kernel(tok_ref, gain_ref, *refs):
    grad_refs, out_ref = refs[:-1], refs[-1]
    model = tok_ref.shape[-1]
    width = grad_refs[0].shape[-1]
    tok = tok_ref[...].astype(f32)
    inv_rms = lax.rsqrt(jnp.mean(tok * tok, axis=-1, keepdims=True) + norm_eps)
    total = jnp.zeros((tok.shape[0], 1), f32)
    for k, grad_ref in enumerate(grad_refs):
        for j in range(2):
            cols = column_block(k, j, width)
            weighted = gain_ref[:, cols] * grad_ref[j].astype(f32)
            scaled = tok_ref[:, cols].astype(f32) * inv_rms
            total += jnp.sum(weighted * scaled, axis=-1, keepdims=True)
    mean = total / model
    for k, grad_ref in enumerate(grad_refs):
        for j in range(2):
            cols = column_block(k, j, width)
            weighted = gain_ref[:, cols] * grad_ref[j].astype(f32)
            scaled = tok_ref[:, cols].astype(f32) * inv_rms
            out_ref[:, cols] = (inv_rms * (weighted - scaled * mean)).astype(bf16)


def grad_x_blocks(tokens, gain, grads):
    rows, model = tokens.shape
    width = grads[0].shape[-1]
    step = min(rows, 32)
    return pl.pallas_call(
        grad_x_kernel,
        grid=(rows // step,),
        in_specs=[
            pl.BlockSpec((step, model), lambda i: (i, 0)),
            pl.BlockSpec((1, model), lambda i: (0, 0)),
        ]
        + [pl.BlockSpec((2, step, width), lambda i: (0, i, 0))] * len(grads),
        out_specs=pl.BlockSpec((step, model), lambda i: (i, 0)),
        out_shape=jax.ShapeDtypeStruct((rows, model), bf16),
        compiler_params=limit(24),
        cost_estimate=cost(16 * rows * model, 6 * rows * model),
        name="grad_x_blocks",
    )(tokens, gain, *grads)


def select_kernel(slots, owner_row_ref, owner_col_ref, *refs):
    grad_refs, out_ref, held = refs[:-2], refs[-2], refs[-1]
    rows = grad_refs[0].shape[0]
    feats = owner_row_ref.shape[1]
    owner = owner_row_ref[...]
    lower = lax.broadcasted_iota(jnp.int32, (feats, feats), 0) < lax.broadcasted_iota(
        jnp.int32, (feats, feats), 1
    )
    same = (owner_col_ref[...] == owner) & lower
    place = jnp.sum(same.astype(f32), axis=0, keepdims=True).astype(jnp.int32)
    own_x = lax.axis_index("dp") % 2
    slot = (owner ^ own_x) * slots + place
    for i, grad_ref in enumerate(grad_refs):
        held[i * rows : (i + 1) * rows, :] = grad_ref[...]
    step = 256
    for at in range(0, out_ref.shape[0], step):
        index = at + lax.broadcasted_iota(jnp.int32, (step, feats), 0)
        chosen = (index == slot).astype(f32).astype(bf16)
        out_ref[at : at + step, :] = lax.dot_general(
            chosen, held[...], (((1,), (1,)), ((), ())), preferred_element_type=f32
        ).astype(bf16)


def select_grads(owner, grads, groups, slots):
    feats = owner.shape[0]
    total = grads[0].shape[0] * len(grads)
    return pl.pallas_call(
        functools.partial(select_kernel, slots),
        out_shape=jax.ShapeDtypeStruct((groups * slots, total), bf16),
        scratch_shapes=[pltpu.VMEM((total, feats), bf16)],
        compiler_params=limit(40),
        cost_estimate=cost(2 * groups * slots * total * feats, 2 * groups * slots * total),
        name="select_grads",
    )(owner[None, :], owner[:, None], *grads)


def weight_kernel(planes, sel_ref, *refs):
    count = 2 * planes
    piece_refs, out_refs, held = refs[: -count - 1], refs[-count - 1 : -1], refs[-1]
    rights, lefts = out_refs[: planes - 1], out_refs[planes - 1 : 2 * planes - 2]
    mine_ref, other_ref = out_refs[-2:]
    rows = piece_refs[0].shape[1]
    block = sel_ref.shape[0] // planes
    slots = block // 2
    z = lax.axis_index("dp") // 2
    for i, ref in enumerate(piece_refs):
        held[i * rows : (i + 1) * rows, :] = ref[0]

    def product(plane, part, height):
        at = pl.multiple_of(plane * block + part * height, height)
        return jnp.dot(sel_ref[pl.ds(at, height), :], held[...], preferred_element_type=f32)

    for step in range(1, planes):
        far = planes - step

        @pl.when(z + far < planes)
        def _():
            rights[step - 1][...] = product(z + far, 0, block).astype(bf16)

        @pl.when(z - far >= 0)
        def _():
            lefts[step - 1][...] = product(z - far, 0, block).astype(bf16)

    other_ref[...] = product(z, 1, slots).astype(bf16)
    mine_ref[...] = product(z, 0, slots)


def weight_blocks(selected, own_pieces, far_pieces, planes):
    slots_all, total = selected.shape
    _, rows, width = own_pieces[0].shape
    block = slots_all // planes
    shapes = [jax.ShapeDtypeStruct((block, width), bf16)] * (2 * planes - 2) + [
        jax.ShapeDtypeStruct((block // 2, width), f32),
        jax.ShapeDtypeStruct((block // 2, width), bf16),
    ]
    whole = lambda shape: pl.BlockSpec(shape, lambda i: (0,) * len(shape))
    outs = pl.pallas_call(
        functools.partial(weight_kernel, planes),
        grid=(1,),
        in_specs=[whole(selected.shape)]
        + [pl.BlockSpec((1, rows, width), lambda i: (0, 0, 0))] * len(own_pieces)
        + [pl.BlockSpec((1, rows, width), lambda i: (1, 0, 0))] * len(far_pieces),
        out_specs=[whole(s.shape) for s in shapes],
        out_shape=shapes,
        scratch_shapes=[pltpu.VMEM((total, width), bf16)],
        compiler_params=limit(40),
        cost_estimate=cost(2 * slots_all * total * width, 4 * total * width),
        name="weight_blocks",
    )(selected, *own_pieces, *far_pieces)
    return outs[: planes - 1], outs[planes - 1 : 2 * planes - 2], outs[-2], outs[-1]


def gather_weight(planes, piece_refs, held):
    dp = lax.axis_index("dp")
    own_x, own_z = dp % 2, dp // 2
    for j in range(2):
        for turn in range(planes):
            ref = piece_refs[j * planes + turn]
            share = ref.shape[0] // 2
            plane = lax.rem(own_z + planes - turn, planes)
            for i in range(2):
                at = pl.multiple_of((plane * 2 + (own_x ^ i)) * share, share)
                held[j, pl.ds(at, share), :] = ref[i * share : (i + 1) * share, :]


def grad_normed_kernel(planes, chips, *refs):
    grad_refs, piece_refs, out_refs, held = (
        refs[:chips],
        refs[chips : chips + 2 * planes],
        refs[chips + 2 * planes : -1],
        refs[-1],
    )
    gather_weight(planes, piece_refs, held)
    for k in (*range(1, chips), 0):
        for j in range(2):
            out_refs[k][j] = jnp.dot(
                grad_refs[k][...], held[j], preferred_element_type=f32
            ).astype(bf16)


def grad_normed_blocks(grads, weights, planes):
    chips = len(grads)
    rows, feats = grads[0].shape
    width = weights[0].shape[-1]
    return pl.pallas_call(
        functools.partial(grad_normed_kernel, planes, chips),
        out_shape=[jax.ShapeDtypeStruct((2, rows, width), bf16)] * chips,
        scratch_shapes=[pltpu.VMEM((2, feats, width), bf16)],
        compiler_params=limit(40),
        cost_estimate=cost(4 * chips * rows * feats * width, 4 * chips * rows * width),
        name="grad_normed_blocks",
    )(*grads, *weights)


def values_kernel(planes, chips, *refs):
    piece_refs, weight_refs, out_refs, held = (
        refs[:chips],
        refs[chips : chips + 2 * planes],
        refs[chips + 2 * planes : -1],
        refs[-1],
    )
    gather_weight(planes, weight_refs, held)
    dims = (((1,), (1,)), ((), ()))
    for k in (*range(1, chips), 0):
        part = lax.dot_general(piece_refs[k][0], held[0], dims, preferred_element_type=f32)
        part += lax.dot_general(piece_refs[k][1], held[1], dims, preferred_element_type=f32)
        out_refs[k][...] = part.astype(out_refs[k].dtype)


def value_parts(pieces, weights, planes, feats):
    chips = len(pieces)
    _, rows, width = pieces[0].shape
    return pl.pallas_call(
        functools.partial(values_kernel, planes, chips),
        out_shape=[
            jax.ShapeDtypeStruct((rows, feats), bf16 if k else f32) for k in range(chips)
        ],
        scratch_shapes=[pltpu.VMEM((2, feats, width), bf16)],
        compiler_params=limit(40),
        cost_estimate=cost(4 * chips * rows * feats * width, 4 * chips * rows * width),
        name="value_parts",
    )(*pieces, *weights)


def relay_kernel(a_ref, b_ref, c_ref, d_ref, *out_refs):
    half = len(out_refs) // 2
    for add_ref, got_ref, outs in (
        (a_ref, b_ref, out_refs[:half]),
        (c_ref, d_ref, out_refs[half:]),
    ):
        height = outs[0].shape[0]
        for i, out_ref in enumerate(outs):
            part = slice(i * height, (i + 1) * height)
            total = add_ref[part, :].astype(f32) + got_ref[part, :].astype(f32)
            out_ref[...] = total.astype(bf16)


def relay(right, got_right, left, got_left, parts):
    height, width = right.shape
    outs = pl.pallas_call(
        relay_kernel,
        out_shape=[jax.ShapeDtypeStruct((height // parts, width), bf16)] * (2 * parts),
        compiler_params=limit(16),
        cost_estimate=cost(2 * height * width, 12 * height * width),
        name="relay",
    )(right, got_right, left, got_left)
    return outs[:parts], outs[parts:]


def adam_kernel(token_total, owner_ref, *refs):
    part_refs, state_refs, out_refs = refs[:6], refs[6:9], refs[9:]
    master_ref, moment1_ref, moment2_ref = state_refs
    width = part_refs[0].shape[-1]
    step = part_refs[0].shape[0]
    dp = lax.axis_index("dp")
    owned = (owner_ref[...] == dp).astype(f32)
    count = jnp.sum(owned, axis=1, keepdims=True)
    index = pl.program_id(0) * step + lax.broadcasted_iota(jnp.int32, (step, 1), 0)
    occupied = (index.astype(f32) < count).astype(f32)
    for i in range(2):
        total = part_refs[3 * i][...].astype(f32)
        total += part_refs[3 * i + 1][...].astype(f32)
        total += part_refs[3 * i + 2][...].astype(f32)
        cols = pl.ds(pl.multiple_of(((dp % 2) ^ i) * width, width), width)
        slot_grad = total / token_total
        new_moment1 = (
            beta_one * moment1_ref[:, cols] + (1.0 - beta_one) * slot_grad
        ) * occupied
        new_moment2 = (
            beta_two * moment2_ref[:, cols] + (1.0 - beta_two) * slot_grad * slot_grad
        ) * occupied
        step_dir = new_moment1 / bias_one / (jnp.sqrt(new_moment2 / bias_two) + adam_eps)
        out_refs[0][:, cols] = (master_ref[:, cols] - learn_rate * step_dir) * occupied
        out_refs[1][:, cols] = new_moment1
        out_refs[2][:, cols] = new_moment2


def adam(owner, parts, states, token_total):
    slots, cols = states[0].shape
    width = parts[0].shape[-1]
    step = min(slots, 32)
    return pl.pallas_call(
        functools.partial(adam_kernel, token_total),
        grid=(slots // step,),
        in_specs=[pl.BlockSpec((1, owner.shape[0]), lambda i: (0, 0))]
        + [pl.BlockSpec((step, width), lambda i: (i, 0))] * 6
        + [pl.BlockSpec((step, cols), lambda i: (i, 0))] * 3,
        out_specs=[pl.BlockSpec((step, cols), lambda i: (i, 0))] * 3,
        out_shape=[jax.ShapeDtypeStruct((slots, cols), f32)] * 3,
        compiler_params=limit(24),
        cost_estimate=cost(20 * slots * cols, 30 * slots * cols),
        name="adam",
    )(owner[None, :], *parts, *states)


def on_device(groups, seqs, tokens, gain, w_t, grad_values, owner, master, moment1, moment2):
    planes = groups // 2
    chips = seqs
    tokens, value_grad = tokens[0], grad_values[0]
    rows, model = tokens.shape
    feats = owner.shape[0]
    slots = master.shape[1]
    width = model // (2 * seqs)
    own_x = lax.axis_index("dp") % 2

    def permute(value, target):
        pairs = []
        for dp in range(groups):
            for seq in range(seqs):
                to = target(dp, seq)
                if to is not None:
                    pairs.append((dp * seqs + seq, to[0] * seqs + to[1]))
        return lax.ppermute(value, ("dp", "seq"), pairs)

    def to_chip(value, k):
        return permute(value, lambda dp, seq: (dp ^ (k & 1), seq ^ (k >> 1 << 1)))

    def to_core(value):
        return permute(value, lambda dp, seq: (dp, seq ^ 1))

    def to_x(value):
        return permute(value, lambda dp, seq: (dp ^ 1, seq))

    def to_plane(value, turn):
        return permute(value, lambda dp, seq: ((dp + 2 * turn) % groups, seq))

    def along(value, step, way, flip=0):
        def target(dp, seq):
            z = dp // 2 if way > 0 else planes - 1 - dp // 2
            return ((dp + 2 * way) ^ flip, seq) if z < step else None

        return permute(value, target)

    w_keep = lax.dynamic_slice_in_dim(w_t, own_x * width, width, 1)
    w_got = to_x(lax.dynamic_slice_in_dim(w_t, (1 - own_x) * width, width, 1))

    grads = [value_grad] + [to_chip(value_grad, k) for k in range(1, chips)]
    grads_far = [to_core(g) for g in grads]

    gain_row = gain[None, :]
    normed = norm_blocks(tokens, gain_row, chips, width)
    normed = [normed[0]] + [to_chip(normed[k], k) for k in range(1, chips)]
    normed_far = [to_core(n) for n in normed]

    w_plane = jnp.concatenate([w_keep, w_got], axis=0)
    w_own = [w_plane] + [to_plane(w_plane, turn) for turn in range(1, planes)]
    weights = w_own + [to_core(w) for w in w_own]

    selected = select_grads(owner, grads + grads_far, groups, slots)

    grad_blocks = grad_normed_blocks(grads, weights, planes)
    grad_home = [grad_blocks[0]] + [to_chip(grad_blocks[k], k) for k in range(1, chips)]

    rights, lefts, mine, other = weight_blocks(selected, normed, normed_far, planes)
    other = to_x(other)
    right, left = along(rights[0], 1, 1), along(lefts[0], 1, -1)
    for step in range(2, planes - 1):
        (right,), (left,) = relay(rights[step - 1], right, lefts[step - 1], left, 1)
        right, left = along(right, step, 1), along(left, step, -1)
    last = planes - 1
    send_right, send_left = relay(rights[last - 1], right, lefts[last - 1], left, 2)
    parts = [mine, along(send_right[0], last, 1), along(send_left[0], last, -1)]
    parts += [other, along(send_right[1], last, 1, 1), along(send_left[1], last, -1, 1)]

    value_part = value_parts(normed, weights, planes, feats)
    values = value_part[0]
    for k in range(1, chips):
        values += to_chip(value_part[k], k).astype(f32)
    values = values.astype(bf16)

    grad_x = grad_x_blocks(tokens, gain_row, grad_home)
    states = adam(owner, parts, (master[0], moment1[0], moment2[0]), rows * seqs * groups)
    return (values[None], grad_x[None], *(s[None] for s in states))


def solution(mesh):
    placed = (
        P("dp", "seq", None),
        P(),
        P("dp", "seq"),
        P("dp", "seq", None),
        P(),
        P("dp", None, "seq"),
        P("dp", None, "seq"),
        P("dp", None, "seq"),
    )
    return jax.shard_map(
        functools.partial(on_device, mesh.shape["dp"], mesh.shape["seq"]),
        mesh=mesh,
        in_specs=placed,
        out_specs=(
            P("dp", "seq", None),
            P("dp", "seq", None),
            P("dp", None, "seq"),
            P("dp", None, "seq"),
            P("dp", None, "seq"),
        ),
        check_vma=False,
    )
```

time: 300 us -> 160 us (0.53)
  waiting for transfers between devices: 210 us -> 80.4 us
  starting transfers between devices: 4.78 us -> 46.9 us
  blocking collectives: 29.9 us -> 0 us
  matrix products: 21.4 us -> 0 us
  Pallas kernels: 0 us -> 20.1 us
  between operations: 13.9 us -> 0.99 us
  other arithmetic: 10.3 us -> 0.74 us
    psum x1 -> x0, waiting for transfers between devices: 156 us -> none  [on_device(): summed = lax.psum(grad_block, 'dp')]
    ppermute x0 -> x37, waiting for transfers between devices: none -> 80.4 us  [permute(): return lax.ppermute(value, ('dp', 'seq'), pairs)]
    all_gather x2 -> x0, waiting for transfers between devices: 53.7 us -> none  [the longest x1 51.4 us: on_device(): full_weight = lax.all_gather(col_block, 'seq', axis=1, tiled=True)]
    ppermute x0 -> x37, starting transfers between devices: none -> 46.9 us  [permute(): return lax.ppermute(value, ('dp', 'seq'), pairs)]
    all_gather x1 -> x0, blocking collectives: 29.9 us -> none  [on_device(): grads_all = lax.all_gather(value_grad, 'seq', axis=0, tiled=True)]
    dot_general x4 -> x0, matrix products: 21.4 us -> none  [the longest x1 7.52 us: on_device(): slot_grad = jnp.dot(select_mine, summed, precision=lax.Precision.HIGHEST)]
    pallas_call x0 -> x9, Pallas kernels: none -> 20.1 us  [the longest x1 4.05 us: weight_blocks(): pl.pallas_call(functools.partial(weight_kernel, planes), grid=(1,), in_sp...]
    unnamed x14 -> x44, local copies, waits for them, and re-layouts: 2.69 us -> 10.2 us
  transfers between devices with their start and end apart: 4 -> 37, of which waited for: 3 -> 11; matrix products, arithmetic and copies ran while one was open for 9% -> 1% of each run, Pallas kernels for 0% -> 8%
where the time goes in v2:
time: 160 us
  waiting for transfers between devices  80.4 us (50%)
  starting transfers between devices  46.9 us (29%)
  Pallas kernels  20.1 us (13%)
  local copies, waits for them, and re-layouts  10.4 us (6%)
    ppermute x37, waiting for transfers between devices, permute(): return lax.ppermute(value, ('dp', 'seq'), pairs)  80.4 us
    ppermute x37, starting transfers between devices, permute(): return lax.ppermute(value, ('dp', 'seq'), pairs)  46.9 us
    unnamed x44, local copies, waits for them, and re-layouts  10.2 us
    pallas_call x1, Pallas kernels, weight_blocks(): pl.pallas_call(functools.partial(weight_kernel, planes), grid=(1,), in_sp...  4.05 us
    pallas_call x1, Pallas kernels, grad_x_blocks(): pl.pallas_call(grad_x_kernel, grid=(rows // step,), in_specs=[pl.BlockSpe...  3.76 us
  transfers between devices with their start and end apart: 37, of which 11 were waited for; matrix products, arithmetic and copies ran while one was open for 1% of the time, Pallas kernels for 8%

profile of v2, /device:TPU:0, one launch (start us, length us, event | category | flops | bytes accessed | tf_op | source)
XLA Modules:
  0.0 159.5 jit_solution(16038426820185849993)
XLA Ops:
  0.7 1.6 copy-done
  2.2 0.8 copy-done.5
  3.0 1.3 norm_blocks.1
  4.3 3.0 %collective-permute-start = (bf16[2,128,1024]{2,1,0:T(8,128)(2,1)S(1)}, bf16[2,128,1024]{2,1,0:T(8,128)(2,1)S(1)}, u32[]{:S(2)}, u32[]{:S(2)}) collective-permute-start(bf16[2,128,1024]{2,1,0:T(8,128)(2,1)S(1)} %get-tuple-element.35), channel_id=1, source_target_pairs={{0,4},{1,5},{2,6},{3,7},{4,0},{5,1},{6,2},{7,3},{8,12},{9,13},{10,... | collective-permute-start | bytes 1572872 | tf_op jit(solution)/shard_map/ppermute | solution.py:359
  7.3 1.5 collective-permute-start.1
  8.9 1.9 %collective-permute-start.14 = (bf16[128,512]{1,0:T(8,128)(2,1)S(1)}, bf16[128,512]{1,0:T(8,128)(2,1)S(1)}, u32[]{:S(2)}, u32[]{:S(2)}) collective-permute-start(bf16[128,512]{1,0:T(8,128)(2,1)S(1)} %bitcast.24), channel_id=1, source_target_pairs={{0,4},{1,5},{2,6},{3,7},{4,0},{5,1},{6,2},{7,3},{8,12},{9,13},{10,... | collective-permute-start | bytes 393224 | tf_op jit(solution)/shard_map/ppermute | solution.py:359
  10.8 1.5 collective-permute-start.15
  12.3 21.0 %collective-permute-done.14.refs_1_ = bf16[128,512]{1,0:T(8,128)(2,1)S(1)} collective-permute-done((bf16[128,512]{1,0:T(8,128)(2,1)S(1)}, bf16[128,512]{1,0:T(8,128)(2,1)S(1)}, u32[]{:S(2)}, u32[]{:S(2)}) %collective-permute-start.14) | collective-permute-done | bytes 131104 | tf_op jit(solution)/shard_map/ppermute | solution.py:359
  33.4 2.7 %collective-permute-start.16 = (bf16[128,512]{1,0:T(8,128)(2,1)S(1)}, bf16[128,512]{1,0:T(8,128)(2,1)}, u32[]{:S(2)}, u32[]{:S(2)}) collective-permute-start(bf16[128,512]{1,0:T(8,128)(2,1)S(1)} %bitcast.26), channel_id=1, source_target_pairs={{0,6},{1,7},{2,4},{3,5},{4,2},{5,3},{6,0},{7,1},{8,14},{9,15},{10,... | collective-permute-start | bytes 393224 | tf_op jit(solution)/shard_map/ppermute | solution.py:359
  36.1 3.3 %collective-permute-done.16.refs_3_ = bf16[128,512]{1,0:T(8,128)(2,1)} collective-permute-done((bf16[128,512]{1,0:T(8,128)(2,1)S(1)}, bf16[128,512]{1,0:T(8,128)(2,1)}, u32[]{:S(2)}, u32[]{:S(2)}) %collective-permute-start.16) | collective-permute-done | bytes 131104 | tf_op jit(solution)/shard_map/ppermute | solution.py:359
  40.4 0.7 copy-done.15
  41.7 1.4 collective-permute-done.21.refs_5_
  43.1 0.7 copy-done.17
  43.9 0.7 copy-done.12
  45.1 0.7 copy-done.19
  46.1 1.4 collective-permute-done.23.refs_7_
  47.5 0.9 copy-done.10
  48.4 0.9 copy-done.13
  49.3 0.9 copy-done.16
  50.2 0.9 copy-done.18
  51.1 0.9 copy-done.20
  52.0 2.4 %select_grads.1.sel_ref = bf16[1024,1024]{1,0:T(8,128)(2,1)S(1)} custom-call(s32[1,512]{1,0:T(1,128)S(1)} %bitcast.22, s32[512,1]{1,0:T(8,128)S(1)} %copy.13.owner_col_ref, bf16[128,512]{1,0:T(8,128)(2,1)S(1)} %bitcast.28, bf16[128,512]{1,0:T(8,128)(2,1)S(1)} %copy-done.10, bf16[128,512]{1,0:T(8,128)(2,1)S(1)} %copy-done.13, ...), custom_call_target="tpu_custom_call" | custom-call | flops 1073741824 | bytes 2097152 | tf_op jit(solution)/shard_map/select_grads/pallas_call | solution.py:133
  54.4 4.1 %weight_blocks.1 = (bf16[256,1024]{1,0:T(8,128)(2,1)S(1)}, bf16[256,1024]{1,0:T(8,128)(2,1)S(1)}, bf16[256,1024]{1,0:T(8,128)(2,1)S(1)}, bf16[256,1024]{1,0:T(8,...) custom-call(bf16[1024,1024]{1,0:T(8,128)(2,1)S(1)} %select_grads.1.s, ...), custom_call_target="tpu_custom_call" | custom-call | flops 2147483648 | bytes 4194304 | tf_op jit(solution)/shard_map/weight_blocks/pallas_call | solution.py:183
  58.5 3.8 %collective-permute-start.28 = (bf16[256,1024]{1,0:T(8,128)(2,1)S(1)}, bf16[256,1024]{1,0:T(8,128)(2,1)S(1)}, u32[]{:S(2)}, u32[]{:S(2)}) collective-permute-start(bf16[256,1024]{1,0:T(8,128)(2,1)S(1)} %get-tuple-element.49), channel_id=1, source_target_pairs={{0,8},{1,9},{2,10},{3,11},{4,12},{5,13},{6,14},{7,15}} | collective-permute-start | bytes 1572872 | tf_op jit(solution)/shard_map/ppermute | solution.py:359
  62.3 1.6 collective-permute-start.3
  63.9 0.7 collective-permute-start.29
  64.6 3.1 %collective-permute-done.3 = bf16[64,1024]{1,0:T(8,128)(2,1)S(1)} collective-permute-done((bf16[64,1024]{1,0:T(8,128)(2,1)S(1)}, bf16[64,1024]{1,0:T(8,128)(2,1)S(1)}, u32[]{:S(2)}, u32[]{:S(2)}) %collective-permute-start.3) | collective-permute-done | bytes 131104 | tf_op jit(solution)/shard_map/ppermute | solution.py:359
  67.7 1.1 collective-permute-start.6
  68.8 1.0 collective-permute-start.4
  69.8 10.8 %collective-permute-done.6.refs_7_ = bf16[128,1024]{1,0:T(8,128)(2,1)S(1)} collective-permute-done((bf16[128,1024]{1,0:T(8,128)(2,1)S(1)}, bf16[128,1024]{1,0:T(8,128)(2,1)S(1)}, u32[]{:S(2)}, u32[]{:S(2)}) %collective-permute-start.6) | collective-permute-done | bytes 262176 | tf_op jit(solution)/shard_map/ppermute | solution.py:359
  80.6 10.4 %collective-permute-done.4.refs_5_ = bf16[128,1024]{1,0:T(8,128)(2,1)S(1)} collective-permute-done((bf16[128,1024]{1,0:T(8,128)(2,1)S(1)}, bf16[128,1024]{1,0:T(8,128)(2,1)S(1)}, u32[]{:S(2)}, u32[]{:S(2)}) %collective-permute-start.4) | collective-permute-done | bytes 262176 | tf_op jit(solution)/shard_map/ppermute | solution.py:359
  91.8 6.9 %collective-permute-start.30 = (bf16[256,1024]{1,0:T(8,128)(2,1)S(1)}, bf16[256,1024]{1,0:T(8,128)(2,1)S(1)}, u32[]{:S(2)}, u32[]{:S(2)}) collective-permute-start(bf16[256,1024]{1,0:T(8,128)(2,1)S(1)} %get-tuple-element.52), channel_id=1, source_target_pairs={{0,8},{1,9},{2,10},{3,11},{4,12},{5,13},{6,14},{7,15},{8,16},{9,17... | collective-permute-start | bytes 1572872 | tf_op jit(solution)/shard_map/ppermute | solution.py:359
  98.8 0.8 collective-permute-start.31
  99.7 3.1 %value_parts.1 = (f32[128,512]{1,0:T(8,128)S(1)}, bf16[128,512]{1,0:T(8,128)(2,1)S(1)}, bf16[128,512]{1,0:T(8,128)(2,1)S(1)}, bf16[128,512]{1,0:T(8,128)(2,1)S(1)}) custom-call(bf16[2,128,1024]{2,1,0:T(8,128)(2,1)S(1)} %get-tuple-element.34.refs_0_, bf16[2,128,1024]{2,1,0:T(8,128)(2,1)S(1)} %collective-permute-done.refs_1_, ...), custom_call_target="tpu_custom_call" | custom-call | flops 1073741824 | bytes 2097152 | tf_op jit(solution)/shard_map/value_parts/pallas_call | solution.py:259
  103.4 2.4 %grad_normed_blocks.1 = (bf16[2,128,1024]{2,1,0:T(8,128)(2,1)S(1)}, bf16[2,128,1024]{2,1,0:T(8,128)(2,1)S(1)}, bf16[2,128,1024]{2,1,0:T(8,128)(2,1)S(1)}, bf16[2,128,1024]{2,1,0:T(8,128)(2,1)S(1)}) custom-call(bf16[128,512]{1,0:T(8,128)(2,1)S(1)} %bitcast.29, bf16[128,512]{1,0:T(8,128)(2,1)S(1)} %copy-done.11, bf16[128,512]{1,0:T(8,128)(2,1)S(1)} %copy-done.14, ...), custom_call_target="tpu_custom_call" | custom-call | flops 1073741824 | bytes 2097152 | tf_op jit(solution)/shard_map/grad_normed_blocks/pallas_call | solution.py:231
  105.7 1.6 collective-permute-start.17
  107.3 1.5 collective-permute-start.18
  110.1 1.5 collective-permute-start.12
  111.6 0.8 collective-permute-start.13
  112.7 24.5 %collective-permute-done.12 = bf16[128,512]{1,0:T(8,128)(2,1)S(1)} collective-permute-done((bf16[128,512]{1,0:T(8,128)(2,1)S(1)}, bf16[128,512]{1,0:T(8,128)(2,1)S(1)}, u32[]{:S(2)}, u32[]{:S(2)}) %collective-permute-start.12) | collective-permute-done | bytes 131104 | tf_op jit(solution)/shard_map/ppermute | solution.py:359
  137.7 2.8 %collective-permute-start.32 = (bf16[128,1024]{1,0:T(8,128)(2,1)S(1)}, bf16[128,1024]{1,0:T(8,128)(2,1)S(1)}, u32[]{:S(2)}, u32[]{:S(2)}) collective-permute-start(bf16[128,1024]{1,0:T(8,128)(2,1)S(1)} %get-tuple-element.55), channel_id=1, source_target_pairs={{0,8},{1,9},{2,10},{3,11},{4,12},{5,13},{6,14},{7,15},{8,16},{9,17... | collective-permute-start | bytes 786440 | tf_op jit(solution)/shard_map/ppermute | solution.py:359
  140.5 1.3 collective-permute-start.33
  141.8 5.8 %collective-permute-start.35 = (bf16[128,1024]{1,0:T(8,128)(2,1)S(1)}, bf16[128,1024]{1,0:T(8,128)(2,1)S(1)}, u32[]{:S(2)}, u32[]{:S(2)}) collective-permute-start(bf16[128,1024]{1,0:T(8,128)(2,1)S(1)} %get-tuple-element.58), channel_id=1, source_target_pairs={{0,12},{1,13},{2,14},{3,15},{4,8},{5,9},{6,10},{7,11},{8,20},{9,21... | collective-permute-start | bytes 786440 | tf_op jit(solution)/shard_map/ppermute | solution.py:359
  147.6 1.3 collective-permute-start.36
  148.9 0.7 fusion
  149.7 3.8 %grad_x_blocks.1 = bf16[128,8192]{1,0:T(8,128)(2,1)} custom-call(bf16[128,8192]{1,0:T(8,128)(2,1)S(1)} %bitcast.15, f32[1,8192]{1,0:T(1,128)S(1)} %bitcast.20, bf16[2,128,1024]{2,1,0:T(8,128)(2,1)S(1)} %get-tuple-element.42.refs_0_, bf16[2,128,1024]{2,1,0:T(8,128)(2,1)S(1)} %collective-permute-done.17.refs_1_, ...), custom_call_target="tpu_custom_call" | custom-call | flops 16777216 | bytes 6291456 | tf_op jit(solution)/shard_map/grad_x_blocks/pallas_call | solution.py:91
  153.5 3.3 %collective-permute-done.36.refs_5_ = bf16[128,1024]{1,0:T(8,128)(2,1)S(1)} collective-permute-done((bf16[128,1024]{1,0:T(8,128)(2,1)S(1)}, bf16[128,1024]{1,0:T(8,128)(2,1)S(1)}, u32[]{:S(2)}, u32[]{:S(2)}) %collective-permute-start.36) | collective-permute-done | bytes 262176 | tf_op jit(solution)/shard_map/ppermute | solution.py:359
  156.8 2.7 %adam.1 = (f32[128,2048]{1,0:T(8,128)}, f32[128,2048]{1,0:T(8,128)}, f32[128,2048]{1,0:T(8,128)}) custom-call(s32[1,512]{1,0:T(1,128)S(1)} %bitcast.23, f32[128,1024]{1,0:T(8,128)S(1)} %get-tuple-element.46.refs_0_, bf16[128,1024]{1,0:T(8,128)(2,1)S(1)} %collective-permute-done.32.refs_1_, bf16[128,1024]{1,0:T(8,128)(2,1)S(1)} %collective-permute-done.33.refs_2_, ...), custom_call_target="tpu_custom_call" | custom-call | flops 5242880 | bytes 7864320 | tf_op jit(solution)/shard_map/adam/pallas_call | solution.py:328
  (83 shorter events, 6.4 us)
Async XLA Ops:
  0.6 45.3 %copy-start.7 = (s32[512]{0:T(512)S(1)}, s32[512]{0:T(512)}, u32[]{:S(2)}) copy-start(s32[512]{0:T(512)} %param.12) | copy-start | bytes 6148
  0.6 1.6 %copy-start = (bf16[1,128,8192]{2,1,0:T(8,128)(2,1)S(1)}, bf16[1,128,8192]{2,1,0:T(8,128)(2,1)}, u32[]{:S(2)}) copy-start(bf16[1,128,8192]{2,1,0:T(8,128)(2,1)} %param.8) | copy-start | bytes 6291460
  3.0 5.9 %copy-start.8 = (bf16[1,128,512]{2,1,0:T(8,128)(2,1)S(1)}, bf16[1,128,512]{2,1,0:T(8,128)(2,1)}, u32[]{:S(2)}) copy-start(bf16[1,128,512]{2,1,0:T(8,128)(2,1)} %param.11) | copy-start | bytes 393220
  4.3 35.0 %collective-permute-start = (bf16[2,128,1024]{2,1,0:T(8,128)(2,1)S(1)}, bf16[2,128,1024]{2,1,0:T(8,128)(2,1)S(1)}, u32[]{:S(2)}, u32[]{:S(2)}) collective-permute-start(bf16[2,128,1024]{2,1,0:T(8,128)(2,1)S(1)} %get-tuple-element.35), channel_id=1, source_target_pairs={{0,4},{1,5},{2,6},{3,7},{4,0},{5,1},{6,2},{7,3},{8,12},{9,13},{10,... | collective-permute-start | bytes 1572872 | tf_op jit(solution)/shard_map/ppermute | solution.py:359
  7.3 32.5 %collective-permute-start.1 = (bf16[2,128,1024]{2,1,0:T(8,128)(2,1)S(1)}, bf16[2,128,1024]{2,1,0:T(8,128)(2,1)S(1)}, u32[]{:S(2)}, u32[]{:S(2)}) collective-permute-start(bf16[2,128,1024]{2,1,0:T(8,128)(2,1)S(1)} %get-tuple-element.36), channel_id=1, source_target_pairs={{0,2},{1,3},{2,0},{3,1},{4,6},{5,7},{6,4},{7,5},{8,10},{9,11},{10,... | collective-permute-start | bytes 1572872 | tf_op jit(solution)/shard_map/ppermute | solution.py:359
  8.9 31.1 %collective-permute-start.2 = (bf16[2,128,1024]{2,1,0:T(8,128)(2,1)S(1)}, bf16[2,128,1024]{2,1,0:T(8,128)(2,1)S(1)}, u32[]{:S(2)}, u32[]{:S(2)}) collective-permute-start(bf16[2,128,1024]{2,1,0:T(8,128)(2,1)S(1)} %get-tuple-element.37), channel_id=1, source_target_pairs={{0,6},{1,7},{2,4},{3,5},{4,2},{5,3},{6,0},{7,1},{8,14},{9,15},{10,... | collective-permute-start | bytes 1572872 | tf_op jit(solution)/shard_map/ppermute | solution.py:359
  8.9 24.5 %collective-permute-start.14 = (bf16[128,512]{1,0:T(8,128)(2,1)S(1)}, bf16[128,512]{1,0:T(8,128)(2,1)S(1)}, u32[]{:S(2)}, u32[]{:S(2)}) collective-permute-start(bf16[128,512]{1,0:T(8,128)(2,1)S(1)} %bitcast.24), channel_id=1, source_target_pairs={{0,4},{1,5},{2,6},{3,7},{4,0},{5,1},{6,2},{7,3},{8,12},{9,13},{10,... | collective-permute-start | bytes 393224 | tf_op jit(solution)/shard_map/ppermute | solution.py:359
  10.8 25.2 %collective-permute-start.15 = (bf16[128,512]{1,0:T(8,128)(2,1)S(1)}, bf16[128,512]{1,0:T(8,128)(2,1)S(1)}, u32[]{:S(2)}, u32[]{:S(2)}) collective-permute-start(bf16[128,512]{1,0:T(8,128)(2,1)S(1)} %bitcast.25), channel_id=1, source_target_pairs={{0,2},{1,3},{2,0},{3,1},{4,6},{5,7},{6,4},{7,5},{8,10},{9,11},{10,... | collective-permute-start | bytes 393224 | tf_op jit(solution)/shard_map/ppermute | solution.py:359
  33.4 6.0 %collective-permute-start.16 = (bf16[128,512]{1,0:T(8,128)(2,1)S(1)}, bf16[128,512]{1,0:T(8,128)(2,1)}, u32[]{:S(2)}, u32[]{:S(2)}) collective-permute-start(bf16[128,512]{1,0:T(8,128)(2,1)S(1)} %bitcast.26), channel_id=1, source_target_pairs={{0,6},{1,7},{2,4},{3,5},{4,2},{5,3},{6,0},{7,1},{8,14},{9,15},{10,... | collective-permute-start | bytes 393224 | tf_op jit(solution)/shard_map/ppermute | solution.py:359
  36.0 4.3 %collective-permute-start.20 = (bf16[128,512]{1,0:T(8,128)(2,1)S(1)}, bf16[128,512]{1,0:T(8,128)(2,1)S(1)}, u32[]{:S(2)}, u32[]{:S(2)}) collective-permute-start(bf16[128,512]{1,0:T(8,128)(2,1)S(1)} %bitcast.27), channel_id=1, source_target_pairs={{0,1},{1,0},{2,3},{3,2},{4,5},{5,4},{6,7},{7,6},{8,9},{9,8},{10,11... | collective-permute-start | bytes 393224 | tf_op jit(solution)/shard_map/ppermute | solution.py:359
  39.3 15.1 %collective-permute-start.24 = (bf16[2,128,1024]{2,1,0:T(8,128)(2,1)S(1)}, bf16[2,128,1024]{2,1,0:T(8,128)(2,1)S(1)}, u32[]{:S(2)}, u32[]{:S(2)}) collective-permute-start(bf16[2,128,1024]{2,1,0:T(8,128)(2,1)S(1)} %get-tuple-element.34.refs_0_), channel_id=1, source_target_pairs={{0,1},{1,0},{2,3},{3,2},{4,5},{5,4},{6,7},{7,6},{8,9},{9,8},{10,11... | collective-permute-start | bytes 1572872 | tf_op jit(solution)/shard_map/ppermute | solution.py:359
  39.3 15.1 %collective-permute-start.25 = (bf16[2,128,1024]{2,1,0:T(8,128)(2,1)S(1)}, bf16[2,128,1024]{2,1,0:T(8,128)(2,1)S(1)}, u32[]{:S(2)}, u32[]{:S(2)}) collective-permute-start(bf16[2,128,1024]{2,1,0:T(8,128)(2,1)S(1)} %collective-permute-done.refs_1_), channel_id=1, source_target_pairs={{0,1},{1,0},{2,3},{3,2},{4,5},{5,4},{6,7},{7,6},{8,9},{9,8},{10,11... | collective-permute-start | bytes 1572872 | tf_op jit(solution)/shard_map/ppermute | solution.py:359
  39.8 14.6 %collective-permute-start.26 = (bf16[2,128,1024]{2,1,0:T(8,128)(2,1)S(1)}, bf16[2,128,1024]{2,1,0:T(8,128)(2,1)}, u32[]{:S(2)}, u32[]{:S(2)}) collective-permute-start(bf16[2,128,1024]{2,1,0:T(8,128)(2,1)S(1)} %collective-permute-done.1.refs_2_), channel_id=1, source_target_pairs={{0,1},{1,0},{2,3},{3,2},{4,5},{5,4},{6,7},{7,6},{8,9},{9,8},{10,11... | collective-permute-start | bytes 1572872 | tf_op jit(solution)/shard_map/ppermute | solution.py:359
  39.9 14.5 %collective-permute-start.27 = (bf16[2,128,1024]{2,1,0:T(8,128)(2,1)S(1)}, bf16[2,128,1024]{2,1,0:T(8,128)(2,1)}, u32[]{:S(2)}, u32[]{:S(2)}) collective-permute-start(bf16[2,128,1024]{2,1,0:T(8,128)(2,1)S(1)} %collective-permute-done.2.refs_3_), channel_id=1, source_target_pairs={{0,1},{1,0},{2,3},{3,2},{4,5},{5,4},{6,7},{7,6},{8,9},{9,8},{10,11... | collective-permute-start | bytes 1572872 | tf_op jit(solution)/shard_map/ppermute | solution.py:359
  41.0 2.1 %collective-permute-start.21 = (bf16[128,512]{1,0:T(8,128)(2,1)S(1)}, bf16[128,512]{1,0:T(8,128)(2,1)S(1)}, u32[]{:S(2)}, u32[]{:S(2)}) collective-permute-start(bf16[128,512]{1,0:T(8,128)(2,1)S(1)} %collective-permute-done.14.refs_1_), channel_id=1, source_target_pairs={{0,1},{1,0},{2,3},{3,2},{4,5},{5,4},{6,7},{7,6},{8,9},{9,8},{10,11... | collective-permute-start | bytes 393224 | tf_op jit(solution)/shard_map/ppermute | solution.py:359
  43.8 1.3 collective-permute-start.22
  45.8 1.7 %collective-permute-start.23 = (bf16[128,512]{1,0:T(8,128)(2,1)}, bf16[128,512]{1,0:T(8,128)(2,1)}, u32[]{:S(2)}, u32[]{:S(2)}) collective-permute-start(bf16[128,512]{1,0:T(8,128)(2,1)} %collective-permute-done.16.refs_3_), channel_id=1, source_target_pairs={{0,1},{1,0},{2,3},{3,2},{4,5},{5,4},{6,7},{7,6},{8,9},{9,8},{10,11... | collective-permute-start | bytes 393224 | tf_op jit(solution)/shard_map/ppermute | solution.py:359
  54.4 7.9 %copy-start.21 = (bf16[64,2048]{1,0:T(8,128)(2,1)S(1)}, bf16[64,2048]{1,0:T(8,128)(2,1)}, u32[]{:S(2)}) copy-start(bf16[64,2048]{1,0:T(8,128)(2,1)} %param.10) | copy-start | bytes 786436
  58.5 33.0 %collective-permute-start.28 = (bf16[256,1024]{1,0:T(8,128)(2,1)S(1)}, bf16[256,1024]{1,0:T(8,128)(2,1)S(1)}, u32[]{:S(2)}, u32[]{:S(2)}) collective-permute-start(bf16[256,1024]{1,0:T(8,128)(2,1)S(1)} %get-tuple-element.49), channel_id=1, source_target_pairs={{0,8},{1,9},{2,10},{3,11},{4,12},{5,13},{6,14},{7,15}} | collective-permute-start | bytes 1572872 | tf_op jit(solution)/shard_map/ppermute | solution.py:359
  62.3 5.3 %collective-permute-start.3 = (bf16[64,1024]{1,0:T(8,128)(2,1)S(1)}, bf16[64,1024]{1,0:T(8,128)(2,1)S(1)}, u32[]{:S(2)}, u32[]{:S(2)}) collective-permute-start(bf16[64,1024]{1,0:T(8,128)(2,1)S(1)} %get-tuple-element.64), channel_id=1, source_target_pairs={{0,4},{1,5},{2,6},{3,7},{4,0},{5,1},{6,2},{7,3},{8,12},{9,13},{10,... | collective-permute-start | bytes 393224 | tf_op jit(solution)/shard_map/ppermute | solution.py:359
  63.9 27.7 %collective-permute-start.29 = (bf16[256,1024]{1,0:T(8,128)(2,1)S(1)}, bf16[256,1024]{1,0:T(8,128)(2,1)S(1)}, u32[]{:S(2)}, u32[]{:S(2)}) collective-permute-start(bf16[256,1024]{1,0:T(8,128)(2,1)S(1)} %get-tuple-element.51), channel_id=1, source_target_pairs={{24,16},{25,17},{26,18},{27,19},{28,20},{29,21},{30,22},{31,23}} | collective-permute-start | bytes 1572872 | tf_op jit(solution)/shard_map/ppermute | solution.py:359
  67.7 12.9 %collective-permute-start.6 = (bf16[128,1024]{1,0:T(8,128)(2,1)S(1)}, bf16[128,1024]{1,0:T(8,128)(2,1)S(1)}, u32[]{:S(2)}, u32[]{:S(2)}) collective-permute-start(bf16[128,1024]{1,0:T(8,128)(2,1)S(1)} %pad_maximum_fusion.refs_4_), channel_id=1, source_target_pairs={{0,24},{1,25},{2,26},{3,27},{4,28},{5,29},{6,30},{7,31},{8,0},{9,1... | collective-permute-start | bytes 786440 | tf_op jit(solution)/shard_map/ppermute | solution.py:359
  68.8 22.2 %collective-permute-start.4 = (bf16[128,1024]{1,0:T(8,128)(2,1)S(1)}, bf16[128,1024]{1,0:T(8,128)(2,1)S(1)}, u32[]{:S(2)}, u32[]{:S(2)}) collective-permute-start(bf16[128,1024]{1,0:T(8,128)(2,1)S(1)} %pad_maximum_fusion.refs_4_), channel_id=1, source_target_pairs={{0,8},{1,9},{2,10},{3,11},{4,12},{5,13},{6,14},{7,15},{8,16},{9,17... | collective-permute-start | bytes 786440 | tf_op jit(solution)/shard_map/ppermute | solution.py:359
  69.8 21.3 %collective-permute-start.5 = (bf16[128,1024]{1,0:T(8,128)(2,1)S(1)}, bf16[128,1024]{1,0:T(8,128)(2,1)S(1)}, u32[]{:S(2)}, u32[]{:S(2)}) collective-permute-start(bf16[128,1024]{1,0:T(8,128)(2,1)S(1)} %pad_maximum_fusion.refs_4_), channel_id=1, source_target_pairs={{0,16},{1,17},{2,18},{3,19},{4,20},{5,21},{6,22},{7,23},{8,24},{9,... | collective-permute-start | bytes 786440 | tf_op jit(solution)/shard_map/ppermute | solution.py:359
  80.6 18.2 %collective-permute-start.7 = (bf16[128,1024]{1,0:T(8,128)(2,1)S(1)}, bf16[128,1024]{1,0:T(8,128)(2,1)S(1)}, u32[]{:S(2)}, u32[]{:S(2)}) collective-permute-start(bf16[128,1024]{1,0:T(8,128)(2,1)S(1)} %pad_maximum_fusion.refs_4_), channel_id=1, source_target_pairs={{0,1},{1,0},{2,3},{3,2},{4,5},{5,4},{6,7},{7,6},{8,9},{9,8},{10,11... | collective-permute-start | bytes 786440 | tf_op jit(solution)/shard_map/ppermute | solution.py:359
  91.0 8.6 %collective-permute-start.10 = (bf16[128,1024]{1,0:T(8,128)(2,1)S(1)}, bf16[128,1024]{1,0:T(8,128)(2,1)S(1)}, u32[]{:S(2)}, u32[]{:S(2)}) collective-permute-start(bf16[128,1024]{1,0:T(8,128)(2,1)S(1)} %collective-permute-done.6.refs_7_), channel_id=1, source_target_pairs={{0,1},{1,0},{2,3},{3,2},{4,5},{5,4},{6,7},{7,6},{8,9},{9,8},{10,11... | collective-permute-start | bytes 786440 | tf_op jit(solution)/shard_map/ppermute | solution.py:359
  91.0 8.7 %collective-permute-start.8 = (bf16[128,1024]{1,0:T(8,128)(2,1)S(1)}, bf16[128,1024]{1,0:T(8,128)(2,1)S(1)}, u32[]{:S(2)}, u32[]{:S(2)}) collective-permute-start(bf16[128,1024]{1,0:T(8,128)(2,1)S(1)} %collective-permute-done.4.refs_5_), channel_id=1, source_target_pairs={{0,1},{1,0},{2,3},{3,2},{4,5},{5,4},{6,7},{7,6},{8,9},{9,8},{10,11... | collective-permute-start | bytes 786440 | tf_op jit(solution)/shard_map/ppermute | solution.py:359
  91.5 8.2 %collective-permute-start.9 = (bf16[128,1024]{1,0:T(8,128)(2,1)S(1)}, bf16[128,1024]{1,0:T(8,128)(2,1)S(1)}, u32[]{:S(2)}, u32[]{:S(2)}) collective-permute-start(bf16[128,1024]{1,0:T(8,128)(2,1)S(1)} %collective-permute-done.5.refs_6_), channel_id=1, source_target_pairs={{0,1},{1,0},{2,3},{3,2},{4,5},{5,4},{6,7},{7,6},{8,9},{9,8},{10,11... | collective-permute-start | bytes 786440 | tf_op jit(solution)/shard_map/ppermute | solution.py:359
  91.8 18.3 %collective-permute-start.30 = (bf16[256,1024]{1,0:T(8,128)(2,1)S(1)}, bf16[256,1024]{1,0:T(8,128)(2,1)S(1)}, u32[]{:S(2)}, u32[]{:S(2)}) collective-permute-start(bf16[256,1024]{1,0:T(8,128)(2,1)S(1)} %get-tuple-element.52), channel_id=1, source_target_pairs={{0,8},{1,9},{2,10},{3,11},{4,12},{5,13},{6,14},{7,15},{8,16},{9,17... | collective-permute-start | bytes 1572872 | tf_op jit(solution)/shard_map/ppermute | solution.py:359
  98.8 4.6 %copy-start.11 = (bf16[128,512]{1,0:T(8,128)(2,1)S(1)}, bf16[128,512]{1,0:T(8,128)(2,1)}, u32[]{:S(2)}) copy-start(bf16[128,512]{1,0:T(8,128)(2,1)} %copy-done.9) | copy-start | bytes 393220
  98.8 4.5 %copy-start.14 = (bf16[128,512]{1,0:T(8,128)(2,1)S(1)}, bf16[128,512]{1,0:T(8,128)(2,1)}, u32[]{:S(2)}) copy-start(bf16[128,512]{1,0:T(8,128)(2,1)} %copy-done.12) | copy-start | bytes 393220
  98.8 12.8 %collective-permute-start.31 = (bf16[256,1024]{1,0:T(8,128)(2,1)S(1)}, bf16[256,1024]{1,0:T(8,128)(2,1)S(1)}, u32[]{:S(2)}, u32[]{:S(2)}) collective-permute-start(bf16[256,1024]{1,0:T(8,128)(2,1)S(1)} %get-tuple-element.54), channel_id=1, source_target_pairs={{16,8},{17,9},{18,10},{19,11},{20,12},{21,13},{22,14},{23,15},{24,... | collective-permute-start | bytes 1572872 | tf_op jit(solution)/shard_map/ppermute | solution.py:359
  102.8 6.1 %collective-permute-start.11 = (bf16[128,512]{1,0:T(8,128)(2,1)S(1)}, bf16[128,512]{1,0:T(8,128)(2,1)S(1)}, u32[]{:S(2)}, u32[]{:S(2)}) collective-permute-start(bf16[128,512]{1,0:T(8,128)(2,1)S(1)} %get-tuple-element.39), channel_id=1, source_target_pairs={{0,4},{1,5},{2,6},{3,7},{4,0},{5,1},{6,2},{7,3},{8,12},{9,13},{10,... | collective-permute-start | bytes 393224 | tf_op jit(solution)/shard_map/ppermute | solution.py:359
  105.7 43.9 %copy-start.1 = (bf16[1,128,8192]{2,1,0:T(8,128)(2,1)S(1)}, bf16[1,128,8192]{2,1,0:T(8,128)(2,1)}, u32[]{:S(2)}) copy-start(bf16[1,128,8192]{2,1,0:T(8,128)(2,1)} %param.8) | copy-start | bytes 6291460
  105.7 43.9 %copy-start.6 = (f32[8192]{0:T(1024)S(1)}, f32[8192]{0:T(1024)}, u32[]{:S(2)}) copy-start(f32[8192]{0:T(1024)} %param.9) | copy-start | bytes 98308
  105.7 34.7 %collective-permute-start.17 = (bf16[2,128,1024]{2,1,0:T(8,128)(2,1)S(1)}, bf16[2,128,1024]{2,1,0:T(8,128)(2,1)S(1)}, u32[]{:S(2)}, u32[]{:S(2)}) collective-permute-start(bf16[2,128,1024]{2,1,0:T(8,128)(2,1)S(1)} %get-tuple-element.43), channel_id=1, source_target_pairs={{0,4},{1,5},{2,6},{3,7},{4,0},{5,1},{6,2},{7,3},{8,12},{9,13},{10,... | collective-permute-start | bytes 1572872 | tf_op jit(solution)/shard_map/ppermute | solution.py:359
  107.3 34.5 %collective-permute-start.18 = (bf16[2,128,1024]{2,1,0:T(8,128)(2,1)S(1)}, bf16[2,128,1024]{2,1,0:T(8,128)(2,1)S(1)}, u32[]{:S(2)}, u32[]{:S(2)}) collective-permute-start(bf16[2,128,1024]{2,1,0:T(8,128)(2,1)S(1)} %get-tuple-element.44), channel_id=1, source_target_pairs={{0,2},{1,3},{2,0},{3,1},{4,6},{5,7},{6,4},{7,5},{8,10},{9,11},{10,... | collective-permute-start | bytes 1572872 | tf_op jit(solution)/shard_map/ppermute | solution.py:359
  108.8 38.8 %collective-permute-start.19 = (bf16[2,128,1024]{2,1,0:T(8,128)(2,1)S(1)}, bf16[2,128,1024]{2,1,0:T(8,128)(2,1)S(1)}, u32[]{:S(2)}, u32[]{:S(2)}) collective-permute-start(bf16[2,128,1024]{2,1,0:T(8,128)(2,1)S(1)} %get-tuple-element.45), channel_id=1, source_target_pairs={{0,6},{1,7},{2,4},{3,5},{4,2},{5,3},{6,0},{7,1},{8,14},{9,15},{10,... | collective-permute-start | bytes 1572872 | tf_op jit(solution)/shard_map/ppermute | solution.py:359
  110.1 27.1 %collective-permute-start.12 = (bf16[128,512]{1,0:T(8,128)(2,1)S(1)}, bf16[128,512]{1,0:T(8,128)(2,1)S(1)}, u32[]{:S(2)}, u32[]{:S(2)}) collective-permute-start(bf16[128,512]{1,0:T(8,128)(2,1)S(1)} %get-tuple-element.40), channel_id=1, source_target_pairs={{0,2},{1,3},{2,0},{3,1},{4,6},{5,7},{6,4},{7,5},{8,10},{9,11},{10,... | collective-permute-start | bytes 393224 | tf_op jit(solution)/shard_map/ppermute | solution.py:359
  111.6 26.1 %collective-permute-start.13 = (bf16[128,512]{1,0:T(8,128)(2,1)S(1)}, bf16[128,512]{1,0:T(8,128)(2,1)S(1)}, u32[]{:S(2)}, u32[]{:S(2)}) collective-permute-start(bf16[128,512]{1,0:T(8,128)(2,1)S(1)} %get-tuple-element.41), channel_id=1, source_target_pairs={{0,6},{1,7},{2,4},{3,5},{4,2},{5,3},{6,0},{7,1},{8,14},{9,15},{10,... | collective-permute-start | bytes 393224 | tf_op jit(solution)/shard_map/ppermute | solution.py:359
  137.2 16.3 %collective-permute-start.34 = (bf16[128,1024]{1,0:T(8,128)(2,1)S(1)}, bf16[128,1024]{1,0:T(8,128)(2,1)S(1)}, u32[]{:S(2)}, u32[]{:S(2)}) collective-permute-start(bf16[128,1024]{1,0:T(8,128)(2,1)S(1)} %get-tuple-element.57), channel_id=1, source_target_pairs={{0,4},{1,5},{2,6},{3,7},{4,0},{5,1},{6,2},{7,3},{8,12},{9,13},{10,... | collective-permute-start | bytes 786440 | tf_op jit(solution)/shard_map/ppermute | solution.py:359
  137.7 15.7 %collective-permute-start.32 = (bf16[128,1024]{1,0:T(8,128)(2,1)S(1)}, bf16[128,1024]{1,0:T(8,128)(2,1)S(1)}, u32[]{:S(2)}, u32[]{:S(2)}) collective-permute-start(bf16[128,1024]{1,0:T(8,128)(2,1)S(1)} %get-tuple-element.55), channel_id=1, source_target_pairs={{0,8},{1,9},{2,10},{3,11},{4,12},{5,13},{6,14},{7,15},{8,16},{9,17... | collective-permute-start | bytes 786440 | tf_op jit(solution)/shard_map/ppermute | solution.py:359
  140.5 13.0 %collective-permute-start.33 = (bf16[128,1024]{1,0:T(8,128)(2,1)S(1)}, bf16[128,1024]{1,0:T(8,128)(2,1)S(1)}, u32[]{:S(2)}, u32[]{:S(2)}) collective-permute-start(bf16[128,1024]{1,0:T(8,128)(2,1)S(1)} %get-tuple-element.56), channel_id=1, source_target_pairs={{8,0},{9,1},{10,2},{11,3},{12,4},{13,5},{14,6},{15,7},{16,8},{17,9... | collective-permute-start | bytes 786440 | tf_op jit(solution)/shard_map/ppermute | solution.py:359
  141.8 11.7 %collective-permute-start.35 = (bf16[128,1024]{1,0:T(8,128)(2,1)S(1)}, bf16[128,1024]{1,0:T(8,128)(2,1)S(1)}, u32[]{:S(2)}, u32[]{:S(2)}) collective-permute-start(bf16[128,1024]{1,0:T(8,128)(2,1)S(1)} %get-tuple-element.58), channel_id=1, source_target_pairs={{0,12},{1,13},{2,14},{3,15},{4,8},{5,9},{6,10},{7,11},{8,20},{9,21... | collective-permute-start | bytes 786440 | tf_op jit(solution)/shard_map/ppermute | solution.py:359
  147.6 9.2 %collective-permute-start.36 = (bf16[128,1024]{1,0:T(8,128)(2,1)S(1)}, bf16[128,1024]{1,0:T(8,128)(2,1)S(1)}, u32[]{:S(2)}, u32[]{:S(2)}) collective-permute-start(bf16[128,1024]{1,0:T(8,128)(2,1)S(1)} %get-tuple-element.59), channel_id=1, source_target_pairs={{8,4},{9,5},{10,6},{11,7},{12,0},{13,1},{14,2},{15,3},{16,12},{17,... | collective-permute-start | bytes 786440 | tf_op jit(solution)/shard_map/ppermute | solution.py:359
  149.7 7.1 %copy-start.2 = (f32[1,128,2048]{2,1,0:T(8,128)S(1)}, f32[1,128,2048]{2,1,0:T(8,128)}, u32[]{:S(2)}) copy-start(f32[1,128,2048]{2,1,0:T(8,128)} %param.13) | copy-start | bytes 3145732
  149.7 7.1 %copy-start.3 = (f32[1,128,2048]{2,1,0:T(8,128)S(1)}, f32[1,128,2048]{2,1,0:T(8,128)}, u32[]{:S(2)}) copy-start(f32[1,128,2048]{2,1,0:T(8,128)} %param.14) | copy-start | bytes 3145732
  149.7 7.1 %copy-start.4 = (f32[1,128,2048]{2,1,0:T(8,128)S(1)}, f32[1,128,2048]{2,1,0:T(8,128)}, u32[]{:S(2)}) copy-start(f32[1,128,2048]{2,1,0:T(8,128)} %param.15) | copy-start | bytes 3145732
  (11 other events, 8.6 us)

commit v3 on v0

v3 whole, which is shorter than its diff:
```python
import functools

import jax
import jax.numpy as jnp
from jax import lax
from jax.experimental import pallas as pl
from jax.experimental.pallas import tpu as pltpu
from jax.sharding import PartitionSpec as P

beta_one = 0.9
beta_two = 0.95
learn_rate = 0.001
adam_eps = 1e-08
bias_one = 1.0 - 0.9**10
bias_two = 1.0 - 0.95**10
norm_eps = 1e-05
column_parts = 1

bf16 = jnp.bfloat16
f32 = jnp.float32


def cost(flops, moved):
    return pl.CostEstimate(flops=flops, bytes_accessed=moved, transcendentals=0)


def limit(mib):
    return pltpu.CompilerParams(vmem_limit_bytes=mib * 1024 * 1024)


def column_block(k, j, width, part=0, parts=1):
    seq = lax.axis_index("seq") ^ (k >> 1 << 1) ^ j
    x = (lax.axis_index("dp") % 2) ^ (k & 1)
    return pl.ds(pl.multiple_of(((seq * 2 + x) * parts + part) * width, width), width)


def norm_kernel(parts, tok_ref, gain_ref, grad_ref, *refs):
    out_refs = [refs[i : i + parts] for i in range(0, len(refs), parts)]
    chips = len(out_refs)
    feats = grad_ref.shape[-1]
    width = (out_refs[0][0].shape[-1] - feats) // 2
    tok = tok_ref[...].astype(f32)
    inv_rms = lax.rsqrt(jnp.mean(tok * tok, axis=-1, keepdims=True) + norm_eps)
    for k in (*range(1, chips), 0):
        for part in range(parts):
            out_ref = out_refs[k][part]
            for j in range(2):
                cols = column_block(k, j, width, part, parts)
                scaled = tok_ref[:, cols].astype(f32) * inv_rms
                out_ref[:, j * width : (j + 1) * width] = (scaled * gain_ref[:, cols]).astype(bf16)
            if part == 0:
                out_ref[:, 2 * width : 2 * width + feats] = grad_ref[...]


def norm_blocks(tokens, gain, grads, chips, width, parts):
    rows, model = tokens.shape
    feats = grads.shape[-1]
    step = min(rows, 32)
    lanes = [2 * width // parts + (feats if part == 0 else 0) for part in range(parts)]
    outs = pl.pallas_call(
        functools.partial(norm_kernel, parts),
        grid=(rows // step,),
        in_specs=[
            pl.BlockSpec((step, model), lambda i: (i, 0)),
            pl.BlockSpec((1, model), lambda i: (0, 0)),
            pl.BlockSpec((step, feats), lambda i: (i, 0)),
        ],
        out_specs=[pl.BlockSpec((step, n), lambda i: (i, 0)) for n in lanes] * chips,
        out_shape=[jax.ShapeDtypeStruct((rows, n), bf16) for n in lanes] * chips,
        compiler_params=limit(24),
        cost_estimate=cost(8 * rows * model, 4 * rows * model),
        name="norm_blocks",
    )(tokens, gain, grads)
    return [outs[i : i + parts] for i in range(0, len(outs), parts)]


def join_kernel(a_ref, b_ref, *refs):
    out_ref = refs[-1]
    half = a_ref.shape[0]
    out_ref[:half, :] = a_ref[...]
    out_ref[half:, :] = b_ref[...]


def join(a, b, after):
    rows, width = a.shape
    return pl.pallas_call(
        join_kernel,
        in_specs=[pl.BlockSpec(memory_space=pltpu.VMEM)] * 2
        + [pl.BlockSpec(memory_space=pl.ANY)] * len(after),
        out_shape=jax.ShapeDtypeStruct((2 * rows, width), a.dtype),
        compiler_params=limit(16),
        cost_estimate=cost(0, 8 * rows * width),
        name="join",
    )(a, b, *after)


def select_kernel(slots, owner_row_ref, owner_col_ref, out_ref):
    feats = owner_row_ref.shape[1]
    owner = owner_row_ref[...]
    lower = lax.broadcasted_iota(jnp.int32, (feats, feats), 0) < lax.broadcasted_iota(
        jnp.int32, (feats, feats), 1
    )
    same = (owner_col_ref[...] == owner) & lower
    place = jnp.sum(same.astype(f32), axis=0, keepdims=True).astype(jnp.int32)
    own_x = lax.axis_index("dp") % 2
    slot = (owner ^ own_x) * slots + place
    step = 256
    for at in range(0, out_ref.shape[0], step):
        index = at + lax.broadcasted_iota(jnp.int32, (step, feats), 0)
        out_ref[at : at + step, :] = (index == slot).astype(f32).astype(bf16)


def select_rows(owner, groups, slots):
    feats = owner.shape[0]
    return pl.pallas_call(
        functools.partial(select_kernel, slots),
        out_shape=jax.ShapeDtypeStruct((groups * slots, feats), bf16),
        compiler_params=limit(24),
        cost_estimate=cost(4 * groups * slots * feats, 2 * groups * slots * feats),
        name="select_rows",
    )(owner[None, :], owner[:, None])


def weight_kernel(planes, chips, plan, *refs):
    sel_ref, refs = refs[0], refs[1:]
    first, refs = refs[: 2 * chips], refs[2 * chips :]
    pieces, refs = refs[: 2 * chips], refs[2 * chips :]
    out_refs, (grads, held, base) = refs[-len(plan) - 4 : -3], refs[-3:]
    rows, feats = first[0].shape[0], sel_ref.shape[1]
    width = held.shape[1]
    block = sel_ref.shape[0] // planes
    z = lax.axis_index("dp") // 2
    for i in range(2 * chips):
        j = i // chips
        at = slice(i * rows, (i + 1) * rows)
        grads[at, :] = first[i][:, first[i].shape[1] - feats :]
        held[at, :] = pieces[i][:, j * width : (j + 1) * width]
    for at in range(0, feats, 256):
        base[at : at + 256, :] = lax.dot_general(
            grads[:, at : at + 256],
            held[...],
            (((0,), (0,)), ((), ())),
            preferred_element_type=f32,
        ).astype(bf16)

    def chosen(plane):
        at = pl.multiple_of(plane * block, block)
        return jnp.dot(sel_ref[pl.ds(at, block), :], base[...], preferred_element_type=f32)

    for (step, even), out_ref in zip(plan, out_refs):
        ahead = planes - step
        plane = jnp.where((z % 2 == 0) == even, z + ahead, z - ahead)

        @pl.when((plane >= 0) & (plane < planes))
        def _():
            out_ref[...] = chosen(plane).astype(bf16)

    out_refs[-1][...] = chosen(z).astype(bf16)


def weight_blocks(selected, first, pieces, planes, plan, after):
    chips = len(first) // 2
    slots_all, feats = selected.shape
    rows = first[0].shape[0]
    lanes = pieces[0].shape[1] - (feats if pieces[0] is first[0] else 0)
    width = lanes // 2
    total = 2 * chips * rows
    block = slots_all // planes
    return pl.pallas_call(
        functools.partial(weight_kernel, planes, chips, plan),
        in_specs=[pl.BlockSpec(memory_space=pltpu.VMEM)] * (1 + 4 * chips)
        + [pl.BlockSpec(memory_space=pl.ANY)] * len(after),
        out_shape=[jax.ShapeDtypeStruct((block, width), bf16)] * (len(plan) + 1),
        scratch_shapes=[
            pltpu.VMEM((total, feats), bf16),
            pltpu.VMEM((total, width), bf16),
            pltpu.VMEM((feats, width), bf16),
        ],
        compiler_params=limit(40),
        cost_estimate=cost(2 * (slots_all + total) * feats * width, 4 * total * width),
        name="weight_blocks",
    )(selected, *first, *pieces, *after)


def gather_weight(planes, piece_refs, held):
    dp = lax.axis_index("dp")
    own_x, own_z = dp % 2, dp // 2
    for j in range(2):
        for turn in range(planes):
            ref = piece_refs[j * planes + turn]
            share = ref.shape[0] // 2
            for i in range(2):
                at = pl.multiple_of(((own_z ^ turn) * 2 + (own_x ^ i)) * share, share)
                held[j, pl.ds(at, share), :] = ref[i * share : (i + 1) * share, :]


def back_kernel(planes, chips, parts, *refs):
    piece_refs, refs = refs[: chips * parts], refs[chips * parts :]
    weight_refs, refs = refs[: 2 * planes], refs[2 * planes :]
    out_refs, own_ref, held = refs[-chips - 2 : -2], refs[-2], refs[-1]
    _, feats, width = held.shape
    part_width = width // parts
    gather_weight(planes, weight_refs, held)
    dims = (((1,), (1,)), ((), ()))
    for k in (*range(1, chips), 0):
        pieces = piece_refs[k * parts : (k + 1) * parts]
        grads = pieces[0][:, pieces[0].shape[1] - feats :]
        total = None
        for j in range(2):
            out_refs[k][:, j * width : (j + 1) * width] = jnp.dot(
                grads, held[j], preferred_element_type=f32
            ).astype(bf16)
            for part in range(parts):
                term = lax.dot_general(
                    pieces[part][:, j * part_width : (j + 1) * part_width],
                    held[j, :, part * part_width : (part + 1) * part_width],
                    dims,
                    preferred_element_type=f32,
                )
                total = term if total is None else total + term
        if k == 0:
            own_ref[...] = total
        else:
            out_refs[k][:, 2 * width :] = total.astype(bf16)


def back_blocks(pieces, weights, planes, feats, after):
    chips, parts = len(pieces), len(pieces[0])
    rows = pieces[0][0].shape[0]
    width = weights[0].shape[-1]
    return pl.pallas_call(
        functools.partial(back_kernel, planes, chips, parts),
        in_specs=[pl.BlockSpec(memory_space=pltpu.VMEM)] * (chips * parts + 2 * planes)
        + [pl.BlockSpec(memory_space=pl.ANY)] * len(after),
        out_shape=[
            jax.ShapeDtypeStruct((rows, 2 * width + (feats if k else 0)), bf16)
            for k in range(chips)
        ]
        + [jax.ShapeDtypeStruct((rows, feats), f32)],
        scratch_shapes=[pltpu.VMEM((2, feats, width), bf16)],
        compiler_params=limit(40),
        cost_estimate=cost(8 * chips * rows * feats * width, 4 * chips * rows * width),
        name="back_blocks",
    )(*[p for piece in pieces for p in piece], *weights, *after)


def grad_x_kernel(tok_ref, gain_ref, part_ref, *refs):
    grad_refs, out_ref, values_ref = refs[:-2], refs[-2], refs[-1]
    model = tok_ref.shape[-1]
    width = grad_refs[0].shape[-1] // 2
    values = part_ref[...]
    for grad_ref in grad_refs[1:]:
        values += grad_ref[:, 2 * width :].astype(f32)
    values_ref[...] = values.astype(bf16)
    tok = tok_ref[...].astype(f32)
    inv_rms = lax.rsqrt(jnp.mean(tok * tok, axis=-1, keepdims=True) + norm_eps)
    total = jnp.zeros((tok.shape[0], 1), f32)
    for k, grad_ref in enumerate(grad_refs):
        for j in range(2):
            cols = column_block(k, j, width)
            weighted = gain_ref[:, cols] * grad_ref[:, j * width : (j + 1) * width].astype(f32)
            scaled = tok_ref[:, cols].astype(f32) * inv_rms
            total += jnp.sum(weighted * scaled, axis=-1, keepdims=True)
    mean = total / model
    for k, grad_ref in enumerate(grad_refs):
        for j in range(2):
            cols = column_block(k, j, width)
            weighted = gain_ref[:, cols] * grad_ref[:, j * width : (j + 1) * width].astype(f32)
            scaled = tok_ref[:, cols].astype(f32) * inv_rms
            out_ref[:, cols] = (inv_rms * (weighted - scaled * mean)).astype(bf16)


def grad_x_blocks(tokens, gain, part, grads):
    rows, model = tokens.shape
    feats = part.shape[-1]
    step = min(rows, 32)
    return pl.pallas_call(
        grad_x_kernel,
        grid=(rows // step,),
        in_specs=[
            pl.BlockSpec((step, model), lambda i: (i, 0)),
            pl.BlockSpec((1, model), lambda i: (0, 0)),
            pl.BlockSpec((step, feats), lambda i: (i, 0)),
        ]
        + [pl.BlockSpec((step, g.shape[1]), lambda i: (i, 0)) for g in grads],
        out_specs=[
            pl.BlockSpec((step, model), lambda i: (i, 0)),
            pl.BlockSpec((step, feats), lambda i: (i, 0)),
        ],
        out_shape=[
            jax.ShapeDtypeStruct((rows, model), bf16),
            jax.ShapeDtypeStruct((rows, feats), bf16),
        ],
        compiler_params=limit(24),
        cost_estimate=cost(16 * rows * model, 6 * rows * model),
        name="grad_x_blocks",
    )(tokens, gain, part, *grads)


def add_kernel(count, groups, *refs):
    for i, out_ref in enumerate(refs[-groups:]):
        total = refs[i * count][...].astype(f32)
        for ref in refs[i * count + 1 : (i + 1) * count]:
            total += ref[...].astype(f32)
        out_ref[...] = total.astype(out_ref.dtype)


def relay(sums, after):
    shape = sums[0][0].shape
    size = shape[0] * shape[1]
    return pl.pallas_call(
        functools.partial(add_kernel, len(sums[0]), len(sums)),
        in_specs=[pl.BlockSpec(memory_space=pltpu.VMEM)] * (len(sums) * len(sums[0]))
        + [pl.BlockSpec(memory_space=pl.ANY)] * len(after),
        out_shape=[jax.ShapeDtypeStruct(shape, bf16)] * len(sums),
        compiler_params=limit(16),
        cost_estimate=cost(2 * size, 12 * size),
        name="relay",
    )(*[a for group in sums for a in group], *after)


def finish_kernel(own_ref, even_ref, odd_ref, *refs):
    kept_ref, sent_ref = refs[-2:]
    half = kept_ref.shape[0]
    for part, out_ref in ((slice(half), kept_ref), (slice(half, 2 * half), sent_ref)):
        total = own_ref[part, :].astype(f32) + even_ref[part, :].astype(f32)
        out_ref[...] = (total + odd_ref[part, :].astype(f32)).astype(out_ref.dtype)


def finish(own, even, odd, after):
    height, width = own.shape
    return pl.pallas_call(
        finish_kernel,
        in_specs=[pl.BlockSpec(memory_space=pltpu.VMEM)] * 3
        + [pl.BlockSpec(memory_space=pl.ANY)] * len(after),
        out_shape=[
            jax.ShapeDtypeStruct((height // 2, width), f32),
            jax.ShapeDtypeStruct((height // 2, width), bf16),
        ],
        compiler_params=limit(16),
        cost_estimate=cost(2 * height * width, 9 * height * width),
        name="finish",
    )(own, even, odd, *after)


def adam_kernel(token_total, parts, owner_ref, *refs):
    kept_refs, got_refs, refs = refs[:parts], refs[parts : 2 * parts], refs[2 * parts :]
    master_ref, moment1_ref, moment2_ref = refs[:3]
    out_refs = refs[3:]
    step, width = kept_refs[0].shape
    dp = lax.axis_index("dp")
    owned = (owner_ref[...] == dp).astype(f32)
    count = jnp.sum(owned, axis=1, keepdims=True)
    index = pl.program_id(0) * step + lax.broadcasted_iota(jnp.int32, (step, 1), 0)
    occupied = (index.astype(f32) < count).astype(f32)
    for i, refs in enumerate((kept_refs, got_refs)):
        for part, ref in enumerate(refs):
            at = (((dp % 2) ^ i) * parts + part) * width
            cols = pl.ds(pl.multiple_of(at, width), width)
            slot_grad = ref[...].astype(f32) / token_total
            new_moment1 = (
                beta_one * moment1_ref[:, cols] + (1.0 - beta_one) * slot_grad
            ) * occupied
            new_moment2 = (
                beta_two * moment2_ref[:, cols] + (1.0 - beta_two) * slot_grad * slot_grad
            ) * occupied
            step_dir = new_moment1 / bias_one / (jnp.sqrt(new_moment2 / bias_two) + adam_eps)
            out_refs[0][:, cols] = (master_ref[:, cols] - learn_rate * step_dir) * occupied
            out_refs[1][:, cols] = new_moment1
            out_refs[2][:, cols] = new_moment2


def adam(owner, kept, got, states, token_total):
    slots, cols = states[0].shape
    width = kept[0].shape[-1]
    step = min(slots, 32)
    return pl.pallas_call(
        functools.partial(adam_kernel, token_total, len(kept)),
        grid=(slots // step,),
        in_specs=[pl.BlockSpec((1, owner.shape[0]), lambda i: (0, 0))]
        + [pl.BlockSpec((step, width), lambda i: (i, 0))] * (2 * len(kept))
        + [pl.BlockSpec((step, cols), lambda i: (i, 0))] * 3,
        out_specs=[pl.BlockSpec((step, cols), lambda i: (i, 0))] * 3,
        out_shape=[jax.ShapeDtypeStruct((slots, cols), f32)] * 3,
        compiler_params=limit(24),
        cost_estimate=cost(20 * slots * cols, 30 * slots * cols),
        name="adam",
    )(owner[None, :], *kept, *got, *states)


def on_device(groups, seqs, tokens, gain, w_t, grad_values, owner, master, moment1, moment2):
    planes = groups // 2
    chips = seqs
    parts = column_parts
    tokens, value_grad = tokens[0], grad_values[0]
    rows, model = tokens.shape
    feats = owner.shape[0]
    slots = master.shape[1]
    width = model // (2 * seqs)
    own_x = lax.axis_index("dp") % 2

    def permute(value, target):
        pairs = []
        for dp in range(groups):
            for seq in range(seqs):
                to = target(dp, seq)
                if to is not None:
                    pairs.append((dp * seqs + seq, to[0] * seqs + to[1]))
        return lax.ppermute(value, ("dp", "seq"), pairs)

    def to_chip(value, k):
        return permute(value, lambda dp, seq: (dp ^ (k & 1), seq ^ (k >> 1 << 1)))

    def to_core(value):
        return permute(value, lambda dp, seq: (dp, seq ^ 1))

    def to_x(value):
        return permute(value, lambda dp, seq: (dp ^ 1, seq))

    def to_plane(value, turn):
        return permute(value, lambda dp, seq: (dp ^ (2 * turn), seq))

    def busy(z, step, even):
        rightward = (z % 2 == 0) == even
        return z < step if rightward else planes - 1 - z < step

    def across(value, step, even):
        def target(dp, seq):
            z = dp // 2
            way = 1 if (z % 2 == 0) == even else -1
            return (dp + 2 * way, seq) if busy(z, step, even) else None

        return permute(value, target)

    w_keep = lax.dynamic_slice_in_dim(w_t, own_x * width, width, 1)
    w_got = to_x(lax.dynamic_slice_in_dim(w_t, (1 - own_x) * width, width, 1))
    gain_row = gain[None, :]
    sent = norm_blocks(tokens, gain_row, value_grad, chips, width, parts)
    near = [sent[0]] + [[to_chip(p, k) for p in sent[k]] for k in range(1, chips)]
    far = [[to_core(p) for p in piece] for piece in near]
    selected = select_rows(owner, groups, slots)

    w_plane = join(w_keep, w_got, (sent[0][0], selected))
    w_own = [w_plane] + [to_plane(w_plane, turn) for turn in range(1, planes)]
    weights = w_own + [to_core(w) for w in w_own]

    plan = [
        (step, even)
        for step in range(1, planes)
        for even in (True, False)
        if any(busy(z, step, even) for z in range(planes))
    ]
    kept, got = [], []
    first = [piece[0] for piece in near + far]
    for part in range(parts):
        pieces = [piece[part] for piece in near + far]
        after = weights if part == parts - 1 else []
        outs = weight_blocks(selected, first, pieces, planes, plan, after)
        ready = dict(zip(plan, outs))
        if part == parts - 1:
            back = back_blocks(near, weights, planes, feats, [outs[0]])
            home = [back[0]] + [to_chip(back[k], k) for k in range(1, chips)]
        held = {}
        for step in range(1, planes):
            here = [even for even in (True, False) if (step, even) in ready]
            send = [ready[step, even] for even in here]
            if held:
                sums = [[ready[step, even], held[not even]] for even in here if (not even) in held]
                sums = list(relay(sums, [back[0]] if step == 2 else home[-1:])) if sums else []
                send = []
                for even in here:
                    send.append(sums.pop(0) if (not even) in held else ready[step, even])
            held = {even: across(value, step, even) for even, value in zip(here, send)}
        keep, send = finish(outs[-1], held[True], held[False], home[1:])
        kept.append(keep)
        got.append(to_x(send))

    grad_x, values = grad_x_blocks(tokens, gain_row, back[-1], home)

    states = adam(owner, kept, got, (master[0], moment1[0], moment2[0]), rows * seqs * groups)
    return (values[None], grad_x[None], *(s[None] for s in states))


def solution(mesh):
    placed = (
        P("dp", "seq", None),
        P(),
        P("dp", "seq"),
        P("dp", "seq", None),
        P(),
        P("dp", None, "seq"),
        P("dp", None, "seq"),
        P("dp", None, "seq"),
    )
    return jax.shard_map(
        functools.partial(on_device, mesh.shape["dp"], mesh.shape["seq"]),
        mesh=mesh,
        in_specs=placed,
        out_specs=(
            P("dp", "seq", None),
            P("dp", "seq", None),
            P("dp", None, "seq"),
            P("dp", None, "seq"),
            P("dp", None, "seq"),
        ),
        check_vma=False,
    )
```

time: 300 us -> 105 us (0.35)
  waiting for transfers between devices: 210 us -> 44.9 us
  starting transfers between devices: 4.78 us -> 38.9 us
  blocking collectives: 29.9 us -> 0 us
  matrix products: 21.4 us -> 0 us
  Pallas kernels: 0 us -> 15.5 us
  between operations: 13.9 us -> 0.86 us
  other arithmetic: 10.3 us -> 0 us
  local copies, waits for them, and re-layouts: 8.92 us -> 3.56 us
    psum x1 -> x0, waiting for transfers between devices: 156 us -> none  [on_device(): summed = lax.psum(grad_block, 'dp')]
    all_gather x2 -> x0, waiting for transfers between devices: 53.7 us -> none  [the longest x1 51.4 us: on_device(): full_weight = lax.all_gather(col_block, 'seq', axis=1, tiled=True)]
    ppermute x0 -> x24, waiting for transfers between devices: none -> 44.9 us  [permute(): return lax.ppermute(value, ('dp', 'seq'), pairs)]
    ppermute x0 -> x24, starting transfers between devices: none -> 38.9 us  [permute(): return lax.ppermute(value, ('dp', 'seq'), pairs)]
    all_gather x1 -> x0, blocking collectives: 29.9 us -> none  [on_device(): grads_all = lax.all_gather(value_grad, 'seq', axis=0, tiled=True)]
    dot_general x4 -> x0, matrix products: 21.4 us -> none  [the longest x1 7.52 us: on_device(): slot_grad = jnp.dot(select_mine, summed, precision=lax.Precision.HIGHEST)]
    pallas_call x0 -> x10, Pallas kernels: none -> 15.5 us  [the longest x1 4.11 us: back_blocks(): pl.pallas_call(functools.partial(back_kernel, planes, chips, parts), in_s...]
    convert_element_type x1 -> x0, local copies, waits for them, and re-layouts: 6 us -> none  [on_device(): tok_float = tokens[0].astype(jnp.float32)]
  transfers between devices with their start and end apart: 4 -> 24, of which waited for: 3 -> 10; matrix products, arithmetic and copies ran while one was open for 9% -> 1% of each run, Pallas kernels for 0% -> 9%
where the time goes in v3:
time: 105 us; the launch traced here: 104 us
  waiting for transfers between devices  44.9 us (43%)
  starting transfers between devices  38.9 us (37%)
  Pallas kernels  15.5 us (15%)
  local copies, waits for them, and re-layouts  3.56 us (3%)
    ppermute x24, waiting for transfers between devices, permute(): return lax.ppermute(value, ('dp', 'seq'), pairs)  44.9 us
    ppermute x24, starting transfers between devices, permute(): return lax.ppermute(value, ('dp', 'seq'), pairs)  38.9 us
    pallas_call x1, Pallas kernels, back_blocks(): pl.pallas_call(functools.partial(back_kernel, planes, chips, parts), in_s...  4.11 us
    pallas_call x1, Pallas kernels, grad_x_blocks(): pl.pallas_call(grad_x_kernel, grid=(rows // step,), in_specs=[pl.BlockSpe...  3.62 us
    pallas_call x1, Pallas kernels, weight_blocks(): pl.pallas_call(functools.partial(weight_kernel, planes, chips, plan), in_...  3.04 us
    pallas_call x1, Pallas kernels, adam(): pl.pallas_call(functools.partial(adam_kernel, token_total, len(kept)), gr...  2.6 us
  transfers between devices with their start and end apart: 24, of which 10 were waited for; matrix products, arithmetic and copies ran while one was open for 1% of the time, Pallas kernels for 9%

profile of v3, /device:TPU:0, one launch (start us, length us, event | category | flops | bytes accessed | tf_op | source)
XLA Modules:
  0.0 103.8 jit_solution(13356407752479116578)
XLA Ops:
  0.7 1.1 %constant_dynamic-slice_fusion = (bf16[64,1024]{1,0:T(8,128)(2,1)S(1)}, bf16[64,1024]{1,0:T(8,128)(2,1)S(1)}) fusion(bf16[64,2048]{1,0:T(8,128)(2,1)} %param.10, s32[]{:T(128)S(6)} %select_n.15, s32[]{:T(128)S(6)} %select_n.14), kind=kLoop, calls=%fused_computation | loop fusion | bytes 524296 | tf_op jit(solution)/shard_map/dynamic_slice | solution.py:436
  1.8 3.0 %collective-permute-start.3 = (bf16[64,1024]{1,0:T(8,128)(2,1)S(1)}, bf16[64,1024]{1,0:T(8,128)(2,1)S(1)}, u32[]{:S(2)}, u32[]{:S(2)}) collective-permute-start(bf16[64,1024]{1,0:T(8,128)(2,1)S(1)} %get-tuple-element.53), channel_id=1, source_target_pairs={{0,4},{1,5},{2,6},{3,7},{4,0},{5,1},{6,2},{7,3},{8,12},{9,13},{10,... | collective-permute-start | bytes 393224 | tf_op jit(solution)/shard_map/ppermute | solution.py:409
  4.8 0.8 copy.13.owner_col_ref
  5.6 0.0 copy-start.6
  5.7 0.7 copy-done.6
  6.3 0.4 select_rows.1.refs_1_.refs_0_
  6.8 0.0 copy-start.5
  6.8 0.9 copy-done.5
  7.7 1.2 %norm_blocks.1 = (bf16[128,2560]{1,0:T(8,128)(2,1)S(1)}, bf16[128,2560]{1,0:T(8,128)(2,1)S(1)}, bf16[128,2560]{1,0:T(8,128)(2,1)S(1)}, bf16[128,2560]{1,0:T(8,128)(2,1)S(1)}) custom-call(bf16[128,8192]{1,0:T(8,128)(2,1)S(1)} %bitcast.13, f32[1,8192]{1,0:T(1,128)S(1)} %bitcast.18, bf16[128,512]{1,0:T(8,128)(2,1)S(1)} %bitcast.20), custom_call_target="tpu_custom_call" | custom-call | flops 8388608 | bytes 4194304 | tf_op jit(solution)/shard_map/norm_blocks/pallas_call | solution.py:60
  8.9 0.0 collective-permute-done.3.b_ref
  8.9 0.1 collective-permute-start.7
  9.0 1.2 %collective-permute-start = (bf16[128,2560]{1,0:T(8,128)(2,1)S(1)}, bf16[128,2560]{1,0:T(8,128)(2,1)S(1)}, u32[]{:S(2)}, u32[]{:S(2)}) collective-permute-start(bf16[128,2560]{1,0:T(8,128)(2,1)S(1)} %get-tuple-element.30), channel_id=1, source_target_pairs={{0,4},{1,5},{2,6},{3,7},{4,0},{5,1},{6,2},{7,3},{8,12},{9,13},{10,... | collective-permute-start | bytes 1966088 | tf_op jit(solution)/shard_map/ppermute | solution.py:409
  10.2 1.5 %collective-permute-start.1 = (bf16[128,2560]{1,0:T(8,128)(2,1)S(1)}, bf16[128,2560]{1,0:T(8,128)(2,1)S(1)}, u32[]{:S(2)}, u32[]{:S(2)}) collective-permute-start(bf16[128,2560]{1,0:T(8,128)(2,1)S(1)} %get-tuple-element.31), channel_id=1, source_target_pairs={{0,2},{1,3},{2,0},{3,1},{4,6},{5,7},{6,4},{7,5},{8,10},{9,11},{10,... | collective-permute-start | bytes 1966088 | tf_op jit(solution)/shard_map/ppermute | solution.py:409
  11.7 0.8 collective-permute-start.2
  12.6 3.6 %collective-permute-start.6 = (bf16[128,1024]{1,0:T(8,128)(2,1)S(1)}, bf16[128,1024]{1,0:T(8,128)(2,1)S(1)}, u32[]{:S(2)}, u32[]{:S(2)}) collective-permute-start(bf16[128,1024]{1,0:T(8,128)(2,1)S(1)} %join.1.refs_17_.refs_4_), channel_id=1, source_target_pairs={{0,24},{1,25},{2,26},{3,27},{4,28},{5,29},{6,30},{7,31},{8,16},{9,... | collective-permute-start | bytes 786440 | tf_op jit(solution)/shard_map/ppermute | solution.py:409
  16.2 0.0 collective-permute-done.7.refs_21_.refs_8_
  16.2 7.5 %collective-permute-done.6.refs_20_.refs_7_ = bf16[128,1024]{1,0:T(8,128)(2,1)S(1)} collective-permute-done((bf16[128,1024]{1,0:T(8,128)(2,1)S(1)}, bf16[128,1024]{1,0:T(8,128)(2,1)S(1)}, u32[]{:S(2)}, u32[]{:S(2)}) %collective-permute-start.6) | collective-permute-done | bytes 262176 | tf_op jit(solution)/shard_map/ppermute | solution.py:409
  23.6 10.6 %collective-permute-start.4 = (bf16[128,1024]{1,0:T(8,128)(2,1)S(1)}, bf16[128,1024]{1,0:T(8,128)(2,1)S(1)}, u32[]{:S(2)}, u32[]{:S(2)}) collective-permute-start(bf16[128,1024]{1,0:T(8,128)(2,1)S(1)} %join.1.refs_17_.refs_4_), channel_id=1, source_target_pairs={{0,8},{1,9},{2,10},{3,11},{4,12},{5,13},{6,14},{7,15},{8,0},{9,1},... | collective-permute-start | bytes 786440 | tf_op jit(solution)/shard_map/ppermute | solution.py:409
  34.2 4.2 %collective-permute-done.5.refs_19_.refs_6_ = bf16[128,1024]{1,0:T(8,128)(2,1)S(1)} collective-permute-done((bf16[128,1024]{1,0:T(8,128)(2,1)S(1)}, bf16[128,1024]{1,0:T(8,128)(2,1)S(1)}, u32[]{:S(2)}, u32[]{:S(2)}) %collective-permute-start.5) | collective-permute-done | bytes 262176 | tf_op jit(solution)/shard_map/ppermute | solution.py:409
  38.4 5.3 %collective-permute-done.4.refs_18_.refs_5_ = bf16[128,1024]{1,0:T(8,128)(2,1)S(1)} collective-permute-done((bf16[128,1024]{1,0:T(8,128)(2,1)S(1)}, bf16[128,1024]{1,0:T(8,128)(2,1)S(1)}, u32[]{:S(2)}, u32[]{:S(2)}) %collective-permute-start.4) | collective-permute-done | bytes 262176 | tf_op jit(solution)/shard_map/ppermute | solution.py:409
  43.6 0.5 collective-permute-start.12
  44.1 0.1 collective-permute-start.13
  44.2 0.4 collective-permute-start.14
  44.7 0.1 collective-permute-start.9
  44.7 4.2 %collective-permute-done.9.refs_23_.refs_10_ = bf16[128,1024]{1,0:T(8,128)(2,1)S(1)} collective-permute-done((bf16[128,1024]{1,0:T(8,128)(2,1)S(1)}, bf16[128,1024]{1,0:T(8,128)(2,1)S(1)}, u32[]{:S(2)}, u32[]{:S(2)}) %collective-permute-start.9) | collective-permute-done | bytes 262176 | tf_op jit(solution)/shard_map/ppermute | solution.py:409
  48.9 0.1 collective-permute-start.8
  49.1 1.4 %collective-permute-done.8.refs_22_.refs_9_ = bf16[128,1024]{1,0:T(8,128)(2,1)S(1)} collective-permute-done((bf16[128,1024]{1,0:T(8,128)(2,1)S(1)}, bf16[128,1024]{1,0:T(8,128)(2,1)S(1)}, u32[]{:S(2)}, u32[]{:S(2)}) %collective-permute-start.8) | collective-permute-done | bytes 262176 | tf_op jit(solution)/shard_map/ppermute | solution.py:409
  50.5 3.0 %weight_blocks.1 = (bf16[256,1024]{1,0:T(8,128)(2,1)S(1)}, bf16[256,1024]{1,0:T(8,128)(2,1)S(1)}, bf16[256,1024]{1,0:T(8,128)(2,1)S(1)}, bf16[256,1024]{1,0:T(8,...) custom-call(bf16[1024,512]{1,0:T(8,128)(2,1)S(1)} %select_rows.1.refs_1_.refs_0_, ...), custom_call_target="tpu_custom_call" | custom-call | flops 2147483648 | bytes 4194304 | tf_op jit(solution)/shard_map/weight_blocks/pallas_call | solution.py:169
  53.5 1.5 %collective-permute-start.18 = (bf16[256,1024]{1,0:T(8,128)(2,1)S(1)}, bf16[256,1024]{1,0:T(8,128)(2,1)S(1)}, u32[]{:S(2)}, u32[]{:S(2)}) collective-permute-start(bf16[256,1024]{1,0:T(8,128)(2,1)S(1)} %get-tuple-element.33.refs_12_), channel_id=1, source_target_pairs={{0,8},{1,9},{2,10},{3,11},{4,12},{5,13},{6,14},{7,15},{24,16},{25,... | collective-permute-start | bytes 1572872 | tf_op jit(solution)/shard_map/ppermute | solution.py:409
  55.0 4.1 %back_blocks.1 = (bf16[128,2048]{1,0:T(8,128)(2,1)S(1)}, bf16[128,2560]{1,0:T(8,128)(2,1)S(1)}, bf16[128,2560]{1,0:T(8,128)(2,1)S(1)}, bf16[128,2560]{1,0:T(8,128)(2,1)S(1)}, f32[128,512]{1,0:T(8,128)S(1)}) custom-call(bf16[128,2560]{1,0:T(8,128)(2,1)S(1)} %get-tuple-element.29.refs_0_.refs_1_.refs_9_, ...), custom_call_target="tpu_custom_call" | custom-call | flops 2147483648 | bytes 2097152 | tf_op jit(solution)/shard_map/back_blocks/pallas_call | solution.py:231
  59.2 2.2 %collective-permute-start.17 = (bf16[128,2560]{1,0:T(8,128)(2,1)S(1)}, bf16[128,2560]{1,0:T(8,128)(2,1)S(1)}, u32[]{:S(2)}, u32[]{:S(2)}) collective-permute-start(bf16[128,2560]{1,0:T(8,128)(2,1)S(1)} %get-tuple-element.38), channel_id=1, source_target_pairs={{0,6},{1,7},{2,4},{3,5},{4,2},{5,3},{6,0},{7,1},{8,14},{9,15},{10,... | collective-permute-start | bytes 1966088 | tf_op jit(solution)/shard_map/ppermute | solution.py:409
  61.3 1.3 %collective-permute-start.20 = (bf16[256,1024]{1,0:T(8,128)(2,1)S(1)}, bf16[256,1024]{1,0:T(8,128)(2,1)S(1)}, u32[]{:S(2)}, u32[]{:S(2)}) collective-permute-start(bf16[256,1024]{1,0:T(8,128)(2,1)S(1)} %get-tuple-element.45), channel_id=1, source_target_pairs={{0,8},{1,9},{2,10},{3,11},{4,12},{5,13},{6,14},{7,15},{24,16},{25,... | collective-permute-start | bytes 1572872 | tf_op jit(solution)/shard_map/ppermute | solution.py:409
  62.7 4.6 %collective-permute-done.18.refs_1_ = bf16[256,1024]{1,0:T(8,128)(2,1)S(1)} collective-permute-done((bf16[256,1024]{1,0:T(8,128)(2,1)S(1)}, bf16[256,1024]{1,0:T(8,128)(2,1)S(1)}, u32[]{:S(2)}, u32[]{:S(2)}) %collective-permute-start.18) | collective-permute-done | bytes 524320 | tf_op jit(solution)/shard_map/ppermute | solution.py:409
  67.3 0.1 relay.2
  67.4 0.7 collective-permute-start.19
  68.1 1.2 %collective-permute-start.15 = (bf16[128,2560]{1,0:T(8,128)(2,1)S(1)}, bf16[128,2560]{1,0:T(8,128)(2,1)S(1)}, u32[]{:S(2)}, u32[]{:S(2)}) collective-permute-start(bf16[128,2560]{1,0:T(8,128)(2,1)S(1)} %get-tuple-element.36), channel_id=1, source_target_pairs={{0,4},{1,5},{2,6},{3,7},{4,0},{5,1},{6,2},{7,3},{8,12},{9,13},{10,... | collective-permute-start | bytes 1966088 | tf_op jit(solution)/shard_map/ppermute | solution.py:409
  69.3 1.5 %collective-permute-start.16 = (bf16[128,2560]{1,0:T(8,128)(2,1)S(1)}, bf16[128,2560]{1,0:T(8,128)(2,1)S(1)}, u32[]{:S(2)}, u32[]{:S(2)}) collective-permute-start(bf16[128,2560]{1,0:T(8,128)(2,1)S(1)} %get-tuple-element.37), channel_id=1, source_target_pairs={{0,2},{1,3},{2,0},{3,1},{4,6},{5,7},{6,4},{7,5},{8,10},{9,11},{10,... | collective-permute-start | bytes 1966088 | tf_op jit(solution)/shard_map/ppermute | solution.py:409
  70.8 7.0 %collective-permute-done.20.refs_3_ = bf16[256,1024]{1,0:T(8,128)(2,1)S(1)} collective-permute-done((bf16[256,1024]{1,0:T(8,128)(2,1)S(1)}, bf16[256,1024]{1,0:T(8,128)(2,1)S(1)}, u32[]{:S(2)}, u32[]{:S(2)}) %collective-permute-start.20) | collective-permute-done | bytes 524320 | tf_op jit(solution)/shard_map/ppermute | solution.py:409
  77.8 0.2 relay.3
  78.1 6.6 %collective-permute-start.21 = (bf16[256,1024]{1,0:T(8,128)(2,1)S(1)}, bf16[256,1024]{1,0:T(8,128)(2,1)S(1)}, u32[]{:S(2)}, u32[]{:S(2)}) collective-permute-start(bf16[256,1024]{1,0:T(8,128)(2,1)S(1)} %get-tuple-element.46), channel_id=1, source_target_pairs={{0,8},{1,9},{2,10},{3,11},{4,12},{5,13},{6,14},{7,15},{8,0},{9,1},... | collective-permute-start | bytes 1572872 | tf_op jit(solution)/shard_map/ppermute | solution.py:409
  84.6 0.7 collective-permute-start.22
  85.3 5.6 %collective-permute-done.15.refs_1_.refs_0_ = bf16[128,2560]{1,0:T(8,128)(2,1)S(1)} collective-permute-done((bf16[128,2560]{1,0:T(8,128)(2,1)S(1)}, bf16[128,2560]{1,0:T(8,128)(2,1)S(1)}, u32[]{:S(2)}, u32[]{:S(2)}) %collective-permute-start.15) | collective-permute-done | bytes 655392 | tf_op jit(solution)/shard_map/ppermute | solution.py:409
  90.9 3.6 %collective-permute-done.21.even_ref = bf16[256,1024]{1,0:T(8,128)(2,1)S(1)} collective-permute-done((bf16[256,1024]{1,0:T(8,128)(2,1)S(1)}, bf16[256,1024]{1,0:T(8,128)(2,1)S(1)}, u32[]{:S(2)}, u32[]{:S(2)}) %collective-permute-start.21) | collective-permute-done | bytes 524320 | tf_op jit(solution)/shard_map/ppermute | solution.py:409
  94.5 0.2 finish.1
  94.7 1.2 %collective-permute-start.23 = (bf16[128,1024]{1,0:T(8,128)(2,1)S(1)}, bf16[128,1024]{1,0:T(8,128)(2,1)S(1)}, u32[]{:S(2)}, u32[]{:S(2)}) collective-permute-start(bf16[128,1024]{1,0:T(8,128)(2,1)S(1)} %get-tuple-element.49), channel_id=1, source_target_pairs={{0,4},{1,5},{2,6},{3,7},{4,0},{5,1},{6,2},{7,3},{8,12},{9,13},{10,... | collective-permute-start | bytes 786440 | tf_op jit(solution)/shard_map/ppermute | solution.py:409
  95.9 3.6 %grad_x_blocks.1 = (bf16[128,8192]{1,0:T(8,128)(2,1)}, bf16[128,512]{1,0:T(8,128)(2,1)}) custom-call(bf16[128,8192]{1,0:T(8,128)(2,1)S(1)} %bitcast.14, f32[1,8192]{1,0:T(1,128)S(1)} %bitcast.19, f32[128,512]{1,0:T(8,128)S(1)} %get-tuple-element.34.part_ref, bf16[128,2048]{1,0:T(8,128)(2,1)S(1)} %get-tuple-element.35.refs_0_.refs_2_, ...), custom_call_target="tpu_custom_call" | custom-call | flops 16777216 | bytes 6291456 | tf_op jit(solution)/shard_map/grad_x_blocks/pallas_call | solution.py:277
  99.6 1.6 %collective-permute-done.23.refs_1_ = bf16[128,1024]{1,0:T(8,128)(2,1)S(1)} collective-permute-done((bf16[128,1024]{1,0:T(8,128)(2,1)S(1)}, bf16[128,1024]{1,0:T(8,128)(2,1)S(1)}, u32[]{:S(2)}, u32[]{:S(2)}) %collective-permute-start.23) | collective-permute-done | bytes 262176 | tf_op jit(solution)/shard_map/ppermute | solution.py:409
  101.2 2.6 %adam.1 = (f32[128,2048]{1,0:T(8,128)}, f32[128,2048]{1,0:T(8,128)}, f32[128,2048]{1,0:T(8,128)}) custom-call(s32[1,512]{1,0:T(1,128)S(1)} %bitcast.23, f32[128,1024]{1,0:T(8,128)S(1)} %get-tuple-element.48.refs_0_, bf16[128,1024]{1,0:T(8,128)(2,1)S(1)} %collective-permute-done.23.refs_1_, f32[128,2048]{1,0:T(8,128)S(1)} %bitcast.15, ...), custom_call_target="tpu_custom_call" | custom-call | flops 5242880 | bytes 7864320 | tf_op jit(solution)/shard_map/adam/pallas_call | solution.py:377
  (28 shorter events, 0.1 us)
Async XLA Ops:
  0.6 6.1 %copy-start.4 = (f32[8192]{0:T(1024)S(1)}, f32[8192]{0:T(1024)}, u32[]{:S(2)}) copy-start(f32[8192]{0:T(1024)} %param.9) | copy-start | bytes 98308
  0.6 6.1 %copy-start = (bf16[1,128,8192]{2,1,0:T(8,128)(2,1)S(1)}, bf16[1,128,8192]{2,1,0:T(8,128)(2,1)}, u32[]{:S(2)}) copy-start(bf16[1,128,8192]{2,1,0:T(8,128)(2,1)} %param.8) | copy-start | bytes 6291460
  1.8 7.1 %collective-permute-start.3 = (bf16[64,1024]{1,0:T(8,128)(2,1)S(1)}, bf16[64,1024]{1,0:T(8,128)(2,1)S(1)}, u32[]{:S(2)}, u32[]{:S(2)}) collective-permute-start(bf16[64,1024]{1,0:T(8,128)(2,1)S(1)} %get-tuple-element.53), channel_id=1, source_target_pairs={{0,4},{1,5},{2,6},{3,7},{4,0},{5,1},{6,2},{7,3},{8,12},{9,13},{10,... | collective-permute-start | bytes 393224 | tf_op jit(solution)/shard_map/ppermute | solution.py:409
  5.6 0.7 copy-start.6
  6.8 0.9 copy-start.5
  8.9 7.2 %collective-permute-start.7 = (bf16[128,1024]{1,0:T(8,128)(2,1)S(1)}, bf16[128,1024]{1,0:T(8,128)(2,1)S(1)}, u32[]{:S(2)}, u32[]{:S(2)}) collective-permute-start(bf16[128,1024]{1,0:T(8,128)(2,1)S(1)} %join.1.refs_17_.refs_4_), channel_id=1, source_target_pairs={{0,1},{1,0},{2,3},{3,2},{4,5},{5,4},{6,7},{7,6},{8,9},{9,8},{10,11... | collective-permute-start | bytes 786440 | tf_op jit(solution)/shard_map/ppermute | solution.py:409
  9.0 34.6 %collective-permute-start = (bf16[128,2560]{1,0:T(8,128)(2,1)S(1)}, bf16[128,2560]{1,0:T(8,128)(2,1)S(1)}, u32[]{:S(2)}, u32[]{:S(2)}) collective-permute-start(bf16[128,2560]{1,0:T(8,128)(2,1)S(1)} %get-tuple-element.30), channel_id=1, source_target_pairs={{0,4},{1,5},{2,6},{3,7},{4,0},{5,1},{6,2},{7,3},{8,12},{9,13},{10,... | collective-permute-start | bytes 1966088 | tf_op jit(solution)/shard_map/ppermute | solution.py:409
  10.2 33.9 %collective-permute-start.1 = (bf16[128,2560]{1,0:T(8,128)(2,1)S(1)}, bf16[128,2560]{1,0:T(8,128)(2,1)S(1)}, u32[]{:S(2)}, u32[]{:S(2)}) collective-permute-start(bf16[128,2560]{1,0:T(8,128)(2,1)S(1)} %get-tuple-element.31), channel_id=1, source_target_pairs={{0,2},{1,3},{2,0},{3,1},{4,6},{5,7},{6,4},{7,5},{8,10},{9,11},{10,... | collective-permute-start | bytes 1966088 | tf_op jit(solution)/shard_map/ppermute | solution.py:409
  11.7 32.5 %collective-permute-start.2 = (bf16[128,2560]{1,0:T(8,128)(2,1)S(1)}, bf16[128,2560]{1,0:T(8,128)(2,1)S(1)}, u32[]{:S(2)}, u32[]{:S(2)}) collective-permute-start(bf16[128,2560]{1,0:T(8,128)(2,1)S(1)} %get-tuple-element.32), channel_id=1, source_target_pairs={{0,6},{1,7},{2,4},{3,5},{4,2},{5,3},{6,0},{7,1},{8,14},{9,15},{10,... | collective-permute-start | bytes 1966088 | tf_op jit(solution)/shard_map/ppermute | solution.py:409
  12.6 11.1 %collective-permute-start.6 = (bf16[128,1024]{1,0:T(8,128)(2,1)S(1)}, bf16[128,1024]{1,0:T(8,128)(2,1)S(1)}, u32[]{:S(2)}, u32[]{:S(2)}) collective-permute-start(bf16[128,1024]{1,0:T(8,128)(2,1)S(1)} %join.1.refs_17_.refs_4_), channel_id=1, source_target_pairs={{0,24},{1,25},{2,26},{3,27},{4,28},{5,29},{6,30},{7,31},{8,16},{9,... | collective-permute-start | bytes 786440 | tf_op jit(solution)/shard_map/ppermute | solution.py:409
  16.2 22.2 %collective-permute-start.5 = (bf16[128,1024]{1,0:T(8,128)(2,1)S(1)}, bf16[128,1024]{1,0:T(8,128)(2,1)S(1)}, u32[]{:S(2)}, u32[]{:S(2)}) collective-permute-start(bf16[128,1024]{1,0:T(8,128)(2,1)S(1)} %join.1.refs_17_.refs_4_), channel_id=1, source_target_pairs={{0,16},{1,17},{2,18},{3,19},{4,20},{5,21},{6,22},{7,23},{8,24},{9,... | collective-permute-start | bytes 786440 | tf_op jit(solution)/shard_map/ppermute | solution.py:409
  23.6 20.0 %collective-permute-start.4 = (bf16[128,1024]{1,0:T(8,128)(2,1)S(1)}, bf16[128,1024]{1,0:T(8,128)(2,1)S(1)}, u32[]{:S(2)}, u32[]{:S(2)}) collective-permute-start(bf16[128,1024]{1,0:T(8,128)(2,1)S(1)} %join.1.refs_17_.refs_4_), channel_id=1, source_target_pairs={{0,8},{1,9},{2,10},{3,11},{4,12},{5,13},{6,14},{7,15},{8,0},{9,1},... | collective-permute-start | bytes 786440 | tf_op jit(solution)/shard_map/ppermute | solution.py:409
  38.4 6.3 %collective-permute-start.10 = (bf16[128,1024]{1,0:T(8,128)(2,1)S(1)}, bf16[128,1024]{1,0:T(8,128)(2,1)S(1)}, u32[]{:S(2)}, u32[]{:S(2)}) collective-permute-start(bf16[128,1024]{1,0:T(8,128)(2,1)S(1)} %collective-permute-done.6.refs_20_.refs_7_), channel_id=1, source_target_pairs={{0,1},{1,0},{2,3},{3,2},{4,5},{5,4},{6,7},{7,6},{8,9},{9,8},{10,11... | collective-permute-start | bytes 786440 | tf_op jit(solution)/shard_map/ppermute | solution.py:409
  43.6 6.8 %collective-permute-start.11 = (bf16[128,2560]{1,0:T(8,128)(2,1)S(1)}, bf16[128,2560]{1,0:T(8,128)(2,1)S(1)}, u32[]{:S(2)}, u32[]{:S(2)}) collective-permute-start(bf16[128,2560]{1,0:T(8,128)(2,1)S(1)} %get-tuple-element.29.refs_0_.refs_1_.refs_9_), channel_id=1, source_target_pairs={{0,1},{1,0},{2,3},{3,2},{4,5},{5,4},{6,7},{7,6},{8,9},{9,8},{10,11... | collective-permute-start | bytes 1966088 | tf_op jit(solution)/shard_map/ppermute | solution.py:409
  43.6 6.8 %collective-permute-start.12 = (bf16[128,2560]{1,0:T(8,128)(2,1)S(1)}, bf16[128,2560]{1,0:T(8,128)(2,1)S(1)}, u32[]{:S(2)}, u32[]{:S(2)}) collective-permute-start(bf16[128,2560]{1,0:T(8,128)(2,1)S(1)} %collective-permute-done.refs_2_.refs_10_.refs_1_), channel_id=1, source_target_pairs={{0,1},{1,0},{2,3},{3,2},{4,5},{5,4},{6,7},{7,6},{8,9},{9,8},{10,11... | collective-permute-start | bytes 1966088 | tf_op jit(solution)/shard_map/ppermute | solution.py:409
  44.1 6.3 %collective-permute-start.13 = (bf16[128,2560]{1,0:T(8,128)(2,1)S(1)}, bf16[128,2560]{1,0:T(8,128)(2,1)S(1)}, u32[]{:S(2)}, u32[]{:S(2)}) collective-permute-start(bf16[128,2560]{1,0:T(8,128)(2,1)S(1)} %collective-permute-done.1.refs_3_.refs_11_.refs_2_), channel_id=1, source_target_pairs={{0,1},{1,0},{2,3},{3,2},{4,5},{5,4},{6,7},{7,6},{8,9},{9,8},{10,11... | collective-permute-start | bytes 1966088 | tf_op jit(solution)/shard_map/ppermute | solution.py:409
  44.2 6.2 %collective-permute-start.14 = (bf16[128,2560]{1,0:T(8,128)(2,1)S(1)}, bf16[128,2560]{1,0:T(8,128)(2,1)S(1)}, u32[]{:S(2)}, u32[]{:S(2)}) collective-permute-start(bf16[128,2560]{1,0:T(8,128)(2,1)S(1)} %collective-permute-done.2.refs_4_.refs_12_.refs_3_), channel_id=1, source_target_pairs={{0,1},{1,0},{2,3},{3,2},{4,5},{5,4},{6,7},{7,6},{8,9},{9,8},{10,11... | collective-permute-start | bytes 1966088 | tf_op jit(solution)/shard_map/ppermute | solution.py:409
  44.7 4.2 %collective-permute-start.9 = (bf16[128,1024]{1,0:T(8,128)(2,1)S(1)}, bf16[128,1024]{1,0:T(8,128)(2,1)S(1)}, u32[]{:S(2)}, u32[]{:S(2)}) collective-permute-start(bf16[128,1024]{1,0:T(8,128)(2,1)S(1)} %collective-permute-done.5.refs_19_.refs_6_), channel_id=1, source_target_pairs={{0,1},{1,0},{2,3},{3,2},{4,5},{5,4},{6,7},{7,6},{8,9},{9,8},{10,11... | collective-permute-start | bytes 786440 | tf_op jit(solution)/shard_map/ppermute | solution.py:409
  48.9 1.5 %collective-permute-start.8 = (bf16[128,1024]{1,0:T(8,128)(2,1)S(1)}, bf16[128,1024]{1,0:T(8,128)(2,1)S(1)}, u32[]{:S(2)}, u32[]{:S(2)}) collective-permute-start(bf16[128,1024]{1,0:T(8,128)(2,1)S(1)} %collective-permute-done.4.refs_18_.refs_5_), channel_id=1, source_target_pairs={{0,1},{1,0},{2,3},{3,2},{4,5},{5,4},{6,7},{7,6},{8,9},{9,8},{10,11... | collective-permute-start | bytes 786440 | tf_op jit(solution)/shard_map/ppermute | solution.py:409
  53.5 13.7 %collective-permute-start.18 = (bf16[256,1024]{1,0:T(8,128)(2,1)S(1)}, bf16[256,1024]{1,0:T(8,128)(2,1)S(1)}, u32[]{:S(2)}, u32[]{:S(2)}) collective-permute-start(bf16[256,1024]{1,0:T(8,128)(2,1)S(1)} %get-tuple-element.33.refs_12_), channel_id=1, source_target_pairs={{0,8},{1,9},{2,10},{3,11},{4,12},{5,13},{6,14},{7,15},{24,16},{25,... | collective-permute-start | bytes 1572872 | tf_op jit(solution)/shard_map/ppermute | solution.py:409
  59.2 18.7 %collective-permute-start.17 = (bf16[128,2560]{1,0:T(8,128)(2,1)S(1)}, bf16[128,2560]{1,0:T(8,128)(2,1)S(1)}, u32[]{:S(2)}, u32[]{:S(2)}) collective-permute-start(bf16[128,2560]{1,0:T(8,128)(2,1)S(1)} %get-tuple-element.38), channel_id=1, source_target_pairs={{0,6},{1,7},{2,4},{3,5},{4,2},{5,3},{6,0},{7,1},{8,14},{9,15},{10,... | collective-permute-start | bytes 1966088 | tf_op jit(solution)/shard_map/ppermute | solution.py:409
  61.3 16.5 %collective-permute-start.20 = (bf16[256,1024]{1,0:T(8,128)(2,1)S(1)}, bf16[256,1024]{1,0:T(8,128)(2,1)S(1)}, u32[]{:S(2)}, u32[]{:S(2)}) collective-permute-start(bf16[256,1024]{1,0:T(8,128)(2,1)S(1)} %get-tuple-element.45), channel_id=1, source_target_pairs={{0,8},{1,9},{2,10},{3,11},{4,12},{5,13},{6,14},{7,15},{24,16},{25,... | collective-permute-start | bytes 1572872 | tf_op jit(solution)/shard_map/ppermute | solution.py:409
  67.4 10.4 %collective-permute-start.19 = (bf16[256,1024]{1,0:T(8,128)(2,1)S(1)}, bf16[256,1024]{1,0:T(8,128)(2,1)S(1)}, u32[]{:S(2)}, u32[]{:S(2)}) collective-permute-start(bf16[256,1024]{1,0:T(8,128)(2,1)S(1)} %relay.2), channel_id=1, source_target_pairs={{8,16},{9,17},{10,18},{11,19},{12,20},{13,21},{14,22},{15,23},{16,... | collective-permute-start | bytes 1572872 | tf_op jit(solution)/shard_map/ppermute | solution.py:409
  68.1 22.8 %collective-permute-start.15 = (bf16[128,2560]{1,0:T(8,128)(2,1)S(1)}, bf16[128,2560]{1,0:T(8,128)(2,1)S(1)}, u32[]{:S(2)}, u32[]{:S(2)}) collective-permute-start(bf16[128,2560]{1,0:T(8,128)(2,1)S(1)} %get-tuple-element.36), channel_id=1, source_target_pairs={{0,4},{1,5},{2,6},{3,7},{4,0},{5,1},{6,2},{7,3},{8,12},{9,13},{10,... | collective-permute-start | bytes 1966088 | tf_op jit(solution)/shard_map/ppermute | solution.py:409
  69.3 21.6 %collective-permute-start.16 = (bf16[128,2560]{1,0:T(8,128)(2,1)S(1)}, bf16[128,2560]{1,0:T(8,128)(2,1)S(1)}, u32[]{:S(2)}, u32[]{:S(2)}) collective-permute-start(bf16[128,2560]{1,0:T(8,128)(2,1)S(1)} %get-tuple-element.37), channel_id=1, source_target_pairs={{0,2},{1,3},{2,0},{3,1},{4,6},{5,7},{6,4},{7,5},{8,10},{9,11},{10,... | collective-permute-start | bytes 1966088 | tf_op jit(solution)/shard_map/ppermute | solution.py:409
  78.1 16.5 %collective-permute-start.21 = (bf16[256,1024]{1,0:T(8,128)(2,1)S(1)}, bf16[256,1024]{1,0:T(8,128)(2,1)S(1)}, u32[]{:S(2)}, u32[]{:S(2)}) collective-permute-start(bf16[256,1024]{1,0:T(8,128)(2,1)S(1)} %get-tuple-element.46), channel_id=1, source_target_pairs={{0,8},{1,9},{2,10},{3,11},{4,12},{5,13},{6,14},{7,15},{8,0},{9,1},... | collective-permute-start | bytes 1572872 | tf_op jit(solution)/shard_map/ppermute | solution.py:409
  84.6 9.9 %collective-permute-start.22 = (bf16[256,1024]{1,0:T(8,128)(2,1)S(1)}, bf16[256,1024]{1,0:T(8,128)(2,1)S(1)}, u32[]{:S(2)}, u32[]{:S(2)}) collective-permute-start(bf16[256,1024]{1,0:T(8,128)(2,1)S(1)} %get-tuple-element.47), channel_id=1, source_target_pairs={{8,16},{9,17},{10,18},{11,19},{12,20},{13,21},{14,22},{15,23},{16,... | collective-permute-start | bytes 1572872 | tf_op jit(solution)/shard_map/ppermute | solution.py:409
  94.7 6.4 %collective-permute-start.23 = (bf16[128,1024]{1,0:T(8,128)(2,1)S(1)}, bf16[128,1024]{1,0:T(8,128)(2,1)S(1)}, u32[]{:S(2)}, u32[]{:S(2)}) collective-permute-start(bf16[128,1024]{1,0:T(8,128)(2,1)S(1)} %get-tuple-element.49), channel_id=1, source_target_pairs={{0,4},{1,5},{2,6},{3,7},{4,0},{5,1},{6,2},{7,3},{8,12},{9,13},{10,... | collective-permute-start | bytes 786440 | tf_op jit(solution)/shard_map/ppermute | solution.py:409
  95.9 5.2 %copy-start.1 = (f32[1,128,2048]{2,1,0:T(8,128)S(1)}, f32[1,128,2048]{2,1,0:T(8,128)}, u32[]{:S(2)}) copy-start(f32[1,128,2048]{2,1,0:T(8,128)} %param.13) | copy-start | bytes 3145732
  95.9 5.2 %copy-start.2 = (f32[1,128,2048]{2,1,0:T(8,128)S(1)}, f32[1,128,2048]{2,1,0:T(8,128)}, u32[]{:S(2)}) copy-start(f32[1,128,2048]{2,1,0:T(8,128)} %param.14) | copy-start | bytes 3145732
  95.9 5.2 %copy-start.3 = (f32[1,128,2048]{2,1,0:T(8,128)S(1)}, f32[1,128,2048]{2,1,0:T(8,128)}, u32[]{:S(2)}) copy-start(f32[1,128,2048]{2,1,0:T(8,128)} %param.15) | copy-start | bytes 3145732
  95.9 5.2 %copy-start.7 = (s32[512]{0:T(512)S(1)}, s32[512]{0:T(512)}, u32[]{:S(2)}) copy-start(s32[512]{0:T(512)} %param.12) | copy-start | bytes 6148

commit v4 on v3

--- a/solution.py
+++ b/solution.py
@@ -34,74 +34,116 @@
     return pl.ds(pl.multiple_of(((seq * 2 + x) * parts + part) * width, width), width)
 
 
-def norm_kernel(parts, tok_ref, gain_ref, grad_ref, *refs):
+def norm_kernel(parts, tok_ref, far_ref, gain_ref, *refs):
     out_refs = [refs[i : i + parts] for i in range(0, len(refs), parts)]
     chips = len(out_refs)
-    feats = grad_ref.shape[-1]
-    width = (out_refs[0][0].shape[-1] - feats) // 2
-    tok = tok_ref[...].astype(f32)
-    inv_rms = lax.rsqrt(jnp.mean(tok * tok, axis=-1, keepdims=True) + norm_eps)
-    for k in (*range(1, chips), 0):
-        for part in range(parts):
-            out_ref = out_refs[k][part]
-            for j in range(2):
-                cols = column_block(k, j, width, part, parts)
-                scaled = tok_ref[:, cols].astype(f32) * inv_rms
-                out_ref[:, j * width : (j + 1) * width] = (scaled * gain_ref[:, cols]).astype(bf16)
-            if part == 0:
-                out_ref[:, 2 * width : 2 * width + feats] = grad_ref[...]
-
-
-def norm_blocks(tokens, gain, grads, chips, width, parts):
+    width = out_refs[0][0].shape[-1]
+    for i, ref in enumerate((tok_ref, far_ref)):
+        tok = ref[...].astype(f32)
+        inv_rms = lax.rsqrt(jnp.mean(tok * tok, axis=-1, keepdims=True) + norm_eps)
+        for k in (*range(1, chips), 0):
+            for part in range(parts):
+                cols = column_block(k, 0, width, part, parts)
+                scaled = ref[:, cols].astype(f32) * inv_rms
+                out_refs[k][part][i] = (scaled * gain_ref[:, cols]).astype(bf16)
+
+
+def norm_blocks(tokens, far, gain, chips, width, parts):
     rows, model = tokens.shape
-    feats = grads.shape[-1]
     step = min(rows, 32)
-    lanes = [2 * width // parts + (feats if part == 0 else 0) for part in range(parts)]
     outs = pl.pallas_call(
         functools.partial(norm_kernel, parts),
         grid=(rows // step,),
         in_specs=[
             pl.BlockSpec((step, model), lambda i: (i, 0)),
+            pl.BlockSpec((step, model), lambda i: (i, 0)),
             pl.BlockSpec((1, model), lambda i: (0, 0)),
-            pl.BlockSpec((step, feats), lambda i: (i, 0)),
-        ],
-        out_specs=[pl.BlockSpec((step, n), lambda i: (i, 0)) for n in lanes] * chips,
-        out_shape=[jax.ShapeDtypeStruct((rows, n), bf16) for n in lanes] * chips,
+        ],
+        out_specs=[pl.BlockSpec((2, step, width // parts), lambda i: (0, i, 0))] * (chips * parts),
+        out_shape=[jax.ShapeDtypeStruct((2, rows, width // parts), bf16)] * (chips * parts),
         compiler_params=limit(24),
-        cost_estimate=cost(8 * rows * model, 4 * rows * model),
+        cost_estimate=cost(8 * rows * model, 6 * rows * model),
         name="norm_blocks",
-    )(tokens, gain, grads)
+    )(tokens, far, gain)
     return [outs[i : i + parts] for i in range(0, len(outs), parts)]
 
 
-def join_kernel(a_ref, b_ref, *refs):
+def pack_kernel(w_ref, grad_ref, keep_ref, send_ref):
+    share, width = keep_ref.shape
+    rows, feats = grad_ref.shape
+    own_x = lax.axis_index("dp") % 2
+    keep_ref[...] = w_ref[:, pl.ds(pl.multiple_of(own_x * width, width), width)]
+    send_ref[:share, :] = w_ref[:, pl.ds(pl.multiple_of((1 - own_x) * width, width), width)]
+    pieces = feats // width if feats > width else 1
+    for at in range(0, rows * pieces, rows):
+        send_ref[share + at : share + at + rows, : feats // pieces] = grad_ref[
+            :, at // rows * width : at // rows * width + feats // pieces
+        ]
+
+
+def pack(w_t, grads, width):
+    share, (rows, feats) = w_t.shape[0], grads.shape
+    pieces = max(feats // width, 1)
+    return pl.pallas_call(
+        pack_kernel,
+        out_shape=[
+            jax.ShapeDtypeStruct((share, width), bf16),
+            jax.ShapeDtypeStruct((share + pieces * rows, width), bf16),
+        ],
+        compiler_params=limit(16),
+        cost_estimate=cost(0, 8 * rows * feats),
+        name="pack",
+    )(w_t, grads)
+
+
+def unpack_kernel(keep_ref, got_ref, *refs):
+    plane_ref, grads_ref = refs[-2:]
+    chips = grads_ref.shape[0] // refs[0].shape[0]
+    share, width = keep_ref.shape
+    rows, feats = refs[0].shape
+    plane_ref[:share, :] = keep_ref[...]
+    plane_ref[share:, :] = got_ref[:share, :]
+    for k in range(chips):
+        at = slice(k * rows, (k + 1) * rows)
+        if k != 1:
+            grads_ref[at, :] = refs[k - (k > 1)][...]
+            continue
+        pieces = feats // width if feats > width else 1
+        lanes = feats // pieces
+        for i in range(pieces):
+            part = got_ref[share + i * rows : share + (i + 1) * rows, :lanes]
+            grads_ref[at, i * lanes : (i + 1) * lanes] = part
+
+
+def unpack(keep, got, grads, after):
+    share, width = keep.shape
+    rows, feats = grads[0].shape
+    return pl.pallas_call(
+        unpack_kernel,
+        in_specs=[pl.BlockSpec(memory_space=pltpu.VMEM)] * (2 + len(grads))
+        + [pl.BlockSpec(memory_space=pl.ANY)] * len(after),
+        out_shape=[
+            jax.ShapeDtypeStruct((2 * share, width), bf16),
+            jax.ShapeDtypeStruct(((len(grads) + 1) * rows, feats), bf16),
+        ],
+        compiler_params=limit(16),
+        cost_estimate=cost(0, 0),
+        name="unpack",
+    )(keep, got, *grads, *after)
+
+
+def select_kernel(groups, slots, owner_ref, *refs):
     out_ref = refs[-1]
-    half = a_ref.shape[0]
-    out_ref[:half, :] = a_ref[...]
-    out_ref[half:, :] = b_ref[...]
-
-
-def join(a, b, after):
-    rows, width = a.shape
-    return pl.pallas_call(
-        join_kernel,
-        in_specs=[pl.BlockSpec(memory_space=pltpu.VMEM)] * 2
-        + [pl.BlockSpec(memory_space=pl.ANY)] * len(after),
-        out_shape=jax.ShapeDtypeStruct((2 * rows, width), a.dtype),
-        compiler_params=limit(16),
-        cost_estimate=cost(0, 8 * rows * width),
-        name="join",
-    )(a, b, *after)
-
-
-def select_kernel(slots, owner_row_ref, owner_col_ref, out_ref):
-    feats = owner_row_ref.shape[1]
-    owner = owner_row_ref[...]
+    feats = owner_ref.shape[1]
+    owner = owner_ref[...]
     lower = lax.broadcasted_iota(jnp.int32, (feats, feats), 0) < lax.broadcasted_iota(
         jnp.int32, (feats, feats), 1
     )
-    same = (owner_col_ref[...] == owner) & lower
-    place = jnp.sum(same.astype(f32), axis=0, keepdims=True).astype(jnp.int32)
+    owned = (lax.broadcasted_iota(jnp.int32, (groups, feats), 0) == owner).astype(f32)
+    before = jnp.dot(
+        owned.astype(bf16), lower.astype(f32).astype(bf16), preferred_element_type=f32
+    )
+    place = jnp.sum(owned * before, axis=0, keepdims=True).astype(jnp.int32)
     own_x = lax.axis_index("dp") % 2
     slot = (owner ^ own_x) * slots + place
     step = 256
@@ -110,38 +152,42 @@
         out_ref[at : at + step, :] = (index == slot).astype(f32).astype(bf16)
 
 
-def select_rows(owner, groups, slots):
-    feats = owner.shape[0]
-    return pl.pallas_call(
-        functools.partial(select_kernel, slots),
+def select_rows(owner, groups, slots, after):
+    feats = owner.shape[1]
+    return pl.pallas_call(
+        functools.partial(select_kernel, groups, slots),
+        in_specs=[pl.BlockSpec(memory_space=pltpu.VMEM)]
+        + [pl.BlockSpec(memory_space=pl.ANY)] * len(after),
         out_shape=jax.ShapeDtypeStruct((groups * slots, feats), bf16),
         compiler_params=limit(24),
         cost_estimate=cost(4 * groups * slots * feats, 2 * groups * slots * feats),
         name="select_rows",
-    )(owner[None, :], owner[:, None])
+    )(owner, *after)
 
 
 def weight_kernel(planes, chips, plan, *refs):
     sel_ref, refs = refs[0], refs[1:]
-    first, refs = refs[: 2 * chips], refs[2 * chips :]
-    pieces, refs = refs[: 2 * chips], refs[2 * chips :]
-    out_refs, (grads, held, base) = refs[-len(plan) - 4 : -3], refs[-3:]
-    rows, feats = first[0].shape[0], sel_ref.shape[1]
-    width = held.shape[1]
+    grad_refs, refs = refs[:2], refs[2:]
+    pieces, refs = refs[:chips], refs[chips:]
+    out_refs, (held, base) = refs[-len(plan) - 3 : -2], refs[-2:]
+    rows = pieces[0].shape[1]
+    feats = sel_ref.shape[1]
     block = sel_ref.shape[0] // planes
     z = lax.axis_index("dp") // 2
-    for i in range(2 * chips):
-        j = i // chips
-        at = slice(i * rows, (i + 1) * rows)
-        grads[at, :] = first[i][:, first[i].shape[1] - feats :]
-        held[at, :] = pieces[i][:, j * width : (j + 1) * width]
+    for k in range(chips):
+        for i in range(2):
+            held[i, k * rows : (k + 1) * rows, :] = pieces[k][i]
     for at in range(0, feats, 256):
-        base[at : at + 256, :] = lax.dot_general(
-            grads[:, at : at + 256],
-            held[...],
-            (((0,), (0,)), ((), ())),
-            preferred_element_type=f32,
-        ).astype(bf16)
+        total = None
+        for i in range(2):
+            term = lax.dot_general(
+                grad_refs[i][:, at : at + 256],
+                held[i],
+                (((0,), (0,)), ((), ())),
+                preferred_element_type=f32,
+            )
+            total = term if total is None else total + term
+        base[at : at + 256, :] = total.astype(bf16)
 
     def chosen(plane):
         at = pl.multiple_of(plane * block, block)
@@ -158,90 +204,114 @@
     out_refs[-1][...] = chosen(z).astype(bf16)
 
 
-def weight_blocks(selected, first, pieces, planes, plan, after):
-    chips = len(first) // 2
+def weight_blocks(selected, grads, pieces, planes, plan, after):
+    chips = len(pieces)
     slots_all, feats = selected.shape
-    rows = first[0].shape[0]
-    lanes = pieces[0].shape[1] - (feats if pieces[0] is first[0] else 0)
-    width = lanes // 2
+    _, rows, width = pieces[0].shape
     total = 2 * chips * rows
     block = slots_all // planes
     return pl.pallas_call(
         functools.partial(weight_kernel, planes, chips, plan),
-        in_specs=[pl.BlockSpec(memory_space=pltpu.VMEM)] * (1 + 4 * chips)
+        in_specs=[pl.BlockSpec(memory_space=pltpu.VMEM)] * (3 + chips)
         + [pl.BlockSpec(memory_space=pl.ANY)] * len(after),
         out_shape=[jax.ShapeDtypeStruct((block, width), bf16)] * (len(plan) + 1),
         scratch_shapes=[
-            pltpu.VMEM((total, feats), bf16),
-            pltpu.VMEM((total, width), bf16),
+            pltpu.VMEM((2, total // 2, width), bf16),
             pltpu.VMEM((feats, width), bf16),
         ],
         compiler_params=limit(40),
         cost_estimate=cost(2 * (slots_all + total) * feats * width, 4 * total * width),
         name="weight_blocks",
-    )(selected, *first, *pieces, *after)
-
-
-def gather_weight(planes, piece_refs, held):
+    )(selected, *grads, *pieces, *after)
+
+
+def gather_weight(piece_refs, held):
     dp = lax.axis_index("dp")
     own_x, own_z = dp % 2, dp // 2
-    for j in range(2):
-        for turn in range(planes):
-            ref = piece_refs[j * planes + turn]
-            share = ref.shape[0] // 2
-            for i in range(2):
-                at = pl.multiple_of(((own_z ^ turn) * 2 + (own_x ^ i)) * share, share)
-                held[j, pl.ds(at, share), :] = ref[i * share : (i + 1) * share, :]
-
-
-def back_kernel(planes, chips, parts, *refs):
+    for turn, ref in enumerate(piece_refs):
+        share = ref.shape[0] // 2
+        for i in range(2):
+            at = pl.multiple_of(((own_z ^ turn) * 2 + (own_x ^ i)) * share, share)
+            held[pl.ds(at, share), :] = ref[i * share : (i + 1) * share, :]
+
+
+def back_kernel(planes, chips, parts, grads_ref, far_ref, *refs):
     piece_refs, refs = refs[: chips * parts], refs[chips * parts :]
-    weight_refs, refs = refs[: 2 * planes], refs[2 * planes :]
-    out_refs, own_ref, held = refs[-chips - 2 : -2], refs[-2], refs[-1]
-    _, feats, width = held.shape
+    (*far_refs, far_value_ref, out_ref, value_ref), held = refs[-6:-1], refs[-1]
+    rows = grads_ref.shape[0] // chips
+    feats, width = held.shape
     part_width = width // parts
-    gather_weight(planes, weight_refs, held)
-    dims = (((1,), (1,)), ((), ()))
-    for k in (*range(1, chips), 0):
-        pieces = piece_refs[k * parts : (k + 1) * parts]
-        grads = pieces[0][:, pieces[0].shape[1] - feats :]
-        total = None
-        for j in range(2):
-            out_refs[k][:, j * width : (j + 1) * width] = jnp.dot(
-                grads, held[j], preferred_element_type=f32
-            ).astype(bf16)
+    gather_weight(refs[:planes], held)
+    for core in (1, 0):
+        for k in range(chips):
+            at = slice(k * rows, (k + 1) * rows)
+            from_ref = far_ref if core else grads_ref
+            block = jnp.dot(from_ref[at, :], held[...], preferred_element_type=f32).astype(bf16)
+            if core:
+                half = chips // 2
+                far_refs[k // half][k % half * rows : (k % half + 1) * rows, :] = block
+            else:
+                out_ref[at, :] = block
+            total = None
             for part in range(parts):
                 term = lax.dot_general(
-                    pieces[part][:, j * part_width : (j + 1) * part_width],
-                    held[j, :, part * part_width : (part + 1) * part_width],
-                    dims,
+                    piece_refs[k * parts + part][core],
+                    held[:, part * part_width : (part + 1) * part_width],
+                    (((1,), (1,)), ((), ())),
                     preferred_element_type=f32,
                 )
                 total = term if total is None else total + term
+            (far_value_ref if core else value_ref)[at, :] = total.astype(bf16)
+
+
+def back_blocks(grads, grads_far, pieces, weights, after):
+    chips, parts = len(pieces), len(pieces[0])
+    rows, feats = grads.shape[0] // chips, grads.shape[1]
+    width = weights[0].shape[-1]
+    half = jax.ShapeDtypeStruct((chips // 2 * rows, width), bf16)
+    value = jax.ShapeDtypeStruct((chips * rows, feats), bf16)
+    outs = pl.pallas_call(
+        functools.partial(back_kernel, len(weights), chips, parts),
+        in_specs=[pl.BlockSpec(memory_space=pltpu.VMEM)] * (2 + chips * parts + len(weights))
+        + [pl.BlockSpec(memory_space=pl.ANY)] * len(after),
+        out_shape=[half, half, value, jax.ShapeDtypeStruct((chips * rows, width), bf16), value],
+        scratch_shapes=[pltpu.VMEM((feats, width), bf16)],
+        compiler_params=limit(40),
+        name="back_blocks",
+    )(grads, grads_far, *[p for piece in pieces for p in piece], *weights, *after)
+    return outs[:3], outs[3:]
+
+
+def home_kernel(own_ref, own_value_ref, got_a_ref, got_b_ref, got_value_ref, *out_refs):
+    chips = len(out_refs) - 1
+    rows = out_refs[0].shape[0]
+    width = out_refs[0].shape[1] // 2
+    half = chips // 2
+    for k in range(chips):
+        at = slice(k * rows, (k + 1) * rows)
+        got_ref = got_b_ref if k // half else got_a_ref
+        out_refs[k][:, :width] = own_ref[at, :]
+        out_refs[k][:, width : 2 * width] = got_ref[k % half * rows : (k % half + 1) * rows, :]
+        values = own_value_ref[at, :].astype(f32) + got_value_ref[at, :].astype(f32)
         if k == 0:
-            own_ref[...] = total
+            out_refs[-1][...] = values
         else:
-            out_refs[k][:, 2 * width :] = total.astype(bf16)
-
-
-def back_blocks(pieces, weights, planes, feats, after):
-    chips, parts = len(pieces), len(pieces[0])
-    rows = pieces[0][0].shape[0]
-    width = weights[0].shape[-1]
-    return pl.pallas_call(
-        functools.partial(back_kernel, planes, chips, parts),
-        in_specs=[pl.BlockSpec(memory_space=pltpu.VMEM)] * (chips * parts + 2 * planes)
-        + [pl.BlockSpec(memory_space=pl.ANY)] * len(after),
+            out_refs[k][:, 2 * width :] = values.astype(bf16)
+
+
+def home_blocks(own, got, chips):
+    rows, width = own[0].shape[0] // chips, own[0].shape[1]
+    feats = own[1].shape[1]
+    return pl.pallas_call(
+        home_kernel,
         out_shape=[
             jax.ShapeDtypeStruct((rows, 2 * width + (feats if k else 0)), bf16)
             for k in range(chips)
         ]
         + [jax.ShapeDtypeStruct((rows, feats), f32)],
-        scratch_shapes=[pltpu.VMEM((2, feats, width), bf16)],
-        compiler_params=limit(40),
-        cost_estimate=cost(8 * chips * rows * feats * width, 4 * chips * rows * width),
-        name="back_blocks",
-    )(*[p for piece in pieces for p in piece], *weights, *after)
+        compiler_params=limit(24),
+        name="home_blocks",
+    )(*own, *got)
 
 
 def grad_x_kernel(tok_ref, gain_ref, part_ref, *refs):
@@ -377,7 +447,7 @@
     return pl.pallas_call(
         functools.partial(adam_kernel, token_total, len(kept)),
         grid=(slots // step,),
-        in_specs=[pl.BlockSpec((1, owner.shape[0]), lambda i: (0, 0))]
+        in_specs=[pl.BlockSpec(owner.shape, lambda i: (0, 0))]
         + [pl.BlockSpec((step, width), lambda i: (i, 0))] * (2 * len(kept))
         + [pl.BlockSpec((step, cols), lambda i: (i, 0))] * 3,
         out_specs=[pl.BlockSpec((step, cols), lambda i: (i, 0))] * 3,
@@ -385,7 +455,7 @@
         compiler_params=limit(24),
         cost_estimate=cost(20 * slots * cols, 30 * slots * cols),
         name="adam",
-    )(owner[None, :], *kept, *got, *states)
+    )(owner, *kept, *got, *states)
 
 
 def on_device(groups, seqs, tokens, gain, w_t, grad_values, owner, master, moment1, moment2):
@@ -432,17 +502,19 @@
 
         return permute(value, target)
 
-    w_keep = lax.dynamic_slice_in_dim(w_t, own_x * width, width, 1)
-    w_got = to_x(lax.dynamic_slice_in_dim(w_t, (1 - own_x) * width, width, 1))
-    gain_row = gain[None, :]
-    sent = norm_blocks(tokens, gain_row, value_grad, chips, width, parts)
-    near = [sent[0]] + [[to_chip(p, k) for p in sent[k]] for k in range(1, chips)]
-    far = [[to_core(p) for p in piece] for piece in near]
-    selected = select_rows(owner, groups, slots)
-
-    w_plane = join(w_keep, w_got, (sent[0][0], selected))
-    w_own = [w_plane] + [to_plane(w_plane, turn) for turn in range(1, planes)]
-    weights = w_own + [to_core(w) for w in w_own]
+    tokens_far = to_core(tokens)
+    w_keep, packed = pack(w_t, value_grad, width)
+    packed = to_chip(packed, 1)
+    grads = [to_chip(value_grad, k) for k in range(chips - 1, 1, -1)][::-1]
+
+    gain_row, owner_row = gain[None, :], owner[None, :]
+    sent = norm_blocks(tokens, tokens_far, gain_row, chips, width, parts)
+    w_plane, grads = unpack(w_keep, packed, [value_grad] + grads, (sent[0][0],))
+    pieces = [sent[0]] + [[to_chip(p, k) for p in sent[k]] for k in range(1, chips)]
+    grads_far = to_core(grads)
+    selected = select_rows(owner_row, groups, slots, (sent[0][0],))
+
+    weights = [w_plane] + [to_plane(w_plane, turn) for turn in range(1, planes)]
 
     plan = [
         (step, even)
@@ -451,14 +523,19 @@
         if any(busy(z, step, even) for z in range(planes))
     ]
     kept, got = [], []
-    first = [piece[0] for piece in near + far]
     for part in range(parts):
-        pieces = [piece[part] for piece in near + far]
-        after = weights if part == parts - 1 else []
-        outs = weight_blocks(selected, first, pieces, planes, plan, after)
+        outs = weight_blocks(
+            selected,
+            [grads, grads_far],
+            [piece[part] for piece in pieces],
+            planes,
+            plan,
+            weights if part == parts - 1 else [],
+        )
         ready = dict(zip(plan, outs))
         if part == parts - 1:
-            back = back_blocks(near, weights, planes, feats, [outs[0]])
+            back_far, back_own = back_blocks(grads, grads_far, pieces, weights, [outs[0]])
+            back = home_blocks(back_own, [to_core(b) for b in back_far], chips)
             home = [back[0]] + [to_chip(back[k], k) for k in range(1, chips)]
         held = {}
         for step in range(1, planes):
@@ -466,18 +543,18 @@
             send = [ready[step, even] for even in here]
             if held:
                 sums = [[ready[step, even], held[not even]] for even in here if (not even) in held]
-                sums = list(relay(sums, [back[0]] if step == 2 else home[-1:])) if sums else []
+                sums = list(relay(sums, back_own[:1] if step == 2 else [back[0]])) if sums else []
                 send = []
                 for even in here:
                     send.append(sums.pop(0) if (not even) in held else ready[step, even])
             held = {even: across(value, step, even) for even, value in zip(here, send)}
-        keep, send = finish(outs[-1], held[True], held[False], home[1:])
+        keep, send = finish(outs[-1], held[True], held[False], home[-1:])
         kept.append(keep)
         got.append(to_x(send))
 
     grad_x, values = grad_x_blocks(tokens, gain_row, back[-1], home)
 
-    states = adam(owner, kept, got, (master[0], moment1[0], moment2[0]), rows * seqs * groups)
+    states = adam(owner_row, kept, got, (master[0], moment1[0], moment2[0]), rows * seqs * groups)
     return (values[None], grad_x[None], *(s[None] for s in states))
 
 

time: 105 us -> 108 us (1.029)
  waiting for transfers between devices: 44.9 us -> 57.7 us
  starting transfers between devices: 38.9 us -> 27.7 us
  Pallas kernels: 15.5 us -> 18.2 us
    ppermute x24 -> x23, waiting for transfers between devices: 44.9 us -> 57.7 us  [permute(): return lax.ppermute(value, ('dp', 'seq'), pairs)]
    ppermute x24 -> x23, starting transfers between devices: 38.9 us -> 27.7 us  [permute(): return lax.ppermute(value, ('dp', 'seq'), pairs)]
    pallas_call x3 -> x5, Pallas kernels: 4.57 us -> 6.71 us  [the longest x1 4.15 us: back_blocks(): pl.pallas_call(functools.partial(back_kernel, len(weights), chips, parts)...]
    unnamed x16 -> x18, local copies, waits for them, and re-layouts: 1.6 us -> 3.33 us
    dynamic_slice x1 -> x0, local copies, waits for them, and re-layouts: 1.14 us -> none  [on_device(): w_got = to_x(lax.dynamic_slice_in_dim(w_t, (1 - own_x) * width, width, 1))]
  transfers between devices with their start and end apart: 24 -> 23, of which waited for: 10 -> 8; matrix products, arithmetic and copies ran while one was open for 1% -> 0% of each run, Pallas kernels for 9% -> 11%
where the time goes in v4:
time: 108 us
  waiting for transfers between devices  57.7 us (53%)
  starting transfers between devices  27.7 us (26%)
  Pallas kernels  18.2 us (17%)
  local copies, waits for them, and re-layouts  3.33 us (3%)
    ppermute x23, waiting for transfers between devices, permute(): return lax.ppermute(value, ('dp', 'seq'), pairs)  57.7 us
    ppermute x23, starting transfers between devices, permute(): return lax.ppermute(value, ('dp', 'seq'), pairs)  27.7 us
    pallas_call x1, Pallas kernels, back_blocks(): pl.pallas_call(functools.partial(back_kernel, len(weights), chips, parts)...  4.15 us
    pallas_call x1, Pallas kernels, grad_x_blocks(): pl.pallas_call(grad_x_kernel, grid=(rows // step,), in_specs=[pl.BlockSpe...  3.62 us
    unnamed x18, local copies, waits for them, and re-layouts  3.33 us
    pallas_call x1, Pallas kernels, weight_blocks(): pl.pallas_call(functools.partial(weight_kernel, planes, chips, plan), in_...  3.03 us
    pallas_call x1, Pallas kernels, adam(): pl.pallas_call(functools.partial(adam_kernel, token_total, len(kept)), gr...  2.6 us
  transfers between devices with their start and end apart: 23, of which 8 were waited for; matrix products, arithmetic and copies ran while one was open for 0% of the time, Pallas kernels for 11%

profile of v4, /device:TPU:0, one launch (start us, length us, event | category | flops | bytes accessed | tf_op | source)
XLA Modules:
  0.0 107.8 jit_solution(1963084880407813534)
XLA Ops:
  0.6 0.5 collective-permute-start.3
  1.2 0.9 copy-done.5
  2.1 0.9 pack.1
  3.0 2.6 %collective-permute-start = (bf16[192,1024]{1,0:T(8,128)(2,1)S(1)}, bf16[192,1024]{1,0:T(8,128)(2,1)S(1)}, u32[]{:S(2)}, u32[]{:S(2)}) collective-permute-start(bf16[192,1024]{1,0:T(8,128)(2,1)S(1)} %get-tuple-element.39), channel_id=1, source_target_pairs={{0,4},{1,5},{2,6},{3,7},{4,0},{5,1},{6,2},{7,3},{8,12},{9,13},{10,... | collective-permute-start | bytes 1179656 | tf_op jit(solution)/shard_map/ppermute | solution.py:479
  5.6 1.5 %collective-permute-start.2 = (bf16[128,512]{1,0:T(8,128)(2,1)}, bf16[128,512]{1,0:T(8,128)(2,1)S(1)}, u32[]{:S(2)}, u32[]{:S(2)}) collective-permute-start(bf16[128,512]{1,0:T(8,128)(2,1)} %bitcast.2.grad_ref.refs_0_), channel_id=1, source_target_pairs={{0,6},{1,7},{2,4},{3,5},{4,2},{5,3},{6,0},{7,1},{8,14},{9,15},{10,... | collective-permute-start | bytes 393224 | tf_op jit(solution)/shard_map/ppermute | solution.py:479
  7.1 0.1 collective-permute-start.1
  7.1 0.0 collective-permute-done.3.far_ref
  7.1 1.6 %copy-done = bf16[1,128,8192]{2,1,0:T(8,128)(2,1)S(1)} copy-done((bf16[1,128,8192]{2,1,0:T(8,128)(2,1)S(1)}, bf16[1,128,8192]{2,1,0:T(8,128)(2,1)}, u32[]{:S(2)}) %copy-start) | copy-done | bytes 2097176
  8.7 0.8 copy-done.6
  9.5 1.7 %norm_blocks.1 = (bf16[2,128,1024]{2,1,0:T(8,128)(2,1)S(1)}, bf16[2,128,1024]{2,1,0:T(8,128)(2,1)S(1)}, bf16[2,128,1024]{2,1,0:T(8,128)(2,1)S(1)}, bf16[2,128,1024]{2,1,0:T(8,128)(2,1)S(1)}) custom-call(bf16[128,8192]{1,0:T(8,128)(2,1)S(1)} %bitcast.13, bf16[128,8192]{1,0:T(8,128)(2,1)S(1)} %collective-permute-done.3.far_ref, f32[1,8192]{1,0:T(1,128)S(1)} %bitcast.18), custom_call_target="tpu_custom_call" | custom-call | flops 8388608 | bytes 6291456 | tf_op jit(solution)/shard_map/norm_blocks/pallas_call | solution.py:54
  11.2 8.2 %collective-permute-done.2.refs_2_ = bf16[128,512]{1,0:T(8,128)(2,1)S(1)} collective-permute-done((bf16[128,512]{1,0:T(8,128)(2,1)}, bf16[128,512]{1,0:T(8,128)(2,1)S(1)}, u32[]{:S(2)}, u32[]{:S(2)}) %collective-permute-start.2) | collective-permute-done | bytes 131104 | tf_op jit(solution)/shard_map/ppermute | solution.py:479
  19.4 0.0 collective-permute-done.got_ref
  19.4 1.0 unpack.1
  20.4 3.7 %collective-permute-start.10 = (bf16[128,1024]{1,0:T(8,128)(2,1)S(1)}, bf16[128,1024]{1,0:T(8,128)(2,1)S(1)}, u32[]{:S(2)}, u32[]{:S(2)}) collective-permute-start(bf16[128,1024]{1,0:T(8,128)(2,1)S(1)} %get-tuple-element.45.refs_7_.refs_4_), channel_id=1, source_target_pairs={{0,24},{1,25},{2,26},{3,27},{4,28},{5,29},{6,30},{7,31},{8,16},{9,... | collective-permute-start | bytes 786440 | tf_op jit(solution)/shard_map/ppermute | solution.py:479
  24.0 1.5 %collective-permute-start.5 = (bf16[2,128,1024]{2,1,0:T(8,128)(2,1)S(1)}, bf16[2,128,1024]{2,1,0:T(8,128)(2,1)S(1)}, u32[]{:S(2)}, u32[]{:S(2)}) collective-permute-start(bf16[2,128,1024]{2,1,0:T(8,128)(2,1)S(1)} %get-tuple-element.42), channel_id=1, source_target_pairs={{0,4},{1,5},{2,6},{3,7},{4,0},{5,1},{6,2},{7,3},{8,12},{9,13},{10,... | collective-permute-start | bytes 1572872 | tf_op jit(solution)/shard_map/ppermute | solution.py:479
  25.5 0.5 collective-permute-start.6
  26.0 5.4 %collective-permute-done.10.refs_10_.refs_7_ = bf16[128,1024]{1,0:T(8,128)(2,1)S(1)} collective-permute-done((bf16[128,1024]{1,0:T(8,128)(2,1)S(1)}, bf16[128,1024]{1,0:T(8,128)(2,1)S(1)}, u32[]{:S(2)}, u32[]{:S(2)}) %collective-permute-start.10) | collective-permute-done | bytes 262176 | tf_op jit(solution)/shard_map/ppermute | solution.py:479
  31.5 1.4 %collective-permute-start.7 = (bf16[2,128,1024]{2,1,0:T(8,128)(2,1)S(1)}, bf16[2,128,1024]{2,1,0:T(8,128)(2,1)S(1)}, u32[]{:S(2)}, u32[]{:S(2)}) collective-permute-start(bf16[2,128,1024]{2,1,0:T(8,128)(2,1)S(1)} %get-tuple-element.44), channel_id=1, source_target_pairs={{0,6},{1,7},{2,4},{3,5},{4,2},{5,3},{6,0},{7,1},{8,14},{9,15},{10,... | collective-permute-start | bytes 1572872 | tf_op jit(solution)/shard_map/ppermute | solution.py:479
  32.9 13.3 %collective-permute-done.9.refs_9_.refs_6_ = bf16[128,1024]{1,0:T(8,128)(2,1)S(1)} collective-permute-done((bf16[128,1024]{1,0:T(8,128)(2,1)S(1)}, bf16[128,1024]{1,0:T(8,128)(2,1)S(1)}, u32[]{:S(2)}, u32[]{:S(2)}) %collective-permute-start.9) | collective-permute-done | bytes 262176 | tf_op jit(solution)/shard_map/ppermute | solution.py:479
  46.2 0.5 select_rows.1.refs_0_
  46.7 6.9 %collective-permute-done.8.refs_8_.refs_5_ = bf16[128,1024]{1,0:T(8,128)(2,1)S(1)} collective-permute-done((bf16[128,1024]{1,0:T(8,128)(2,1)S(1)}, bf16[128,1024]{1,0:T(8,128)(2,1)S(1)}, u32[]{:S(2)}, u32[]{:S(2)}) %collective-permute-start.8) | collective-permute-done | bytes 262176 | tf_op jit(solution)/shard_map/ppermute | solution.py:479
  53.6 3.0 %weight_blocks.1 = (bf16[256,1024]{1,0:T(8,128)(2,1)S(1)}, bf16[256,1024]{1,0:T(8,128)(2,1)S(1)}, bf16[256,1024]{1,0:T(8,128)(2,1)S(1)}, bf16[256,1024]{1,0:T(8,...) custom-call(bf16[1024,512]{1,0:T(8,128)(2,1)S(1)} %select_rows.1.refs_0_, ...), custom_call_target="tpu_custom_call" | custom-call | flops 2147483648 | bytes 4194304 | tf_op jit(solution)/shard_map/weight_blocks/pallas_call | solution.py:213
  56.6 3.4 %collective-permute-start.17 = (bf16[256,1024]{1,0:T(8,128)(2,1)S(1)}, bf16[256,1024]{1,0:T(8,128)(2,1)S(1)}, u32[]{:S(2)}, u32[]{:S(2)}) collective-permute-start(bf16[256,1024]{1,0:T(8,128)(2,1)S(1)} %get-tuple-element.46.refs_8_), channel_id=1, source_target_pairs={{0,8},{1,9},{2,10},{3,11},{4,12},{5,13},{6,14},{7,15},{24,16},{25,... | collective-permute-start | bytes 1572872 | tf_op jit(solution)/shard_map/ppermute | solution.py:479
  60.0 4.1 %back_blocks.1 = (bf16[256,1024]{1,0:T(8,128)(2,1)S(1)}, bf16[256,1024]{1,0:T(8,128)(2,1)S(1)}, bf16[512,512]{1,0:T(8,128)(2,1)S(1)}, bf16[512,1024]{1,0:T(8,128)(2,1)S(1)}, bf16[512,512]{1,0:T(8,128)(2,1)S(1)}) custom-call(bf16[512,512]{1,0:T(8,128)(2,1)S(1)} %get-tuple-element.41.refs_1_.grads_ref, ...), custom_call_target="tpu_custom_call" | custom-call | tf_op jit(solution)/shard_map/back_blocks/pallas_call | solution.py:273
  64.2 0.1 collective-permute-start.11
  64.2 0.5 collective-permute-start.12
  64.7 0.1 collective-permute-start.13
  64.8 1.3 %collective-permute-start.19 = (bf16[256,1024]{1,0:T(8,128)(2,1)S(1)}, bf16[256,1024]{1,0:T(8,128)(2,1)S(1)}, u32[]{:S(2)}, u32[]{:S(2)}) collective-permute-start(bf16[256,1024]{1,0:T(8,128)(2,1)S(1)} %get-tuple-element.63), channel_id=1, source_target_pairs={{0,8},{1,9},{2,10},{3,11},{4,12},{5,13},{6,14},{7,15},{24,16},{25,... | collective-permute-start | bytes 1572872 | tf_op jit(solution)/shard_map/ppermute | solution.py:479
  66.1 4.2 %collective-permute-done.17.refs_1_ = bf16[256,1024]{1,0:T(8,128)(2,1)S(1)} collective-permute-done((bf16[256,1024]{1,0:T(8,128)(2,1)S(1)}, bf16[256,1024]{1,0:T(8,128)(2,1)S(1)}, u32[]{:S(2)}, u32[]{:S(2)}) %collective-permute-start.17) | collective-permute-done | bytes 524320 | tf_op jit(solution)/shard_map/ppermute | solution.py:479
  70.3 0.1 relay.2
  70.4 0.7 collective-permute-start.18
  71.2 0.2 home_blocks.1
  71.4 1.5 %collective-permute-start.16 = (bf16[128,2560]{1,0:T(8,128)(2,1)S(1)}, bf16[128,2560]{1,0:T(8,128)(2,1)S(1)}, u32[]{:S(2)}, u32[]{:S(2)}) collective-permute-start(bf16[128,2560]{1,0:T(8,128)(2,1)S(1)} %get-tuple-element.56), channel_id=1, source_target_pairs={{0,6},{1,7},{2,4},{3,5},{4,2},{5,3},{6,0},{7,1},{8,14},{9,15},{10,... | collective-permute-start | bytes 1966088 | tf_op jit(solution)/shard_map/ppermute | solution.py:479
  72.9 7.0 %collective-permute-done.19.refs_3_ = bf16[256,1024]{1,0:T(8,128)(2,1)S(1)} collective-permute-done((bf16[256,1024]{1,0:T(8,128)(2,1)S(1)}, bf16[256,1024]{1,0:T(8,128)(2,1)S(1)}, u32[]{:S(2)}, u32[]{:S(2)}) %collective-permute-start.19) | collective-permute-done | bytes 524320 | tf_op jit(solution)/shard_map/ppermute | solution.py:479
  79.9 0.2 relay.3
  80.1 4.2 %collective-permute-start.20 = (bf16[256,1024]{1,0:T(8,128)(2,1)S(1)}, bf16[256,1024]{1,0:T(8,128)(2,1)S(1)}, u32[]{:S(2)}, u32[]{:S(2)}) collective-permute-start(bf16[256,1024]{1,0:T(8,128)(2,1)S(1)} %get-tuple-element.64), channel_id=1, source_target_pairs={{0,8},{1,9},{2,10},{3,11},{4,12},{5,13},{6,14},{7,15},{8,0},{9,1},... | collective-permute-start | bytes 1572872 | tf_op jit(solution)/shard_map/ppermute | solution.py:479
  84.3 0.7 collective-permute-start.21
  85.0 1.6 %collective-permute-start.14 = (bf16[128,2560]{1,0:T(8,128)(2,1)S(1)}, bf16[128,2560]{1,0:T(8,128)(2,1)S(1)}, u32[]{:S(2)}, u32[]{:S(2)}) collective-permute-start(bf16[128,2560]{1,0:T(8,128)(2,1)S(1)} %get-tuple-element.54), channel_id=1, source_target_pairs={{0,4},{1,5},{2,6},{3,7},{4,0},{5,1},{6,2},{7,3},{8,12},{9,13},{10,... | collective-permute-start | bytes 1966088 | tf_op jit(solution)/shard_map/ppermute | solution.py:479
  86.5 0.5 collective-permute-start.15
  87.1 6.2 %collective-permute-done.20.even_ref = bf16[256,1024]{1,0:T(8,128)(2,1)S(1)} collective-permute-done((bf16[256,1024]{1,0:T(8,128)(2,1)S(1)}, bf16[256,1024]{1,0:T(8,128)(2,1)S(1)}, u32[]{:S(2)}, u32[]{:S(2)}) %collective-permute-start.20) | collective-permute-done | bytes 524320 | tf_op jit(solution)/shard_map/ppermute | solution.py:479
  93.2 0.2 finish.1
  93.4 1.6 %collective-permute-start.22 = (bf16[128,1024]{1,0:T(8,128)(2,1)S(1)}, bf16[128,1024]{1,0:T(8,128)(2,1)S(1)}, u32[]{:S(2)}, u32[]{:S(2)}) collective-permute-start(bf16[128,1024]{1,0:T(8,128)(2,1)S(1)} %get-tuple-element.67), channel_id=1, source_target_pairs={{0,4},{1,5},{2,6},{3,7},{4,0},{5,1},{6,2},{7,3},{8,12},{9,13},{10,... | collective-permute-start | bytes 786440 | tf_op jit(solution)/shard_map/ppermute | solution.py:479
  95.0 6.5 %collective-permute-done.14.refs_1_ = bf16[128,2560]{1,0:T(8,128)(2,1)S(1)} collective-permute-done((bf16[128,2560]{1,0:T(8,128)(2,1)S(1)}, bf16[128,2560]{1,0:T(8,128)(2,1)S(1)}, u32[]{:S(2)}, u32[]{:S(2)}) %collective-permute-start.14) | collective-permute-done | bytes 655392 | tf_op jit(solution)/shard_map/ppermute | solution.py:479
  101.5 0.0 copy-start.2
  101.5 0.0 copy-start.3
  101.5 0.0 copy-start.4
  101.5 3.6 %grad_x_blocks.1 = (bf16[128,8192]{1,0:T(8,128)(2,1)}, bf16[128,512]{1,0:T(8,128)(2,1)}) custom-call(bf16[128,8192]{1,0:T(8,128)(2,1)S(1)} %bitcast.14, f32[1,8192]{1,0:T(1,128)S(1)} %bitcast.19, f32[128,512]{1,0:T(8,128)S(1)} %get-tuple-element.52.part_ref, bf16[128,2048]{1,0:T(8,128)(2,1)S(1)} %get-tuple-element.53.refs_0_.refs_4_, ...), custom_call_target="tpu_custom_call" | custom-call | flops 16777216 | bytes 6291456 | tf_op jit(solution)/shard_map/grad_x_blocks/pallas_call | solution.py:347
  105.2 2.6 %adam.1 = (f32[128,2048]{1,0:T(8,128)}, f32[128,2048]{1,0:T(8,128)}, f32[128,2048]{1,0:T(8,128)}) custom-call(s32[1,512]{1,0:T(1,128)S(1)} %bitcast.21, f32[128,1024]{1,0:T(8,128)S(1)} %get-tuple-element.66.refs_0_, bf16[128,1024]{1,0:T(8,128)(2,1)S(1)} %collective-permute-done.22.refs_1_, f32[128,2048]{1,0:T(8,128)S(1)} %bitcast.15, ...), custom_call_target="tpu_custom_call" | custom-call | flops 5242880 | bytes 7864320 | tf_op jit(solution)/shard_map/adam/pallas_call | solution.py:447
  (28 shorter events, 0.1 us)
Async XLA Ops:
  0.6 6.5 %collective-permute-start.3 = (bf16[128,8192]{1,0:T(8,128)(2,1)}, bf16[128,8192]{1,0:T(8,128)(2,1)S(1)}, u32[]{:S(2)}, u32[]{:S(2)}) collective-permute-start(bf16[128,8192]{1,0:T(8,128)(2,1)} %bitcast.12), channel_id=1, source_target_pairs={{0,1},{1,0},{2,3},{3,2},{4,5},{5,4},{6,7},{7,6},{8,9},{9,8},{10,11... | collective-permute-start | bytes 6291464 | tf_op jit(solution)/shard_map/ppermute | solution.py:479
  1.1 0.9 copy-start.5
  3.0 16.4 %collective-permute-start = (bf16[192,1024]{1,0:T(8,128)(2,1)S(1)}, bf16[192,1024]{1,0:T(8,128)(2,1)S(1)}, u32[]{:S(2)}, u32[]{:S(2)}) collective-permute-start(bf16[192,1024]{1,0:T(8,128)(2,1)S(1)} %get-tuple-element.39), channel_id=1, source_target_pairs={{0,4},{1,5},{2,6},{3,7},{4,0},{5,1},{6,2},{7,3},{8,12},{9,13},{10,... | collective-permute-start | bytes 1179656 | tf_op jit(solution)/shard_map/ppermute | solution.py:479
  5.6 13.8 %collective-permute-start.2 = (bf16[128,512]{1,0:T(8,128)(2,1)}, bf16[128,512]{1,0:T(8,128)(2,1)S(1)}, u32[]{:S(2)}, u32[]{:S(2)}) collective-permute-start(bf16[128,512]{1,0:T(8,128)(2,1)} %bitcast.2.grad_ref.refs_0_), channel_id=1, source_target_pairs={{0,6},{1,7},{2,4},{3,5},{4,2},{5,3},{6,0},{7,1},{8,14},{9,15},{10,... | collective-permute-start | bytes 393224 | tf_op jit(solution)/shard_map/ppermute | solution.py:479
  7.1 12.3 %collective-permute-start.1 = (bf16[128,512]{1,0:T(8,128)(2,1)}, bf16[128,512]{1,0:T(8,128)(2,1)S(1)}, u32[]{:S(2)}, u32[]{:S(2)}) collective-permute-start(bf16[128,512]{1,0:T(8,128)(2,1)} %bitcast.2.grad_ref.refs_0_), channel_id=1, source_target_pairs={{0,2},{1,3},{2,0},{3,1},{4,6},{5,7},{6,4},{7,5},{8,10},{9,11},{10,... | collective-permute-start | bytes 393224 | tf_op jit(solution)/shard_map/ppermute | solution.py:479
  7.1 1.6 %copy-start = (bf16[1,128,8192]{2,1,0:T(8,128)(2,1)S(1)}, bf16[1,128,8192]{2,1,0:T(8,128)(2,1)}, u32[]{:S(2)}) copy-start(bf16[1,128,8192]{2,1,0:T(8,128)(2,1)} %param.8) | copy-start | bytes 6291460
  8.7 0.8 copy-start.6
  9.5 36.7 %copy-start.8 = (s32[512]{0:T(512)S(1)}, s32[512]{0:T(512)}, u32[]{:S(2)}) copy-start(s32[512]{0:T(512)} %param.12) | copy-start | bytes 6148
  20.4 11.1 %collective-permute-start.10 = (bf16[128,1024]{1,0:T(8,128)(2,1)S(1)}, bf16[128,1024]{1,0:T(8,128)(2,1)S(1)}, u32[]{:S(2)}, u32[]{:S(2)}) collective-permute-start(bf16[128,1024]{1,0:T(8,128)(2,1)S(1)} %get-tuple-element.45.refs_7_.refs_4_), channel_id=1, source_target_pairs={{0,24},{1,25},{2,26},{3,27},{4,28},{5,29},{6,30},{7,31},{8,16},{9,... | collective-permute-start | bytes 786440 | tf_op jit(solution)/shard_map/ppermute | solution.py:479
  24.0 22.2 %collective-permute-start.9 = (bf16[128,1024]{1,0:T(8,128)(2,1)S(1)}, bf16[128,1024]{1,0:T(8,128)(2,1)S(1)}, u32[]{:S(2)}, u32[]{:S(2)}) collective-permute-start(bf16[128,1024]{1,0:T(8,128)(2,1)S(1)} %get-tuple-element.45.refs_7_.refs_4_), channel_id=1, source_target_pairs={{0,16},{1,17},{2,18},{3,19},{4,20},{5,21},{6,22},{7,23},{8,24},{9,... | collective-permute-start | bytes 786440 | tf_op jit(solution)/shard_map/ppermute | solution.py:479
  24.0 29.5 %collective-permute-start.4 = (bf16[512,512]{1,0:T(8,128)(2,1)S(1)}, bf16[512,512]{1,0:T(8,128)(2,1)S(1)}, u32[]{:S(2)}, u32[]{:S(2)}) collective-permute-start(bf16[512,512]{1,0:T(8,128)(2,1)S(1)} %get-tuple-element.41.refs_1_.grads_ref), channel_id=1, source_target_pairs={{0,1},{1,0},{2,3},{3,2},{4,5},{5,4},{6,7},{7,6},{8,9},{9,8},{10,11... | collective-permute-start | bytes 1572872 | tf_op jit(solution)/shard_map/ppermute | solution.py:479
  24.0 29.5 %collective-permute-start.5 = (bf16[2,128,1024]{2,1,0:T(8,128)(2,1)S(1)}, bf16[2,128,1024]{2,1,0:T(8,128)(2,1)S(1)}, u32[]{:S(2)}, u32[]{:S(2)}) collective-permute-start(bf16[2,128,1024]{2,1,0:T(8,128)(2,1)S(1)} %get-tuple-element.42), channel_id=1, source_target_pairs={{0,4},{1,5},{2,6},{3,7},{4,0},{5,1},{6,2},{7,3},{8,12},{9,13},{10,... | collective-permute-start | bytes 1572872 | tf_op jit(solution)/shard_map/ppermute | solution.py:479
  25.5 28.0 %collective-permute-start.6 = (bf16[2,128,1024]{2,1,0:T(8,128)(2,1)S(1)}, bf16[2,128,1024]{2,1,0:T(8,128)(2,1)S(1)}, u32[]{:S(2)}, u32[]{:S(2)}) collective-permute-start(bf16[2,128,1024]{2,1,0:T(8,128)(2,1)S(1)} %get-tuple-element.43), channel_id=1, source_target_pairs={{0,2},{1,3},{2,0},{3,1},{4,6},{5,7},{6,4},{7,5},{8,10},{9,11},{10,... | collective-permute-start | bytes 1572872 | tf_op jit(solution)/shard_map/ppermute | solution.py:479
  31.5 22.1 %collective-permute-start.7 = (bf16[2,128,1024]{2,1,0:T(8,128)(2,1)S(1)}, bf16[2,128,1024]{2,1,0:T(8,128)(2,1)S(1)}, u32[]{:S(2)}, u32[]{:S(2)}) collective-permute-start(bf16[2,128,1024]{2,1,0:T(8,128)(2,1)S(1)} %get-tuple-element.44), channel_id=1, source_target_pairs={{0,6},{1,7},{2,4},{3,5},{4,2},{5,3},{6,0},{7,1},{8,14},{9,15},{10,... | collective-permute-start | bytes 1572872 | tf_op jit(solution)/shard_map/ppermute | solution.py:479
  46.2 7.3 %collective-permute-start.8 = (bf16[128,1024]{1,0:T(8,128)(2,1)S(1)}, bf16[128,1024]{1,0:T(8,128)(2,1)S(1)}, u32[]{:S(2)}, u32[]{:S(2)}) collective-permute-start(bf16[128,1024]{1,0:T(8,128)(2,1)S(1)} %get-tuple-element.45.refs_7_.refs_4_), channel_id=1, source_target_pairs={{0,8},{1,9},{2,10},{3,11},{4,12},{5,13},{6,14},{7,15},{8,0},{9,1},... | collective-permute-start | bytes 786440 | tf_op jit(solution)/shard_map/ppermute | solution.py:479
  56.6 13.7 %collective-permute-start.17 = (bf16[256,1024]{1,0:T(8,128)(2,1)S(1)}, bf16[256,1024]{1,0:T(8,128)(2,1)S(1)}, u32[]{:S(2)}, u32[]{:S(2)}) collective-permute-start(bf16[256,1024]{1,0:T(8,128)(2,1)S(1)} %get-tuple-element.46.refs_8_), channel_id=1, source_target_pairs={{0,8},{1,9},{2,10},{3,11},{4,12},{5,13},{6,14},{7,15},{24,16},{25,... | collective-permute-start | bytes 1572872 | tf_op jit(solution)/shard_map/ppermute | solution.py:479
  64.2 7.0 %collective-permute-start.11 = (bf16[256,1024]{1,0:T(8,128)(2,1)S(1)}, bf16[256,1024]{1,0:T(8,128)(2,1)S(1)}, u32[]{:S(2)}, u32[]{:S(2)}) collective-permute-start(bf16[256,1024]{1,0:T(8,128)(2,1)S(1)} %get-tuple-element.49), channel_id=1, source_target_pairs={{0,1},{1,0},{2,3},{3,2},{4,5},{5,4},{6,7},{7,6},{8,9},{9,8},{10,11... | collective-permute-start | bytes 1572872 | tf_op jit(solution)/shard_map/ppermute | solution.py:479
  64.2 6.9 %collective-permute-start.12 = (bf16[256,1024]{1,0:T(8,128)(2,1)S(1)}, bf16[256,1024]{1,0:T(8,128)(2,1)S(1)}, u32[]{:S(2)}, u32[]{:S(2)}) collective-permute-start(bf16[256,1024]{1,0:T(8,128)(2,1)S(1)} %get-tuple-element.50), channel_id=1, source_target_pairs={{0,1},{1,0},{2,3},{3,2},{4,5},{5,4},{6,7},{7,6},{8,9},{9,8},{10,11... | collective-permute-start | bytes 1572872 | tf_op jit(solution)/shard_map/ppermute | solution.py:479
  64.7 6.4 %collective-permute-start.13 = (bf16[512,512]{1,0:T(8,128)(2,1)S(1)}, bf16[512,512]{1,0:T(8,128)(2,1)S(1)}, u32[]{:S(2)}, u32[]{:S(2)}) collective-permute-start(bf16[512,512]{1,0:T(8,128)(2,1)S(1)} %get-tuple-element.51), channel_id=1, source_target_pairs={{0,1},{1,0},{2,3},{3,2},{4,5},{5,4},{6,7},{7,6},{8,9},{9,8},{10,11... | collective-permute-start | bytes 1572872 | tf_op jit(solution)/shard_map/ppermute | solution.py:479
  64.8 15.1 %collective-permute-start.19 = (bf16[256,1024]{1,0:T(8,128)(2,1)S(1)}, bf16[256,1024]{1,0:T(8,128)(2,1)S(1)}, u32[]{:S(2)}, u32[]{:S(2)}) collective-permute-start(bf16[256,1024]{1,0:T(8,128)(2,1)S(1)} %get-tuple-element.63), channel_id=1, source_target_pairs={{0,8},{1,9},{2,10},{3,11},{4,12},{5,13},{6,14},{7,15},{24,16},{25,... | collective-permute-start | bytes 1572872 | tf_op jit(solution)/shard_map/ppermute | solution.py:479
  70.4 9.4 %collective-permute-start.18 = (bf16[256,1024]{1,0:T(8,128)(2,1)S(1)}, bf16[256,1024]{1,0:T(8,128)(2,1)S(1)}, u32[]{:S(2)}, u32[]{:S(2)}) collective-permute-start(bf16[256,1024]{1,0:T(8,128)(2,1)S(1)} %relay.2), channel_id=1, source_target_pairs={{8,16},{9,17},{10,18},{11,19},{12,20},{13,21},{14,22},{15,23},{16,... | collective-permute-start | bytes 1572872 | tf_op jit(solution)/shard_map/ppermute | solution.py:479
  71.4 15.7 %collective-permute-start.16 = (bf16[128,2560]{1,0:T(8,128)(2,1)S(1)}, bf16[128,2560]{1,0:T(8,128)(2,1)S(1)}, u32[]{:S(2)}, u32[]{:S(2)}) collective-permute-start(bf16[128,2560]{1,0:T(8,128)(2,1)S(1)} %get-tuple-element.56), channel_id=1, source_target_pairs={{0,6},{1,7},{2,4},{3,5},{4,2},{5,3},{6,0},{7,1},{8,14},{9,15},{10,... | collective-permute-start | bytes 1966088 | tf_op jit(solution)/shard_map/ppermute | solution.py:479
  79.9 21.6 %copy-start.1 = (bf16[1,128,8192]{2,1,0:T(8,128)(2,1)S(1)}, bf16[1,128,8192]{2,1,0:T(8,128)(2,1)}, u32[]{:S(2)}) copy-start(bf16[1,128,8192]{2,1,0:T(8,128)(2,1)} %param.8) | copy-start | bytes 6291460
  79.9 21.6 %copy-start.7 = (f32[8192]{0:T(1024)S(1)}, f32[8192]{0:T(1024)}, u32[]{:S(2)}) copy-start(f32[8192]{0:T(1024)} %param.9) | copy-start | bytes 98308
  80.1 13.1 %collective-permute-start.20 = (bf16[256,1024]{1,0:T(8,128)(2,1)S(1)}, bf16[256,1024]{1,0:T(8,128)(2,1)S(1)}, u32[]{:S(2)}, u32[]{:S(2)}) collective-permute-start(bf16[256,1024]{1,0:T(8,128)(2,1)S(1)} %get-tuple-element.64), channel_id=1, source_target_pairs={{0,8},{1,9},{2,10},{3,11},{4,12},{5,13},{6,14},{7,15},{8,0},{9,1},... | collective-permute-start | bytes 1572872 | tf_op jit(solution)/shard_map/ppermute | solution.py:479
  84.3 8.9 %collective-permute-start.21 = (bf16[256,1024]{1,0:T(8,128)(2,1)S(1)}, bf16[256,1024]{1,0:T(8,128)(2,1)S(1)}, u32[]{:S(2)}, u32[]{:S(2)}) collective-permute-start(bf16[256,1024]{1,0:T(8,128)(2,1)S(1)} %get-tuple-element.65), channel_id=1, source_target_pairs={{8,16},{9,17},{10,18},{11,19},{12,20},{13,21},{14,22},{15,23},{16,... | collective-permute-start | bytes 1572872 | tf_op jit(solution)/shard_map/ppermute | solution.py:479
  85.0 16.5 %collective-permute-start.14 = (bf16[128,2560]{1,0:T(8,128)(2,1)S(1)}, bf16[128,2560]{1,0:T(8,128)(2,1)S(1)}, u32[]{:S(2)}, u32[]{:S(2)}) collective-permute-start(bf16[128,2560]{1,0:T(8,128)(2,1)S(1)} %get-tuple-element.54), channel_id=1, source_target_pairs={{0,4},{1,5},{2,6},{3,7},{4,0},{5,1},{6,2},{7,3},{8,12},{9,13},{10,... | collective-permute-start | bytes 1966088 | tf_op jit(solution)/shard_map/ppermute | solution.py:479
  86.5 15.0 %collective-permute-start.15 = (bf16[128,2560]{1,0:T(8,128)(2,1)S(1)}, bf16[128,2560]{1,0:T(8,128)(2,1)S(1)}, u32[]{:S(2)}, u32[]{:S(2)}) collective-permute-start(bf16[128,2560]{1,0:T(8,128)(2,1)S(1)} %get-tuple-element.55), channel_id=1, source_target_pairs={{0,2},{1,3},{2,0},{3,1},{4,6},{5,7},{6,4},{7,5},{8,10},{9,11},{10,... | collective-permute-start | bytes 1966088 | tf_op jit(solution)/shard_map/ppermute | solution.py:479
  93.4 11.8 %collective-permute-start.22 = (bf16[128,1024]{1,0:T(8,128)(2,1)S(1)}, bf16[128,1024]{1,0:T(8,128)(2,1)S(1)}, u32[]{:S(2)}, u32[]{:S(2)}) collective-permute-start(bf16[128,1024]{1,0:T(8,128)(2,1)S(1)} %get-tuple-element.67), channel_id=1, source_target_pairs={{0,4},{1,5},{2,6},{3,7},{4,0},{5,1},{6,2},{7,3},{8,12},{9,13},{10,... | collective-permute-start | bytes 786440 | tf_op jit(solution)/shard_map/ppermute | solution.py:479
  101.5 3.7 %copy-start.2 = (f32[1,128,2048]{2,1,0:T(8,128)S(1)}, f32[1,128,2048]{2,1,0:T(8,128)}, u32[]{:S(2)}) copy-start(f32[1,128,2048]{2,1,0:T(8,128)} %param.13) | copy-start | bytes 3145732
  101.5 3.7 %copy-start.3 = (f32[1,128,2048]{2,1,0:T(8,128)S(1)}, f32[1,128,2048]{2,1,0:T(8,128)}, u32[]{:S(2)}) copy-start(f32[1,128,2048]{2,1,0:T(8,128)} %param.14) | copy-start | bytes 3145732
  101.5 3.7 %copy-start.4 = (f32[1,128,2048]{2,1,0:T(8,128)S(1)}, f32[1,128,2048]{2,1,0:T(8,128)}, u32[]{:S(2)}) copy-start(f32[1,128,2048]{2,1,0:T(8,128)} %param.15) | copy-start | bytes 3145732

commit v5 on v4

--- a/solution.py
+++ b/solution.py
@@ -68,51 +68,45 @@
     return [outs[i : i + parts] for i in range(0, len(outs), parts)]
 
 
-def pack_kernel(w_ref, grad_ref, keep_ref, send_ref):
-    share, width = keep_ref.shape
-    rows, feats = grad_ref.shape
+def late_kernel(a_ref, *refs):
+    refs[-1][...] = a_ref[...]
+
+
+def late(a, after):
+    return pl.pallas_call(
+        late_kernel,
+        in_specs=[pl.BlockSpec(memory_space=pltpu.VMEM)]
+        + [pl.BlockSpec(memory_space=pl.ANY)] * len(after),
+        out_shape=jax.ShapeDtypeStruct(a.shape, a.dtype),
+        compiler_params=limit(16),
+        name="late",
+    )(a, *after)
+
+
+def halves_kernel(w_ref, keep_ref, send_ref):
+    width = keep_ref.shape[1]
     own_x = lax.axis_index("dp") % 2
     keep_ref[...] = w_ref[:, pl.ds(pl.multiple_of(own_x * width, width), width)]
-    send_ref[:share, :] = w_ref[:, pl.ds(pl.multiple_of((1 - own_x) * width, width), width)]
-    pieces = feats // width if feats > width else 1
-    for at in range(0, rows * pieces, rows):
-        send_ref[share + at : share + at + rows, : feats // pieces] = grad_ref[
-            :, at // rows * width : at // rows * width + feats // pieces
-        ]
-
-
-def pack(w_t, grads, width):
-    share, (rows, feats) = w_t.shape[0], grads.shape
-    pieces = max(feats // width, 1)
-    return pl.pallas_call(
-        pack_kernel,
-        out_shape=[
-            jax.ShapeDtypeStruct((share, width), bf16),
-            jax.ShapeDtypeStruct((share + pieces * rows, width), bf16),
-        ],
+    send_ref[...] = w_ref[:, pl.ds(pl.multiple_of((1 - own_x) * width, width), width)]
+
+
+def halves(w_t, width):
+    return pl.pallas_call(
+        halves_kernel,
+        out_shape=[jax.ShapeDtypeStruct((w_t.shape[0], width), bf16)] * 2,
         compiler_params=limit(16),
-        cost_estimate=cost(0, 8 * rows * feats),
-        name="pack",
-    )(w_t, grads)
+        name="halves",
+    )(w_t)
 
 
 def unpack_kernel(keep_ref, got_ref, *refs):
     plane_ref, grads_ref = refs[-2:]
-    chips = grads_ref.shape[0] // refs[0].shape[0]
-    share, width = keep_ref.shape
-    rows, feats = refs[0].shape
+    share = keep_ref.shape[0]
+    rows = refs[0].shape[0]
     plane_ref[:share, :] = keep_ref[...]
-    plane_ref[share:, :] = got_ref[:share, :]
-    for k in range(chips):
-        at = slice(k * rows, (k + 1) * rows)
-        if k != 1:
-            grads_ref[at, :] = refs[k - (k > 1)][...]
-            continue
-        pieces = feats // width if feats > width else 1
-        lanes = feats // pieces
-        for i in range(pieces):
-            part = got_ref[share + i * rows : share + (i + 1) * rows, :lanes]
-            grads_ref[at, i * lanes : (i + 1) * lanes] = part
+    plane_ref[share:, :] = got_ref[...]
+    for k in range(grads_ref.shape[0] // rows):
+        grads_ref[k * rows : (k + 1) * rows, :] = refs[k][...]
 
 
 def unpack(keep, got, grads, after):
@@ -124,10 +118,9 @@
         + [pl.BlockSpec(memory_space=pl.ANY)] * len(after),
         out_shape=[
             jax.ShapeDtypeStruct((2 * share, width), bf16),
-            jax.ShapeDtypeStruct(((len(grads) + 1) * rows, feats), bf16),
+            jax.ShapeDtypeStruct((len(grads) * rows, feats), bf16),
         ],
         compiler_params=limit(16),
-        cost_estimate=cost(0, 0),
         name="unpack",
     )(keep, got, *grads, *after)
 
@@ -235,23 +228,15 @@
             held[pl.ds(at, share), :] = ref[i * share : (i + 1) * share, :]
 
 
-def back_kernel(planes, chips, parts, grads_ref, far_ref, *refs):
+def value_kernel(planes, chips, parts, *refs):
     piece_refs, refs = refs[: chips * parts], refs[chips * parts :]
-    (*far_refs, far_value_ref, out_ref, value_ref), held = refs[-6:-1], refs[-1]
-    rows = grads_ref.shape[0] // chips
-    feats, width = held.shape
-    part_width = width // parts
+    far_refs, out_ref, held = refs[-4:-2], refs[-2], refs[-1]
+    rows = out_ref.shape[0] // chips
+    half = chips // 2
+    part_width = held.shape[1] // parts
     gather_weight(refs[:planes], held)
     for core in (1, 0):
         for k in range(chips):
-            at = slice(k * rows, (k + 1) * rows)
-            from_ref = far_ref if core else grads_ref
-            block = jnp.dot(from_ref[at, :], held[...], preferred_element_type=f32).astype(bf16)
-            if core:
-                half = chips // 2
-                far_refs[k // half][k % half * rows : (k % half + 1) * rows, :] = block
-            else:
-                out_ref[at, :] = block
             total = None
             for part in range(parts):
                 term = lax.dot_general(
@@ -261,61 +246,71 @@
                     preferred_element_type=f32,
                 )
                 total = term if total is None else total + term
-            (far_value_ref if core else value_ref)[at, :] = total.astype(bf16)
-
-
-def back_blocks(grads, grads_far, pieces, weights, after):
+            if core:
+                at = k % half * rows
+                far_refs[k // half][at : at + rows, :] = total.astype(bf16)
+            else:
+                out_ref[k * rows : (k + 1) * rows, :] = total
+
+
+def value_parts(pieces, weights, feats, after):
     chips, parts = len(pieces), len(pieces[0])
+    rows = pieces[0][0].shape[1]
+    width = weights[0].shape[-1]
+    return pl.pallas_call(
+        functools.partial(value_kernel, len(weights), chips, parts),
+        in_specs=[pl.BlockSpec(memory_space=pltpu.VMEM)] * (chips * parts + len(weights))
+        + [pl.BlockSpec(memory_space=pl.ANY)] * len(after),
+        out_shape=[jax.ShapeDtypeStruct((chips // 2 * rows, feats), bf16)] * 2
+        + [jax.ShapeDtypeStruct((chips * rows, feats), f32)],
+        scratch_shapes=[pltpu.VMEM((feats, width), bf16)],
+        compiler_params=limit(40),
+        name="value_parts",
+    )(*[p for piece in pieces for p in piece], *weights, *after)
+
+
+def back_kernel(planes, chips, grads_ref, value_ref, got_a_ref, got_b_ref, *refs):
+    weight_refs, refs = refs[: 2 * planes], refs[2 * planes :]
+    out_refs, own_ref, held = refs[-chips - 2 : -2], refs[-2], refs[-1]
+    rows, feats = own_ref.shape
+    width = held.shape[1]
+    half = chips // 2
+    for k in range(chips):
+        got_ref = got_b_ref if k // half else got_a_ref
+        total = value_ref[k * rows : (k + 1) * rows, :]
+        total += got_ref[k % half * rows : (k % half + 1) * rows, :].astype(f32)
+        if k == 0:
+            own_ref[...] = total
+        else:
+            out_refs[k][:, 2 * width :] = total.astype(bf16)
+    for j in range(2):
+        gather_weight(weight_refs[j * planes : (j + 1) * planes], held)
+        for k in range(chips):
+            out_refs[k][:, j * width : (j + 1) * width] = jnp.dot(
+                grads_ref[k * rows : (k + 1) * rows, :],
+                held[...],
+                preferred_element_type=f32,
+            ).astype(bf16)
+
+
+def back_blocks(grads, sums, weights, chips):
     rows, feats = grads.shape[0] // chips, grads.shape[1]
     width = weights[0].shape[-1]
-    half = jax.ShapeDtypeStruct((chips // 2 * rows, width), bf16)
-    value = jax.ShapeDtypeStruct((chips * rows, feats), bf16)
-    outs = pl.pallas_call(
-        functools.partial(back_kernel, len(weights), chips, parts),
-        in_specs=[pl.BlockSpec(memory_space=pltpu.VMEM)] * (2 + chips * parts + len(weights))
-        + [pl.BlockSpec(memory_space=pl.ANY)] * len(after),
-        out_shape=[half, half, value, jax.ShapeDtypeStruct((chips * rows, width), bf16), value],
-        scratch_shapes=[pltpu.VMEM((feats, width), bf16)],
-        compiler_params=limit(40),
-        name="back_blocks",
-    )(grads, grads_far, *[p for piece in pieces for p in piece], *weights, *after)
-    return outs[:3], outs[3:]
-
-
-def home_kernel(own_ref, own_value_ref, got_a_ref, got_b_ref, got_value_ref, *out_refs):
-    chips = len(out_refs) - 1
-    rows = out_refs[0].shape[0]
-    width = out_refs[0].shape[1] // 2
-    half = chips // 2
-    for k in range(chips):
-        at = slice(k * rows, (k + 1) * rows)
-        got_ref = got_b_ref if k // half else got_a_ref
-        out_refs[k][:, :width] = own_ref[at, :]
-        out_refs[k][:, width : 2 * width] = got_ref[k % half * rows : (k % half + 1) * rows, :]
-        values = own_value_ref[at, :].astype(f32) + got_value_ref[at, :].astype(f32)
-        if k == 0:
-            out_refs[-1][...] = values
-        else:
-            out_refs[k][:, 2 * width :] = values.astype(bf16)
-
-
-def home_blocks(own, got, chips):
-    rows, width = own[0].shape[0] // chips, own[0].shape[1]
-    feats = own[1].shape[1]
-    return pl.pallas_call(
-        home_kernel,
+    return pl.pallas_call(
+        functools.partial(back_kernel, len(weights) // 2, chips),
         out_shape=[
             jax.ShapeDtypeStruct((rows, 2 * width + (feats if k else 0)), bf16)
             for k in range(chips)
         ]
         + [jax.ShapeDtypeStruct((rows, feats), f32)],
-        compiler_params=limit(24),
-        name="home_blocks",
-    )(*own, *got)
+        scratch_shapes=[pltpu.VMEM((feats, width), bf16)],
+        compiler_params=limit(40),
+        name="back_blocks",
+    )(grads, *sums, *weights)
 
 
 def grad_x_kernel(tok_ref, gain_ref, part_ref, *refs):
-    grad_refs, out_ref, values_ref = refs[:-2], refs[-2], refs[-1]
+    grad_refs, (out_ref, values_ref) = refs[:-2], refs[-2:]
     model = tok_ref.shape[-1]
     width = grad_refs[0].shape[-1] // 2
     values = part_ref[...]
@@ -503,18 +498,21 @@
         return permute(value, target)
 
     tokens_far = to_core(tokens)
-    w_keep, packed = pack(w_t, value_grad, width)
-    packed = to_chip(packed, 1)
-    grads = [to_chip(value_grad, k) for k in range(chips - 1, 1, -1)][::-1]
+    grads = [value_grad] + [to_chip(value_grad, k) for k in range(chips - 1, 0, -1)][::-1]
+    w_keep, w_send = halves(w_t, width)
+    w_got = to_x(w_send)
 
     gain_row, owner_row = gain[None, :], owner[None, :]
     sent = norm_blocks(tokens, tokens_far, gain_row, chips, width, parts)
-    w_plane, grads = unpack(w_keep, packed, [value_grad] + grads, (sent[0][0],))
+    w_plane, grads = unpack(w_keep, w_got, grads, (sent[0][0],))
     pieces = [sent[0]] + [[to_chip(p, k) for p in sent[k]] for k in range(1, chips)]
-    grads_far = to_core(grads)
     selected = select_rows(owner_row, groups, slots, (sent[0][0],))
 
-    weights = [w_plane] + [to_plane(w_plane, turn) for turn in range(1, planes)]
+    weights = [w_plane]
+    while len(weights) < planes:
+        weights += [to_plane(w, len(weights)) for w in weights]
+    weights_far = [to_core(w) for w in weights]
+    grads_far = to_core(late(grads, weights[1:2]))
 
     plan = [
         (step, even)
@@ -534,8 +532,9 @@
         )
         ready = dict(zip(plan, outs))
         if part == parts - 1:
-            back_far, back_own = back_blocks(grads, grads_far, pieces, weights, [outs[0]])
-            back = home_blocks(back_own, [to_core(b) for b in back_far], chips)
+            *far_sums, near_sum = value_parts(pieces, weights, feats, outs[:1])
+            sums = [near_sum] + [to_core(f) for f in far_sums]
+            back = back_blocks(grads, sums, weights + weights_far, chips)
             home = [back[0]] + [to_chip(back[k], k) for k in range(1, chips)]
         held = {}
         for step in range(1, planes):
@@ -543,12 +542,13 @@
             send = [ready[step, even] for even in here]
             if held:
                 sums = [[ready[step, even], held[not even]] for even in here if (not even) in held]
-                sums = list(relay(sums, back_own[:1] if step == 2 else [back[0]])) if sums else []
+                if sums:
+                    sums = list(relay(sums, back[:1] if step == 2 else home[-1:]))
                 send = []
                 for even in here:
                     send.append(sums.pop(0) if (not even) in held else ready[step, even])
             held = {even: across(value, step, even) for even, value in zip(here, send)}
-        keep, send = finish(outs[-1], held[True], held[False], home[-1:])
+        keep, send = finish(outs[-1], held[True], held[False], home[1:])
         kept.append(keep)
         got.append(to_x(send))
 

time: 108 us -> 100 us (0.926)
  waiting for transfers between devices: 57.7 us -> 52.7 us
  Pallas kernels: 18.2 us -> 16.5 us
  starting transfers between devices: 27.7 us -> 26.6 us
    ppermute x23 -> x27, waiting for transfers between devices: 57.7 us -> 52.7 us  [permute(): return lax.ppermute(value, ('dp', 'seq'), pairs)]
    ppermute x23 -> x27, starting transfers between devices: 27.7 us -> 26.6 us  [permute(): return lax.ppermute(value, ('dp', 'seq'), pairs)]
    pallas_call x3 -> x4, Pallas kernels: 5.29 us -> 4.51 us  [the longest x1 2.98 us: value_parts(): pl.pallas_call(functools.partial(value_kernel, len(weights), chips, parts...]
    unnamed x18 -> x20, local copies, waits for them, and re-layouts: 3.33 us -> 3.33 us
  transfers between devices with their start and end apart: 23 -> 27, of which waited for: 8 -> 14; matrix products, arithmetic and copies ran while one was open for 0% -> 0% of each run, Pallas kernels for 11% -> 14%
where the time goes in v5:
time: 100 us; the launch traced here: 99.9 us
  waiting for transfers between devices  52.7 us (53%)
  starting transfers between devices  26.6 us (27%)
  Pallas kernels  16.5 us (16%)
  local copies, waits for them, and re-layouts  3.33 us (3%)
    ppermute x27, waiting for transfers between devices, permute(): return lax.ppermute(value, ('dp', 'seq'), pairs)  52.7 us
    ppermute x27, starting transfers between devices, permute(): return lax.ppermute(value, ('dp', 'seq'), pairs)  26.6 us
    pallas_call x1, Pallas kernels, grad_x_blocks(): pl.pallas_call(grad_x_kernel, grid=(rows // step,), in_specs=[pl.BlockSpe...  3.62 us
    unnamed x20, local copies, waits for them, and re-layouts  3.33 us
    pallas_call x1, Pallas kernels, weight_blocks(): pl.pallas_call(functools.partial(weight_kernel, planes, chips, plan), in_...  3.02 us
    pallas_call x1, Pallas kernels, value_parts(): pl.pallas_call(functools.partial(value_kernel, len(weights), chips, parts...  2.98 us
    pallas_call x1, Pallas kernels, adam(): pl.pallas_call(functools.partial(adam_kernel, token_total, len(kept)), gr...  2.6 us
  transfers between devices with their start and end apart: 27, of which 14 were waited for; matrix products, arithmetic and copies ran while one was open for 0% of the time, Pallas kernels for 14%

profile of v5, /device:TPU:0, one launch (start us, length us, event | category | flops | bytes accessed | tf_op | source)
XLA Modules:
  0.0 99.9 jit_solution(4779190028249020135)
XLA Ops:
  0.6 0.5 collective-permute-start.4
  1.1 3.5 %collective-permute-start.3 = (bf16[128,512]{1,0:T(8,128)(2,1)}, bf16[128,512]{1,0:T(8,128)(2,1)S(1)}, u32[]{:S(2)}, u32[]{:S(2)}) collective-permute-start(bf16[128,512]{1,0:T(8,128)(2,1)} %bitcast.20), channel_id=1, source_target_pairs={{0,6},{1,7},{2,4},{3,5},{4,2},{5,3},{6,0},{7,1},{8,14},{9,15},{10,... | collective-permute-start | bytes 393224 | tf_op jit(solution)/shard_map/ppermute | solution.py:474
  4.7 0.5 collective-permute-start.2
  5.2 0.1 collective-permute-start.1
  5.3 0.9 copy-done.5
  6.3 2.0 %collective-permute-start = (bf16[64,1024]{1,0:T(8,128)(2,1)S(1)}, bf16[64,1024]{1,0:T(8,128)(2,1)S(1)}, u32[]{:S(2)}, u32[]{:S(2)}) collective-permute-start(bf16[64,1024]{1,0:T(8,128)(2,1)S(1)} %get-tuple-element.37), channel_id=1, source_target_pairs={{0,4},{1,5},{2,6},{3,7},{4,0},{5,1},{6,2},{7,3},{8,12},{9,13},{10,... | collective-permute-start | bytes 393224 | tf_op jit(solution)/shard_map/ppermute | solution.py:474
  8.2 1.6 %copy-done = bf16[1,128,8192]{2,1,0:T(8,128)(2,1)S(1)} copy-done((bf16[1,128,8192]{2,1,0:T(8,128)(2,1)S(1)}, bf16[1,128,8192]{2,1,0:T(8,128)(2,1)}, u32[]{:S(2)}) %copy-start) | copy-done | bytes 2097176
  9.8 0.8 copy-done.6
  10.6 1.7 %norm_blocks.1 = (bf16[2,128,1024]{2,1,0:T(8,128)(2,1)S(1)}, bf16[2,128,1024]{2,1,0:T(8,128)(2,1)S(1)}, bf16[2,128,1024]{2,1,0:T(8,128)(2,1)S(1)}, bf16[2,128,1024]{2,1,0:T(8,128)(2,1)S(1)}) custom-call(bf16[128,8192]{1,0:T(8,128)(2,1)S(1)} %bitcast.13, bf16[128,8192]{1,0:T(8,128)(2,1)S(1)} %collective-permute-done.4.far_ref, f32[1,8192]{1,0:T(1,128)S(1)} %bitcast.18), custom_call_target="tpu_custom_call" | custom-call | flops 8388608 | bytes 6291456 | tf_op jit(solution)/shard_map/norm_blocks/pallas_call | solution.py:54
  12.3 0.2 collective-permute-done.1.refs_1_
  12.5 2.4 %collective-permute-done.got_ref = bf16[64,1024]{1,0:T(8,128)(2,1)S(1)} collective-permute-done((bf16[64,1024]{1,0:T(8,128)(2,1)S(1)}, bf16[64,1024]{1,0:T(8,128)(2,1)S(1)}, u32[]{:S(2)}, u32[]{:S(2)}) %collective-permute-start) | collective-permute-done | bytes 131104 | tf_op jit(solution)/shard_map/ppermute | solution.py:474
  15.0 1.6 %collective-permute-start.8 = (bf16[128,1024]{1,0:T(8,128)(2,1)S(1)}, bf16[128,1024]{1,0:T(8,128)(2,1)S(1)}, u32[]{:S(2)}, u32[]{:S(2)}) collective-permute-start(bf16[128,1024]{1,0:T(8,128)(2,1)S(1)} %get-tuple-element.43.refs_7_.refs_4_.refs_0_), channel_id=1, source_target_pairs={{0,8},{1,9},{2,10},{3,11},{4,12},{5,13},{6,14},{7,15},{8,0},{9,1},... | collective-permute-start | bytes 786440 | tf_op jit(solution)/shard_map/ppermute | solution.py:474
  16.6 2.6 %collective-permute-start.9 = (bf16[128,1024]{1,0:T(8,128)(2,1)S(1)}, bf16[128,1024]{1,0:T(8,128)(2,1)S(1)}, u32[]{:S(2)}, u32[]{:S(2)}) collective-permute-start(bf16[128,1024]{1,0:T(8,128)(2,1)S(1)} %get-tuple-element.43.refs_7_.refs_4_.refs_0_), channel_id=1, source_target_pairs={{0,16},{1,17},{2,18},{3,19},{4,20},{5,21},{6,22},{7,23},{8,24},{9,... | collective-permute-start | bytes 786440 | tf_op jit(solution)/shard_map/ppermute | solution.py:474
  19.2 1.5 %collective-permute-start.5 = (bf16[2,128,1024]{2,1,0:T(8,128)(2,1)S(1)}, bf16[2,128,1024]{2,1,0:T(8,128)(2,1)S(1)}, u32[]{:S(2)}, u32[]{:S(2)}) collective-permute-start(bf16[2,128,1024]{2,1,0:T(8,128)(2,1)S(1)} %get-tuple-element.40), channel_id=1, source_target_pairs={{0,4},{1,5},{2,6},{3,7},{4,0},{5,1},{6,2},{7,3},{8,12},{9,13},{10,... | collective-permute-start | bytes 1572872 | tf_op jit(solution)/shard_map/ppermute | solution.py:474
  20.7 0.5 collective-permute-start.6
  21.2 1.5 %collective-permute-start.7 = (bf16[2,128,1024]{2,1,0:T(8,128)(2,1)S(1)}, bf16[2,128,1024]{2,1,0:T(8,128)(2,1)S(1)}, u32[]{:S(2)}, u32[]{:S(2)}) collective-permute-start(bf16[2,128,1024]{2,1,0:T(8,128)(2,1)S(1)} %get-tuple-element.42), channel_id=1, source_target_pairs={{0,6},{1,7},{2,4},{3,5},{4,2},{5,3},{6,0},{7,1},{8,14},{9,15},{10,... | collective-permute-start | bytes 1572872 | tf_op jit(solution)/shard_map/ppermute | solution.py:474
  22.7 5.7 %collective-permute-done.8.refs_0_.refs_8_.refs_5_.refs_1_ = bf16[128,1024]{1,0:T(8,128)(2,1)S(1)} collective-permute-done((bf16[128,1024]{1,0:T(8,128)(2,1)S(1)}, bf16[128,1024]{1,0:T(8,128)(2,1)S(1)}, u32[]{:S(2)}, u32[]{:S(2)}) %collective-permute-start.8) | collective-permute-done | bytes 262176 | tf_op jit(solution)/shard_map/ppermute | solution.py:474
  28.5 2.2 %collective-permute-done.9.refs_9_.refs_6_.refs_2_ = bf16[128,1024]{1,0:T(8,128)(2,1)S(1)} collective-permute-done((bf16[128,1024]{1,0:T(8,128)(2,1)S(1)}, bf16[128,1024]{1,0:T(8,128)(2,1)S(1)}, u32[]{:S(2)}, u32[]{:S(2)}) %collective-permute-start.9) | collective-permute-done | bytes 262176 | tf_op jit(solution)/shard_map/ppermute | solution.py:474
  30.8 0.3 collective-permute-start.10
  31.1 0.5 select_rows.1.refs_0_
  31.6 12.2 %collective-permute-done.10.refs_10_.refs_7_.refs_3_ = bf16[128,1024]{1,0:T(8,128)(2,1)S(1)} collective-permute-done((bf16[128,1024]{1,0:T(8,128)(2,1)S(1)}, bf16[128,1024]{1,0:T(8,128)(2,1)S(1)}, u32[]{:S(2)}, u32[]{:S(2)}) %collective-permute-start.10) | collective-permute-done | bytes 262176 | tf_op jit(solution)/shard_map/ppermute | solution.py:474
  43.7 0.5 collective-permute-start.16
  44.3 0.3 collective-permute-done.6.refs_5_.refs_2_
  44.6 3.0 %weight_blocks.1 = (bf16[256,1024]{1,0:T(8,128)(2,1)S(1)}, bf16[256,1024]{1,0:T(8,128)(2,1)S(1)}, bf16[256,1024]{1,0:T(8,128)(2,1)S(1)}, bf16[256,1024]{1,0:T(8,...) custom-call(bf16[1024,512]{1,0:T(8,128)(2,1)S(1)} %select_rows.1.refs_0_, ...), custom_call_target="tpu_custom_call" | custom-call | flops 2147483648 | bytes 4194304 | tf_op jit(solution)/shard_map/weight_blocks/pallas_call | solution.py:206
  47.6 2.4 %collective-permute-start.21 = (bf16[256,1024]{1,0:T(8,128)(2,1)S(1)}, bf16[256,1024]{1,0:T(8,128)(2,1)S(1)}, u32[]{:S(2)}, u32[]{:S(2)}) collective-permute-start(bf16[256,1024]{1,0:T(8,128)(2,1)S(1)} %get-tuple-element.44.refs_8_), channel_id=1, source_target_pairs={{0,8},{1,9},{2,10},{3,11},{4,12},{5,13},{6,14},{7,15},{24,16},{25,... | collective-permute-start | bytes 1572872 | tf_op jit(solution)/shard_map/ppermute | solution.py:474
  50.1 0.5 collective-permute-start.17
  50.6 3.0 %value_parts.1 = (bf16[256,512]{1,0:T(8,128)(2,1)S(1)}, bf16[256,512]{1,0:T(8,128)(2,1)S(1)}, f32[512,512]{1,0:T(8,128)S(1)}) custom-call(bf16[2,128,1024]{2,1,0:T(8,128)(2,1)S(1)} %get-tuple-element.38.refs_4_.refs_0_.refs_3_, bf16[2,128,1024]{2,1,0:T(8,128)(2,1)S(1)} %collective-permute-done.5.refs_4_.refs_1_, ...), custom_call_target="tpu_custom_call" | custom-call | tf_op jit(solution)/shard_map/value_parts/pallas_call | solution.py:260
  53.7 0.4 collective-permute-start.13
  54.2 1.0 %collective-permute-done.12.got_a_ref = bf16[256,512]{1,0:T(8,128)(2,1)S(1)} collective-permute-done((bf16[256,512]{1,0:T(8,128)(2,1)S(1)}, bf16[256,512]{1,0:T(8,128)(2,1)S(1)}, u32[]{:S(2)}, u32[]{:S(2)}) %collective-permute-start.12) | collective-permute-done | bytes 262176 | tf_op jit(solution)/shard_map/ppermute | solution.py:474
  55.2 0.4 collective-permute-done.13.got_b_ref
  55.6 1.5 %back_blocks.1 = (bf16[128,2048]{1,0:T(8,128)(2,1)S(1)}, bf16[128,2560]{1,0:T(8,128)(2,1)S(1)}, bf16[128,2560]{1,0:T(8,128)(2,1)S(1)}, bf16[128,2560]{1,0:T(8,128)(2,1)S(1)}, f32[128,512]{1,0:T(8,128)S(1)}) custom-call(bf16[512,512]{1,0:T(8,128)(2,1)S(1)} %get-tuple-element.39.a_ref.refs_1_.grads_ref, f32[512,512]{1,0:T(8,128)S(1)} %get-tuple-element.45.value_ref, ...), custom_call_target="tpu_custom_call" | custom-call | tf_op jit(solution)/shard_map/back_blocks/pallas_call | solution.py:299
  57.0 1.2 %collective-permute-start.20 = (bf16[128,2560]{1,0:T(8,128)(2,1)S(1)}, bf16[128,2560]{1,0:T(8,128)(2,1)S(1)}, u32[]{:S(2)}, u32[]{:S(2)}) collective-permute-start(bf16[128,2560]{1,0:T(8,128)(2,1)S(1)} %get-tuple-element.52), channel_id=1, source_target_pairs={{0,6},{1,7},{2,4},{3,5},{4,2},{5,3},{6,0},{7,1},{8,14},{9,15},{10,... | collective-permute-start | bytes 1966088 | tf_op jit(solution)/shard_map/ppermute | solution.py:474
  58.3 1.3 %collective-permute-start.23 = (bf16[256,1024]{1,0:T(8,128)(2,1)S(1)}, bf16[256,1024]{1,0:T(8,128)(2,1)S(1)}, u32[]{:S(2)}, u32[]{:S(2)}) collective-permute-start(bf16[256,1024]{1,0:T(8,128)(2,1)S(1)} %get-tuple-element.59), channel_id=1, source_target_pairs={{0,8},{1,9},{2,10},{3,11},{4,12},{5,13},{6,14},{7,15},{24,16},{25,... | collective-permute-start | bytes 1572872 | tf_op jit(solution)/shard_map/ppermute | solution.py:474
  59.6 1.0 collective-permute-done.21.refs_1_
  60.7 0.7 collective-permute-start.22
  61.4 2.3 %collective-permute-start.18 = (bf16[128,2560]{1,0:T(8,128)(2,1)S(1)}, bf16[128,2560]{1,0:T(8,128)(2,1)S(1)}, u32[]{:S(2)}, u32[]{:S(2)}) collective-permute-start(bf16[128,2560]{1,0:T(8,128)(2,1)S(1)} %get-tuple-element.50), channel_id=1, source_target_pairs={{0,4},{1,5},{2,6},{3,7},{4,0},{5,1},{6,2},{7,3},{8,12},{9,13},{10,... | collective-permute-start | bytes 1966088 | tf_op jit(solution)/shard_map/ppermute | solution.py:474
  63.7 7.8 %collective-permute-done.23.refs_3_ = bf16[256,1024]{1,0:T(8,128)(2,1)S(1)} collective-permute-done((bf16[256,1024]{1,0:T(8,128)(2,1)S(1)}, bf16[256,1024]{1,0:T(8,128)(2,1)S(1)}, u32[]{:S(2)}, u32[]{:S(2)}) %collective-permute-start.23) | collective-permute-done | bytes 524320 | tf_op jit(solution)/shard_map/ppermute | solution.py:474
  71.5 4.2 %collective-permute-done.20.refs_3_.refs_4_.refs_2_ = bf16[128,2560]{1,0:T(8,128)(2,1)S(1)} collective-permute-done((bf16[128,2560]{1,0:T(8,128)(2,1)S(1)}, bf16[128,2560]{1,0:T(8,128)(2,1)S(1)}, u32[]{:S(2)}, u32[]{:S(2)}) %collective-permute-start.20) | collective-permute-done | bytes 655392 | tf_op jit(solution)/shard_map/ppermute | solution.py:474
  75.6 0.2 relay.3
  75.9 1.0 collective-permute-start.24
  76.9 0.7 collective-permute-start.25
  77.6 10.3 %collective-permute-done.18.refs_1_.refs_0_ = bf16[128,2560]{1,0:T(8,128)(2,1)S(1)} collective-permute-done((bf16[128,2560]{1,0:T(8,128)(2,1)S(1)}, bf16[128,2560]{1,0:T(8,128)(2,1)S(1)}, u32[]{:S(2)}, u32[]{:S(2)}) %collective-permute-start.18) | collective-permute-done | bytes 655392 | tf_op jit(solution)/shard_map/ppermute | solution.py:474
  87.9 0.9 collective-permute-done.19.refs_2_.refs_1_
  88.8 0.2 finish.1
  89.0 0.6 collective-permute-start.26
  89.7 3.6 %grad_x_blocks.1 = (bf16[128,8192]{1,0:T(8,128)(2,1)}, bf16[128,512]{1,0:T(8,128)(2,1)}) custom-call(bf16[128,8192]{1,0:T(8,128)(2,1)S(1)} %bitcast.14, f32[1,8192]{1,0:T(1,128)S(1)} %bitcast.19, f32[128,512]{1,0:T(8,128)S(1)} %get-tuple-element.48.part_ref, bf16[128,2048]{1,0:T(8,128)(2,1)S(1)} %get-tuple-element.49.refs_0_.refs_2_, ...), custom_call_target="tpu_custom_call" | custom-call | flops 16777216 | bytes 6291456 | tf_op jit(solution)/shard_map/grad_x_blocks/pallas_call | solution.py:342
  93.3 4.0 %collective-permute-done.26.refs_1_ = bf16[128,1024]{1,0:T(8,128)(2,1)S(1)} collective-permute-done((bf16[128,1024]{1,0:T(8,128)(2,1)S(1)}, bf16[128,1024]{1,0:T(8,128)(2,1)S(1)}, u32[]{:S(2)}, u32[]{:S(2)}) %collective-permute-start.26) | collective-permute-done | bytes 262176 | tf_op jit(solution)/shard_map/ppermute | solution.py:474
  97.3 2.6 %adam.1 = (f32[128,2048]{1,0:T(8,128)}, f32[128,2048]{1,0:T(8,128)}, f32[128,2048]{1,0:T(8,128)}) custom-call(s32[1,512]{1,0:T(1,128)S(1)} %bitcast.25, f32[128,1024]{1,0:T(8,128)S(1)} %get-tuple-element.62.refs_0_, bf16[128,1024]{1,0:T(8,128)(2,1)S(1)} %collective-permute-done.26.refs_1_, f32[128,2048]{1,0:T(8,128)S(1)} %bitcast.15, ...), custom_call_target="tpu_custom_call" | custom-call | flops 5242880 | bytes 7864320 | tf_op jit(solution)/shard_map/adam/pallas_call | solution.py:442
  (39 shorter events, 0.6 us)
Async XLA Ops:
  0.6 7.6 %collective-permute-start.4 = (bf16[128,8192]{1,0:T(8,128)(2,1)}, bf16[128,8192]{1,0:T(8,128)(2,1)S(1)}, u32[]{:S(2)}, u32[]{:S(2)}) collective-permute-start(bf16[128,8192]{1,0:T(8,128)(2,1)} %bitcast.12), channel_id=1, source_target_pairs={{0,1},{1,0},{2,3},{3,2},{4,5},{5,4},{6,7},{7,6},{8,9},{9,8},{10,11... | collective-permute-start | bytes 6291464 | tf_op jit(solution)/shard_map/ppermute | solution.py:474
  1.1 11.1 %collective-permute-start.3 = (bf16[128,512]{1,0:T(8,128)(2,1)}, bf16[128,512]{1,0:T(8,128)(2,1)S(1)}, u32[]{:S(2)}, u32[]{:S(2)}) collective-permute-start(bf16[128,512]{1,0:T(8,128)(2,1)} %bitcast.20), channel_id=1, source_target_pairs={{0,6},{1,7},{2,4},{3,5},{4,2},{5,3},{6,0},{7,1},{8,14},{9,15},{10,... | collective-permute-start | bytes 393224 | tf_op jit(solution)/shard_map/ppermute | solution.py:474
  4.7 7.6 %collective-permute-start.2 = (bf16[128,512]{1,0:T(8,128)(2,1)}, bf16[128,512]{1,0:T(8,128)(2,1)S(1)}, u32[]{:S(2)}, u32[]{:S(2)}) collective-permute-start(bf16[128,512]{1,0:T(8,128)(2,1)} %bitcast.21), channel_id=1, source_target_pairs={{0,2},{1,3},{2,0},{3,1},{4,6},{5,7},{6,4},{7,5},{8,10},{9,11},{10,... | collective-permute-start | bytes 393224 | tf_op jit(solution)/shard_map/ppermute | solution.py:474
  5.2 7.4 %collective-permute-start.1 = (bf16[128,512]{1,0:T(8,128)(2,1)}, bf16[128,512]{1,0:T(8,128)(2,1)S(1)}, u32[]{:S(2)}, u32[]{:S(2)}) collective-permute-start(bf16[128,512]{1,0:T(8,128)(2,1)} %bitcast.22), channel_id=1, source_target_pairs={{0,4},{1,5},{2,6},{3,7},{4,0},{5,1},{6,2},{7,3},{8,12},{9,13},{10,... | collective-permute-start | bytes 393224 | tf_op jit(solution)/shard_map/ppermute | solution.py:474
  5.3 0.9 copy-start.5
  6.3 8.6 %collective-permute-start = (bf16[64,1024]{1,0:T(8,128)(2,1)S(1)}, bf16[64,1024]{1,0:T(8,128)(2,1)S(1)}, u32[]{:S(2)}, u32[]{:S(2)}) collective-permute-start(bf16[64,1024]{1,0:T(8,128)(2,1)S(1)} %get-tuple-element.37), channel_id=1, source_target_pairs={{0,4},{1,5},{2,6},{3,7},{4,0},{5,1},{6,2},{7,3},{8,12},{9,13},{10,... | collective-permute-start | bytes 393224 | tf_op jit(solution)/shard_map/ppermute | solution.py:474
  8.2 1.6 %copy-start = (bf16[1,128,8192]{2,1,0:T(8,128)(2,1)S(1)}, bf16[1,128,8192]{2,1,0:T(8,128)(2,1)}, u32[]{:S(2)}) copy-start(bf16[1,128,8192]{2,1,0:T(8,128)(2,1)} %param.8) | copy-start | bytes 6291460
  9.8 0.8 copy-start.6
  10.6 4.3 %copy-start.8 = (bf16[1,128,512]{2,1,0:T(8,128)(2,1)S(1)}, bf16[1,128,512]{2,1,0:T(8,128)(2,1)}, u32[]{:S(2)}) copy-start(bf16[1,128,512]{2,1,0:T(8,128)(2,1)} %param.11) | copy-start | bytes 393220
  12.3 18.8 %copy-start.9 = (s32[512]{0:T(512)S(1)}, s32[512]{0:T(512)}, u32[]{:S(2)}) copy-start(s32[512]{0:T(512)} %param.12) | copy-start | bytes 6148
  15.0 13.4 %collective-permute-start.8 = (bf16[128,1024]{1,0:T(8,128)(2,1)S(1)}, bf16[128,1024]{1,0:T(8,128)(2,1)S(1)}, u32[]{:S(2)}, u32[]{:S(2)}) collective-permute-start(bf16[128,1024]{1,0:T(8,128)(2,1)S(1)} %get-tuple-element.43.refs_7_.refs_4_.refs_0_), channel_id=1, source_target_pairs={{0,8},{1,9},{2,10},{3,11},{4,12},{5,13},{6,14},{7,15},{8,0},{9,1},... | collective-permute-start | bytes 786440 | tf_op jit(solution)/shard_map/ppermute | solution.py:474
  16.6 14.2 %collective-permute-start.9 = (bf16[128,1024]{1,0:T(8,128)(2,1)S(1)}, bf16[128,1024]{1,0:T(8,128)(2,1)S(1)}, u32[]{:S(2)}, u32[]{:S(2)}) collective-permute-start(bf16[128,1024]{1,0:T(8,128)(2,1)S(1)} %get-tuple-element.43.refs_7_.refs_4_.refs_0_), channel_id=1, source_target_pairs={{0,16},{1,17},{2,18},{3,19},{4,20},{5,21},{6,22},{7,23},{8,24},{9,... | collective-permute-start | bytes 786440 | tf_op jit(solution)/shard_map/ppermute | solution.py:474
  19.2 24.6 %collective-permute-start.5 = (bf16[2,128,1024]{2,1,0:T(8,128)(2,1)S(1)}, bf16[2,128,1024]{2,1,0:T(8,128)(2,1)S(1)}, u32[]{:S(2)}, u32[]{:S(2)}) collective-permute-start(bf16[2,128,1024]{2,1,0:T(8,128)(2,1)S(1)} %get-tuple-element.40), channel_id=1, source_target_pairs={{0,4},{1,5},{2,6},{3,7},{4,0},{5,1},{6,2},{7,3},{8,12},{9,13},{10,... | collective-permute-start | bytes 1572872 | tf_op jit(solution)/shard_map/ppermute | solution.py:474
  20.7 23.9 %collective-permute-start.6 = (bf16[2,128,1024]{2,1,0:T(8,128)(2,1)S(1)}, bf16[2,128,1024]{2,1,0:T(8,128)(2,1)S(1)}, u32[]{:S(2)}, u32[]{:S(2)}) collective-permute-start(bf16[2,128,1024]{2,1,0:T(8,128)(2,1)S(1)} %get-tuple-element.41), channel_id=1, source_target_pairs={{0,2},{1,3},{2,0},{3,1},{4,6},{5,7},{6,4},{7,5},{8,10},{9,11},{10,... | collective-permute-start | bytes 1572872 | tf_op jit(solution)/shard_map/ppermute | solution.py:474
  21.2 23.4 %collective-permute-start.7 = (bf16[2,128,1024]{2,1,0:T(8,128)(2,1)S(1)}, bf16[2,128,1024]{2,1,0:T(8,128)(2,1)S(1)}, u32[]{:S(2)}, u32[]{:S(2)}) collective-permute-start(bf16[2,128,1024]{2,1,0:T(8,128)(2,1)S(1)} %get-tuple-element.42), channel_id=1, source_target_pairs={{0,6},{1,7},{2,4},{3,5},{4,2},{5,3},{6,0},{7,1},{8,14},{9,15},{10,... | collective-permute-start | bytes 1572872 | tf_op jit(solution)/shard_map/ppermute | solution.py:474
  28.4 16.1 %collective-permute-start.11 = (bf16[512,512]{1,0:T(8,128)(2,1)S(1)}, bf16[512,512]{1,0:T(8,128)(2,1)S(1)}, u32[]{:S(2)}, u32[]{:S(2)}) collective-permute-start(bf16[512,512]{1,0:T(8,128)(2,1)S(1)} %late.1), channel_id=1, source_target_pairs={{0,1},{1,0},{2,3},{3,2},{4,5},{5,4},{6,7},{7,6},{8,9},{9,8},{10,11... | collective-permute-start | bytes 1572872 | tf_op jit(solution)/shard_map/ppermute | solution.py:474
  30.8 13.0 %collective-permute-start.10 = (bf16[128,1024]{1,0:T(8,128)(2,1)S(1)}, bf16[128,1024]{1,0:T(8,128)(2,1)S(1)}, u32[]{:S(2)}, u32[]{:S(2)}) collective-permute-start(bf16[128,1024]{1,0:T(8,128)(2,1)S(1)} %collective-permute-done.8.refs_0_.refs_8_.refs_5_.refs_1_), channel_id=1, source_target_pairs={{0,16},{1,17},{2,18},{3,19},{4,20},{5,21},{6,22},{7,23},{8,24},{9,... | collective-permute-start | bytes 786440 | tf_op jit(solution)/shard_map/ppermute | solution.py:474
  43.7 9.8 %collective-permute-start.14 = (bf16[128,1024]{1,0:T(8,128)(2,1)S(1)}, bf16[128,1024]{1,0:T(8,128)(2,1)S(1)}, u32[]{:S(2)}, u32[]{:S(2)}) collective-permute-start(bf16[128,1024]{1,0:T(8,128)(2,1)S(1)} %get-tuple-element.43.refs_7_.refs_4_.refs_0_), channel_id=1, source_target_pairs={{0,1},{1,0},{2,3},{3,2},{4,5},{5,4},{6,7},{7,6},{8,9},{9,8},{10,11... | collective-permute-start | bytes 786440 | tf_op jit(solution)/shard_map/ppermute | solution.py:474
  43.7 10.0 %collective-permute-start.16 = (bf16[128,1024]{1,0:T(8,128)(2,1)S(1)}, bf16[128,1024]{1,0:T(8,128)(2,1)S(1)}, u32[]{:S(2)}, u32[]{:S(2)}) collective-permute-start(bf16[128,1024]{1,0:T(8,128)(2,1)S(1)} %collective-permute-done.9.refs_9_.refs_6_.refs_2_), channel_id=1, source_target_pairs={{0,1},{1,0},{2,3},{3,2},{4,5},{5,4},{6,7},{7,6},{8,9},{9,8},{10,11... | collective-permute-start | bytes 786440 | tf_op jit(solution)/shard_map/ppermute | solution.py:474
  47.6 13.0 %collective-permute-start.21 = (bf16[256,1024]{1,0:T(8,128)(2,1)S(1)}, bf16[256,1024]{1,0:T(8,128)(2,1)S(1)}, u32[]{:S(2)}, u32[]{:S(2)}) collective-permute-start(bf16[256,1024]{1,0:T(8,128)(2,1)S(1)} %get-tuple-element.44.refs_8_), channel_id=1, source_target_pairs={{0,8},{1,9},{2,10},{3,11},{4,12},{5,13},{6,14},{7,15},{24,16},{25,... | collective-permute-start | bytes 1572872 | tf_op jit(solution)/shard_map/ppermute | solution.py:474
  50.0 4.2 %collective-permute-start.15 = (bf16[128,1024]{1,0:T(8,128)(2,1)S(1)}, bf16[128,1024]{1,0:T(8,128)(2,1)S(1)}, u32[]{:S(2)}, u32[]{:S(2)}) collective-permute-start(bf16[128,1024]{1,0:T(8,128)(2,1)S(1)} %collective-permute-done.8.refs_0_.refs_8_.refs_5_.refs_1_), channel_id=1, source_target_pairs={{0,1},{1,0},{2,3},{3,2},{4,5},{5,4},{6,7},{7,6},{8,9},{9,8},{10,11... | collective-permute-start | bytes 786440 | tf_op jit(solution)/shard_map/ppermute | solution.py:474
  50.1 4.1 %collective-permute-start.17 = (bf16[128,1024]{1,0:T(8,128)(2,1)S(1)}, bf16[128,1024]{1,0:T(8,128)(2,1)S(1)}, u32[]{:S(2)}, u32[]{:S(2)}) collective-permute-start(bf16[128,1024]{1,0:T(8,128)(2,1)S(1)} %collective-permute-done.10.refs_10_.refs_7_.refs_3_), channel_id=1, source_target_pairs={{0,1},{1,0},{2,3},{3,2},{4,5},{5,4},{6,7},{7,6},{8,9},{9,8},{10,11... | collective-permute-start | bytes 786440 | tf_op jit(solution)/shard_map/ppermute | solution.py:474
  53.6 1.6 %collective-permute-start.12 = (bf16[256,512]{1,0:T(8,128)(2,1)S(1)}, bf16[256,512]{1,0:T(8,128)(2,1)S(1)}, u32[]{:S(2)}, u32[]{:S(2)}) collective-permute-start(bf16[256,512]{1,0:T(8,128)(2,1)S(1)} %get-tuple-element.46), channel_id=1, source_target_pairs={{0,1},{1,0},{2,3},{3,2},{4,5},{5,4},{6,7},{7,6},{8,9},{9,8},{10,11... | collective-permute-start | bytes 786440 | tf_op jit(solution)/shard_map/ppermute | solution.py:474
  53.7 1.8 %collective-permute-start.13 = (bf16[256,512]{1,0:T(8,128)(2,1)S(1)}, bf16[256,512]{1,0:T(8,128)(2,1)S(1)}, u32[]{:S(2)}, u32[]{:S(2)}) collective-permute-start(bf16[256,512]{1,0:T(8,128)(2,1)S(1)} %get-tuple-element.47), channel_id=1, source_target_pairs={{0,1},{1,0},{2,3},{3,2},{4,5},{5,4},{6,7},{7,6},{8,9},{9,8},{10,11... | collective-permute-start | bytes 786440 | tf_op jit(solution)/shard_map/ppermute | solution.py:474
  57.0 18.6 %collective-permute-start.20 = (bf16[128,2560]{1,0:T(8,128)(2,1)S(1)}, bf16[128,2560]{1,0:T(8,128)(2,1)S(1)}, u32[]{:S(2)}, u32[]{:S(2)}) collective-permute-start(bf16[128,2560]{1,0:T(8,128)(2,1)S(1)} %get-tuple-element.52), channel_id=1, source_target_pairs={{0,6},{1,7},{2,4},{3,5},{4,2},{5,3},{6,0},{7,1},{8,14},{9,15},{10,... | collective-permute-start | bytes 1966088 | tf_op jit(solution)/shard_map/ppermute | solution.py:474
  58.3 13.2 %collective-permute-start.23 = (bf16[256,1024]{1,0:T(8,128)(2,1)S(1)}, bf16[256,1024]{1,0:T(8,128)(2,1)S(1)}, u32[]{:S(2)}, u32[]{:S(2)}) collective-permute-start(bf16[256,1024]{1,0:T(8,128)(2,1)S(1)} %get-tuple-element.59), channel_id=1, source_target_pairs={{0,8},{1,9},{2,10},{3,11},{4,12},{5,13},{6,14},{7,15},{24,16},{25,... | collective-permute-start | bytes 1572872 | tf_op jit(solution)/shard_map/ppermute | solution.py:474
  60.7 14.9 %collective-permute-start.22 = (bf16[256,1024]{1,0:T(8,128)(2,1)S(1)}, bf16[256,1024]{1,0:T(8,128)(2,1)S(1)}, u32[]{:S(2)}, u32[]{:S(2)}) collective-permute-start(bf16[256,1024]{1,0:T(8,128)(2,1)S(1)} %relay.2), channel_id=1, source_target_pairs={{8,16},{9,17},{10,18},{11,19},{12,20},{13,21},{14,22},{15,23},{16,... | collective-permute-start | bytes 1572872 | tf_op jit(solution)/shard_map/ppermute | solution.py:474
  61.4 26.5 %collective-permute-start.18 = (bf16[128,2560]{1,0:T(8,128)(2,1)S(1)}, bf16[128,2560]{1,0:T(8,128)(2,1)S(1)}, u32[]{:S(2)}, u32[]{:S(2)}) collective-permute-start(bf16[128,2560]{1,0:T(8,128)(2,1)S(1)} %get-tuple-element.50), channel_id=1, source_target_pairs={{0,4},{1,5},{2,6},{3,7},{4,0},{5,1},{6,2},{7,3},{8,12},{9,13},{10,... | collective-permute-start | bytes 1966088 | tf_op jit(solution)/shard_map/ppermute | solution.py:474
  63.7 25.1 %collective-permute-start.19 = (bf16[128,2560]{1,0:T(8,128)(2,1)S(1)}, bf16[128,2560]{1,0:T(8,128)(2,1)S(1)}, u32[]{:S(2)}, u32[]{:S(2)}) collective-permute-start(bf16[128,2560]{1,0:T(8,128)(2,1)S(1)} %get-tuple-element.51), channel_id=1, source_target_pairs={{0,2},{1,3},{2,0},{3,1},{4,6},{5,7},{6,4},{7,5},{8,10},{9,11},{10,... | collective-permute-start | bytes 1966088 | tf_op jit(solution)/shard_map/ppermute | solution.py:474
  75.9 13.7 %copy-start.1 = (bf16[1,128,8192]{2,1,0:T(8,128)(2,1)S(1)}, bf16[1,128,8192]{2,1,0:T(8,128)(2,1)}, u32[]{:S(2)}) copy-start(bf16[1,128,8192]{2,1,0:T(8,128)(2,1)} %param.8) | copy-start | bytes 6291460
  75.9 13.7 %copy-start.7 = (f32[8192]{0:T(1024)S(1)}, f32[8192]{0:T(1024)}, u32[]{:S(2)}) copy-start(f32[8192]{0:T(1024)} %param.9) | copy-start | bytes 98308
  75.9 12.9 %collective-permute-start.24 = (bf16[256,1024]{1,0:T(8,128)(2,1)S(1)}, bf16[256,1024]{1,0:T(8,128)(2,1)S(1)}, u32[]{:S(2)}, u32[]{:S(2)}) collective-permute-start(bf16[256,1024]{1,0:T(8,128)(2,1)S(1)} %get-tuple-element.60), channel_id=1, source_target_pairs={{0,8},{1,9},{2,10},{3,11},{4,12},{5,13},{6,14},{7,15},{8,0},{9,1},... | collective-permute-start | bytes 1572872 | tf_op jit(solution)/shard_map/ppermute | solution.py:474
  76.9 12.0 %collective-permute-start.25 = (bf16[256,1024]{1,0:T(8,128)(2,1)S(1)}, bf16[256,1024]{1,0:T(8,128)(2,1)S(1)}, u32[]{:S(2)}, u32[]{:S(2)}) collective-permute-start(bf16[256,1024]{1,0:T(8,128)(2,1)S(1)} %get-tuple-element.61), channel_id=1, source_target_pairs={{8,16},{9,17},{10,18},{11,19},{12,20},{13,21},{14,22},{15,23},{16,... | collective-permute-start | bytes 1572872 | tf_op jit(solution)/shard_map/ppermute | solution.py:474
  89.0 8.3 %collective-permute-start.26 = (bf16[128,1024]{1,0:T(8,128)(2,1)S(1)}, bf16[128,1024]{1,0:T(8,128)(2,1)S(1)}, u32[]{:S(2)}, u32[]{:S(2)}) collective-permute-start(bf16[128,1024]{1,0:T(8,128)(2,1)S(1)} %get-tuple-element.63), channel_id=1, source_target_pairs={{0,4},{1,5},{2,6},{3,7},{4,0},{5,1},{6,2},{7,3},{8,12},{9,13},{10,... | collective-permute-start | bytes 786440 | tf_op jit(solution)/shard_map/ppermute | solution.py:474
  89.6 7.7 %copy-start.2 = (f32[1,128,2048]{2,1,0:T(8,128)S(1)}, f32[1,128,2048]{2,1,0:T(8,128)}, u32[]{:S(2)}) copy-start(f32[1,128,2048]{2,1,0:T(8,128)} %param.13) | copy-start | bytes 3145732
  89.6 7.7 %copy-start.3 = (f32[1,128,2048]{2,1,0:T(8,128)S(1)}, f32[1,128,2048]{2,1,0:T(8,128)}, u32[]{:S(2)}) copy-start(f32[1,128,2048]{2,1,0:T(8,128)} %param.14) | copy-start | bytes 3145732
  89.6 7.7 %copy-start.4 = (f32[1,128,2048]{2,1,0:T(8,128)S(1)}, f32[1,128,2048]{2,1,0:T(8,128)}, u32[]{:S(2)}) copy-start(f32[1,128,2048]{2,1,0:T(8,128)} %param.15) | copy-start | bytes 3145732

commit v6 on v5

--- a/solution.py
+++ b/solution.py
@@ -68,21 +68,6 @@
     return [outs[i : i + parts] for i in range(0, len(outs), parts)]
 
 
-def late_kernel(a_ref, *refs):
-    refs[-1][...] = a_ref[...]
-
-
-def late(a, after):
-    return pl.pallas_call(
-        late_kernel,
-        in_specs=[pl.BlockSpec(memory_space=pltpu.VMEM)]
-        + [pl.BlockSpec(memory_space=pl.ANY)] * len(after),
-        out_shape=jax.ShapeDtypeStruct(a.shape, a.dtype),
-        compiler_params=limit(16),
-        name="late",
-    )(a, *after)
-
-
 def halves_kernel(w_ref, keep_ref, send_ref):
     width = keep_ref.shape[1]
     own_x = lax.axis_index("dp") % 2
@@ -99,30 +84,25 @@
     )(w_t)
 
 
-def unpack_kernel(keep_ref, got_ref, *refs):
-    plane_ref, grads_ref = refs[-2:]
-    share = keep_ref.shape[0]
+def stack_kernel(count, *refs):
+    out_refs = refs[-(len(refs) - count) :]
     rows = refs[0].shape[0]
-    plane_ref[:share, :] = keep_ref[...]
-    plane_ref[share:, :] = got_ref[...]
-    for k in range(grads_ref.shape[0] // rows):
-        grads_ref[k * rows : (k + 1) * rows, :] = refs[k][...]
-
-
-def unpack(keep, got, grads, after):
-    share, width = keep.shape
-    rows, feats = grads[0].shape
-    return pl.pallas_call(
-        unpack_kernel,
-        in_specs=[pl.BlockSpec(memory_space=pltpu.VMEM)] * (2 + len(grads))
+    each = out_refs[0].shape[0] // rows
+    for i, ref in enumerate(refs[:count]):
+        out_refs[i // each][i % each * rows : (i % each + 1) * rows, :] = ref[...]
+
+
+def stack(pieces, outs, after):
+    count = len(pieces)
+    rows, width = pieces[0].shape
+    return pl.pallas_call(
+        lambda *refs: stack_kernel(count, *refs[:count], *refs[count + len(after) :]),
+        in_specs=[pl.BlockSpec(memory_space=pltpu.VMEM)] * count
         + [pl.BlockSpec(memory_space=pl.ANY)] * len(after),
-        out_shape=[
-            jax.ShapeDtypeStruct((2 * share, width), bf16),
-            jax.ShapeDtypeStruct((len(grads) * rows, feats), bf16),
-        ],
+        out_shape=[jax.ShapeDtypeStruct((count // outs * rows, width), bf16)] * outs,
         compiler_params=limit(16),
-        name="unpack",
-    )(keep, got, *grads, *after)
+        name="stack",
+    )(*pieces, *after)
 
 
 def select_kernel(groups, slots, owner_ref, *refs):
@@ -160,19 +140,21 @@
 
 def weight_kernel(planes, chips, plan, *refs):
     sel_ref, refs = refs[0], refs[1:]
-    grad_refs, refs = refs[:2], refs[2:]
+    grad_refs, refs = refs[:4], refs[4:]
     pieces, refs = refs[:chips], refs[chips:]
     out_refs, (held, base) = refs[-len(plan) - 3 : -2], refs[-2:]
     rows = pieces[0].shape[1]
     feats = sel_ref.shape[1]
     block = sel_ref.shape[0] // planes
+    half = chips // 2
     z = lax.axis_index("dp") // 2
     for k in range(chips):
         for i in range(2):
-            held[i, k * rows : (k + 1) * rows, :] = pieces[k][i]
+            at = k % half * rows
+            held[2 * i + k // half, at : at + rows, :] = pieces[k][i]
     for at in range(0, feats, 256):
         total = None
-        for i in range(2):
+        for i in range(4):
             term = lax.dot_general(
                 grad_refs[i][:, at : at + 256],
                 held[i],
@@ -205,11 +187,11 @@
     block = slots_all // planes
     return pl.pallas_call(
         functools.partial(weight_kernel, planes, chips, plan),
-        in_specs=[pl.BlockSpec(memory_space=pltpu.VMEM)] * (3 + chips)
+        in_specs=[pl.BlockSpec(memory_space=pltpu.VMEM)] * (5 + chips)
         + [pl.BlockSpec(memory_space=pl.ANY)] * len(after),
         out_shape=[jax.ShapeDtypeStruct((block, width), bf16)] * (len(plan) + 1),
         scratch_shapes=[
-            pltpu.VMEM((2, total // 2, width), bf16),
+            pltpu.VMEM((4, total // 4, width), bf16),
             pltpu.VMEM((feats, width), bf16),
         ],
         compiler_params=limit(40),
@@ -269,7 +251,7 @@
     )(*[p for piece in pieces for p in piece], *weights, *after)
 
 
-def back_kernel(planes, chips, grads_ref, value_ref, got_a_ref, got_b_ref, *refs):
+def back_kernel(planes, chips, grads_a_ref, grads_b_ref, value_ref, got_a_ref, got_b_ref, *refs):
     weight_refs, refs = refs[: 2 * planes], refs[2 * planes :]
     out_refs, own_ref, held = refs[-chips - 2 : -2], refs[-2], refs[-1]
     rows, feats = own_ref.shape
@@ -286,15 +268,16 @@
     for j in range(2):
         gather_weight(weight_refs[j * planes : (j + 1) * planes], held)
         for k in range(chips):
+            grads_ref = grads_b_ref if k // half else grads_a_ref
             out_refs[k][:, j * width : (j + 1) * width] = jnp.dot(
-                grads_ref[k * rows : (k + 1) * rows, :],
+                grads_ref[k % half * rows : (k % half + 1) * rows, :],
                 held[...],
                 preferred_element_type=f32,
             ).astype(bf16)
 
 
 def back_blocks(grads, sums, weights, chips):
-    rows, feats = grads.shape[0] // chips, grads.shape[1]
+    rows, feats = 2 * grads[0].shape[0] // chips, grads[0].shape[1]
     width = weights[0].shape[-1]
     return pl.pallas_call(
         functools.partial(back_kernel, len(weights) // 2, chips),
@@ -306,7 +289,7 @@
         scratch_shapes=[pltpu.VMEM((feats, width), bf16)],
         compiler_params=limit(40),
         name="back_blocks",
-    )(grads, *sums, *weights)
+    )(*grads, *sums, *weights)
 
 
 def grad_x_kernel(tok_ref, gain_ref, part_ref, *refs):
@@ -504,15 +487,17 @@
 
     gain_row, owner_row = gain[None, :], owner[None, :]
     sent = norm_blocks(tokens, tokens_far, gain_row, chips, width, parts)
-    w_plane, grads = unpack(w_keep, w_got, grads, (sent[0][0],))
+    grads = stack(grads, 2, sent[0][:1])
     pieces = [sent[0]] + [[to_chip(p, k) for p in sent[k]] for k in range(1, chips)]
+    grads_far = [to_core(g) for g in grads]
     selected = select_rows(owner_row, groups, slots, (sent[0][0],))
 
-    weights = [w_plane]
-    while len(weights) < planes:
-        weights += [to_plane(w, len(weights)) for w in weights]
+    weights = stack([w_keep, w_got], 1, grads[:1])
+    turn = planes // 2
+    while turn:
+        weights = [w for value in weights for w in (value, to_plane(value, turn))]
+        turn //= 2
     weights_far = [to_core(w) for w in weights]
-    grads_far = to_core(late(grads, weights[1:2]))
 
     plan = [
         (step, even)
@@ -524,11 +509,11 @@
     for part in range(parts):
         outs = weight_blocks(
             selected,
-            [grads, grads_far],
+            [*grads, *grads_far],
             [piece[part] for piece in pieces],
             planes,
             plan,
-            weights if part == parts - 1 else [],
+            weights[:1] if part == parts - 1 else [],
         )
         ready = dict(zip(plan, outs))
         if part == parts - 1:

time: 100 us -> 101 us (1.010)
  starting transfers between devices: 26.6 us -> 30.8 us
  waiting for transfers between devices: 52.7 us -> 49.1 us
    ppermute x27 -> x28, starting transfers between devices: 26.6 us -> 30.8 us  [permute(): return lax.ppermute(value, ('dp', 'seq'), pairs)]
    ppermute x27 -> x28, waiting for transfers between devices: 52.7 us -> 49.1 us  [permute(): return lax.ppermute(value, ('dp', 'seq'), pairs)]
  transfers between devices with their start and end apart: 27 -> 28, of which waited for: 14 -> 15; matrix products, arithmetic and copies ran while one was open for 0% -> 0% of each run, Pallas kernels for 14% -> 14%
where the time goes in v6:
time: 101 us
  waiting for transfers between devices  49.1 us (49%)
  starting transfers between devices  30.8 us (30%)
  Pallas kernels  16.4 us (16%)
  local copies, waits for them, and re-layouts  3.34 us (3%)
    ppermute x28, waiting for transfers between devices, permute(): return lax.ppermute(value, ('dp', 'seq'), pairs)  49.1 us
    ppermute x28, starting transfers between devices, permute(): return lax.ppermute(value, ('dp', 'seq'), pairs)  30.8 us
    pallas_call x1, Pallas kernels, grad_x_blocks(): pl.pallas_call(grad_x_kernel, grid=(rows // step,), in_specs=[pl.BlockSpe...  3.62 us
    unnamed x20, local copies, waits for them, and re-layouts  3.34 us
    pallas_call x1, Pallas kernels, weight_blocks(): pl.pallas_call(functools.partial(weight_kernel, planes, chips, plan), in_...  3.02 us
    pallas_call x1, Pallas kernels, value_parts(): pl.pallas_call(functools.partial(value_kernel, len(weights), chips, parts...  2.98 us
    pallas_call x1, Pallas kernels, adam(): pl.pallas_call(functools.partial(adam_kernel, token_total, len(kept)), gr...  2.6 us
  transfers between devices with their start and end apart: 28, of which 15 were waited for; matrix products, arithmetic and copies ran while one was open for 0% of the time, Pallas kernels for 14%

profile of v6, /device:TPU:0, one launch (start us, length us, event | category | flops | bytes accessed | tf_op | source)
XLA Modules:
  0.0 100.5 jit_solution(14004364839710504530)
XLA Ops:
  0.6 0.5 collective-permute-start.3
  1.1 3.5 %collective-permute-start.2 = (bf16[128,512]{1,0:T(8,128)(2,1)}, bf16[128,512]{1,0:T(8,128)(2,1)S(1)}, u32[]{:S(2)}, u32[]{:S(2)}) collective-permute-start(bf16[128,512]{1,0:T(8,128)(2,1)} %bitcast.20), channel_id=1, source_target_pairs={{0,6},{1,7},{2,4},{3,5},{4,2},{5,3},{6,0},{7,1},{8,14},{9,15},{10,... | collective-permute-start | bytes 393224 | tf_op jit(solution)/shard_map/ppermute | solution.py:457
  4.7 0.5 collective-permute-start.1
  5.2 0.1 collective-permute-start
  5.3 0.9 copy-done.5
  6.3 2.0 %collective-permute-start.7 = (bf16[64,1024]{1,0:T(8,128)(2,1)S(1)}, bf16[64,1024]{1,0:T(8,128)(2,1)S(1)}, u32[]{:S(2)}, u32[]{:S(2)}) collective-permute-start(bf16[64,1024]{1,0:T(8,128)(2,1)S(1)} %get-tuple-element.43), channel_id=1, source_target_pairs={{0,4},{1,5},{2,6},{3,7},{4,0},{5,1},{6,2},{7,3},{8,12},{9,13},{10,... | collective-permute-start | bytes 393224 | tf_op jit(solution)/shard_map/ppermute | solution.py:457
  8.2 1.6 %copy-done = bf16[1,128,8192]{2,1,0:T(8,128)(2,1)S(1)} copy-done((bf16[1,128,8192]{2,1,0:T(8,128)(2,1)S(1)}, bf16[1,128,8192]{2,1,0:T(8,128)(2,1)}, u32[]{:S(2)}) %copy-start) | copy-done | bytes 2097176
  9.8 0.8 copy-done.6
  10.6 1.7 %norm_blocks.1 = (bf16[2,128,1024]{2,1,0:T(8,128)(2,1)S(1)}, bf16[2,128,1024]{2,1,0:T(8,128)(2,1)S(1)}, bf16[2,128,1024]{2,1,0:T(8,128)(2,1)S(1)}, bf16[2,128,1024]{2,1,0:T(8,128)(2,1)S(1)}) custom-call(bf16[128,8192]{1,0:T(8,128)(2,1)S(1)} %bitcast.13, bf16[128,8192]{1,0:T(8,128)(2,1)S(1)} %collective-permute-done.3.far_ref, f32[1,8192]{1,0:T(1,128)S(1)} %bitcast.18), custom_call_target="tpu_custom_call" | custom-call | flops 8388608 | bytes 6291456 | tf_op jit(solution)/shard_map/norm_blocks/pallas_call | solution.py:54
  12.3 0.3 collective-permute-done.refs_1_
  12.6 2.3 %collective-permute-done.7.refs_1_ = bf16[64,1024]{1,0:T(8,128)(2,1)S(1)} collective-permute-done((bf16[64,1024]{1,0:T(8,128)(2,1)S(1)}, bf16[64,1024]{1,0:T(8,128)(2,1)S(1)}, u32[]{:S(2)}, u32[]{:S(2)}) %collective-permute-start.7) | collective-permute-done | bytes 131104 | tf_op jit(solution)/shard_map/ppermute | solution.py:457
  14.9 2.7 %collective-permute-start.9 = (bf16[128,1024]{1,0:T(8,128)(2,1)S(1)}, bf16[128,1024]{1,0:T(8,128)(2,1)S(1)}, u32[]{:S(2)}, u32[]{:S(2)}) collective-permute-start(bf16[128,1024]{1,0:T(8,128)(2,1)S(1)} %stack.3.refs_9_.refs_4_.refs_0_), channel_id=1, source_target_pairs={{0,16},{1,17},{2,18},{3,19},{4,20},{5,21},{6,22},{7,23},{8,24},{9,... | collective-permute-start | bytes 786440 | tf_op jit(solution)/shard_map/ppermute | solution.py:457
  17.6 1.5 %collective-permute-start.4 = (bf16[2,128,1024]{2,1,0:T(8,128)(2,1)S(1)}, bf16[2,128,1024]{2,1,0:T(8,128)(2,1)S(1)}, u32[]{:S(2)}, u32[]{:S(2)}) collective-permute-start(bf16[2,128,1024]{2,1,0:T(8,128)(2,1)S(1)} %get-tuple-element.39), channel_id=1, source_target_pairs={{0,4},{1,5},{2,6},{3,7},{4,0},{5,1},{6,2},{7,3},{8,12},{9,13},{10,... | collective-permute-start | bytes 1572872 | tf_op jit(solution)/shard_map/ppermute | solution.py:457
  19.1 0.5 collective-permute-start.5
  19.6 1.5 %collective-permute-start.6 = (bf16[2,128,1024]{2,1,0:T(8,128)(2,1)S(1)}, bf16[2,128,1024]{2,1,0:T(8,128)(2,1)S(1)}, u32[]{:S(2)}, u32[]{:S(2)}) collective-permute-start(bf16[2,128,1024]{2,1,0:T(8,128)(2,1)S(1)} %get-tuple-element.41), channel_id=1, source_target_pairs={{0,6},{1,7},{2,4},{3,5},{4,2},{5,3},{6,0},{7,1},{8,14},{9,15},{10,... | collective-permute-start | bytes 1572872 | tf_op jit(solution)/shard_map/ppermute | solution.py:457
  21.1 8.3 %collective-permute-done.9.refs_6_.refs_2_ = bf16[128,1024]{1,0:T(8,128)(2,1)S(1)} collective-permute-done((bf16[128,1024]{1,0:T(8,128)(2,1)S(1)}, bf16[128,1024]{1,0:T(8,128)(2,1)S(1)}, u32[]{:S(2)}, u32[]{:S(2)}) %collective-permute-start.9) | collective-permute-done | bytes 262176 | tf_op jit(solution)/shard_map/ppermute | solution.py:457
  29.4 0.5 select_rows.1.refs_0_
  29.9 0.6 collective-permute-start.15
  30.4 0.5 collective-permute-done.11.refs_3_
  30.9 0.7 collective-permute-start.8
  31.6 0.9 collective-permute-done.4.refs_6_.refs_1_
  32.4 10.8 %collective-permute-done.5.refs_7_.refs_2_ = bf16[2,128,1024]{2,1,0:T(8,128)(2,1)S(1)} collective-permute-done((bf16[2,128,1024]{2,1,0:T(8,128)(2,1)S(1)}, bf16[2,128,1024]{2,1,0:T(8,128)(2,1)S(1)}, u32[]{:S(2)}, u32[]{:S(2)}) %collective-permute-start.5) | collective-permute-done | bytes 524320 | tf_op jit(solution)/shard_map/ppermute | solution.py:457
  43.2 1.6 %collective-permute-start.10 = (bf16[128,1024]{1,0:T(8,128)(2,1)S(1)}, bf16[128,1024]{1,0:T(8,128)(2,1)S(1)}, u32[]{:S(2)}, u32[]{:S(2)}) collective-permute-start(bf16[128,1024]{1,0:T(8,128)(2,1)S(1)} %collective-permute-done.9.refs_6_.refs_2_), channel_id=1, source_target_pairs={{0,8},{1,9},{2,10},{3,11},{4,12},{5,13},{6,14},{7,15},{8,0},{9,1},... | collective-permute-start | bytes 786440 | tf_op jit(solution)/shard_map/ppermute | solution.py:457
  44.8 3.0 %weight_blocks.1 = (bf16[256,1024]{1,0:T(8,128)(2,1)S(1)}, bf16[256,1024]{1,0:T(8,128)(2,1)S(1)}, bf16[256,1024]{1,0:T(8,128)(2,1)S(1)}, bf16[256,1024]{1,0:T(8,...) custom-call(bf16[1024,512]{1,0:T(8,128)(2,1)S(1)} %select_rows.1.refs_0_, ...), custom_call_target="tpu_custom_call" | custom-call | flops 2147483648 | bytes 4194304 | tf_op jit(solution)/shard_map/weight_blocks/pallas_call | solution.py:188
  47.8 2.4 %collective-permute-start.22 = (bf16[256,1024]{1,0:T(8,128)(2,1)S(1)}, bf16[256,1024]{1,0:T(8,128)(2,1)S(1)}, u32[]{:S(2)}, u32[]{:S(2)}) collective-permute-start(bf16[256,1024]{1,0:T(8,128)(2,1)S(1)} %get-tuple-element.44.refs_8_), channel_id=1, source_target_pairs={{0,8},{1,9},{2,10},{3,11},{4,12},{5,13},{6,14},{7,15},{24,16},{25,... | collective-permute-start | bytes 1572872 | tf_op jit(solution)/shard_map/ppermute | solution.py:457
  50.3 0.5 collective-permute-done.10.refs_7_.refs_3_
  50.8 3.0 %value_parts.1 = (bf16[256,512]{1,0:T(8,128)(2,1)S(1)}, bf16[256,512]{1,0:T(8,128)(2,1)S(1)}, f32[512,512]{1,0:T(8,128)S(1)}) custom-call(bf16[2,128,1024]{2,1,0:T(8,128)(2,1)S(1)} %get-tuple-element.36.refs_4_.refs_0_.refs_5_, bf16[2,128,1024]{2,1,0:T(8,128)(2,1)S(1)} %collective-permute-done.4.refs_6_.refs_1_, ...), custom_call_target="tpu_custom_call" | custom-call | tf_op jit(solution)/shard_map/value_parts/pallas_call | solution.py:242
  53.8 0.6 collective-permute-start.13
  54.5 1.1 %collective-permute-done.13.got_a_ref = bf16[256,512]{1,0:T(8,128)(2,1)S(1)} collective-permute-done((bf16[256,512]{1,0:T(8,128)(2,1)S(1)}, bf16[256,512]{1,0:T(8,128)(2,1)S(1)}, u32[]{:S(2)}, u32[]{:S(2)}) %collective-permute-start.13) | collective-permute-done | bytes 262176 | tf_op jit(solution)/shard_map/ppermute | solution.py:457
  55.6 0.4 collective-permute-done.14.got_b_ref
  55.9 1.5 %back_blocks.1 = (bf16[128,2048]{1,0:T(8,128)(2,1)S(1)}, bf16[128,2560]{1,0:T(8,128)(2,1)S(1)}, bf16[128,2560]{1,0:T(8,128)(2,1)S(1)}, bf16[128,2560]{1,0:T(8,128)(2,1)S(1)}, f32[128,512]{1,0:T(8,128)S(1)}) custom-call(bf16[256,512]{1,0:T(8,128)(2,1)S(1)} %get-tuple-element.37.refs_2_.refs_1_.grads_a_ref, ...), custom_call_target="tpu_custom_call" | custom-call | tf_op jit(solution)/shard_map/back_blocks/pallas_call | solution.py:282
  57.4 0.7 collective-permute-start.21
  58.1 3.8 %collective-permute-start.24 = (bf16[256,1024]{1,0:T(8,128)(2,1)S(1)}, bf16[256,1024]{1,0:T(8,128)(2,1)S(1)}, u32[]{:S(2)}, u32[]{:S(2)}) collective-permute-start(bf16[256,1024]{1,0:T(8,128)(2,1)S(1)} %get-tuple-element.59), channel_id=1, source_target_pairs={{0,8},{1,9},{2,10},{3,11},{4,12},{5,13},{6,14},{7,15},{24,16},{25,... | collective-permute-start | bytes 1572872 | tf_op jit(solution)/shard_map/ppermute | solution.py:457
  62.1 0.7 collective-permute-start.23
  62.8 0.4 collective-permute-start.19
  63.2 3.1 %collective-permute-start.20 = (bf16[128,2560]{1,0:T(8,128)(2,1)S(1)}, bf16[128,2560]{1,0:T(8,128)(2,1)S(1)}, u32[]{:S(2)}, u32[]{:S(2)}) collective-permute-start(bf16[128,2560]{1,0:T(8,128)(2,1)S(1)} %get-tuple-element.51), channel_id=1, source_target_pairs={{0,2},{1,3},{2,0},{3,1},{4,6},{5,7},{6,4},{7,5},{8,10},{9,11},{10,... | collective-permute-start | bytes 1966088 | tf_op jit(solution)/shard_map/ppermute | solution.py:457
  66.3 7.3 %collective-permute-done.24.refs_3_ = bf16[256,1024]{1,0:T(8,128)(2,1)S(1)} collective-permute-done((bf16[256,1024]{1,0:T(8,128)(2,1)S(1)}, bf16[256,1024]{1,0:T(8,128)(2,1)S(1)}, u32[]{:S(2)}, u32[]{:S(2)}) %collective-permute-start.24) | collective-permute-done | bytes 524320 | tf_op jit(solution)/shard_map/ppermute | solution.py:457
  73.6 2.4 %collective-permute-done.21.refs_3_.refs_4_.refs_2_ = bf16[128,2560]{1,0:T(8,128)(2,1)S(1)} collective-permute-done((bf16[128,2560]{1,0:T(8,128)(2,1)S(1)}, bf16[128,2560]{1,0:T(8,128)(2,1)S(1)}, u32[]{:S(2)}, u32[]{:S(2)}) %collective-permute-start.21) | collective-permute-done | bytes 655392 | tf_op jit(solution)/shard_map/ppermute | solution.py:457
  76.0 0.2 relay.3
  76.3 2.5 %collective-permute-start.25 = (bf16[256,1024]{1,0:T(8,128)(2,1)S(1)}, bf16[256,1024]{1,0:T(8,128)(2,1)S(1)}, u32[]{:S(2)}, u32[]{:S(2)}) collective-permute-start(bf16[256,1024]{1,0:T(8,128)(2,1)S(1)} %get-tuple-element.60), channel_id=1, source_target_pairs={{0,8},{1,9},{2,10},{3,11},{4,12},{5,13},{6,14},{7,15},{8,0},{9,1},... | collective-permute-start | bytes 1572872 | tf_op jit(solution)/shard_map/ppermute | solution.py:457
  78.8 0.7 collective-permute-start.26
  79.5 8.7 %collective-permute-done.19.refs_1_.refs_0_ = bf16[128,2560]{1,0:T(8,128)(2,1)S(1)} collective-permute-done((bf16[128,2560]{1,0:T(8,128)(2,1)S(1)}, bf16[128,2560]{1,0:T(8,128)(2,1)S(1)}, u32[]{:S(2)}, u32[]{:S(2)}) %collective-permute-start.19) | collective-permute-done | bytes 655392 | tf_op jit(solution)/shard_map/ppermute | solution.py:457
  88.2 1.3 %collective-permute-done.20.refs_2_.refs_1_ = bf16[128,2560]{1,0:T(8,128)(2,1)S(1)} collective-permute-done((bf16[128,2560]{1,0:T(8,128)(2,1)S(1)}, bf16[128,2560]{1,0:T(8,128)(2,1)S(1)}, u32[]{:S(2)}, u32[]{:S(2)}) %collective-permute-start.20) | collective-permute-done | bytes 655392 | tf_op jit(solution)/shard_map/ppermute | solution.py:457
  89.4 0.4 collective-permute-done.25.even_ref
  89.9 0.2 finish.1
  90.2 3.6 %grad_x_blocks.1 = (bf16[128,8192]{1,0:T(8,128)(2,1)}, bf16[128,512]{1,0:T(8,128)(2,1)}) custom-call(bf16[128,8192]{1,0:T(8,128)(2,1)S(1)} %bitcast.14, f32[1,8192]{1,0:T(1,128)S(1)} %bitcast.19, f32[128,512]{1,0:T(8,128)S(1)} %get-tuple-element.48.part_ref, bf16[128,2048]{1,0:T(8,128)(2,1)S(1)} %get-tuple-element.49.refs_0_.refs_2_, ...), custom_call_target="tpu_custom_call" | custom-call | flops 16777216 | bytes 6291456 | tf_op jit(solution)/shard_map/grad_x_blocks/pallas_call | solution.py:325
  93.8 4.1 %collective-permute-done.27.refs_1_ = bf16[128,1024]{1,0:T(8,128)(2,1)S(1)} collective-permute-done((bf16[128,1024]{1,0:T(8,128)(2,1)S(1)}, bf16[128,1024]{1,0:T(8,128)(2,1)S(1)}, u32[]{:S(2)}, u32[]{:S(2)}) %collective-permute-start.27) | collective-permute-done | bytes 262176 | tf_op jit(solution)/shard_map/ppermute | solution.py:457
  97.9 2.6 %adam.1 = (f32[128,2048]{1,0:T(8,128)}, f32[128,2048]{1,0:T(8,128)}, f32[128,2048]{1,0:T(8,128)}) custom-call(s32[1,512]{1,0:T(1,128)S(1)} %bitcast.25, f32[128,1024]{1,0:T(8,128)S(1)} %get-tuple-element.62.refs_0_, bf16[128,1024]{1,0:T(8,128)(2,1)S(1)} %collective-permute-done.27.refs_1_, f32[128,2048]{1,0:T(8,128)S(1)} %bitcast.15, ...), custom_call_target="tpu_custom_call" | custom-call | flops 5242880 | bytes 7864320 | tf_op jit(solution)/shard_map/adam/pallas_call | solution.py:425
  (41 shorter events, 0.5 us)
Async XLA Ops:
  0.6 7.6 %collective-permute-start.3 = (bf16[128,8192]{1,0:T(8,128)(2,1)}, bf16[128,8192]{1,0:T(8,128)(2,1)S(1)}, u32[]{:S(2)}, u32[]{:S(2)}) collective-permute-start(bf16[128,8192]{1,0:T(8,128)(2,1)} %bitcast.12), channel_id=1, source_target_pairs={{0,1},{1,0},{2,3},{3,2},{4,5},{5,4},{6,7},{7,6},{8,9},{9,8},{10,11... | collective-permute-start | bytes 6291464 | tf_op jit(solution)/shard_map/ppermute | solution.py:457
  1.1 11.1 %collective-permute-start.2 = (bf16[128,512]{1,0:T(8,128)(2,1)}, bf16[128,512]{1,0:T(8,128)(2,1)S(1)}, u32[]{:S(2)}, u32[]{:S(2)}) collective-permute-start(bf16[128,512]{1,0:T(8,128)(2,1)} %bitcast.20), channel_id=1, source_target_pairs={{0,6},{1,7},{2,4},{3,5},{4,2},{5,3},{6,0},{7,1},{8,14},{9,15},{10,... | collective-permute-start | bytes 393224 | tf_op jit(solution)/shard_map/ppermute | solution.py:457
  4.7 7.6 %collective-permute-start.1 = (bf16[128,512]{1,0:T(8,128)(2,1)}, bf16[128,512]{1,0:T(8,128)(2,1)S(1)}, u32[]{:S(2)}, u32[]{:S(2)}) collective-permute-start(bf16[128,512]{1,0:T(8,128)(2,1)} %bitcast.21), channel_id=1, source_target_pairs={{0,2},{1,3},{2,0},{3,1},{4,6},{5,7},{6,4},{7,5},{8,10},{9,11},{10,... | collective-permute-start | bytes 393224 | tf_op jit(solution)/shard_map/ppermute | solution.py:457
  5.2 7.4 %collective-permute-start = (bf16[128,512]{1,0:T(8,128)(2,1)}, bf16[128,512]{1,0:T(8,128)(2,1)S(1)}, u32[]{:S(2)}, u32[]{:S(2)}) collective-permute-start(bf16[128,512]{1,0:T(8,128)(2,1)} %bitcast.22), channel_id=1, source_target_pairs={{0,4},{1,5},{2,6},{3,7},{4,0},{5,1},{6,2},{7,3},{8,12},{9,13},{10,... | collective-permute-start | bytes 393224 | tf_op jit(solution)/shard_map/ppermute | solution.py:457
  5.3 0.9 copy-start.5
  6.3 8.6 %collective-permute-start.7 = (bf16[64,1024]{1,0:T(8,128)(2,1)S(1)}, bf16[64,1024]{1,0:T(8,128)(2,1)S(1)}, u32[]{:S(2)}, u32[]{:S(2)}) collective-permute-start(bf16[64,1024]{1,0:T(8,128)(2,1)S(1)} %get-tuple-element.43), channel_id=1, source_target_pairs={{0,4},{1,5},{2,6},{3,7},{4,0},{5,1},{6,2},{7,3},{8,12},{9,13},{10,... | collective-permute-start | bytes 393224 | tf_op jit(solution)/shard_map/ppermute | solution.py:457
  8.2 1.6 %copy-start = (bf16[1,128,8192]{2,1,0:T(8,128)(2,1)S(1)}, bf16[1,128,8192]{2,1,0:T(8,128)(2,1)}, u32[]{:S(2)}) copy-start(bf16[1,128,8192]{2,1,0:T(8,128)(2,1)} %param.8) | copy-start | bytes 6291460
  9.8 0.8 copy-start.6
  10.6 1.9 %copy-start.8 = (bf16[1,128,512]{2,1,0:T(8,128)(2,1)S(1)}, bf16[1,128,512]{2,1,0:T(8,128)(2,1)}, u32[]{:S(2)}) copy-start(bf16[1,128,512]{2,1,0:T(8,128)(2,1)} %param.11) | copy-start | bytes 393220
  10.6 18.8 %copy-start.9 = (s32[512]{0:T(512)S(1)}, s32[512]{0:T(512)}, u32[]{:S(2)}) copy-start(s32[512]{0:T(512)} %param.12) | copy-start | bytes 6148
  14.9 14.5 %collective-permute-start.9 = (bf16[128,1024]{1,0:T(8,128)(2,1)S(1)}, bf16[128,1024]{1,0:T(8,128)(2,1)S(1)}, u32[]{:S(2)}, u32[]{:S(2)}) collective-permute-start(bf16[128,1024]{1,0:T(8,128)(2,1)S(1)} %stack.3.refs_9_.refs_4_.refs_0_), channel_id=1, source_target_pairs={{0,16},{1,17},{2,18},{3,19},{4,20},{5,21},{6,22},{7,23},{8,24},{9,... | collective-permute-start | bytes 786440 | tf_op jit(solution)/shard_map/ppermute | solution.py:457
  17.6 14.9 %collective-permute-start.4 = (bf16[2,128,1024]{2,1,0:T(8,128)(2,1)S(1)}, bf16[2,128,1024]{2,1,0:T(8,128)(2,1)S(1)}, u32[]{:S(2)}, u32[]{:S(2)}) collective-permute-start(bf16[2,128,1024]{2,1,0:T(8,128)(2,1)S(1)} %get-tuple-element.39), channel_id=1, source_target_pairs={{0,4},{1,5},{2,6},{3,7},{4,0},{5,1},{6,2},{7,3},{8,12},{9,13},{10,... | collective-permute-start | bytes 1572872 | tf_op jit(solution)/shard_map/ppermute | solution.py:457
  19.1 24.2 %collective-permute-start.5 = (bf16[2,128,1024]{2,1,0:T(8,128)(2,1)S(1)}, bf16[2,128,1024]{2,1,0:T(8,128)(2,1)S(1)}, u32[]{:S(2)}, u32[]{:S(2)}) collective-permute-start(bf16[2,128,1024]{2,1,0:T(8,128)(2,1)S(1)} %get-tuple-element.40), channel_id=1, source_target_pairs={{0,2},{1,3},{2,0},{3,1},{4,6},{5,7},{6,4},{7,5},{8,10},{9,11},{10,... | collective-permute-start | bytes 1572872 | tf_op jit(solution)/shard_map/ppermute | solution.py:457
  19.6 25.2 %collective-permute-start.6 = (bf16[2,128,1024]{2,1,0:T(8,128)(2,1)S(1)}, bf16[2,128,1024]{2,1,0:T(8,128)(2,1)S(1)}, u32[]{:S(2)}, u32[]{:S(2)}) collective-permute-start(bf16[2,128,1024]{2,1,0:T(8,128)(2,1)S(1)} %get-tuple-element.41), channel_id=1, source_target_pairs={{0,6},{1,7},{2,4},{3,5},{4,2},{5,3},{6,0},{7,1},{8,14},{9,15},{10,... | collective-permute-start | bytes 1572872 | tf_op jit(solution)/shard_map/ppermute | solution.py:457
  21.1 8.8 %collective-permute-start.12 = (bf16[256,512]{1,0:T(8,128)(2,1)S(1)}, bf16[256,512]{1,0:T(8,128)(2,1)S(1)}, u32[]{:S(2)}, u32[]{:S(2)}) collective-permute-start(bf16[256,512]{1,0:T(8,128)(2,1)S(1)} %get-tuple-element.38.refs_2_.grads_b_ref), channel_id=1, source_target_pairs={{0,1},{1,0},{2,3},{3,2},{4,5},{5,4},{6,7},{7,6},{8,9},{9,8},{10,11... | collective-permute-start | bytes 786440 | tf_op jit(solution)/shard_map/ppermute | solution.py:457
  29.4 1.5 %collective-permute-start.11 = (bf16[256,512]{1,0:T(8,128)(2,1)S(1)}, bf16[256,512]{1,0:T(8,128)(2,1)S(1)}, u32[]{:S(2)}, u32[]{:S(2)}) collective-permute-start(bf16[256,512]{1,0:T(8,128)(2,1)S(1)} %get-tuple-element.37.refs_2_.refs_1_.grads_a_ref), channel_id=1, source_target_pairs={{0,1},{1,0},{2,3},{3,2},{4,5},{5,4},{6,7},{7,6},{8,9},{9,8},{10,11... | collective-permute-start | bytes 786440 | tf_op jit(solution)/shard_map/ppermute | solution.py:457
  29.9 24.0 %collective-permute-start.15 = (bf16[128,1024]{1,0:T(8,128)(2,1)S(1)}, bf16[128,1024]{1,0:T(8,128)(2,1)S(1)}, u32[]{:S(2)}, u32[]{:S(2)}) collective-permute-start(bf16[128,1024]{1,0:T(8,128)(2,1)S(1)} %stack.3.refs_9_.refs_4_.refs_0_), channel_id=1, source_target_pairs={{0,1},{1,0},{2,3},{3,2},{4,5},{5,4},{6,7},{7,6},{8,9},{9,8},{10,11... | collective-permute-start | bytes 786440 | tf_op jit(solution)/shard_map/ppermute | solution.py:457
  30.9 19.3 %collective-permute-start.8 = (bf16[128,1024]{1,0:T(8,128)(2,1)S(1)}, bf16[128,1024]{1,0:T(8,128)(2,1)S(1)}, u32[]{:S(2)}, u32[]{:S(2)}) collective-permute-start(bf16[128,1024]{1,0:T(8,128)(2,1)S(1)} %stack.3.refs_9_.refs_4_.refs_0_), channel_id=1, source_target_pairs={{0,8},{1,9},{2,10},{3,11},{4,12},{5,13},{6,14},{7,15},{8,0},{9,1},... | collective-permute-start | bytes 786440 | tf_op jit(solution)/shard_map/ppermute | solution.py:457
  32.4 22.0 %collective-permute-start.17 = (bf16[128,1024]{1,0:T(8,128)(2,1)S(1)}, bf16[128,1024]{1,0:T(8,128)(2,1)S(1)}, u32[]{:S(2)}, u32[]{:S(2)}) collective-permute-start(bf16[128,1024]{1,0:T(8,128)(2,1)S(1)} %collective-permute-done.9.refs_6_.refs_2_), channel_id=1, source_target_pairs={{0,1},{1,0},{2,3},{3,2},{4,5},{5,4},{6,7},{7,6},{8,9},{9,8},{10,11... | collective-permute-start | bytes 786440 | tf_op jit(solution)/shard_map/ppermute | solution.py:457
  43.2 7.6 %collective-permute-start.10 = (bf16[128,1024]{1,0:T(8,128)(2,1)S(1)}, bf16[128,1024]{1,0:T(8,128)(2,1)S(1)}, u32[]{:S(2)}, u32[]{:S(2)}) collective-permute-start(bf16[128,1024]{1,0:T(8,128)(2,1)S(1)} %collective-permute-done.9.refs_6_.refs_2_), channel_id=1, source_target_pairs={{0,8},{1,9},{2,10},{3,11},{4,12},{5,13},{6,14},{7,15},{8,0},{9,1},... | collective-permute-start | bytes 786440 | tf_op jit(solution)/shard_map/ppermute | solution.py:457
  47.8 14.1 %collective-permute-start.22 = (bf16[256,1024]{1,0:T(8,128)(2,1)S(1)}, bf16[256,1024]{1,0:T(8,128)(2,1)S(1)}, u32[]{:S(2)}, u32[]{:S(2)}) collective-permute-start(bf16[256,1024]{1,0:T(8,128)(2,1)S(1)} %get-tuple-element.44.refs_8_), channel_id=1, source_target_pairs={{0,8},{1,9},{2,10},{3,11},{4,12},{5,13},{6,14},{7,15},{24,16},{25,... | collective-permute-start | bytes 1572872 | tf_op jit(solution)/shard_map/ppermute | solution.py:457
  50.3 4.2 %collective-permute-start.16 = (bf16[128,1024]{1,0:T(8,128)(2,1)S(1)}, bf16[128,1024]{1,0:T(8,128)(2,1)S(1)}, u32[]{:S(2)}, u32[]{:S(2)}) collective-permute-start(bf16[128,1024]{1,0:T(8,128)(2,1)S(1)} %collective-permute-done.8.refs_5_.refs_1_), channel_id=1, source_target_pairs={{0,1},{1,0},{2,3},{3,2},{4,5},{5,4},{6,7},{7,6},{8,9},{9,8},{10,11... | collective-permute-start | bytes 786440 | tf_op jit(solution)/shard_map/ppermute | solution.py:457
  50.8 3.7 %collective-permute-start.18 = (bf16[128,1024]{1,0:T(8,128)(2,1)S(1)}, bf16[128,1024]{1,0:T(8,128)(2,1)S(1)}, u32[]{:S(2)}, u32[]{:S(2)}) collective-permute-start(bf16[128,1024]{1,0:T(8,128)(2,1)S(1)} %collective-permute-done.10.refs_7_.refs_3_), channel_id=1, source_target_pairs={{0,1},{1,0},{2,3},{3,2},{4,5},{5,4},{6,7},{7,6},{8,9},{9,8},{10,11... | collective-permute-start | bytes 786440 | tf_op jit(solution)/shard_map/ppermute | solution.py:457
  53.8 1.7 %collective-permute-start.13 = (bf16[256,512]{1,0:T(8,128)(2,1)S(1)}, bf16[256,512]{1,0:T(8,128)(2,1)S(1)}, u32[]{:S(2)}, u32[]{:S(2)}) collective-permute-start(bf16[256,512]{1,0:T(8,128)(2,1)S(1)} %get-tuple-element.46), channel_id=1, source_target_pairs={{0,1},{1,0},{2,3},{3,2},{4,5},{5,4},{6,7},{7,6},{8,9},{9,8},{10,11... | collective-permute-start | bytes 786440 | tf_op jit(solution)/shard_map/ppermute | solution.py:457
  54.4 1.5 %collective-permute-start.14 = (bf16[256,512]{1,0:T(8,128)(2,1)S(1)}, bf16[256,512]{1,0:T(8,128)(2,1)S(1)}, u32[]{:S(2)}, u32[]{:S(2)}) collective-permute-start(bf16[256,512]{1,0:T(8,128)(2,1)S(1)} %get-tuple-element.47), channel_id=1, source_target_pairs={{0,1},{1,0},{2,3},{3,2},{4,5},{5,4},{6,7},{7,6},{8,9},{9,8},{10,11... | collective-permute-start | bytes 786440 | tf_op jit(solution)/shard_map/ppermute | solution.py:457
  57.4 18.6 %collective-permute-start.21 = (bf16[128,2560]{1,0:T(8,128)(2,1)S(1)}, bf16[128,2560]{1,0:T(8,128)(2,1)S(1)}, u32[]{:S(2)}, u32[]{:S(2)}) collective-permute-start(bf16[128,2560]{1,0:T(8,128)(2,1)S(1)} %get-tuple-element.52), channel_id=1, source_target_pairs={{0,6},{1,7},{2,4},{3,5},{4,2},{5,3},{6,0},{7,1},{8,14},{9,15},{10,... | collective-permute-start | bytes 1966088 | tf_op jit(solution)/shard_map/ppermute | solution.py:457
  58.1 15.5 %collective-permute-start.24 = (bf16[256,1024]{1,0:T(8,128)(2,1)S(1)}, bf16[256,1024]{1,0:T(8,128)(2,1)S(1)}, u32[]{:S(2)}, u32[]{:S(2)}) collective-permute-start(bf16[256,1024]{1,0:T(8,128)(2,1)S(1)} %get-tuple-element.59), channel_id=1, source_target_pairs={{0,8},{1,9},{2,10},{3,11},{4,12},{5,13},{6,14},{7,15},{24,16},{25,... | collective-permute-start | bytes 1572872 | tf_op jit(solution)/shard_map/ppermute | solution.py:457
  62.1 13.9 %collective-permute-start.23 = (bf16[256,1024]{1,0:T(8,128)(2,1)S(1)}, bf16[256,1024]{1,0:T(8,128)(2,1)S(1)}, u32[]{:S(2)}, u32[]{:S(2)}) collective-permute-start(bf16[256,1024]{1,0:T(8,128)(2,1)S(1)} %relay.2), channel_id=1, source_target_pairs={{8,16},{9,17},{10,18},{11,19},{12,20},{13,21},{14,22},{15,23},{16,... | collective-permute-start | bytes 1572872 | tf_op jit(solution)/shard_map/ppermute | solution.py:457
  62.8 25.4 %collective-permute-start.19 = (bf16[128,2560]{1,0:T(8,128)(2,1)S(1)}, bf16[128,2560]{1,0:T(8,128)(2,1)S(1)}, u32[]{:S(2)}, u32[]{:S(2)}) collective-permute-start(bf16[128,2560]{1,0:T(8,128)(2,1)S(1)} %get-tuple-element.50), channel_id=1, source_target_pairs={{0,4},{1,5},{2,6},{3,7},{4,0},{5,1},{6,2},{7,3},{8,12},{9,13},{10,... | collective-permute-start | bytes 1966088 | tf_op jit(solution)/shard_map/ppermute | solution.py:457
  63.2 26.2 %collective-permute-start.20 = (bf16[128,2560]{1,0:T(8,128)(2,1)S(1)}, bf16[128,2560]{1,0:T(8,128)(2,1)S(1)}, u32[]{:S(2)}, u32[]{:S(2)}) collective-permute-start(bf16[128,2560]{1,0:T(8,128)(2,1)S(1)} %get-tuple-element.51), channel_id=1, source_target_pairs={{0,2},{1,3},{2,0},{3,1},{4,6},{5,7},{6,4},{7,5},{8,10},{9,11},{10,... | collective-permute-start | bytes 1966088 | tf_op jit(solution)/shard_map/ppermute | solution.py:457
  76.2 13.9 %copy-start.1 = (bf16[1,128,8192]{2,1,0:T(8,128)(2,1)S(1)}, bf16[1,128,8192]{2,1,0:T(8,128)(2,1)}, u32[]{:S(2)}) copy-start(bf16[1,128,8192]{2,1,0:T(8,128)(2,1)} %param.8) | copy-start | bytes 6291460
  76.3 13.9 %copy-start.7 = (f32[8192]{0:T(1024)S(1)}, f32[8192]{0:T(1024)}, u32[]{:S(2)}) copy-start(f32[8192]{0:T(1024)} %param.9) | copy-start | bytes 98308
  76.3 13.6 %collective-permute-start.25 = (bf16[256,1024]{1,0:T(8,128)(2,1)S(1)}, bf16[256,1024]{1,0:T(8,128)(2,1)S(1)}, u32[]{:S(2)}, u32[]{:S(2)}) collective-permute-start(bf16[256,1024]{1,0:T(8,128)(2,1)S(1)} %get-tuple-element.60), channel_id=1, source_target_pairs={{0,8},{1,9},{2,10},{3,11},{4,12},{5,13},{6,14},{7,15},{8,0},{9,1},... | collective-permute-start | bytes 1572872 | tf_op jit(solution)/shard_map/ppermute | solution.py:457
  78.8 11.1 %collective-permute-start.26 = (bf16[256,1024]{1,0:T(8,128)(2,1)S(1)}, bf16[256,1024]{1,0:T(8,128)(2,1)S(1)}, u32[]{:S(2)}, u32[]{:S(2)}) collective-permute-start(bf16[256,1024]{1,0:T(8,128)(2,1)S(1)} %get-tuple-element.61), channel_id=1, source_target_pairs={{8,16},{9,17},{10,18},{11,19},{12,20},{13,21},{14,22},{15,23},{16,... | collective-permute-start | bytes 1572872 | tf_op jit(solution)/shard_map/ppermute | solution.py:457
  90.1 7.8 %collective-permute-start.27 = (bf16[128,1024]{1,0:T(8,128)(2,1)S(1)}, bf16[128,1024]{1,0:T(8,128)(2,1)S(1)}, u32[]{:S(2)}, u32[]{:S(2)}) collective-permute-start(bf16[128,1024]{1,0:T(8,128)(2,1)S(1)} %get-tuple-element.63), channel_id=1, source_target_pairs={{0,4},{1,5},{2,6},{3,7},{4,0},{5,1},{6,2},{7,3},{8,12},{9,13},{10,... | collective-permute-start | bytes 786440 | tf_op jit(solution)/shard_map/ppermute | solution.py:457
  90.2 7.8 %copy-start.2 = (f32[1,128,2048]{2,1,0:T(8,128)S(1)}, f32[1,128,2048]{2,1,0:T(8,128)}, u32[]{:S(2)}) copy-start(f32[1,128,2048]{2,1,0:T(8,128)} %param.13) | copy-start | bytes 3145732
  90.2 7.7 %copy-start.3 = (f32[1,128,2048]{2,1,0:T(8,128)S(1)}, f32[1,128,2048]{2,1,0:T(8,128)}, u32[]{:S(2)}) copy-start(f32[1,128,2048]{2,1,0:T(8,128)} %param.14) | copy-start | bytes 3145732
  90.2 7.7 %copy-start.4 = (f32[1,128,2048]{2,1,0:T(8,128)S(1)}, f32[1,128,2048]{2,1,0:T(8,128)}, u32[]{:S(2)}) copy-start(f32[1,128,2048]{2,1,0:T(8,128)} %param.15) | copy-start | bytes 3145732

commit v7 on v6

--- a/solution.py
+++ b/solution.py
@@ -64,7 +64,11 @@
         compiler_params=limit(24),
         cost_estimate=cost(8 * rows * model, 6 * rows * model),
         name="norm_blocks",
-    )(tokens, far, gain)
+    )(
+        pltpu.with_memory_space_constraint(tokens, pltpu.HBM),
+        far,
+        pltpu.with_memory_space_constraint(gain, pltpu.HBM),
+    )
     return [outs[i : i + parts] for i in range(0, len(outs), parts)]
 
 
@@ -81,7 +85,7 @@
         out_shape=[jax.ShapeDtypeStruct((w_t.shape[0], width), bf16)] * 2,
         compiler_params=limit(16),
         name="halves",
-    )(w_t)
+    )(pltpu.with_memory_space_constraint(w_t, pltpu.HBM))
 
 
 def stack_kernel(count, *refs):
@@ -391,49 +395,50 @@
     )(own, even, odd, *after)
 
 
-def adam_kernel(token_total, parts, owner_ref, *refs):
-    kept_refs, got_refs, refs = refs[:parts], refs[parts : 2 * parts], refs[2 * parts :]
+def adam_kernel(token_total, parts, at_ref, owner_ref, *refs):
+    grad_refs, refs = refs[:parts], refs[parts:]
     master_ref, moment1_ref, moment2_ref = refs[:3]
-    out_refs = refs[3:]
-    step, width = kept_refs[0].shape
-    dp = lax.axis_index("dp")
-    owned = (owner_ref[...] == dp).astype(f32)
+    out_refs = refs[-3:]
+    step, width = grad_refs[0].shape
+    owned = (owner_ref[...] == lax.axis_index("dp")).astype(f32)
     count = jnp.sum(owned, axis=1, keepdims=True)
     index = pl.program_id(0) * step + lax.broadcasted_iota(jnp.int32, (step, 1), 0)
     occupied = (index.astype(f32) < count).astype(f32)
-    for i, refs in enumerate((kept_refs, got_refs)):
-        for part, ref in enumerate(refs):
-            at = (((dp % 2) ^ i) * parts + part) * width
-            cols = pl.ds(pl.multiple_of(at, width), width)
-            slot_grad = ref[...].astype(f32) / token_total
-            new_moment1 = (
-                beta_one * moment1_ref[:, cols] + (1.0 - beta_one) * slot_grad
-            ) * occupied
-            new_moment2 = (
-                beta_two * moment2_ref[:, cols] + (1.0 - beta_two) * slot_grad * slot_grad
-            ) * occupied
-            step_dir = new_moment1 / bias_one / (jnp.sqrt(new_moment2 / bias_two) + adam_eps)
-            out_refs[0][:, cols] = (master_ref[:, cols] - learn_rate * step_dir) * occupied
-            out_refs[1][:, cols] = new_moment1
-            out_refs[2][:, cols] = new_moment2
-
-
-def adam(owner, kept, got, states, token_total):
+    for part, ref in enumerate(grad_refs):
+        cols = slice(part * width, (part + 1) * width)
+        slot_grad = ref[...].astype(f32) / token_total
+        new_moment1 = (beta_one * moment1_ref[:, cols] + (1.0 - beta_one) * slot_grad) * occupied
+        new_moment2 = (
+            beta_two * moment2_ref[:, cols] + (1.0 - beta_two) * slot_grad * slot_grad
+        ) * occupied
+        step_dir = new_moment1 / bias_one / (jnp.sqrt(new_moment2 / bias_two) + adam_eps)
+        out_refs[0][:, cols] = (master_ref[:, cols] - learn_rate * step_dir) * occupied
+        out_refs[1][:, cols] = new_moment1
+        out_refs[2][:, cols] = new_moment2
+
+
+def adam(at, owner, grads, states, token_total, into, after):
     slots, cols = states[0].shape
-    width = kept[0].shape[-1]
+    parts = len(grads)
+    width = grads[0].shape[-1]
     step = min(slots, 32)
-    return pl.pallas_call(
-        functools.partial(adam_kernel, token_total, len(kept)),
-        grid=(slots // step,),
-        in_specs=[pl.BlockSpec(owner.shape, lambda i: (0, 0))]
-        + [pl.BlockSpec((step, width), lambda i: (i, 0))] * (2 * len(kept))
-        + [pl.BlockSpec((step, cols), lambda i: (i, 0))] * 3,
-        out_specs=[pl.BlockSpec((step, cols), lambda i: (i, 0))] * 3,
+    half = pl.BlockSpec((step, cols // 2), lambda i, at: (i, at[0]))
+    return pl.pallas_call(
+        functools.partial(adam_kernel, token_total, parts),
+        grid_spec=pltpu.PrefetchScalarGridSpec(
+            num_scalar_prefetch=1,
+            grid=(slots // step,),
+            in_specs=[pl.BlockSpec(owner.shape, lambda i, at: (0, 0))]
+            + [pl.BlockSpec((step, width), lambda i, at: (i, 0))] * parts
+            + [half] * 3
+            + [pl.BlockSpec(memory_space=pl.ANY)] * (len(into) + len(after)),
+            out_specs=[half] * 3,
+        ),
         out_shape=[jax.ShapeDtypeStruct((slots, cols), f32)] * 3,
+        input_output_aliases={5 + parts + i: i for i in range(len(into))},
         compiler_params=limit(24),
-        cost_estimate=cost(20 * slots * cols, 30 * slots * cols),
         name="adam",
-    )(owner, *kept, *got, *states)
+    )(at, owner, *grads, *states, *into, *after)
 
 
 def on_device(groups, seqs, tokens, gain, w_t, grad_values, owner, master, moment1, moment2):
@@ -482,6 +487,7 @@
 
     tokens_far = to_core(tokens)
     grads = [value_grad] + [to_chip(value_grad, k) for k in range(chips - 1, 0, -1)][::-1]
+
     w_keep, w_send = halves(w_t, width)
     w_got = to_x(w_send)
 
@@ -492,7 +498,7 @@
     grads_far = [to_core(g) for g in grads]
     selected = select_rows(owner_row, groups, slots, (sent[0][0],))
 
-    weights = stack([w_keep, w_got], 1, grads[:1])
+    weights = stack([w_keep, w_got], 1, grads_far[:1])
     turn = planes // 2
     while turn:
         weights = [w for value in weights for w in (value, to_plane(value, turn))]
@@ -513,7 +519,7 @@
             [piece[part] for piece in pieces],
             planes,
             plan,
-            weights[:1] if part == parts - 1 else [],
+            weights if part == parts - 1 else [],
         )
         ready = dict(zip(plan, outs))
         if part == parts - 1:
@@ -539,8 +545,12 @@
 
     grad_x, values = grad_x_blocks(tokens, gain_row, back[-1], home)
 
-    states = adam(owner_row, kept, got, (master[0], moment1[0], moment2[0]), rows * seqs * groups)
-    return (values[None], grad_x[None], *(s[None] for s in states))
+    states = (master[0], moment1[0], moment2[0])
+    total = rows * seqs * groups
+    at = own_x.astype(jnp.int32)[None]
+    new = adam(at, owner_row, kept, states, total, (), (grad_x,))
+    new = adam(1 - at, owner_row, got, states, total, new, ())
+    return (values[None], grad_x[None], *(n[None] for n in new))
 
 
 def solution(mesh):

time: 101 us -> 107 us (1.059)
  Pallas kernels: 16.4 us -> 22.8 us
  local copies, waits for them, and re-layouts: 3.34 us -> 6.34 us
  waiting for transfers between devices: 49.1 us -> 47 us
  starting transfers between devices: 30.8 us -> 28.9 us
    pallas_call x1 -> x2, Pallas kernels: 2.6 us -> 5.61 us  [adam(): pl.pallas_call(functools.partial(adam_kernel, token_total, parts), grid_s...]
    unnamed x20 -> x32, local copies, waits for them, and re-layouts: 3.34 us -> 6.34 us
    ppermute x28, waiting for transfers between devices: 49.1 us -> 47 us  [permute(): return lax.ppermute(value, ('dp', 'seq'), pairs)]
    ppermute x28, starting transfers between devices: 30.8 us -> 28.9 us  [permute(): return lax.ppermute(value, ('dp', 'seq'), pairs)]
    pallas_call x1, Pallas kernels: 1.66 us -> 3.42 us  [norm_blocks(): pl.pallas_call(functools.partial(norm_kernel, parts), grid=(rows // step,...]
  transfers between devices with their start and end apart: 28 -> 28, of which waited for: 15 -> 12; matrix products, arithmetic and copies ran while one was open for 0% -> 0% of each run, Pallas kernels for 14% -> 17%
where the time goes in v7:
time: 107 us; the launch traced here: 106 us
  waiting for transfers between devices  47 us (44%)
  starting transfers between devices  28.9 us (27%)
  Pallas kernels  22.8 us (21%)
  local copies, waits for them, and re-layouts  6.34 us (6%)
    ppermute x28, waiting for transfers between devices, permute(): return lax.ppermute(value, ('dp', 'seq'), pairs)  47 us
    ppermute x28, starting transfers between devices, permute(): return lax.ppermute(value, ('dp', 'seq'), pairs)  28.9 us
    unnamed x32, local copies, waits for them, and re-layouts  6.34 us
    pallas_call x2, Pallas kernels, adam(): pl.pallas_call(functools.partial(adam_kernel, token_total, parts), grid_s...  5.61 us
    pallas_call x1, Pallas kernels, grad_x_blocks(): pl.pallas_call(grad_x_kernel, grid=(rows // step,), in_specs=[pl.BlockSpe...  3.62 us
    pallas_call x1, Pallas kernels, norm_blocks(): pl.pallas_call(functools.partial(norm_kernel, parts), grid=(rows // step,...  3.42 us
    pallas_call x1, Pallas kernels, weight_blocks(): pl.pallas_call(functools.partial(weight_kernel, planes, chips, plan), in_...  3.02 us
    pallas_call x1, Pallas kernels, value_parts(): pl.pallas_call(functools.partial(value_kernel, len(weights), chips, parts...  2.99 us
  transfers between devices with their start and end apart: 28, of which 12 were waited for; matrix products, arithmetic and copies ran while one was open for 0% of the time, Pallas kernels for 17%

profile of v7, /device:TPU:0, one launch (start us, length us, event | category | flops | bytes accessed | tf_op | source)
XLA Modules:
  0.0 105.9 jit_solution(16665063565358760639)
XLA Ops:
  0.6 0.5 collective-permute-start.3
  1.1 2.6 %collective-permute-start = (bf16[128,512]{1,0:T(8,128)(2,1)}, bf16[128,512]{1,0:T(8,128)(2,1)S(1)}, u32[]{:S(2)}, u32[]{:S(2)}) collective-permute-start(bf16[128,512]{1,0:T(8,128)(2,1)} %bitcast.25), channel_id=1, source_target_pairs={{0,4},{1,5},{2,6},{3,7},{4,0},{5,1},{6,2},{7,3},{8,12},{9,13},{10,... | collective-permute-start | bytes 393224 | tf_op jit(solution)/shard_map/ppermute | solution.py:462
  3.7 1.5 %collective-permute-start.1 = (bf16[128,512]{1,0:T(8,128)(2,1)}, bf16[128,512]{1,0:T(8,128)(2,1)S(1)}, u32[]{:S(2)}, u32[]{:S(2)}) collective-permute-start(bf16[128,512]{1,0:T(8,128)(2,1)} %bitcast.26), channel_id=1, source_target_pairs={{0,2},{1,3},{2,0},{3,1},{4,6},{5,7},{6,4},{7,5},{8,10},{9,11},{10,... | collective-permute-start | bytes 393224 | tf_op jit(solution)/shard_map/ppermute | solution.py:462
  5.3 3.4 %norm_blocks.1 = (bf16[2,128,1024]{2,1,0:T(8,128)(2,1)S(1)}, bf16[2,128,1024]{2,1,0:T(8,128)(2,1)S(1)}, bf16[2,128,1024]{2,1,0:T(8,128)(2,1)S(1)}, bf16[2,128,1024]{2,1,0:T(8,128)(2,1)S(1)}) custom-call(bf16[128,8192]{1,0:T(8,128)(2,1)} %bitcast.14, bf16[128,8192]{1,0:T(8,128)(2,1)S(1)} %collective-permute-done.3.far_ref, f32[1,8192]{1,0:T(1,128)} %bitcast.23), custom_call_target="tpu_custom_call" | custom-call | flops 8388608 | bytes 6291456 | tf_op jit(solution)/shard_map/norm_blocks/pallas_call | solution.py:54
  8.7 3.6 %collective-permute-done.1.refs_2_ = bf16[128,512]{1,0:T(8,128)(2,1)S(1)} collective-permute-done((bf16[128,512]{1,0:T(8,128)(2,1)}, bf16[128,512]{1,0:T(8,128)(2,1)S(1)}, u32[]{:S(2)}, u32[]{:S(2)}) %collective-permute-start.1) | collective-permute-done | bytes 131104 | tf_op jit(solution)/shard_map/ppermute | solution.py:462
  12.4 1.0 halves.1
  13.4 1.3 %collective-permute-start.7 = (bf16[64,1024]{1,0:T(8,128)(2,1)S(1)}, bf16[64,1024]{1,0:T(8,128)(2,1)S(1)}, u32[]{:S(2)}, u32[]{:S(2)}) collective-permute-start(bf16[64,1024]{1,0:T(8,128)(2,1)S(1)} %get-tuple-element.46), channel_id=1, source_target_pairs={{0,4},{1,5},{2,6},{3,7},{4,0},{5,1},{6,2},{7,3},{8,12},{9,13},{10,... | collective-permute-start | bytes 393224 | tf_op jit(solution)/shard_map/ppermute | solution.py:462
  14.9 0.8 collective-permute-start.4
  15.7 1.5 %collective-permute-start.5 = (bf16[2,128,1024]{2,1,0:T(8,128)(2,1)S(1)}, bf16[2,128,1024]{2,1,0:T(8,128)(2,1)S(1)}, u32[]{:S(2)}, u32[]{:S(2)}) collective-permute-start(bf16[2,128,1024]{2,1,0:T(8,128)(2,1)S(1)} %get-tuple-element.43), channel_id=1, source_target_pairs={{0,2},{1,3},{2,0},{3,1},{4,6},{5,7},{6,4},{7,5},{8,10},{9,11},{10,... | collective-permute-start | bytes 1572872 | tf_op jit(solution)/shard_map/ppermute | solution.py:462
  17.2 2.5 %collective-permute-done.7.refs_1_ = bf16[64,1024]{1,0:T(8,128)(2,1)S(1)} collective-permute-done((bf16[64,1024]{1,0:T(8,128)(2,1)S(1)}, bf16[64,1024]{1,0:T(8,128)(2,1)S(1)}, u32[]{:S(2)}, u32[]{:S(2)}) %collective-permute-start.7) | collective-permute-done | bytes 131104 | tf_op jit(solution)/shard_map/ppermute | solution.py:462
  19.8 1.5 %collective-permute-start.6 = (bf16[2,128,1024]{2,1,0:T(8,128)(2,1)S(1)}, bf16[2,128,1024]{2,1,0:T(8,128)(2,1)S(1)}, u32[]{:S(2)}, u32[]{:S(2)}) collective-permute-start(bf16[2,128,1024]{2,1,0:T(8,128)(2,1)S(1)} %get-tuple-element.44), channel_id=1, source_target_pairs={{0,6},{1,7},{2,4},{3,5},{4,2},{5,3},{6,0},{7,1},{8,14},{9,15},{10,... | collective-permute-start | bytes 1572872 | tf_op jit(solution)/shard_map/ppermute | solution.py:462
  21.3 2.7 %collective-permute-start.10 = (bf16[128,1024]{1,0:T(8,128)(2,1)S(1)}, bf16[128,1024]{1,0:T(8,128)(2,1)S(1)}, u32[]{:S(2)}, u32[]{:S(2)}) collective-permute-start(bf16[128,1024]{1,0:T(8,128)(2,1)S(1)} %stack.3.refs_9_.refs_4_.refs_0_), channel_id=1, source_target_pairs={{0,16},{1,17},{2,18},{3,19},{4,20},{5,21},{6,22},{7,23},{8,24},{9,... | collective-permute-start | bytes 786440 | tf_op jit(solution)/shard_map/ppermute | solution.py:462
  23.9 1.6 %collective-permute-start.9 = (bf16[128,1024]{1,0:T(8,128)(2,1)S(1)}, bf16[128,1024]{1,0:T(8,128)(2,1)S(1)}, u32[]{:S(2)}, u32[]{:S(2)}) collective-permute-start(bf16[128,1024]{1,0:T(8,128)(2,1)S(1)} %stack.3.refs_9_.refs_4_.refs_0_), channel_id=1, source_target_pairs={{0,8},{1,9},{2,10},{3,11},{4,12},{5,13},{6,14},{7,15},{8,0},{9,1},... | collective-permute-start | bytes 786440 | tf_op jit(solution)/shard_map/ppermute | solution.py:462
  25.5 9.7 %collective-permute-done.10.refs_11_.refs_6_.refs_2_ = bf16[128,1024]{1,0:T(8,128)(2,1)S(1)} collective-permute-done((bf16[128,1024]{1,0:T(8,128)(2,1)S(1)}, bf16[128,1024]{1,0:T(8,128)(2,1)S(1)}, u32[]{:S(2)}, u32[]{:S(2)}) %collective-permute-start.10) | collective-permute-done | bytes 262176 | tf_op jit(solution)/shard_map/ppermute | solution.py:462
  35.2 0.6 collective-permute-start.11
  35.8 0.5 select_rows.1.refs_0_
  36.4 0.5 collective-permute-start.17
  36.8 5.9 %collective-permute-done.6.refs_8_.refs_3_ = bf16[2,128,1024]{2,1,0:T(8,128)(2,1)S(1)} collective-permute-done((bf16[2,128,1024]{2,1,0:T(8,128)(2,1)S(1)}, bf16[2,128,1024]{2,1,0:T(8,128)(2,1)S(1)}, u32[]{:S(2)}, u32[]{:S(2)}) %collective-permute-start.6) | collective-permute-done | bytes 524320 | tf_op jit(solution)/shard_map/ppermute | solution.py:462
  42.8 3.0 %weight_blocks.1 = (bf16[256,1024]{1,0:T(8,128)(2,1)S(1)}, bf16[256,1024]{1,0:T(8,128)(2,1)S(1)}, bf16[256,1024]{1,0:T(8,128)(2,1)S(1)}, bf16[256,1024]{1,0:T(8,...) custom-call(bf16[1024,512]{1,0:T(8,128)(2,1)S(1)} %select_rows.1.refs_0_, ...), custom_call_target="tpu_custom_call" | custom-call | flops 2147483648 | bytes 4194304 | tf_op jit(solution)/shard_map/weight_blocks/pallas_call | solution.py:192
  45.8 3.5 %collective-permute-start.22 = (bf16[256,1024]{1,0:T(8,128)(2,1)S(1)}, bf16[256,1024]{1,0:T(8,128)(2,1)S(1)}, u32[]{:S(2)}, u32[]{:S(2)}) collective-permute-start(bf16[256,1024]{1,0:T(8,128)(2,1)S(1)} %get-tuple-element.47.refs_8_), channel_id=1, source_target_pairs={{0,8},{1,9},{2,10},{3,11},{4,12},{5,13},{6,14},{7,15},{24,16},{25,... | collective-permute-start | bytes 1572872 | tf_op jit(solution)/shard_map/ppermute | solution.py:462
  49.4 3.0 %value_parts.1 = (bf16[256,512]{1,0:T(8,128)(2,1)S(1)}, bf16[256,512]{1,0:T(8,128)(2,1)S(1)}, f32[512,512]{1,0:T(8,128)S(1)}) custom-call(bf16[2,128,1024]{2,1,0:T(8,128)(2,1)S(1)} %get-tuple-element.39.refs_4_.refs_0_.refs_5_, bf16[2,128,1024]{2,1,0:T(8,128)(2,1)S(1)} %collective-permute-done.4.refs_6_.refs_1_, ...), custom_call_target="tpu_custom_call" | custom-call | tf_op jit(solution)/shard_map/value_parts/pallas_call | solution.py:246
  52.4 0.6 collective-permute-start.13
  53.1 0.4 collective-permute-start.18
  53.5 0.6 collective-permute-done.13.got_a_ref
  54.1 0.4 collective-permute-done.14.got_b_ref
  54.9 1.5 %back_blocks.1 = (bf16[128,2048]{1,0:T(8,128)(2,1)S(1)}, bf16[128,2560]{1,0:T(8,128)(2,1)S(1)}, bf16[128,2560]{1,0:T(8,128)(2,1)S(1)}, bf16[128,2560]{1,0:T(8,128)(2,1)S(1)}, f32[128,512]{1,0:T(8,128)S(1)}) custom-call(bf16[256,512]{1,0:T(8,128)(2,1)S(1)} %get-tuple-element.40.refs_1_.grads_a_ref, ...), custom_call_target="tpu_custom_call" | custom-call | tf_op jit(solution)/shard_map/back_blocks/pallas_call | solution.py:286
  56.4 1.3 %collective-permute-start.21 = (bf16[128,2560]{1,0:T(8,128)(2,1)S(1)}, bf16[128,2560]{1,0:T(8,128)(2,1)S(1)}, u32[]{:S(2)}, u32[]{:S(2)}) collective-permute-start(bf16[128,2560]{1,0:T(8,128)(2,1)S(1)} %get-tuple-element.55), channel_id=1, source_target_pairs={{0,6},{1,7},{2,4},{3,5},{4,2},{5,3},{6,0},{7,1},{8,14},{9,15},{10,... | collective-permute-start | bytes 1966088 | tf_op jit(solution)/shard_map/ppermute | solution.py:462
  57.7 1.3 %collective-permute-start.24 = (bf16[256,1024]{1,0:T(8,128)(2,1)S(1)}, bf16[256,1024]{1,0:T(8,128)(2,1)S(1)}, u32[]{:S(2)}, u32[]{:S(2)}) collective-permute-start(bf16[256,1024]{1,0:T(8,128)(2,1)S(1)} %get-tuple-element.62), channel_id=1, source_target_pairs={{0,8},{1,9},{2,10},{3,11},{4,12},{5,13},{6,14},{7,15},{24,16},{25,... | collective-permute-start | bytes 1572872 | tf_op jit(solution)/shard_map/ppermute | solution.py:462
  59.0 2.3 %collective-permute-done.22.refs_1_ = bf16[256,1024]{1,0:T(8,128)(2,1)S(1)} collective-permute-done((bf16[256,1024]{1,0:T(8,128)(2,1)S(1)}, bf16[256,1024]{1,0:T(8,128)(2,1)S(1)}, u32[]{:S(2)}, u32[]{:S(2)}) %collective-permute-start.22) | collective-permute-done | bytes 524320 | tf_op jit(solution)/shard_map/ppermute | solution.py:462
  61.4 0.7 collective-permute-start.23
  62.2 1.1 %collective-permute-start.20 = (bf16[128,2560]{1,0:T(8,128)(2,1)S(1)}, bf16[128,2560]{1,0:T(8,128)(2,1)S(1)}, u32[]{:S(2)}, u32[]{:S(2)}) collective-permute-start(bf16[128,2560]{1,0:T(8,128)(2,1)S(1)} %get-tuple-element.54), channel_id=1, source_target_pairs={{0,2},{1,3},{2,0},{3,1},{4,6},{5,7},{6,4},{7,5},{8,10},{9,11},{10,... | collective-permute-start | bytes 1966088 | tf_op jit(solution)/shard_map/ppermute | solution.py:462
  63.3 8.3 %collective-permute-done.24.refs_3_ = bf16[256,1024]{1,0:T(8,128)(2,1)S(1)} collective-permute-done((bf16[256,1024]{1,0:T(8,128)(2,1)S(1)}, bf16[256,1024]{1,0:T(8,128)(2,1)S(1)}, u32[]{:S(2)}, u32[]{:S(2)}) %collective-permute-start.24) | collective-permute-done | bytes 524320 | tf_op jit(solution)/shard_map/ppermute | solution.py:462
  71.6 3.4 %collective-permute-done.21.refs_3_.refs_4_.refs_2_ = bf16[128,2560]{1,0:T(8,128)(2,1)S(1)} collective-permute-done((bf16[128,2560]{1,0:T(8,128)(2,1)S(1)}, bf16[128,2560]{1,0:T(8,128)(2,1)S(1)}, u32[]{:S(2)}, u32[]{:S(2)}) %collective-permute-start.21) | collective-permute-done | bytes 655392 | tf_op jit(solution)/shard_map/ppermute | solution.py:462
  75.3 2.6 %collective-permute-start.25 = (bf16[256,1024]{1,0:T(8,128)(2,1)S(1)}, bf16[256,1024]{1,0:T(8,128)(2,1)S(1)}, u32[]{:S(2)}, u32[]{:S(2)}) collective-permute-start(bf16[256,1024]{1,0:T(8,128)(2,1)S(1)} %get-tuple-element.63), channel_id=1, source_target_pairs={{0,8},{1,9},{2,10},{3,11},{4,12},{5,13},{6,14},{7,15},{8,0},{9,1},... | collective-permute-start | bytes 1572872 | tf_op jit(solution)/shard_map/ppermute | solution.py:462
  77.9 0.7 collective-permute-start.26
  78.6 9.3 %collective-permute-done.19.refs_1_.refs_0_ = bf16[128,2560]{1,0:T(8,128)(2,1)S(1)} collective-permute-done((bf16[128,2560]{1,0:T(8,128)(2,1)S(1)}, bf16[128,2560]{1,0:T(8,128)(2,1)S(1)}, u32[]{:S(2)}, u32[]{:S(2)}) %collective-permute-start.19) | collective-permute-done | bytes 655392 | tf_op jit(solution)/shard_map/ppermute | solution.py:462
  87.9 0.6 collective-permute-done.20.refs_2_.refs_1_
  88.4 0.8 finish.1
  89.2 0.8 copy-done.4
  90.1 0.8 copy-done.9
  90.9 1.1 %collective-permute-start.27 = (bf16[128,1024]{1,0:T(8,128)(2,1)}, bf16[128,1024]{1,0:T(8,128)(2,1)}, u32[]{:S(2)}, u32[]{:S(2)}) collective-permute-start(bf16[128,1024]{1,0:T(8,128)(2,1)} %get-tuple-element.65), channel_id=1, source_target_pairs={{0,4},{1,5},{2,6},{3,7},{4,0},{5,1},{6,2},{7,3},{8,12},{9,13},{10,... | collective-permute-start | bytes 786440 | tf_op jit(solution)/shard_map/ppermute | solution.py:462
  92.0 1.1 %copy-done.5 = bf16[128,2560]{1,0:T(8,128)(2,1)S(1)} copy-done((bf16[128,2560]{1,0:T(8,128)(2,1)S(1)}, bf16[128,2560]{1,0:T(8,128)(2,1)}, u32[]{:S(2)}) %copy-start.5) | copy-done | bytes 655384
  93.1 1.0 copy-done.8
  94.1 0.9 copy-done.12
  95.1 3.6 %grad_x_blocks.1 = (bf16[128,8192]{1,0:T(8,128)(2,1)}, bf16[128,512]{1,0:T(8,128)(2,1)}) custom-call(bf16[128,8192]{1,0:T(8,128)(2,1)S(1)} %bitcast.15, f32[1,8192]{1,0:T(1,128)S(1)} %bitcast.24, f32[128,512]{1,0:T(8,128)S(1)} %copy-done.12, bf16[128,2048]{1,0:T(8,128)(2,1)S(1)} %copy-done.8, bf16[128,2560]{1,0:T(8,128)(2,1)S(1)} %collective-permute-done.19.refs_1_.refs_0_, ...), custom_call_target="tpu_custom_call" | custom-call | flops 16777216 | bytes 6291456 | tf_op jit(solution)/shard_map/grad_x_blocks/pallas_call | solution.py:329
  98.7 1.6 %copy-done.6 = bf16[128,8192]{1,0:T(8,128)(2,1)S(1)} copy-done((bf16[128,8192]{1,0:T(8,128)(2,1)S(1)}, bf16[128,8192]{1,0:T(8,128)(2,1)}, u32[]{:S(2)}) %copy-start.6) | copy-done | bytes 2097176
  100.3 2.2 %adam.2 = (f32[128,2048]{1,0:T(8,128)}, f32[128,2048]{1,0:T(8,128)}, f32[128,2048]{1,0:T(8,128)}) custom-call(s32[1]{0:T(128)} %bitcast.6.at_ref, s32[1,512]{1,0:T(1,128)S(1)} %bitcast.30, f32[128,1024]{1,0:T(8,128)S(1)} %copy-done.10, f32[128,2048]{1,0:T(8,128)S(1)} %bitcast.16, f32[128,2048]{1,0:T(8,128)S(1)} %bitcast.18, f32[128,2048]{1,0:T(8,128)S(1)} %bitcast.20, ...), custom_call_target="tpu_custom_call" | custom-call | tf_op jit(solution)/shard_map/adam/pallas_call | solution.py:426
  102.5 3.5 %adam.3 = (f32[128,2048]{1,0:T(8,128)}, f32[128,2048]{1,0:T(8,128)}, f32[128,2048]{1,0:T(8,128)}) custom-call(s32[1]{0:T(128)S(6)} %sub.3.at_ref, s32[1,512]{1,0:T(1,128)S(1)} %bitcast.31, bf16[128,1024]{1,0:T(8,128)(2,1)} %collective-permute-done.27.refs_0_, f32[128,2048]{1,0:T(8,128)S(1)} %bitcast.17, ...), custom_call_target="tpu_custom_call", output_to_operand_aliasing={{0}: (6, {}), {1}: (7, {}), {2}: (8, {})} | custom-call | tf_op jit(solution)/shard_map/adam/pallas_call | solution.py:426
  (54 shorter events, 1.5 us)
Async XLA Ops:
  0.6 4.6 %collective-permute-start.3 = (bf16[128,8192]{1,0:T(8,128)(2,1)}, bf16[128,8192]{1,0:T(8,128)(2,1)S(1)}, u32[]{:S(2)}, u32[]{:S(2)}) collective-permute-start(bf16[128,8192]{1,0:T(8,128)(2,1)} %bitcast.13), channel_id=1, source_target_pairs={{0,1},{1,0},{2,3},{3,2},{4,5},{5,4},{6,7},{7,6},{8,9},{9,8},{10,11... | collective-permute-start | bytes 6291464 | tf_op jit(solution)/shard_map/ppermute | solution.py:462
  1.1 7.6 %collective-permute-start = (bf16[128,512]{1,0:T(8,128)(2,1)}, bf16[128,512]{1,0:T(8,128)(2,1)S(1)}, u32[]{:S(2)}, u32[]{:S(2)}) collective-permute-start(bf16[128,512]{1,0:T(8,128)(2,1)} %bitcast.25), channel_id=1, source_target_pairs={{0,4},{1,5},{2,6},{3,7},{4,0},{5,1},{6,2},{7,3},{8,12},{9,13},{10,... | collective-permute-start | bytes 393224 | tf_op jit(solution)/shard_map/ppermute | solution.py:462
  3.7 8.6 %collective-permute-start.1 = (bf16[128,512]{1,0:T(8,128)(2,1)}, bf16[128,512]{1,0:T(8,128)(2,1)S(1)}, u32[]{:S(2)}, u32[]{:S(2)}) collective-permute-start(bf16[128,512]{1,0:T(8,128)(2,1)} %bitcast.26), channel_id=1, source_target_pairs={{0,2},{1,3},{2,0},{3,1},{4,6},{5,7},{6,4},{7,5},{8,10},{9,11},{10,... | collective-permute-start | bytes 393224 | tf_op jit(solution)/shard_map/ppermute | solution.py:462
  5.2 7.1 %collective-permute-start.2 = (bf16[128,512]{1,0:T(8,128)(2,1)}, bf16[128,512]{1,0:T(8,128)(2,1)S(1)}, u32[]{:S(2)}, u32[]{:S(2)}) collective-permute-start(bf16[128,512]{1,0:T(8,128)(2,1)} %bitcast.27), channel_id=1, source_target_pairs={{0,6},{1,7},{2,4},{3,5},{4,2},{5,3},{6,0},{7,1},{8,14},{9,15},{10,... | collective-permute-start | bytes 393224 | tf_op jit(solution)/shard_map/ppermute | solution.py:462
  5.3 7.0 %copy-start.14 = (bf16[1,128,512]{2,1,0:T(8,128)(2,1)S(1)}, bf16[1,128,512]{2,1,0:T(8,128)(2,1)}, u32[]{:S(2)}) copy-start(bf16[1,128,512]{2,1,0:T(8,128)(2,1)} %param.11) | copy-start | bytes 393220
  8.7 27.1 %copy-start.15 = (s32[512]{0:T(512)S(1)}, s32[512]{0:T(512)}, u32[]{:S(2)}) copy-start(s32[512]{0:T(512)} %param.12) | copy-start | bytes 6148
  12.3 8.9 %collective-permute-start.8 = (bf16[256,512]{1,0:T(8,128)(2,1)S(1)}, bf16[256,512]{1,0:T(8,128)(2,1)S(1)}, u32[]{:S(2)}, u32[]{:S(2)}) collective-permute-start(bf16[256,512]{1,0:T(8,128)(2,1)S(1)} %get-tuple-element.40.refs_1_.grads_a_ref), channel_id=1, source_target_pairs={{0,1},{1,0},{2,3},{3,2},{4,5},{5,4},{6,7},{7,6},{8,9},{9,8},{10,11... | collective-permute-start | bytes 786440 | tf_op jit(solution)/shard_map/ppermute | solution.py:462
  13.4 6.4 %collective-permute-start.7 = (bf16[64,1024]{1,0:T(8,128)(2,1)S(1)}, bf16[64,1024]{1,0:T(8,128)(2,1)S(1)}, u32[]{:S(2)}, u32[]{:S(2)}) collective-permute-start(bf16[64,1024]{1,0:T(8,128)(2,1)S(1)} %get-tuple-element.46), channel_id=1, source_target_pairs={{0,4},{1,5},{2,6},{3,7},{4,0},{5,1},{6,2},{7,3},{8,12},{9,13},{10,... | collective-permute-start | bytes 393224 | tf_op jit(solution)/shard_map/ppermute | solution.py:462
  14.7 9.2 %collective-permute-start.12 = (bf16[256,512]{1,0:T(8,128)(2,1)S(1)}, bf16[256,512]{1,0:T(8,128)(2,1)S(1)}, u32[]{:S(2)}, u32[]{:S(2)}) collective-permute-start(bf16[256,512]{1,0:T(8,128)(2,1)S(1)} %get-tuple-element.41.refs_2_.grads_b_ref), channel_id=1, source_target_pairs={{0,1},{1,0},{2,3},{3,2},{4,5},{5,4},{6,7},{7,6},{8,9},{9,8},{10,11... | collective-permute-start | bytes 786440 | tf_op jit(solution)/shard_map/ppermute | solution.py:462
  14.9 21.4 %collective-permute-start.4 = (bf16[2,128,1024]{2,1,0:T(8,128)(2,1)S(1)}, bf16[2,128,1024]{2,1,0:T(8,128)(2,1)S(1)}, u32[]{:S(2)}, u32[]{:S(2)}) collective-permute-start(bf16[2,128,1024]{2,1,0:T(8,128)(2,1)S(1)} %get-tuple-element.42), channel_id=1, source_target_pairs={{0,4},{1,5},{2,6},{3,7},{4,0},{5,1},{6,2},{7,3},{8,12},{9,13},{10,... | collective-permute-start | bytes 1572872 | tf_op jit(solution)/shard_map/ppermute | solution.py:462
  15.7 21.1 %collective-permute-start.5 = (bf16[2,128,1024]{2,1,0:T(8,128)(2,1)S(1)}, bf16[2,128,1024]{2,1,0:T(8,128)(2,1)S(1)}, u32[]{:S(2)}, u32[]{:S(2)}) collective-permute-start(bf16[2,128,1024]{2,1,0:T(8,128)(2,1)S(1)} %get-tuple-element.43), channel_id=1, source_target_pairs={{0,2},{1,3},{2,0},{3,1},{4,6},{5,7},{6,4},{7,5},{8,10},{9,11},{10,... | collective-permute-start | bytes 1572872 | tf_op jit(solution)/shard_map/ppermute | solution.py:462
  19.8 23.0 %collective-permute-start.6 = (bf16[2,128,1024]{2,1,0:T(8,128)(2,1)S(1)}, bf16[2,128,1024]{2,1,0:T(8,128)(2,1)S(1)}, u32[]{:S(2)}, u32[]{:S(2)}) collective-permute-start(bf16[2,128,1024]{2,1,0:T(8,128)(2,1)S(1)} %get-tuple-element.44), channel_id=1, source_target_pairs={{0,6},{1,7},{2,4},{3,5},{4,2},{5,3},{6,0},{7,1},{8,14},{9,15},{10,... | collective-permute-start | bytes 1572872 | tf_op jit(solution)/shard_map/ppermute | solution.py:462
  21.3 13.9 %collective-permute-start.10 = (bf16[128,1024]{1,0:T(8,128)(2,1)S(1)}, bf16[128,1024]{1,0:T(8,128)(2,1)S(1)}, u32[]{:S(2)}, u32[]{:S(2)}) collective-permute-start(bf16[128,1024]{1,0:T(8,128)(2,1)S(1)} %stack.3.refs_9_.refs_4_.refs_0_), channel_id=1, source_target_pairs={{0,16},{1,17},{2,18},{3,19},{4,20},{5,21},{6,22},{7,23},{8,24},{9,... | collective-permute-start | bytes 786440 | tf_op jit(solution)/shard_map/ppermute | solution.py:462
  23.9 12.3 %collective-permute-start.9 = (bf16[128,1024]{1,0:T(8,128)(2,1)S(1)}, bf16[128,1024]{1,0:T(8,128)(2,1)S(1)}, u32[]{:S(2)}, u32[]{:S(2)}) collective-permute-start(bf16[128,1024]{1,0:T(8,128)(2,1)S(1)} %stack.3.refs_9_.refs_4_.refs_0_), channel_id=1, source_target_pairs={{0,8},{1,9},{2,10},{3,11},{4,12},{5,13},{6,14},{7,15},{8,0},{9,1},... | collective-permute-start | bytes 786440 | tf_op jit(solution)/shard_map/ppermute | solution.py:462
  35.2 7.6 %collective-permute-start.11 = (bf16[128,1024]{1,0:T(8,128)(2,1)S(1)}, bf16[128,1024]{1,0:T(8,128)(2,1)S(1)}, u32[]{:S(2)}, u32[]{:S(2)}) collective-permute-start(bf16[128,1024]{1,0:T(8,128)(2,1)S(1)} %collective-permute-done.10.refs_11_.refs_6_.refs_2_), channel_id=1, source_target_pairs={{0,8},{1,9},{2,10},{3,11},{4,12},{5,13},{6,14},{7,15},{8,0},{9,1},... | collective-permute-start | bytes 786440 | tf_op jit(solution)/shard_map/ppermute | solution.py:462
  36.3 16.7 %collective-permute-start.15 = (bf16[128,1024]{1,0:T(8,128)(2,1)S(1)}, bf16[128,1024]{1,0:T(8,128)(2,1)S(1)}, u32[]{:S(2)}, u32[]{:S(2)}) collective-permute-start(bf16[128,1024]{1,0:T(8,128)(2,1)S(1)} %stack.3.refs_9_.refs_4_.refs_0_), channel_id=1, source_target_pairs={{0,1},{1,0},{2,3},{3,2},{4,5},{5,4},{6,7},{7,6},{8,9},{9,8},{10,11... | collective-permute-start | bytes 786440 | tf_op jit(solution)/shard_map/ppermute | solution.py:462
  36.4 16.7 %collective-permute-start.17 = (bf16[128,1024]{1,0:T(8,128)(2,1)S(1)}, bf16[128,1024]{1,0:T(8,128)(2,1)S(1)}, u32[]{:S(2)}, u32[]{:S(2)}) collective-permute-start(bf16[128,1024]{1,0:T(8,128)(2,1)S(1)} %collective-permute-done.10.refs_11_.refs_6_.refs_2_), channel_id=1, source_target_pairs={{0,1},{1,0},{2,3},{3,2},{4,5},{5,4},{6,7},{7,6},{8,9},{9,8},{10,11... | collective-permute-start | bytes 786440 | tf_op jit(solution)/shard_map/ppermute | solution.py:462
  45.8 15.5 %collective-permute-start.22 = (bf16[256,1024]{1,0:T(8,128)(2,1)S(1)}, bf16[256,1024]{1,0:T(8,128)(2,1)S(1)}, u32[]{:S(2)}, u32[]{:S(2)}) collective-permute-start(bf16[256,1024]{1,0:T(8,128)(2,1)S(1)} %get-tuple-element.47.refs_8_), channel_id=1, source_target_pairs={{0,8},{1,9},{2,10},{3,11},{4,12},{5,13},{6,14},{7,15},{24,16},{25,... | collective-permute-start | bytes 1572872 | tf_op jit(solution)/shard_map/ppermute | solution.py:462
  49.4 4.1 %collective-permute-start.16 = (bf16[128,1024]{1,0:T(8,128)(2,1)S(1)}, bf16[128,1024]{1,0:T(8,128)(2,1)S(1)}, u32[]{:S(2)}, u32[]{:S(2)}) collective-permute-start(bf16[128,1024]{1,0:T(8,128)(2,1)S(1)} %collective-permute-done.9.refs_10_.refs_5_.refs_1_), channel_id=1, source_target_pairs={{0,1},{1,0},{2,3},{3,2},{4,5},{5,4},{6,7},{7,6},{8,9},{9,8},{10,11... | collective-permute-start | bytes 786440 | tf_op jit(solution)/shard_map/ppermute | solution.py:462
  52.4 1.7 %collective-permute-start.13 = (bf16[256,512]{1,0:T(8,128)(2,1)S(1)}, bf16[256,512]{1,0:T(8,128)(2,1)S(1)}, u32[]{:S(2)}, u32[]{:S(2)}) collective-permute-start(bf16[256,512]{1,0:T(8,128)(2,1)S(1)} %get-tuple-element.49), channel_id=1, source_target_pairs={{0,1},{1,0},{2,3},{3,2},{4,5},{5,4},{6,7},{7,6},{8,9},{9,8},{10,11... | collective-permute-start | bytes 786440 | tf_op jit(solution)/shard_map/ppermute | solution.py:462
  53.0 1.5 %collective-permute-start.14 = (bf16[256,512]{1,0:T(8,128)(2,1)S(1)}, bf16[256,512]{1,0:T(8,128)(2,1)S(1)}, u32[]{:S(2)}, u32[]{:S(2)}) collective-permute-start(bf16[256,512]{1,0:T(8,128)(2,1)S(1)} %get-tuple-element.50), channel_id=1, source_target_pairs={{0,1},{1,0},{2,3},{3,2},{4,5},{5,4},{6,7},{7,6},{8,9},{9,8},{10,11... | collective-permute-start | bytes 786440 | tf_op jit(solution)/shard_map/ppermute | solution.py:462
  53.1 1.8 %collective-permute-start.18 = (bf16[128,1024]{1,0:T(8,128)(2,1)S(1)}, bf16[128,1024]{1,0:T(8,128)(2,1)S(1)}, u32[]{:S(2)}, u32[]{:S(2)}) collective-permute-start(bf16[128,1024]{1,0:T(8,128)(2,1)S(1)} %collective-permute-done.11.refs_12_.refs_7_.refs_3_), channel_id=1, source_target_pairs={{0,1},{1,0},{2,3},{3,2},{4,5},{5,4},{6,7},{7,6},{8,9},{9,8},{10,11... | collective-permute-start | bytes 786440 | tf_op jit(solution)/shard_map/ppermute | solution.py:462
  56.4 18.8 %copy-start.7 = (bf16[128,2048]{1,0:T(8,128)(2,1)}, bf16[128,2048]{1,0:T(8,128)(2,1)S(1)}, u32[]{:S(2)}) copy-start(bf16[128,2048]{1,0:T(8,128)(2,1)S(1)} %get-tuple-element.52.refs_0_.refs_2_) | copy-start | bytes 1572868
  56.4 18.8 %copy-start.11 = (f32[128,512]{1,0:T(8,128)}, f32[128,512]{1,0:T(8,128)S(1)}, u32[]{:S(2)}) copy-start(f32[128,512]{1,0:T(8,128)S(1)} %get-tuple-element.51.part_ref) | copy-start | bytes 786436
  56.4 18.6 %collective-permute-start.21 = (bf16[128,2560]{1,0:T(8,128)(2,1)S(1)}, bf16[128,2560]{1,0:T(8,128)(2,1)S(1)}, u32[]{:S(2)}, u32[]{:S(2)}) collective-permute-start(bf16[128,2560]{1,0:T(8,128)(2,1)S(1)} %get-tuple-element.55), channel_id=1, source_target_pairs={{0,6},{1,7},{2,4},{3,5},{4,2},{5,3},{6,0},{7,1},{8,14},{9,15},{10,... | collective-permute-start | bytes 1966088 | tf_op jit(solution)/shard_map/ppermute | solution.py:462
  57.7 13.9 %collective-permute-start.24 = (bf16[256,1024]{1,0:T(8,128)(2,1)S(1)}, bf16[256,1024]{1,0:T(8,128)(2,1)S(1)}, u32[]{:S(2)}, u32[]{:S(2)}) collective-permute-start(bf16[256,1024]{1,0:T(8,128)(2,1)S(1)} %get-tuple-element.62), channel_id=1, source_target_pairs={{0,8},{1,9},{2,10},{3,11},{4,12},{5,13},{6,14},{7,15},{24,16},{25,... | collective-permute-start | bytes 1572872 | tf_op jit(solution)/shard_map/ppermute | solution.py:462
  61.4 13.6 %collective-permute-start.23 = (bf16[256,1024]{1,0:T(8,128)(2,1)S(1)}, bf16[256,1024]{1,0:T(8,128)(2,1)S(1)}, u32[]{:S(2)}, u32[]{:S(2)}) collective-permute-start(bf16[256,1024]{1,0:T(8,128)(2,1)S(1)} %relay.2), channel_id=1, source_target_pairs={{8,16},{9,17},{10,18},{11,19},{12,20},{13,21},{14,22},{15,23},{16,... | collective-permute-start | bytes 1572872 | tf_op jit(solution)/shard_map/ppermute | solution.py:462
  62.1 25.8 %collective-permute-start.19 = (bf16[128,2560]{1,0:T(8,128)(2,1)S(1)}, bf16[128,2560]{1,0:T(8,128)(2,1)S(1)}, u32[]{:S(2)}, u32[]{:S(2)}) collective-permute-start(bf16[128,2560]{1,0:T(8,128)(2,1)S(1)} %get-tuple-element.53), channel_id=1, source_target_pairs={{0,4},{1,5},{2,6},{3,7},{4,0},{5,1},{6,2},{7,3},{8,12},{9,13},{10,... | collective-permute-start | bytes 1966088 | tf_op jit(solution)/shard_map/ppermute | solution.py:462
  62.2 26.2 %collective-permute-start.20 = (bf16[128,2560]{1,0:T(8,128)(2,1)S(1)}, bf16[128,2560]{1,0:T(8,128)(2,1)S(1)}, u32[]{:S(2)}, u32[]{:S(2)}) collective-permute-start(bf16[128,2560]{1,0:T(8,128)(2,1)S(1)} %get-tuple-element.54), channel_id=1, source_target_pairs={{0,2},{1,3},{2,0},{3,1},{4,6},{5,7},{6,4},{7,5},{8,10},{9,11},{10,... | collective-permute-start | bytes 1966088 | tf_op jit(solution)/shard_map/ppermute | solution.py:462
  75.2 16.8 %copy-start = (bf16[1,128,8192]{2,1,0:T(8,128)(2,1)S(1)}, bf16[1,128,8192]{2,1,0:T(8,128)(2,1)}, u32[]{:S(2)}) copy-start(bf16[1,128,8192]{2,1,0:T(8,128)(2,1)} %param.8) | copy-start | bytes 6291460
  75.3 16.7 %copy-start.13 = (f32[8192]{0:T(1024)S(1)}, f32[8192]{0:T(1024)}, u32[]{:S(2)}) copy-start(f32[8192]{0:T(1024)} %param.9) | copy-start | bytes 98308
  75.3 13.2 %collective-permute-start.25 = (bf16[256,1024]{1,0:T(8,128)(2,1)S(1)}, bf16[256,1024]{1,0:T(8,128)(2,1)S(1)}, u32[]{:S(2)}, u32[]{:S(2)}) collective-permute-start(bf16[256,1024]{1,0:T(8,128)(2,1)S(1)} %get-tuple-element.63), channel_id=1, source_target_pairs={{0,8},{1,9},{2,10},{3,11},{4,12},{5,13},{6,14},{7,15},{8,0},{9,1},... | collective-permute-start | bytes 1572872 | tf_op jit(solution)/shard_map/ppermute | solution.py:462
  77.9 10.6 %collective-permute-start.26 = (bf16[256,1024]{1,0:T(8,128)(2,1)S(1)}, bf16[256,1024]{1,0:T(8,128)(2,1)S(1)}, u32[]{:S(2)}, u32[]{:S(2)}) collective-permute-start(bf16[256,1024]{1,0:T(8,128)(2,1)S(1)} %get-tuple-element.64), channel_id=1, source_target_pairs={{8,16},{9,17},{10,18},{11,19},{12,20},{13,21},{14,22},{15,23},{16,... | collective-permute-start | bytes 1572872 | tf_op jit(solution)/shard_map/ppermute | solution.py:462
  89.2 0.8 copy-start.4
  90.1 0.8 copy-start.9
  90.9 11.6 %collective-permute-start.27 = (bf16[128,1024]{1,0:T(8,128)(2,1)}, bf16[128,1024]{1,0:T(8,128)(2,1)}, u32[]{:S(2)}, u32[]{:S(2)}) collective-permute-start(bf16[128,1024]{1,0:T(8,128)(2,1)} %get-tuple-element.65), channel_id=1, source_target_pairs={{0,4},{1,5},{2,6},{3,7},{4,0},{5,1},{6,2},{7,3},{8,12},{9,13},{10,... | collective-permute-start | bytes 786440 | tf_op jit(solution)/shard_map/ppermute | solution.py:462
  92.0 1.1 %copy-start.5 = (bf16[128,2560]{1,0:T(8,128)(2,1)S(1)}, bf16[128,2560]{1,0:T(8,128)(2,1)}, u32[]{:S(2)}) copy-start(bf16[128,2560]{1,0:T(8,128)(2,1)} %copy-done.4) | copy-start | bytes 1966084
  93.1 1.0 copy-start.8
  94.1 0.9 copy-start.12
  95.1 3.6 %copy-start.1 = (f32[1,128,2048]{2,1,0:T(8,128)S(1)}, f32[1,128,2048]{2,1,0:T(8,128)}, u32[]{:S(2)}) copy-start(f32[1,128,2048]{2,1,0:T(8,128)} %param.13) | copy-start | bytes 3145732
  95.1 3.6 %copy-start.2 = (f32[1,128,2048]{2,1,0:T(8,128)S(1)}, f32[1,128,2048]{2,1,0:T(8,128)}, u32[]{:S(2)}) copy-start(f32[1,128,2048]{2,1,0:T(8,128)} %param.14) | copy-start | bytes 3145732
  95.1 3.6 %copy-start.3 = (f32[1,128,2048]{2,1,0:T(8,128)S(1)}, f32[1,128,2048]{2,1,0:T(8,128)}, u32[]{:S(2)}) copy-start(f32[1,128,2048]{2,1,0:T(8,128)} %param.15) | copy-start | bytes 3145732
  95.1 3.6 %copy-start.10 = (f32[128,1024]{1,0:T(8,128)S(1)}, f32[128,1024]{1,0:T(8,128)}, u32[]{:S(2)}) copy-start(f32[128,1024]{1,0:T(8,128)} %copy-done.9) | copy-start | bytes 1572868
  98.7 1.6 %copy-start.6 = (bf16[128,8192]{1,0:T(8,128)(2,1)S(1)}, bf16[128,8192]{1,0:T(8,128)(2,1)}, u32[]{:S(2)}) copy-start(bf16[128,8192]{1,0:T(8,128)(2,1)} %get-tuple-element.57.refs_4_) | copy-start | bytes 6291460

commit v8 on v6

--- a/solution.py
+++ b/solution.py
@@ -64,7 +64,11 @@
         compiler_params=limit(24),
         cost_estimate=cost(8 * rows * model, 6 * rows * model),
         name="norm_blocks",
-    )(tokens, far, gain)
+    )(
+        pltpu.with_memory_space_constraint(tokens, pltpu.HBM),
+        far,
+        pltpu.with_memory_space_constraint(gain, pltpu.HBM),
+    )
     return [outs[i : i + parts] for i in range(0, len(outs), parts)]
 
 
@@ -81,12 +85,15 @@
         out_shape=[jax.ShapeDtypeStruct((w_t.shape[0], width), bf16)] * 2,
         compiler_params=limit(16),
         name="halves",
-    )(w_t)
+    )(pltpu.with_memory_space_constraint(w_t, pltpu.HBM))
 
 
 def stack_kernel(count, *refs):
     out_refs = refs[-(len(refs) - count) :]
     rows = refs[0].shape[0]
+    if len(out_refs) == 3:
+        stack_kernel(count, *refs[:count], out_refs[2])
+        out_refs = out_refs[:2]
     each = out_refs[0].shape[0] // rows
     for i, ref in enumerate(refs[:count]):
         out_refs[i // each][i % each * rows : (i % each + 1) * rows, :] = ref[...]
@@ -99,7 +106,8 @@
         lambda *refs: stack_kernel(count, *refs[:count], *refs[count + len(after) :]),
         in_specs=[pl.BlockSpec(memory_space=pltpu.VMEM)] * count
         + [pl.BlockSpec(memory_space=pl.ANY)] * len(after),
-        out_shape=[jax.ShapeDtypeStruct((count // outs * rows, width), bf16)] * outs,
+        out_shape=[jax.ShapeDtypeStruct((count // outs * rows, width), bf16)] * outs
+        + [jax.ShapeDtypeStruct((count * rows, width), bf16)] * (outs > 1),
         compiler_params=limit(16),
         name="stack",
     )(*pieces, *after)
@@ -140,7 +148,7 @@
 
 def weight_kernel(planes, chips, plan, *refs):
     sel_ref, refs = refs[0], refs[1:]
-    grad_refs, refs = refs[:4], refs[4:]
+    grad_refs, refs = [*refs[:2], refs[2].at[: refs[0].shape[0]], refs[2].at[refs[0].shape[0] :]], refs[3:]
     pieces, refs = refs[:chips], refs[chips:]
     out_refs, (held, base) = refs[-len(plan) - 3 : -2], refs[-2:]
     rows = pieces[0].shape[1]
@@ -187,7 +195,7 @@
     block = slots_all // planes
     return pl.pallas_call(
         functools.partial(weight_kernel, planes, chips, plan),
-        in_specs=[pl.BlockSpec(memory_space=pltpu.VMEM)] * (5 + chips)
+        in_specs=[pl.BlockSpec(memory_space=pltpu.VMEM)] * (4 + chips)
         + [pl.BlockSpec(memory_space=pl.ANY)] * len(after),
         out_shape=[jax.ShapeDtypeStruct((block, width), bf16)] * (len(plan) + 1),
         scratch_shapes=[
@@ -217,22 +225,20 @@
     half = chips // 2
     part_width = held.shape[1] // parts
     gather_weight(refs[:planes], held)
-    for core in (1, 0):
-        for k in range(chips):
-            total = None
-            for part in range(parts):
-                term = lax.dot_general(
-                    piece_refs[k * parts + part][core],
-                    held[:, part * part_width : (part + 1) * part_width],
-                    (((1,), (1,)), ((), ())),
-                    preferred_element_type=f32,
-                )
-                total = term if total is None else total + term
-            if core:
-                at = k % half * rows
-                far_refs[k // half][at : at + rows, :] = total.astype(bf16)
-            else:
-                out_ref[k * rows : (k + 1) * rows, :] = total
+    for k in range(chips):
+        total = None
+        for part in range(parts):
+            piece = piece_refs[k * parts + part][...]
+            term = lax.dot_general(
+                piece.reshape(2 * rows, part_width),
+                held[:, part * part_width : (part + 1) * part_width],
+                (((1,), (1,)), ((), ())),
+                preferred_element_type=f32,
+            )
+            total = term if total is None else total + term
+        out_ref[k * rows : (k + 1) * rows, :] = total[:rows]
+        at = k % half * rows
+        far_refs[k // half][at : at + rows, :] = total[rows:].astype(bf16)
 
 
 def value_parts(pieces, weights, feats, after):
@@ -267,13 +273,12 @@
             out_refs[k][:, 2 * width :] = total.astype(bf16)
     for j in range(2):
         gather_weight(weight_refs[j * planes : (j + 1) * planes], held)
-        for k in range(chips):
-            grads_ref = grads_b_ref if k // half else grads_a_ref
-            out_refs[k][:, j * width : (j + 1) * width] = jnp.dot(
-                grads_ref[k % half * rows : (k % half + 1) * rows, :],
-                held[...],
-                preferred_element_type=f32,
-            ).astype(bf16)
+        for i, grads_ref in enumerate((grads_a_ref, grads_b_ref)):
+            block = jnp.dot(grads_ref[...], held[...], preferred_element_type=f32).astype(bf16)
+            for k in range(half):
+                out_refs[i * half + k][:, j * width : (j + 1) * width] = block[
+                    k * rows : (k + 1) * rows, :
+                ]
 
 
 def back_blocks(grads, sums, weights, chips):
@@ -482,17 +487,19 @@
 
     tokens_far = to_core(tokens)
     grads = [value_grad] + [to_chip(value_grad, k) for k in range(chips - 1, 0, -1)][::-1]
+
     w_keep, w_send = halves(w_t, width)
     w_got = to_x(w_send)
 
     gain_row, owner_row = gain[None, :], owner[None, :]
     sent = norm_blocks(tokens, tokens_far, gain_row, chips, width, parts)
-    grads = stack(grads, 2, sent[0][:1])
+    grads = stack(grads, 2, [sent[0][0], w_keep])
     pieces = [sent[0]] + [[to_chip(p, k) for p in sent[k]] for k in range(1, chips)]
-    grads_far = [to_core(g) for g in grads]
+    grads_far = [to_core(grads[-1])]
+    grads = grads[:2]
     selected = select_rows(owner_row, groups, slots, (sent[0][0],))
 
-    weights = stack([w_keep, w_got], 1, grads[:1])
+    weights = stack([w_keep, w_got], 1, grads_far[:1])
     turn = planes // 2
     while turn:
         weights = [w for value in weights for w in (value, to_plane(value, turn))]
@@ -505,38 +512,42 @@
         for even in (True, False)
         if any(busy(z, step, even) for z in range(planes))
     ]
+    outs = []
+    for part in range(parts):
+        outs.append(
+            weight_blocks(
+                selected,
+                [*grads, *grads_far],
+                [piece[part] for piece in pieces],
+                planes,
+                plan,
+                weights if part == parts - 1 else [],
+            )
+        )
+
+    *far_sums, near_sum = value_parts(pieces, weights, feats, outs[-1][:1])
+    sums = [near_sum] + [to_core(f) for f in far_sums]
+    back = back_blocks(grads, sums, weights + weights_far, chips)
+    home = [back[0]] + [to_chip(back[k], k) for k in range(1, chips)]
+
     kept, got = [], []
     for part in range(parts):
-        outs = weight_blocks(
-            selected,
-            [*grads, *grads_far],
-            [piece[part] for piece in pieces],
-            planes,
-            plan,
-            weights[:1] if part == parts - 1 else [],
-        )
-        ready = dict(zip(plan, outs))
-        if part == parts - 1:
-            *far_sums, near_sum = value_parts(pieces, weights, feats, outs[:1])
-            sums = [near_sum] + [to_core(f) for f in far_sums]
-            back = back_blocks(grads, sums, weights + weights_far, chips)
-            home = [back[0]] + [to_chip(back[k], k) for k in range(1, chips)]
-        held = {}
+        ready, held = dict(zip(plan, outs[part])), {}
+        final = part == parts - 1
         for step in range(1, planes):
             here = [even for even in (True, False) if (step, even) in ready]
-            send = [ready[step, even] for even in here]
-            if held:
-                sums = [[ready[step, even], held[not even]] for even in here if (not even) in held]
-                if sums:
-                    sums = list(relay(sums, back[:1] if step == 2 else home[-1:]))
-                send = []
-                for even in here:
-                    send.append(sums.pop(0) if (not even) in held else ready[step, even])
+            sums = [[ready[step, even], held[not even]] for even in here if (not even) in held]
+            if sums:
+                after = (back[:1] if step == 2 else home[-1:]) if final else []
+                sums = list(relay(sums, after))
+            send = [
+                sums.pop(0) if (not even) in held else ready[step, even] for even in here
+            ]
             held = {even: across(value, step, even) for even, value in zip(here, send)}
-        keep, send = finish(outs[-1], held[True], held[False], home[1:])
+        after = home[1:] if final else []
+        keep, send = finish(outs[part][-1], held[True], held[False], after)
         kept.append(keep)
         got.append(to_x(send))
-
     grad_x, values = grad_x_blocks(tokens, gain_row, back[-1], home)
 
     states = adam(owner_row, kept, got, (master[0], moment1[0], moment2[0]), rows * seqs * groups)

time: 101 us -> 96.8 us (0.958)
  local copies, waits for them, and re-layouts: 3.34 us -> 0.04 us
  waiting for transfers between devices: 49.1 us -> 46.8 us
  Pallas kernels: 16.4 us -> 17.5 us
    unnamed x20 -> x14, local copies, waits for them, and re-layouts: 3.34 us -> 0.04 us
    ppermute x28 -> x27, waiting for transfers between devices: 49.1 us -> 46.8 us  [permute(): return lax.ppermute(value, ('dp', 'seq'), pairs)]
    pallas_call x1, Pallas kernels: 1.66 us -> 3.42 us  [norm_blocks(): pl.pallas_call(functools.partial(norm_kernel, parts), grid=(rows // step,...]
    pallas_call x1, Pallas kernels: 2.98 us -> 1.37 us  [value_parts(): pl.pallas_call(functools.partial(value_kernel, len(weights), chips, parts...]
    ppermute x28 -> x27, starting transfers between devices: 30.8 us -> 31.3 us  [permute(): return lax.ppermute(value, ('dp', 'seq'), pairs)]
  transfers between devices with their start and end apart: 28 -> 27, of which waited for: 15 -> 13; matrix products, arithmetic and copies ran while one was open for 0% -> 0% of each run, Pallas kernels for 14% -> 15%
where the time goes in v8:
time: 96.8 us; the launch traced here: 96.5 us
  waiting for transfers between devices  46.8 us (48%)
  starting transfers between devices  31.3 us (32%)
  Pallas kernels  17.5 us (18%)
    ppermute x27, waiting for transfers between devices, permute(): return lax.ppermute(value, ('dp', 'seq'), pairs)  46.8 us
    ppermute x27, starting transfers between devices, permute(): return lax.ppermute(value, ('dp', 'seq'), pairs)  31.3 us
    pallas_call x1, Pallas kernels, grad_x_blocks(): pl.pallas_call(grad_x_kernel, grid=(rows // step,), in_specs=[pl.BlockSpe...  3.62 us
    pallas_call x1, Pallas kernels, norm_blocks(): pl.pallas_call(functools.partial(norm_kernel, parts), grid=(rows // step,...  3.42 us
    pallas_call x1, Pallas kernels, weight_blocks(): pl.pallas_call(functools.partial(weight_kernel, planes, chips, plan), in_...  3.02 us
    pallas_call x1, Pallas kernels, adam(): pl.pallas_call(functools.partial(adam_kernel, token_total, len(kept)), gr...  2.6 us
  transfers between devices with their start and end apart: 27, of which 13 were waited for; matrix products, arithmetic and copies ran while one was open for 0% of the time, Pallas kernels for 15%

profile of v8, /device:TPU:0, one launch (start us, length us, event | category | flops | bytes accessed | tf_op | source)
XLA Modules:
  0.0 96.5 jit_solution(12938109539000327960)
XLA Ops:
  0.6 0.5 collective-permute-start.3
  1.1 3.5 %collective-permute-start.2 = (bf16[128,512]{1,0:T(8,128)(2,1)}, bf16[128,512]{1,0:T(8,128)(2,1)S(1)}, u32[]{:S(2)}, u32[]{:S(2)}) collective-permute-start(bf16[128,512]{1,0:T(8,128)(2,1)} %bitcast.20), channel_id=1, source_target_pairs={{0,6},{1,7},{2,4},{3,5},{4,2},{5,3},{6,0},{7,1},{8,14},{9,15},{10,... | collective-permute-start | bytes 393224 | tf_op jit(solution)/shard_map/ppermute | solution.py:462
  4.7 0.5 collective-permute-start.1
  5.2 0.1 collective-permute-start
  5.3 1.0 %halves.1 = (bf16[64,1024]{1,0:T(8,128)(2,1)S(1)}, bf16[64,1024]{1,0:T(8,128)(2,1)S(1)}) custom-call(bf16[64,2048]{1,0:T(8,128)(2,1)} %w_ref.1), custom_call_target="tpu_custom_call" | custom-call | tf_op jit(solution)/shard_map/halves/pallas_call | solution.py:83
  6.3 3.4 %norm_blocks.1 = (bf16[2,128,1024]{2,1,0:T(8,128)(2,1)S(1)}, bf16[2,128,1024]{2,1,0:T(8,128)(2,1)S(1)}, bf16[2,128,1024]{2,1,0:T(8,128)(2,1)S(1)}, bf16[2,128,1024]{2,1,0:T(8,128)(2,1)S(1)}) custom-call(bf16[128,8192]{1,0:T(8,128)(2,1)} %bitcast.13, bf16[128,8192]{1,0:T(8,128)(2,1)S(1)} %collective-permute-done.3.far_ref, f32[1,8192]{1,0:T(1,128)} %bitcast.18), custom_call_target="tpu_custom_call" | custom-call | flops 8388608 | bytes 6291456 | tf_op jit(solution)/shard_map/norm_blocks/pallas_call | solution.py:54
  9.8 2.0 %collective-permute-done.1.refs_2_ = bf16[128,512]{1,0:T(8,128)(2,1)S(1)} collective-permute-done((bf16[128,512]{1,0:T(8,128)(2,1)}, bf16[128,512]{1,0:T(8,128)(2,1)S(1)}, u32[]{:S(2)}, u32[]{:S(2)}) %collective-permute-start.1) | collective-permute-done | bytes 131104 | tf_op jit(solution)/shard_map/ppermute | solution.py:462
  11.8 0.3 collective-permute-done.refs_1_
  12.2 1.6 %collective-permute-start.7 = (bf16[64,1024]{1,0:T(8,128)(2,1)S(1)}, bf16[64,1024]{1,0:T(8,128)(2,1)S(1)}, u32[]{:S(2)}, u32[]{:S(2)}) collective-permute-start(bf16[64,1024]{1,0:T(8,128)(2,1)S(1)} %get-tuple-element.44), channel_id=1, source_target_pairs={{0,4},{1,5},{2,6},{3,7},{4,0},{5,1},{6,2},{7,3},{8,12},{9,13},{10,... | collective-permute-start | bytes 393224 | tf_op jit(solution)/shard_map/ppermute | solution.py:462
  13.8 0.5 collective-permute-start.4
  14.3 1.4 %collective-permute-start.5 = (bf16[2,128,1024]{2,1,0:T(8,128)(2,1)S(1)}, bf16[2,128,1024]{2,1,0:T(8,128)(2,1)S(1)}, u32[]{:S(2)}, u32[]{:S(2)}) collective-permute-start(bf16[2,128,1024]{2,1,0:T(8,128)(2,1)S(1)} %get-tuple-element.42), channel_id=1, source_target_pairs={{0,2},{1,3},{2,0},{3,1},{4,6},{5,7},{6,4},{7,5},{8,10},{9,11},{10,... | collective-permute-start | bytes 1572872 | tf_op jit(solution)/shard_map/ppermute | solution.py:462
  15.8 1.5 %collective-permute-start.6 = (bf16[2,128,1024]{2,1,0:T(8,128)(2,1)S(1)}, bf16[2,128,1024]{2,1,0:T(8,128)(2,1)S(1)}, u32[]{:S(2)}, u32[]{:S(2)}) collective-permute-start(bf16[2,128,1024]{2,1,0:T(8,128)(2,1)S(1)} %get-tuple-element.43), channel_id=1, source_target_pairs={{0,6},{1,7},{2,4},{3,5},{4,2},{5,3},{6,0},{7,1},{8,14},{9,15},{10,... | collective-permute-start | bytes 1572872 | tf_op jit(solution)/shard_map/ppermute | solution.py:462
  17.3 1.3 %collective-permute-done.7.refs_1_ = bf16[64,1024]{1,0:T(8,128)(2,1)S(1)} collective-permute-done((bf16[64,1024]{1,0:T(8,128)(2,1)S(1)}, bf16[64,1024]{1,0:T(8,128)(2,1)S(1)}, u32[]{:S(2)}, u32[]{:S(2)}) %collective-permute-start.7) | collective-permute-done | bytes 131104 | tf_op jit(solution)/shard_map/ppermute | solution.py:462
  18.6 2.7 %collective-permute-start.10 = (bf16[128,1024]{1,0:T(8,128)(2,1)S(1)}, bf16[128,1024]{1,0:T(8,128)(2,1)S(1)}, u32[]{:S(2)}, u32[]{:S(2)}) collective-permute-start(bf16[128,1024]{1,0:T(8,128)(2,1)S(1)} %stack.3.refs_8_.refs_4_.refs_0_), channel_id=1, source_target_pairs={{0,16},{1,17},{2,18},{3,19},{4,20},{5,21},{6,22},{7,23},{8,24},{9,... | collective-permute-start | bytes 786440 | tf_op jit(solution)/shard_map/ppermute | solution.py:462
  21.3 1.6 %collective-permute-start.9 = (bf16[128,1024]{1,0:T(8,128)(2,1)S(1)}, bf16[128,1024]{1,0:T(8,128)(2,1)S(1)}, u32[]{:S(2)}, u32[]{:S(2)}) collective-permute-start(bf16[128,1024]{1,0:T(8,128)(2,1)S(1)} %stack.3.refs_8_.refs_4_.refs_0_), channel_id=1, source_target_pairs={{0,8},{1,9},{2,10},{3,11},{4,12},{5,13},{6,14},{7,15},{8,0},{9,1},... | collective-permute-start | bytes 786440 | tf_op jit(solution)/shard_map/ppermute | solution.py:462
  22.9 9.9 %collective-permute-done.10.refs_10_.refs_6_.refs_2_ = bf16[128,1024]{1,0:T(8,128)(2,1)S(1)} collective-permute-done((bf16[128,1024]{1,0:T(8,128)(2,1)S(1)}, bf16[128,1024]{1,0:T(8,128)(2,1)S(1)}, u32[]{:S(2)}, u32[]{:S(2)}) %collective-permute-start.10) | collective-permute-done | bytes 262176 | tf_op jit(solution)/shard_map/ppermute | solution.py:462
  32.7 0.6 collective-permute-start.11
  33.3 0.5 select_rows.1.refs_0_
  33.9 0.5 collective-permute-start.16
  34.4 7.1 %collective-permute-done.6.refs_7_.refs_3_ = bf16[2,128,1024]{2,1,0:T(8,128)(2,1)S(1)} collective-permute-done((bf16[2,128,1024]{2,1,0:T(8,128)(2,1)S(1)}, bf16[2,128,1024]{2,1,0:T(8,128)(2,1)S(1)}, u32[]{:S(2)}, u32[]{:S(2)}) %collective-permute-start.6) | collective-permute-done | bytes 524320 | tf_op jit(solution)/shard_map/ppermute | solution.py:462
  41.5 3.0 %weight_blocks.1 = (bf16[256,1024]{1,0:T(8,128)(2,1)S(1)}, bf16[256,1024]{1,0:T(8,128)(2,1)S(1)}, bf16[256,1024]{1,0:T(8,128)(2,1)S(1)}, bf16[256,1024]{1,0:T(8,...) custom-call(bf16[1024,512]{1,0:T(8,128)(2,1)S(1)} %select_rows.1.refs_0_, ...), custom_call_target="tpu_custom_call" | custom-call | flops 2147483648 | bytes 4194304 | tf_op jit(solution)/shard_map/weight_blocks/pallas_call | solution.py:196
  44.5 3.5 %collective-permute-start.21 = (bf16[256,1024]{1,0:T(8,128)(2,1)S(1)}, bf16[256,1024]{1,0:T(8,128)(2,1)S(1)}, u32[]{:S(2)}, u32[]{:S(2)}) collective-permute-start(bf16[256,1024]{1,0:T(8,128)(2,1)S(1)} %get-tuple-element.46.refs_8_), channel_id=1, source_target_pairs={{0,8},{1,9},{2,10},{3,11},{4,12},{5,13},{6,14},{7,15},{24,16},{25,... | collective-permute-start | bytes 1572872 | tf_op jit(solution)/shard_map/ppermute | solution.py:462
  48.1 1.4 %value_parts.1 = (bf16[256,512]{1,0:T(8,128)(2,1)S(1)}, bf16[256,512]{1,0:T(8,128)(2,1)S(1)}, f32[512,512]{1,0:T(8,128)S(1)}) custom-call(bf16[2,128,1024]{2,1,0:T(8,128)(2,1)S(1)} %get-tuple-element.37.refs_4_.refs_0_, bf16[2,128,1024]{2,1,0:T(8,128)(2,1)S(1)} %collective-permute-done.4.refs_5_.refs_1_, ...), custom_call_target="tpu_custom_call" | custom-call | tf_op jit(solution)/shard_map/value_parts/pallas_call | solution.py:248
  49.5 0.6 collective-permute-start.12
  50.1 0.1 collective-permute-start.17
  50.2 0.4 collective-permute-start.13
  50.6 1.0 %collective-permute-done.17.refs_7_ = bf16[128,1024]{1,0:T(8,128)(2,1)S(1)} collective-permute-done((bf16[128,1024]{1,0:T(8,128)(2,1)S(1)}, bf16[128,1024]{1,0:T(8,128)(2,1)S(1)}, u32[]{:S(2)}, u32[]{:S(2)}) %collective-permute-start.17) | collective-permute-done | bytes 262176 | tf_op jit(solution)/shard_map/ppermute | solution.py:462
  51.6 0.4 collective-permute-done.13.got_b_ref
  52.0 1.4 %back_blocks.1 = (bf16[128,2048]{1,0:T(8,128)(2,1)S(1)}, bf16[128,2560]{1,0:T(8,128)(2,1)S(1)}, bf16[128,2560]{1,0:T(8,128)(2,1)S(1)}, bf16[128,2560]{1,0:T(8,128)(2,1)S(1)}, f32[128,512]{1,0:T(8,128)S(1)}) custom-call(bf16[256,512]{1,0:T(8,128)(2,1)S(1)} %get-tuple-element.39.refs_1_.grads_a_ref, ...), custom_call_target="tpu_custom_call" | custom-call | tf_op jit(solution)/shard_map/back_blocks/pallas_call | solution.py:287
  53.4 1.6 %collective-permute-start.20 = (bf16[128,2560]{1,0:T(8,128)(2,1)S(1)}, bf16[128,2560]{1,0:T(8,128)(2,1)S(1)}, u32[]{:S(2)}, u32[]{:S(2)}) collective-permute-start(bf16[128,2560]{1,0:T(8,128)(2,1)S(1)} %get-tuple-element.54), channel_id=1, source_target_pairs={{0,6},{1,7},{2,4},{3,5},{4,2},{5,3},{6,0},{7,1},{8,14},{9,15},{10,... | collective-permute-start | bytes 1966088 | tf_op jit(solution)/shard_map/ppermute | solution.py:462
  55.0 1.3 %collective-permute-start.23 = (bf16[256,1024]{1,0:T(8,128)(2,1)S(1)}, bf16[256,1024]{1,0:T(8,128)(2,1)S(1)}, u32[]{:S(2)}, u32[]{:S(2)}) collective-permute-start(bf16[256,1024]{1,0:T(8,128)(2,1)S(1)} %get-tuple-element.61), channel_id=1, source_target_pairs={{0,8},{1,9},{2,10},{3,11},{4,12},{5,13},{6,14},{7,15},{24,16},{25,... | collective-permute-start | bytes 1572872 | tf_op jit(solution)/shard_map/ppermute | solution.py:462
  56.4 4.0 %collective-permute-done.21.refs_1_ = bf16[256,1024]{1,0:T(8,128)(2,1)S(1)} collective-permute-done((bf16[256,1024]{1,0:T(8,128)(2,1)S(1)}, bf16[256,1024]{1,0:T(8,128)(2,1)S(1)}, u32[]{:S(2)}, u32[]{:S(2)}) %collective-permute-start.21) | collective-permute-done | bytes 524320 | tf_op jit(solution)/shard_map/ppermute | solution.py:462
  60.4 0.1 relay.2
  60.5 0.7 collective-permute-start.22
  61.2 0.9 collective-permute-start.18
  62.0 1.3 %collective-permute-start.19 = (bf16[128,2560]{1,0:T(8,128)(2,1)S(1)}, bf16[128,2560]{1,0:T(8,128)(2,1)S(1)}, u32[]{:S(2)}, u32[]{:S(2)}) collective-permute-start(bf16[128,2560]{1,0:T(8,128)(2,1)S(1)} %get-tuple-element.53), channel_id=1, source_target_pairs={{0,2},{1,3},{2,0},{3,1},{4,6},{5,7},{6,4},{7,5},{8,10},{9,11},{10,... | collective-permute-start | bytes 1966088 | tf_op jit(solution)/shard_map/ppermute | solution.py:462
  63.4 6.9 %collective-permute-done.23.refs_3_ = bf16[256,1024]{1,0:T(8,128)(2,1)S(1)} collective-permute-done((bf16[256,1024]{1,0:T(8,128)(2,1)S(1)}, bf16[256,1024]{1,0:T(8,128)(2,1)S(1)}, u32[]{:S(2)}, u32[]{:S(2)}) %collective-permute-start.23) | collective-permute-done | bytes 524320 | tf_op jit(solution)/shard_map/ppermute | solution.py:462
  70.3 1.7 %collective-permute-done.20.refs_3_.refs_4_.refs_2_ = bf16[128,2560]{1,0:T(8,128)(2,1)S(1)} collective-permute-done((bf16[128,2560]{1,0:T(8,128)(2,1)S(1)}, bf16[128,2560]{1,0:T(8,128)(2,1)S(1)}, u32[]{:S(2)}, u32[]{:S(2)}) %collective-permute-start.20) | collective-permute-done | bytes 655392 | tf_op jit(solution)/shard_map/ppermute | solution.py:462
  72.0 0.2 relay.3
  72.3 4.2 %collective-permute-start.24 = (bf16[256,1024]{1,0:T(8,128)(2,1)S(1)}, bf16[256,1024]{1,0:T(8,128)(2,1)S(1)}, u32[]{:S(2)}, u32[]{:S(2)}) collective-permute-start(bf16[256,1024]{1,0:T(8,128)(2,1)S(1)} %get-tuple-element.62), channel_id=1, source_target_pairs={{0,8},{1,9},{2,10},{3,11},{4,12},{5,13},{6,14},{7,15},{8,0},{9,1},... | collective-permute-start | bytes 1572872 | tf_op jit(solution)/shard_map/ppermute | solution.py:462
  76.4 0.7 collective-permute-start.25
  77.1 7.5 %collective-permute-done.18.refs_1_.refs_0_ = bf16[128,2560]{1,0:T(8,128)(2,1)S(1)} collective-permute-done((bf16[128,2560]{1,0:T(8,128)(2,1)S(1)}, bf16[128,2560]{1,0:T(8,128)(2,1)S(1)}, u32[]{:S(2)}, u32[]{:S(2)}) %collective-permute-start.18) | collective-permute-done | bytes 655392 | tf_op jit(solution)/shard_map/ppermute | solution.py:462
  84.6 0.8 collective-permute-done.19.refs_2_.refs_1_
  85.5 0.2 finish.1
  85.6 0.9 collective-permute-start.26
  86.5 3.6 %grad_x_blocks.1 = (bf16[128,8192]{1,0:T(8,128)(2,1)}, bf16[128,512]{1,0:T(8,128)(2,1)}) custom-call(bf16[128,8192]{1,0:T(8,128)(2,1)S(1)} %bitcast.14, f32[1,8192]{1,0:T(1,128)S(1)} %bitcast.19, f32[128,512]{1,0:T(8,128)S(1)} %get-tuple-element.50.part_ref, bf16[128,2048]{1,0:T(8,128)(2,1)S(1)} %get-tuple-element.51.refs_0_.refs_2_, ...), custom_call_target="tpu_custom_call" | custom-call | flops 16777216 | bytes 6291456 | tf_op jit(solution)/shard_map/grad_x_blocks/pallas_call | solution.py:330
  90.1 3.8 %collective-permute-done.26.refs_1_ = bf16[128,1024]{1,0:T(8,128)(2,1)S(1)} collective-permute-done((bf16[128,1024]{1,0:T(8,128)(2,1)S(1)}, bf16[128,1024]{1,0:T(8,128)(2,1)S(1)}, u32[]{:S(2)}, u32[]{:S(2)}) %collective-permute-start.26) | collective-permute-done | bytes 262176 | tf_op jit(solution)/shard_map/ppermute | solution.py:462
  93.9 2.6 %adam.1 = (f32[128,2048]{1,0:T(8,128)}, f32[128,2048]{1,0:T(8,128)}, f32[128,2048]{1,0:T(8,128)}) custom-call(s32[1,512]{1,0:T(1,128)S(1)} %bitcast.25, f32[128,1024]{1,0:T(8,128)S(1)} %get-tuple-element.64.refs_0_, bf16[128,1024]{1,0:T(8,128)(2,1)S(1)} %collective-permute-done.26.refs_1_, f32[128,2048]{1,0:T(8,128)S(1)} %bitcast.15, ...), custom_call_target="tpu_custom_call" | custom-call | flops 5242880 | bytes 7864320 | tf_op jit(solution)/shard_map/adam/pallas_call | solution.py:430
  (33 shorter events, 0.4 us)
Async XLA Ops:
  0.6 5.7 %collective-permute-start.3 = (bf16[128,8192]{1,0:T(8,128)(2,1)}, bf16[128,8192]{1,0:T(8,128)(2,1)S(1)}, u32[]{:S(2)}, u32[]{:S(2)}) collective-permute-start(bf16[128,8192]{1,0:T(8,128)(2,1)} %bitcast.12), channel_id=1, source_target_pairs={{0,1},{1,0},{2,3},{3,2},{4,5},{5,4},{6,7},{7,6},{8,9},{9,8},{10,11... | collective-permute-start | bytes 6291464 | tf_op jit(solution)/shard_map/ppermute | solution.py:462
  1.1 8.6 %collective-permute-start.2 = (bf16[128,512]{1,0:T(8,128)(2,1)}, bf16[128,512]{1,0:T(8,128)(2,1)S(1)}, u32[]{:S(2)}, u32[]{:S(2)}) collective-permute-start(bf16[128,512]{1,0:T(8,128)(2,1)} %bitcast.20), channel_id=1, source_target_pairs={{0,6},{1,7},{2,4},{3,5},{4,2},{5,3},{6,0},{7,1},{8,14},{9,15},{10,... | collective-permute-start | bytes 393224 | tf_op jit(solution)/shard_map/ppermute | solution.py:462
  4.7 7.1 %collective-permute-start.1 = (bf16[128,512]{1,0:T(8,128)(2,1)}, bf16[128,512]{1,0:T(8,128)(2,1)S(1)}, u32[]{:S(2)}, u32[]{:S(2)}) collective-permute-start(bf16[128,512]{1,0:T(8,128)(2,1)} %bitcast.21), channel_id=1, source_target_pairs={{0,2},{1,3},{2,0},{3,1},{4,6},{5,7},{6,4},{7,5},{8,10},{9,11},{10,... | collective-permute-start | bytes 393224 | tf_op jit(solution)/shard_map/ppermute | solution.py:462
  5.2 6.9 %collective-permute-start = (bf16[128,512]{1,0:T(8,128)(2,1)}, bf16[128,512]{1,0:T(8,128)(2,1)S(1)}, u32[]{:S(2)}, u32[]{:S(2)}) collective-permute-start(bf16[128,512]{1,0:T(8,128)(2,1)} %bitcast.22), channel_id=1, source_target_pairs={{0,4},{1,5},{2,6},{3,7},{4,0},{5,1},{6,2},{7,3},{8,12},{9,13},{10,... | collective-permute-start | bytes 393224 | tf_op jit(solution)/shard_map/ppermute | solution.py:462
  6.3 5.8 %copy-start.5 = (bf16[1,128,512]{2,1,0:T(8,128)(2,1)S(1)}, bf16[1,128,512]{2,1,0:T(8,128)(2,1)}, u32[]{:S(2)}) copy-start(bf16[1,128,512]{2,1,0:T(8,128)(2,1)} %param.11) | copy-start | bytes 393220
  9.7 23.6 %copy-start.6 = (s32[512]{0:T(512)S(1)}, s32[512]{0:T(512)}, u32[]{:S(2)}) copy-start(s32[512]{0:T(512)} %param.12) | copy-start | bytes 6148
  12.2 6.4 %collective-permute-start.8 = (bf16[512,512]{1,0:T(8,128)(2,1)S(1)}, bf16[512,512]{1,0:T(8,128)(2,1)S(1)}, u32[]{:S(2)}, u32[]{:S(2)}) collective-permute-start(bf16[512,512]{1,0:T(8,128)(2,1)S(1)} %get-tuple-element.45), channel_id=1, source_target_pairs={{0,1},{1,0},{2,3},{3,2},{4,5},{5,4},{6,7},{7,6},{8,9},{9,8},{10,11... | collective-permute-start | bytes 1572872 | tf_op jit(solution)/shard_map/ppermute | solution.py:462
  12.2 6.4 %collective-permute-start.7 = (bf16[64,1024]{1,0:T(8,128)(2,1)S(1)}, bf16[64,1024]{1,0:T(8,128)(2,1)S(1)}, u32[]{:S(2)}, u32[]{:S(2)}) collective-permute-start(bf16[64,1024]{1,0:T(8,128)(2,1)S(1)} %get-tuple-element.44), channel_id=1, source_target_pairs={{0,4},{1,5},{2,6},{3,7},{4,0},{5,1},{6,2},{7,3},{8,12},{9,13},{10,... | collective-permute-start | bytes 393224 | tf_op jit(solution)/shard_map/ppermute | solution.py:462
  13.8 20.0 %collective-permute-start.4 = (bf16[2,128,1024]{2,1,0:T(8,128)(2,1)S(1)}, bf16[2,128,1024]{2,1,0:T(8,128)(2,1)S(1)}, u32[]{:S(2)}, u32[]{:S(2)}) collective-permute-start(bf16[2,128,1024]{2,1,0:T(8,128)(2,1)S(1)} %get-tuple-element.41), channel_id=1, source_target_pairs={{0,4},{1,5},{2,6},{3,7},{4,0},{5,1},{6,2},{7,3},{8,12},{9,13},{10,... | collective-permute-start | bytes 1572872 | tf_op jit(solution)/shard_map/ppermute | solution.py:462
  14.3 19.5 %collective-permute-start.5 = (bf16[2,128,1024]{2,1,0:T(8,128)(2,1)S(1)}, bf16[2,128,1024]{2,1,0:T(8,128)(2,1)S(1)}, u32[]{:S(2)}, u32[]{:S(2)}) collective-permute-start(bf16[2,128,1024]{2,1,0:T(8,128)(2,1)S(1)} %get-tuple-element.42), channel_id=1, source_target_pairs={{0,2},{1,3},{2,0},{3,1},{4,6},{5,7},{6,4},{7,5},{8,10},{9,11},{10,... | collective-permute-start | bytes 1572872 | tf_op jit(solution)/shard_map/ppermute | solution.py:462
  15.8 25.7 %collective-permute-start.6 = (bf16[2,128,1024]{2,1,0:T(8,128)(2,1)S(1)}, bf16[2,128,1024]{2,1,0:T(8,128)(2,1)S(1)}, u32[]{:S(2)}, u32[]{:S(2)}) collective-permute-start(bf16[2,128,1024]{2,1,0:T(8,128)(2,1)S(1)} %get-tuple-element.43), channel_id=1, source_target_pairs={{0,6},{1,7},{2,4},{3,5},{4,2},{5,3},{6,0},{7,1},{8,14},{9,15},{10,... | collective-permute-start | bytes 1572872 | tf_op jit(solution)/shard_map/ppermute | solution.py:462
  18.6 14.1 %collective-permute-start.10 = (bf16[128,1024]{1,0:T(8,128)(2,1)S(1)}, bf16[128,1024]{1,0:T(8,128)(2,1)S(1)}, u32[]{:S(2)}, u32[]{:S(2)}) collective-permute-start(bf16[128,1024]{1,0:T(8,128)(2,1)S(1)} %stack.3.refs_8_.refs_4_.refs_0_), channel_id=1, source_target_pairs={{0,16},{1,17},{2,18},{3,19},{4,20},{5,21},{6,22},{7,23},{8,24},{9,... | collective-permute-start | bytes 786440 | tf_op jit(solution)/shard_map/ppermute | solution.py:462
  21.3 20.2 %collective-permute-start.9 = (bf16[128,1024]{1,0:T(8,128)(2,1)S(1)}, bf16[128,1024]{1,0:T(8,128)(2,1)S(1)}, u32[]{:S(2)}, u32[]{:S(2)}) collective-permute-start(bf16[128,1024]{1,0:T(8,128)(2,1)S(1)} %stack.3.refs_8_.refs_4_.refs_0_), channel_id=1, source_target_pairs={{0,8},{1,9},{2,10},{3,11},{4,12},{5,13},{6,14},{7,15},{8,0},{9,1},... | collective-permute-start | bytes 786440 | tf_op jit(solution)/shard_map/ppermute | solution.py:462
  32.7 8.8 %collective-permute-start.11 = (bf16[128,1024]{1,0:T(8,128)(2,1)S(1)}, bf16[128,1024]{1,0:T(8,128)(2,1)S(1)}, u32[]{:S(2)}, u32[]{:S(2)}) collective-permute-start(bf16[128,1024]{1,0:T(8,128)(2,1)S(1)} %collective-permute-done.10.refs_10_.refs_6_.refs_2_), channel_id=1, source_target_pairs={{0,8},{1,9},{2,10},{3,11},{4,12},{5,13},{6,14},{7,15},{8,0},{9,1},... | collective-permute-start | bytes 786440 | tf_op jit(solution)/shard_map/ppermute | solution.py:462
  33.8 16.3 %collective-permute-start.14 = (bf16[128,1024]{1,0:T(8,128)(2,1)S(1)}, bf16[128,1024]{1,0:T(8,128)(2,1)S(1)}, u32[]{:S(2)}, u32[]{:S(2)}) collective-permute-start(bf16[128,1024]{1,0:T(8,128)(2,1)S(1)} %stack.3.refs_8_.refs_4_.refs_0_), channel_id=1, source_target_pairs={{0,1},{1,0},{2,3},{3,2},{4,5},{5,4},{6,7},{7,6},{8,9},{9,8},{10,11... | collective-permute-start | bytes 786440 | tf_op jit(solution)/shard_map/ppermute | solution.py:462
  33.9 16.3 %collective-permute-start.16 = (bf16[128,1024]{1,0:T(8,128)(2,1)S(1)}, bf16[128,1024]{1,0:T(8,128)(2,1)S(1)}, u32[]{:S(2)}, u32[]{:S(2)}) collective-permute-start(bf16[128,1024]{1,0:T(8,128)(2,1)S(1)} %collective-permute-done.10.refs_10_.refs_6_.refs_2_), channel_id=1, source_target_pairs={{0,1},{1,0},{2,3},{3,2},{4,5},{5,4},{6,7},{7,6},{8,9},{9,8},{10,11... | collective-permute-start | bytes 786440 | tf_op jit(solution)/shard_map/ppermute | solution.py:462
  44.5 15.8 %collective-permute-start.21 = (bf16[256,1024]{1,0:T(8,128)(2,1)S(1)}, bf16[256,1024]{1,0:T(8,128)(2,1)S(1)}, u32[]{:S(2)}, u32[]{:S(2)}) collective-permute-start(bf16[256,1024]{1,0:T(8,128)(2,1)S(1)} %get-tuple-element.46.refs_8_), channel_id=1, source_target_pairs={{0,8},{1,9},{2,10},{3,11},{4,12},{5,13},{6,14},{7,15},{24,16},{25,... | collective-permute-start | bytes 1572872 | tf_op jit(solution)/shard_map/ppermute | solution.py:462
  48.1 2.5 %collective-permute-start.15 = (bf16[128,1024]{1,0:T(8,128)(2,1)S(1)}, bf16[128,1024]{1,0:T(8,128)(2,1)S(1)}, u32[]{:S(2)}, u32[]{:S(2)}) collective-permute-start(bf16[128,1024]{1,0:T(8,128)(2,1)S(1)} %collective-permute-done.9.refs_9_.refs_5_.refs_1_), channel_id=1, source_target_pairs={{0,1},{1,0},{2,3},{3,2},{4,5},{5,4},{6,7},{7,6},{8,9},{9,8},{10,11... | collective-permute-start | bytes 786440 | tf_op jit(solution)/shard_map/ppermute | solution.py:462
  49.5 2.1 %collective-permute-start.12 = (bf16[256,512]{1,0:T(8,128)(2,1)S(1)}, bf16[256,512]{1,0:T(8,128)(2,1)S(1)}, u32[]{:S(2)}, u32[]{:S(2)}) collective-permute-start(bf16[256,512]{1,0:T(8,128)(2,1)S(1)} %get-tuple-element.48), channel_id=1, source_target_pairs={{0,1},{1,0},{2,3},{3,2},{4,5},{5,4},{6,7},{7,6},{8,9},{9,8},{10,11... | collective-permute-start | bytes 786440 | tf_op jit(solution)/shard_map/ppermute | solution.py:462
  50.1 1.5 %collective-permute-start.17 = (bf16[128,1024]{1,0:T(8,128)(2,1)S(1)}, bf16[128,1024]{1,0:T(8,128)(2,1)S(1)}, u32[]{:S(2)}, u32[]{:S(2)}) collective-permute-start(bf16[128,1024]{1,0:T(8,128)(2,1)S(1)} %collective-permute-done.11.refs_11_.refs_7_.refs_3_), channel_id=1, source_target_pairs={{0,1},{1,0},{2,3},{3,2},{4,5},{5,4},{6,7},{7,6},{8,9},{9,8},{10,11... | collective-permute-start | bytes 786440 | tf_op jit(solution)/shard_map/ppermute | solution.py:462
  50.2 1.8 %collective-permute-start.13 = (bf16[256,512]{1,0:T(8,128)(2,1)S(1)}, bf16[256,512]{1,0:T(8,128)(2,1)S(1)}, u32[]{:S(2)}, u32[]{:S(2)}) collective-permute-start(bf16[256,512]{1,0:T(8,128)(2,1)S(1)} %get-tuple-element.49), channel_id=1, source_target_pairs={{0,1},{1,0},{2,3},{3,2},{4,5},{5,4},{6,7},{7,6},{8,9},{9,8},{10,11... | collective-permute-start | bytes 786440 | tf_op jit(solution)/shard_map/ppermute | solution.py:462
  53.4 18.6 %collective-permute-start.20 = (bf16[128,2560]{1,0:T(8,128)(2,1)S(1)}, bf16[128,2560]{1,0:T(8,128)(2,1)S(1)}, u32[]{:S(2)}, u32[]{:S(2)}) collective-permute-start(bf16[128,2560]{1,0:T(8,128)(2,1)S(1)} %get-tuple-element.54), channel_id=1, source_target_pairs={{0,6},{1,7},{2,4},{3,5},{4,2},{5,3},{6,0},{7,1},{8,14},{9,15},{10,... | collective-permute-start | bytes 1966088 | tf_op jit(solution)/shard_map/ppermute | solution.py:462
  55.0 15.2 %collective-permute-start.23 = (bf16[256,1024]{1,0:T(8,128)(2,1)S(1)}, bf16[256,1024]{1,0:T(8,128)(2,1)S(1)}, u32[]{:S(2)}, u32[]{:S(2)}) collective-permute-start(bf16[256,1024]{1,0:T(8,128)(2,1)S(1)} %get-tuple-element.61), channel_id=1, source_target_pairs={{0,8},{1,9},{2,10},{3,11},{4,12},{5,13},{6,14},{7,15},{24,16},{25,... | collective-permute-start | bytes 1572872 | tf_op jit(solution)/shard_map/ppermute | solution.py:462
  60.5 11.5 %collective-permute-start.22 = (bf16[256,1024]{1,0:T(8,128)(2,1)S(1)}, bf16[256,1024]{1,0:T(8,128)(2,1)S(1)}, u32[]{:S(2)}, u32[]{:S(2)}) collective-permute-start(bf16[256,1024]{1,0:T(8,128)(2,1)S(1)} %relay.2), channel_id=1, source_target_pairs={{8,16},{9,17},{10,18},{11,19},{12,20},{13,21},{14,22},{15,23},{16,... | collective-permute-start | bytes 1572872 | tf_op jit(solution)/shard_map/ppermute | solution.py:462
  61.2 23.4 %collective-permute-start.18 = (bf16[128,2560]{1,0:T(8,128)(2,1)S(1)}, bf16[128,2560]{1,0:T(8,128)(2,1)S(1)}, u32[]{:S(2)}, u32[]{:S(2)}) collective-permute-start(bf16[128,2560]{1,0:T(8,128)(2,1)S(1)} %get-tuple-element.52), channel_id=1, source_target_pairs={{0,4},{1,5},{2,6},{3,7},{4,0},{5,1},{6,2},{7,3},{8,12},{9,13},{10,... | collective-permute-start | bytes 1966088 | tf_op jit(solution)/shard_map/ppermute | solution.py:462
  62.0 23.4 %collective-permute-start.19 = (bf16[128,2560]{1,0:T(8,128)(2,1)S(1)}, bf16[128,2560]{1,0:T(8,128)(2,1)S(1)}, u32[]{:S(2)}, u32[]{:S(2)}) collective-permute-start(bf16[128,2560]{1,0:T(8,128)(2,1)S(1)} %get-tuple-element.53), channel_id=1, source_target_pairs={{0,2},{1,3},{2,0},{3,1},{4,6},{5,7},{6,4},{7,5},{8,10},{9,11},{10,... | collective-permute-start | bytes 1966088 | tf_op jit(solution)/shard_map/ppermute | solution.py:462
  72.2 14.3 %copy-start = (bf16[1,128,8192]{2,1,0:T(8,128)(2,1)S(1)}, bf16[1,128,8192]{2,1,0:T(8,128)(2,1)}, u32[]{:S(2)}) copy-start(bf16[1,128,8192]{2,1,0:T(8,128)(2,1)} %param.8) | copy-start | bytes 6291460
  72.3 14.2 %copy-start.4 = (f32[8192]{0:T(1024)S(1)}, f32[8192]{0:T(1024)}, u32[]{:S(2)}) copy-start(f32[8192]{0:T(1024)} %param.9) | copy-start | bytes 98308
  72.3 13.2 %collective-permute-start.24 = (bf16[256,1024]{1,0:T(8,128)(2,1)S(1)}, bf16[256,1024]{1,0:T(8,128)(2,1)S(1)}, u32[]{:S(2)}, u32[]{:S(2)}) collective-permute-start(bf16[256,1024]{1,0:T(8,128)(2,1)S(1)} %get-tuple-element.62), channel_id=1, source_target_pairs={{0,8},{1,9},{2,10},{3,11},{4,12},{5,13},{6,14},{7,15},{8,0},{9,1},... | collective-permute-start | bytes 1572872 | tf_op jit(solution)/shard_map/ppermute | solution.py:462
  76.4 9.0 %collective-permute-start.25 = (bf16[256,1024]{1,0:T(8,128)(2,1)S(1)}, bf16[256,1024]{1,0:T(8,128)(2,1)S(1)}, u32[]{:S(2)}, u32[]{:S(2)}) collective-permute-start(bf16[256,1024]{1,0:T(8,128)(2,1)S(1)} %get-tuple-element.63), channel_id=1, source_target_pairs={{8,16},{9,17},{10,18},{11,19},{12,20},{13,21},{14,22},{15,23},{16,... | collective-permute-start | bytes 1572872 | tf_op jit(solution)/shard_map/ppermute | solution.py:462
  85.6 8.3 %collective-permute-start.26 = (bf16[128,1024]{1,0:T(8,128)(2,1)S(1)}, bf16[128,1024]{1,0:T(8,128)(2,1)S(1)}, u32[]{:S(2)}, u32[]{:S(2)}) collective-permute-start(bf16[128,1024]{1,0:T(8,128)(2,1)S(1)} %get-tuple-element.65), channel_id=1, source_target_pairs={{0,4},{1,5},{2,6},{3,7},{4,0},{5,1},{6,2},{7,3},{8,12},{9,13},{10,... | collective-permute-start | bytes 786440 | tf_op jit(solution)/shard_map/ppermute | solution.py:462
  86.5 7.4 %copy-start.1 = (f32[1,128,2048]{2,1,0:T(8,128)S(1)}, f32[1,128,2048]{2,1,0:T(8,128)}, u32[]{:S(2)}) copy-start(f32[1,128,2048]{2,1,0:T(8,128)} %param.13) | copy-start | bytes 3145732
  86.5 7.4 %copy-start.2 = (f32[1,128,2048]{2,1,0:T(8,128)S(1)}, f32[1,128,2048]{2,1,0:T(8,128)}, u32[]{:S(2)}) copy-start(f32[1,128,2048]{2,1,0:T(8,128)} %param.14) | copy-start | bytes 3145732
  86.5 7.4 %copy-start.3 = (f32[1,128,2048]{2,1,0:T(8,128)S(1)}, f32[1,128,2048]{2,1,0:T(8,128)}, u32[]{:S(2)}) copy-start(f32[1,128,2048]{2,1,0:T(8,128)} %param.15) | copy-start | bytes 3145732

commit v9 on v8

--- a/solution.py
+++ b/solution.py
@@ -281,11 +281,13 @@
                 ]
 
 
-def back_blocks(grads, sums, weights, chips):
+def back_blocks(grads, sums, weights, chips, after):
     rows, feats = 2 * grads[0].shape[0] // chips, grads[0].shape[1]
     width = weights[0].shape[-1]
     return pl.pallas_call(
         functools.partial(back_kernel, len(weights) // 2, chips),
+        in_specs=[pl.BlockSpec(memory_space=pltpu.VMEM)] * (len(grads) + len(sums) + len(weights))
+        + [pl.BlockSpec(memory_space=pl.ANY)] * len(after),
         out_shape=[
             jax.ShapeDtypeStruct((rows, 2 * width + (feats if k else 0)), bf16)
             for k in range(chips)
@@ -294,7 +296,7 @@
         scratch_shapes=[pltpu.VMEM((feats, width), bf16)],
         compiler_params=limit(40),
         name="back_blocks",
-    )(*grads, *sums, *weights)
+    )(*grads, *sums, *weights, *after)
 
 
 def grad_x_kernel(tok_ref, gain_ref, part_ref, *refs):
@@ -350,95 +352,76 @@
     )(tokens, gain, part, *grads)
 
 
-def add_kernel(count, groups, *refs):
-    for i, out_ref in enumerate(refs[-groups:]):
-        total = refs[i * count][...].astype(f32)
-        for ref in refs[i * count + 1 : (i + 1) * count]:
-            total += ref[...].astype(f32)
+def add_kernel(halves_of, *refs):
+    outs = refs[-len(halves_of) :]
+    at = 0
+    for half_of, out_ref in zip(halves_of, outs):
+        rows = out_ref.shape[0]
+        total = None
+        for half in half_of:
+            first = (half or 0) * rows
+            term = refs[at][first : first + rows, :].astype(f32)
+            total = term if total is None else total + term
+            at += 1
         out_ref[...] = total.astype(out_ref.dtype)
 
 
 def relay(sums, after):
-    shape = sums[0][0].shape
-    size = shape[0] * shape[1]
-    return pl.pallas_call(
-        functools.partial(add_kernel, len(sums[0]), len(sums)),
-        in_specs=[pl.BlockSpec(memory_space=pltpu.VMEM)] * (len(sums) * len(sums[0]))
+    arrays = [array for group in sums for array, _ in group]
+    rows, width = sums[0][0][0].shape
+    shape = (rows if sums[0][0][1] is None else rows // 2, width)
+    return pl.pallas_call(
+        functools.partial(add_kernel, [[half for _, half in group] for group in sums]),
+        in_specs=[pl.BlockSpec(memory_space=pltpu.VMEM)] * len(arrays)
         + [pl.BlockSpec(memory_space=pl.ANY)] * len(after),
         out_shape=[jax.ShapeDtypeStruct(shape, bf16)] * len(sums),
         compiler_params=limit(16),
-        cost_estimate=cost(2 * size, 12 * size),
         name="relay",
-    )(*[a for group in sums for a in group], *after)
-
-
-def finish_kernel(own_ref, even_ref, odd_ref, *refs):
-    kept_ref, sent_ref = refs[-2:]
-    half = kept_ref.shape[0]
-    for part, out_ref in ((slice(half), kept_ref), (slice(half, 2 * half), sent_ref)):
-        total = own_ref[part, :].astype(f32) + even_ref[part, :].astype(f32)
-        out_ref[...] = (total + odd_ref[part, :].astype(f32)).astype(out_ref.dtype)
-
-
-def finish(own, even, odd, after):
-    height, width = own.shape
-    return pl.pallas_call(
-        finish_kernel,
-        in_specs=[pl.BlockSpec(memory_space=pltpu.VMEM)] * 3
-        + [pl.BlockSpec(memory_space=pl.ANY)] * len(after),
-        out_shape=[
-            jax.ShapeDtypeStruct((height // 2, width), f32),
-            jax.ShapeDtypeStruct((height // 2, width), bf16),
-        ],
-        compiler_params=limit(16),
-        cost_estimate=cost(2 * height * width, 9 * height * width),
-        name="finish",
-    )(own, even, odd, *after)
-
-
-def adam_kernel(token_total, parts, owner_ref, *refs):
-    kept_refs, got_refs, refs = refs[:parts], refs[parts : 2 * parts], refs[2 * parts :]
+    )(*arrays, *after)
+
+
+def adam_kernel(token_total, count, owner_ref, *refs):
+    part_refs, got_ref, refs = refs[:count], refs[count], refs[count + 1 :]
     master_ref, moment1_ref, moment2_ref = refs[:3]
     out_refs = refs[3:]
-    step, width = kept_refs[0].shape
+    step, width = got_ref.shape
     dp = lax.axis_index("dp")
     owned = (owner_ref[...] == dp).astype(f32)
     count = jnp.sum(owned, axis=1, keepdims=True)
     index = pl.program_id(0) * step + lax.broadcasted_iota(jnp.int32, (step, 1), 0)
     occupied = (index.astype(f32) < count).astype(f32)
-    for i, refs in enumerate((kept_refs, got_refs)):
-        for part, ref in enumerate(refs):
-            at = (((dp % 2) ^ i) * parts + part) * width
-            cols = pl.ds(pl.multiple_of(at, width), width)
-            slot_grad = ref[...].astype(f32) / token_total
-            new_moment1 = (
-                beta_one * moment1_ref[:, cols] + (1.0 - beta_one) * slot_grad
-            ) * occupied
-            new_moment2 = (
-                beta_two * moment2_ref[:, cols] + (1.0 - beta_two) * slot_grad * slot_grad
-            ) * occupied
-            step_dir = new_moment1 / bias_one / (jnp.sqrt(new_moment2 / bias_two) + adam_eps)
-            out_refs[0][:, cols] = (master_ref[:, cols] - learn_rate * step_dir) * occupied
-            out_refs[1][:, cols] = new_moment1
-            out_refs[2][:, cols] = new_moment2
-
-
-def adam(owner, kept, got, states, token_total):
+    for i, refs in enumerate((part_refs, (got_ref,))):
+        total = refs[0][...].astype(f32)
+        for ref in refs[1:]:
+            total += ref[...].astype(f32)
+        cols = pl.ds(pl.multiple_of(((dp % 2) ^ i) * width, width), width)
+        slot_grad = total / token_total
+        new_moment1 = (beta_one * moment1_ref[:, cols] + (1.0 - beta_one) * slot_grad) * occupied
+        new_moment2 = (
+            beta_two * moment2_ref[:, cols] + (1.0 - beta_two) * slot_grad * slot_grad
+        ) * occupied
+        step_dir = new_moment1 / bias_one / (jnp.sqrt(new_moment2 / bias_two) + adam_eps)
+        out_refs[0][:, cols] = (master_ref[:, cols] - learn_rate * step_dir) * occupied
+        out_refs[1][:, cols] = new_moment1
+        out_refs[2][:, cols] = new_moment2
+
+
+def adam(owner, parts, got, states, token_total):
     slots, cols = states[0].shape
-    width = kept[0].shape[-1]
+    width = got.shape[-1]
     step = min(slots, 32)
     return pl.pallas_call(
-        functools.partial(adam_kernel, token_total, len(kept)),
+        functools.partial(adam_kernel, token_total, len(parts)),
         grid=(slots // step,),
         in_specs=[pl.BlockSpec(owner.shape, lambda i: (0, 0))]
-        + [pl.BlockSpec((step, width), lambda i: (i, 0))] * (2 * len(kept))
+        + [pl.BlockSpec((step, width), lambda i: (i, 0))] * (len(parts) + 1)
         + [pl.BlockSpec((step, cols), lambda i: (i, 0))] * 3,
         out_specs=[pl.BlockSpec((step, cols), lambda i: (i, 0))] * 3,
         out_shape=[jax.ShapeDtypeStruct((slots, cols), f32)] * 3,
         compiler_params=limit(24),
         cost_estimate=cost(20 * slots * cols, 30 * slots * cols),
         name="adam",
-    )(owner, *kept, *got, *states)
+    )(owner, *parts, got, *states)
 
 
 def on_device(groups, seqs, tokens, gain, w_t, grad_values, owner, master, moment1, moment2):
@@ -512,45 +495,47 @@
         for even in (True, False)
         if any(busy(z, step, even) for z in range(planes))
     ]
-    outs = []
-    for part in range(parts):
-        outs.append(
-            weight_blocks(
-                selected,
-                [*grads, *grads_far],
-                [piece[part] for piece in pieces],
-                planes,
-                plan,
-                weights if part == parts - 1 else [],
-            )
+    outs = weight_blocks(
+        selected, [*grads, *grads_far], [piece[0] for piece in pieces], planes, plan, weights
+    )
+    ready = dict(zip(plan, outs))
+    got = {even: across(ready[1, even], 1, even) for even in (True, False) if (1, even) in ready}
+    held = [{even: (value, chunk) for even, value in got.items()} for chunk in range(2)]
+
+    def advance(step, chunks, after):
+        here = [even for even in (True, False) if (step, even) in ready]
+        adds = [even for even in here if (not even) in held[0]]
+        keys = [(chunk, even) for chunk in chunks for even in adds]
+        sums = relay(
+            [[(ready[step, even], chunk), held[chunk][not even]] for chunk, even in keys], after
         )
-
-    *far_sums, near_sum = value_parts(pieces, weights, feats, outs[-1][:1])
+        new = [{}, {}]
+        for (chunk, even), value in zip(keys, sums):
+            new[chunk][even] = (across(value, step, even), None)
+        for even in here:
+            if even not in adds:
+                whole = across(ready[step, even], step, even)
+                for chunk in chunks:
+                    new[chunk][even] = (whole, chunk)
+        for chunk in chunks:
+            held[chunk] = new[chunk]
+        return sums
+
+    *far_sums, near_sum = value_parts(pieces, weights, feats, outs[:1])
     sums = [near_sum] + [to_core(f) for f in far_sums]
-    back = back_blocks(grads, sums, weights + weights_far, chips)
+    back = back_blocks(grads, sums, weights + weights_far, chips, [])
     home = [back[0]] + [to_chip(back[k], k) for k in range(1, chips)]
-
-    kept, got = [], []
-    for part in range(parts):
-        ready, held = dict(zip(plan, outs[part])), {}
-        final = part == parts - 1
-        for step in range(1, planes):
-            here = [even for even in (True, False) if (step, even) in ready]
-            sums = [[ready[step, even], held[not even]] for even in here if (not even) in held]
-            if sums:
-                after = (back[:1] if step == 2 else home[-1:]) if final else []
-                sums = list(relay(sums, after))
-            send = [
-                sums.pop(0) if (not even) in held else ready[step, even] for even in here
-            ]
-            held = {even: across(value, step, even) for even, value in zip(here, send)}
-        after = home[1:] if final else []
-        keep, send = finish(outs[part][-1], held[True], held[False], after)
-        kept.append(keep)
-        got.append(to_x(send))
+    advance(2, (1, 0), [])
+    for step in range(3, planes):
+        advance(step, (1,), [])
+        advance(step, (0,), [])
+    other = relay([[(outs[-1], 1), *held[1].values()]], home[-1:])
+    got = to_x(other[0])
     grad_x, values = grad_x_blocks(tokens, gain_row, back[-1], home)
-
-    states = adam(owner_row, kept, got, (master[0], moment1[0], moment2[0]), rows * seqs * groups)
+    mine = [outs[-1][:slots]] + [value for value, _ in held[0].values()]
+    total = rows * seqs * groups
+    states = (master[0], moment1[0], moment2[0])
+    states = adam(owner_row, mine, got, states, total)
     return (values[None], grad_x[None], *(s[None] for s in states))
 
 

time: 96.8 us -> 94.3 us (0.974)
  waiting for transfers between devices: 46.8 us -> 40.1 us
  starting transfers between devices: 31.3 us -> 35.4 us
    ppermute x27 -> x30, waiting for transfers between devices: 46.8 us -> 40.1 us  [permute(): return lax.ppermute(value, ('dp', 'seq'), pairs)]
    ppermute x27 -> x30, starting transfers between devices: 31.3 us -> 35.4 us  [permute(): return lax.ppermute(value, ('dp', 'seq'), pairs)]
    pallas_call x4 -> x5, Pallas kernels: 3.14 us -> 3.09 us  [the longest x1 2.62 us: adam(): pl.pallas_call(functools.partial(adam_kernel, token_total, len(parts)), g...]
  transfers between devices with their start and end apart: 27 -> 30, of which waited for: 13 -> 12; matrix products, arithmetic and copies ran while one was open for 0% -> 0% of each run, Pallas kernels for 15% -> 16%
where the time goes in v9:
time: 94.3 us; the launch traced here: 94 us
  waiting for transfers between devices  40.1 us (43%)
  starting transfers between devices  35.4 us (38%)
  Pallas kernels  17.5 us (19%)
    ppermute x30, waiting for transfers between devices, permute(): return lax.ppermute(value, ('dp', 'seq'), pairs)  40.1 us
    ppermute x30, starting transfers between devices, permute(): return lax.ppermute(value, ('dp', 'seq'), pairs)  35.4 us
    pallas_call x1, Pallas kernels, grad_x_blocks(): pl.pallas_call(grad_x_kernel, grid=(rows // step,), in_specs=[pl.BlockSpe...  3.62 us
    pallas_call x1, Pallas kernels, norm_blocks(): pl.pallas_call(functools.partial(norm_kernel, parts), grid=(rows // step,...  3.42 us
    pallas_call x1, Pallas kernels, weight_blocks(): pl.pallas_call(functools.partial(weight_kernel, planes, chips, plan), in_...  3.02 us
    pallas_call x1, Pallas kernels, adam(): pl.pallas_call(functools.partial(adam_kernel, token_total, len(parts)), g...  2.62 us
  transfers between devices with their start and end apart: 30, of which 12 were waited for; matrix products, arithmetic and copies ran while one was open for 0% of the time, Pallas kernels for 16%

profile of v9, /device:TPU:0, one launch (start us, length us, event | category | flops | bytes accessed | tf_op | source)
XLA Modules:
  0.0 94.0 jit_solution(15895878533807732888)
XLA Ops:
  0.6 0.5 collective-permute-start.3
  1.1 2.6 %collective-permute-start = (bf16[128,512]{1,0:T(8,128)(2,1)}, bf16[128,512]{1,0:T(8,128)(2,1)S(1)}, u32[]{:S(2)}, u32[]{:S(2)}) collective-permute-start(bf16[128,512]{1,0:T(8,128)(2,1)} %bitcast.20), channel_id=1, source_target_pairs={{0,4},{1,5},{2,6},{3,7},{4,0},{5,1},{6,2},{7,3},{8,12},{9,13},{10,... | collective-permute-start | bytes 393224 | tf_op jit(solution)/shard_map/ppermute | solution.py:445
  3.7 1.5 %collective-permute-start.1 = (bf16[128,512]{1,0:T(8,128)(2,1)}, bf16[128,512]{1,0:T(8,128)(2,1)S(1)}, u32[]{:S(2)}, u32[]{:S(2)}) collective-permute-start(bf16[128,512]{1,0:T(8,128)(2,1)} %bitcast.21), channel_id=1, source_target_pairs={{0,2},{1,3},{2,0},{3,1},{4,6},{5,7},{6,4},{7,5},{8,10},{9,11},{10,... | collective-permute-start | bytes 393224 | tf_op jit(solution)/shard_map/ppermute | solution.py:445
  5.3 1.0 %halves.1 = (bf16[64,1024]{1,0:T(8,128)(2,1)S(1)}, bf16[64,1024]{1,0:T(8,128)(2,1)S(1)}) custom-call(bf16[64,2048]{1,0:T(8,128)(2,1)} %w_ref.1), custom_call_target="tpu_custom_call" | custom-call | tf_op jit(solution)/shard_map/halves/pallas_call | solution.py:83
  6.3 3.4 %norm_blocks.1 = (bf16[2,128,1024]{2,1,0:T(8,128)(2,1)S(1)}, bf16[2,128,1024]{2,1,0:T(8,128)(2,1)S(1)}, bf16[2,128,1024]{2,1,0:T(8,128)(2,1)S(1)}, bf16[2,128,1024]{2,1,0:T(8,128)(2,1)S(1)}) custom-call(bf16[128,8192]{1,0:T(8,128)(2,1)} %bitcast.13, bf16[128,8192]{1,0:T(8,128)(2,1)S(1)} %collective-permute-done.3.far_ref, f32[1,8192]{1,0:T(1,128)} %bitcast.18), custom_call_target="tpu_custom_call" | custom-call | flops 8388608 | bytes 6291456 | tf_op jit(solution)/shard_map/norm_blocks/pallas_call | solution.py:54
  9.7 2.6 %collective-permute-done.1.refs_2_ = bf16[128,512]{1,0:T(8,128)(2,1)S(1)} collective-permute-done((bf16[128,512]{1,0:T(8,128)(2,1)}, bf16[128,512]{1,0:T(8,128)(2,1)S(1)}, u32[]{:S(2)}, u32[]{:S(2)}) %collective-permute-start.1) | collective-permute-done | bytes 131104 | tf_op jit(solution)/shard_map/ppermute | solution.py:445
  12.5 1.3 %collective-permute-start.7 = (bf16[64,1024]{1,0:T(8,128)(2,1)S(1)}, bf16[64,1024]{1,0:T(8,128)(2,1)S(1)}, u32[]{:S(2)}, u32[]{:S(2)}) collective-permute-start(bf16[64,1024]{1,0:T(8,128)(2,1)S(1)} %get-tuple-element.46), channel_id=1, source_target_pairs={{0,4},{1,5},{2,6},{3,7},{4,0},{5,1},{6,2},{7,3},{8,12},{9,13},{10,... | collective-permute-start | bytes 393224 | tf_op jit(solution)/shard_map/ppermute | solution.py:445
  13.8 0.8 collective-permute-start.4
  14.6 1.5 %collective-permute-start.5 = (bf16[2,128,1024]{2,1,0:T(8,128)(2,1)S(1)}, bf16[2,128,1024]{2,1,0:T(8,128)(2,1)S(1)}, u32[]{:S(2)}, u32[]{:S(2)}) collective-permute-start(bf16[2,128,1024]{2,1,0:T(8,128)(2,1)S(1)} %get-tuple-element.44), channel_id=1, source_target_pairs={{0,2},{1,3},{2,0},{3,1},{4,6},{5,7},{6,4},{7,5},{8,10},{9,11},{10,... | collective-permute-start | bytes 1572872 | tf_op jit(solution)/shard_map/ppermute | solution.py:445
  16.1 1.2 %collective-permute-start.6 = (bf16[2,128,1024]{2,1,0:T(8,128)(2,1)S(1)}, bf16[2,128,1024]{2,1,0:T(8,128)(2,1)S(1)}, u32[]{:S(2)}, u32[]{:S(2)}) collective-permute-start(bf16[2,128,1024]{2,1,0:T(8,128)(2,1)S(1)} %get-tuple-element.45), channel_id=1, source_target_pairs={{0,6},{1,7},{2,4},{3,5},{4,2},{5,3},{6,0},{7,1},{8,14},{9,15},{10,... | collective-permute-start | bytes 1572872 | tf_op jit(solution)/shard_map/ppermute | solution.py:445
  17.2 1.6 %collective-permute-done.7.refs_1_ = bf16[64,1024]{1,0:T(8,128)(2,1)S(1)} collective-permute-done((bf16[64,1024]{1,0:T(8,128)(2,1)S(1)}, bf16[64,1024]{1,0:T(8,128)(2,1)S(1)}, u32[]{:S(2)}, u32[]{:S(2)}) %collective-permute-start.7) | collective-permute-done | bytes 131104 | tf_op jit(solution)/shard_map/ppermute | solution.py:445
  18.8 2.7 %collective-permute-start.10 = (bf16[128,1024]{1,0:T(8,128)(2,1)S(1)}, bf16[128,1024]{1,0:T(8,128)(2,1)S(1)}, u32[]{:S(2)}, u32[]{:S(2)}) collective-permute-start(bf16[128,1024]{1,0:T(8,128)(2,1)S(1)} %stack.3.refs_8_.refs_4_.refs_0_), channel_id=1, source_target_pairs={{0,16},{1,17},{2,18},{3,19},{4,20},{5,21},{6,22},{7,23},{8,24},{9,... | collective-permute-start | bytes 786440 | tf_op jit(solution)/shard_map/ppermute | solution.py:445
  21.5 1.6 %collective-permute-start.9 = (bf16[128,1024]{1,0:T(8,128)(2,1)S(1)}, bf16[128,1024]{1,0:T(8,128)(2,1)S(1)}, u32[]{:S(2)}, u32[]{:S(2)}) collective-permute-start(bf16[128,1024]{1,0:T(8,128)(2,1)S(1)} %stack.3.refs_8_.refs_4_.refs_0_), channel_id=1, source_target_pairs={{0,8},{1,9},{2,10},{3,11},{4,12},{5,13},{6,14},{7,15},{8,0},{9,1},... | collective-permute-start | bytes 786440 | tf_op jit(solution)/shard_map/ppermute | solution.py:445
  23.1 9.9 %collective-permute-done.10.refs_10_.refs_6_.refs_2_ = bf16[128,1024]{1,0:T(8,128)(2,1)S(1)} collective-permute-done((bf16[128,1024]{1,0:T(8,128)(2,1)S(1)}, bf16[128,1024]{1,0:T(8,128)(2,1)S(1)}, u32[]{:S(2)}, u32[]{:S(2)}) %collective-permute-start.10) | collective-permute-done | bytes 262176 | tf_op jit(solution)/shard_map/ppermute | solution.py:445
  33.0 0.6 collective-permute-start.11
  33.5 0.5 select_rows.1.refs_0_
  34.1 0.5 collective-permute-start.16
  34.7 7.1 %collective-permute-done.6.refs_7_.refs_3_ = bf16[2,128,1024]{2,1,0:T(8,128)(2,1)S(1)} collective-permute-done((bf16[2,128,1024]{2,1,0:T(8,128)(2,1)S(1)}, bf16[2,128,1024]{2,1,0:T(8,128)(2,1)S(1)}, u32[]{:S(2)}, u32[]{:S(2)}) %collective-permute-start.6) | collective-permute-done | bytes 524320 | tf_op jit(solution)/shard_map/ppermute | solution.py:445
  41.8 3.0 %weight_blocks.1 = (bf16[256,1024]{1,0:T(8,128)(2,1)S(1)}, bf16[256,1024]{1,0:T(8,128)(2,1)S(1)}, bf16[256,1024]{1,0:T(8,128)(2,1)S(1)}, bf16[256,1024]{1,0:T(8,...) custom-call(bf16[1024,512]{1,0:T(8,128)(2,1)S(1)} %select_rows.1.refs_0_, ...), custom_call_target="tpu_custom_call" | custom-call | flops 2147483648 | bytes 4194304 | tf_op jit(solution)/shard_map/weight_blocks/pallas_call | solution.py:196
  44.8 3.5 %collective-permute-start.21 = (bf16[256,1024]{1,0:T(8,128)(2,1)S(1)}, bf16[256,1024]{1,0:T(8,128)(2,1)S(1)}, u32[]{:S(2)}, u32[]{:S(2)}) collective-permute-start(bf16[256,1024]{1,0:T(8,128)(2,1)S(1)} %get-tuple-element.48.refs_8_), channel_id=1, source_target_pairs={{0,8},{1,9},{2,10},{3,11},{4,12},{5,13},{6,14},{7,15},{24,16},{25,... | collective-permute-start | bytes 1572872 | tf_op jit(solution)/shard_map/ppermute | solution.py:445
  48.4 1.3 %collective-permute-start.23 = (bf16[256,1024]{1,0:T(8,128)(2,1)S(1)}, bf16[256,1024]{1,0:T(8,128)(2,1)S(1)}, u32[]{:S(2)}, u32[]{:S(2)}) collective-permute-start(bf16[256,1024]{1,0:T(8,128)(2,1)S(1)} %get-tuple-element.64), channel_id=1, source_target_pairs={{0,8},{1,9},{2,10},{3,11},{4,12},{5,13},{6,14},{7,15},{24,16},{25,... | collective-permute-start | bytes 1572872 | tf_op jit(solution)/shard_map/ppermute | solution.py:445
  49.7 1.4 %value_parts.1 = (bf16[256,512]{1,0:T(8,128)(2,1)S(1)}, bf16[256,512]{1,0:T(8,128)(2,1)S(1)}, f32[512,512]{1,0:T(8,128)S(1)}) custom-call(bf16[2,128,1024]{2,1,0:T(8,128)(2,1)S(1)} %get-tuple-element.39.refs_4_.refs_0_, bf16[2,128,1024]{2,1,0:T(8,128)(2,1)S(1)} %collective-permute-done.4.refs_5_.refs_1_, ...), custom_call_target="tpu_custom_call" | custom-call | tf_op jit(solution)/shard_map/value_parts/pallas_call | solution.py:248
  51.2 0.5 collective-permute-start.13
  51.8 0.9 collective-permute-done.12.got_a_ref
  52.7 0.4 collective-permute-done.13.got_b_ref
  53.1 0.4 collective-permute-done.17.refs_7_
  53.4 1.4 %back_blocks.1 = (bf16[128,2048]{1,0:T(8,128)(2,1)S(1)}, bf16[128,2560]{1,0:T(8,128)(2,1)S(1)}, bf16[128,2560]{1,0:T(8,128)(2,1)S(1)}, bf16[128,2560]{1,0:T(8,128)(2,1)S(1)}, f32[128,512]{1,0:T(8,128)S(1)}) custom-call(bf16[256,512]{1,0:T(8,128)(2,1)S(1)} %get-tuple-element.41.refs_1_.grads_a_ref, ...), custom_call_target="tpu_custom_call" | custom-call | tf_op jit(solution)/shard_map/back_blocks/pallas_call | solution.py:287
  54.9 1.2 %collective-permute-start.20 = (bf16[128,2560]{1,0:T(8,128)(2,1)S(1)}, bf16[128,2560]{1,0:T(8,128)(2,1)S(1)}, u32[]{:S(2)}, u32[]{:S(2)}) collective-permute-start(bf16[128,2560]{1,0:T(8,128)(2,1)S(1)} %get-tuple-element.56), channel_id=1, source_target_pairs={{0,6},{1,7},{2,4},{3,5},{4,2},{5,3},{6,0},{7,1},{8,14},{9,15},{10,... | collective-permute-start | bytes 1966088 | tf_op jit(solution)/shard_map/ppermute | solution.py:445
  56.1 4.6 %collective-permute-done.21.refs_1_.refs_3_ = bf16[256,1024]{1,0:T(8,128)(2,1)S(1)} collective-permute-done((bf16[256,1024]{1,0:T(8,128)(2,1)S(1)}, bf16[256,1024]{1,0:T(8,128)(2,1)S(1)}, u32[]{:S(2)}, u32[]{:S(2)}) %collective-permute-start.21) | collective-permute-done | bytes 524320 | tf_op jit(solution)/shard_map/ppermute | solution.py:445
  60.7 0.1 relay.4
  60.8 0.7 collective-permute-start.26
  61.5 0.7 collective-permute-start.22
  62.2 0.6 collective-permute-start.18
  62.8 7.8 %collective-permute-done.23.refs_3_ = bf16[256,1024]{1,0:T(8,128)(2,1)S(1)} collective-permute-done((bf16[256,1024]{1,0:T(8,128)(2,1)S(1)}, bf16[256,1024]{1,0:T(8,128)(2,1)S(1)}, u32[]{:S(2)}, u32[]{:S(2)}) %collective-permute-start.23) | collective-permute-done | bytes 524320 | tf_op jit(solution)/shard_map/ppermute | solution.py:445
  70.6 0.5 collective-permute-start.19
  71.1 0.1 relay.6
  71.2 3.0 %collective-permute-start.27 = (bf16[128,1024]{1,0:T(8,128)(2,1)S(1)}, bf16[128,1024]{1,0:T(8,128)(2,1)S(1)}, u32[]{:S(2)}, u32[]{:S(2)}) collective-permute-start(bf16[128,1024]{1,0:T(8,128)(2,1)S(1)} %get-tuple-element.68), channel_id=1, source_target_pairs={{0,8},{1,9},{2,10},{3,11},{4,12},{5,13},{6,14},{7,15},{8,0},{9,1},... | collective-permute-start | bytes 786440 | tf_op jit(solution)/shard_map/ppermute | solution.py:445
  74.2 0.8 collective-permute-start.28
  75.0 0.1 relay.5
  75.2 5.1 %collective-permute-start.24 = (bf16[128,1024]{1,0:T(8,128)(2,1)S(1)}, bf16[128,1024]{1,0:T(8,128)(2,1)S(1)}, u32[]{:S(2)}, u32[]{:S(2)}) collective-permute-start(bf16[128,1024]{1,0:T(8,128)(2,1)S(1)} %get-tuple-element.65), channel_id=1, source_target_pairs={{0,8},{1,9},{2,10},{3,11},{4,12},{5,13},{6,14},{7,15},{8,0},{9,1},... | collective-permute-start | bytes 786440 | tf_op jit(solution)/shard_map/ppermute | solution.py:445
  80.2 0.7 collective-permute-start.25
  80.9 0.1 relay.7
  81.0 1.7 %collective-permute-start.29 = (bf16[128,1024]{1,0:T(8,128)(2,1)S(1)}, bf16[128,1024]{1,0:T(8,128)(2,1)S(1)}, u32[]{:S(2)}, u32[]{:S(2)}) collective-permute-start(bf16[128,1024]{1,0:T(8,128)(2,1)S(1)} %relay.7), channel_id=1, source_target_pairs={{0,4},{1,5},{2,6},{3,7},{4,0},{5,1},{6,2},{7,3},{8,12},{9,13},{10,... | collective-permute-start | bytes 786440 | tf_op jit(solution)/shard_map/ppermute | solution.py:445
  82.8 3.7 %collective-permute-done.18.refs_1_ = bf16[128,2560]{1,0:T(8,128)(2,1)S(1)} collective-permute-done((bf16[128,2560]{1,0:T(8,128)(2,1)S(1)}, bf16[128,2560]{1,0:T(8,128)(2,1)S(1)}, u32[]{:S(2)}, u32[]{:S(2)}) %collective-permute-start.18) | collective-permute-done | bytes 655392 | tf_op jit(solution)/shard_map/ppermute | solution.py:445
  86.5 0.2 collective-permute-done.19.refs_2_
  86.7 3.6 %grad_x_blocks.1 = (bf16[128,8192]{1,0:T(8,128)(2,1)}, bf16[128,512]{1,0:T(8,128)(2,1)}) custom-call(bf16[128,8192]{1,0:T(8,128)(2,1)S(1)} %bitcast.14, f32[1,8192]{1,0:T(1,128)S(1)} %bitcast.19, f32[128,512]{1,0:T(8,128)S(1)} %get-tuple-element.52.part_ref, bf16[128,2048]{1,0:T(8,128)(2,1)S(1)} %get-tuple-element.53.refs_0_, ...), custom_call_target="tpu_custom_call" | custom-call | flops 16777216 | bytes 6291456 | tf_op jit(solution)/shard_map/grad_x_blocks/pallas_call | solution.py:332
  90.4 1.0 %collective-permute-done.29.refs_3_ = bf16[128,1024]{1,0:T(8,128)(2,1)S(1)} collective-permute-done((bf16[128,1024]{1,0:T(8,128)(2,1)S(1)}, bf16[128,1024]{1,0:T(8,128)(2,1)S(1)}, u32[]{:S(2)}, u32[]{:S(2)}) %collective-permute-start.29) | collective-permute-done | bytes 262176 | tf_op jit(solution)/shard_map/ppermute | solution.py:445
  91.3 2.6 %adam.1 = (f32[128,2048]{1,0:T(8,128)}, f32[128,2048]{1,0:T(8,128)}, f32[128,2048]{1,0:T(8,128)}) custom-call(s32[1,512]{1,0:T(1,128)S(1)} %bitcast.25, bf16[128,1024]{1,0:T(8,128)(2,1)S(1)} %slice.3.refs_0_, bf16[128,1024]{1,0:T(8,128)(2,1)S(1)} %collective-permute-done.24.refs_1_, bf16[128,1024]{1,0:T(8,128)(2,1)S(1)} %collective-permute-done.25.refs_2_, ...), custom_call_target="tpu_custom_call" | custom-call | flops 5242880 | bytes 7864320 | tf_op jit(solution)/shard_map/adam/pallas_call | solution.py:413
  (41 shorter events, 0.6 us)
Async XLA Ops:
  0.6 5.6 %collective-permute-start.3 = (bf16[128,8192]{1,0:T(8,128)(2,1)}, bf16[128,8192]{1,0:T(8,128)(2,1)S(1)}, u32[]{:S(2)}, u32[]{:S(2)}) collective-permute-start(bf16[128,8192]{1,0:T(8,128)(2,1)} %bitcast.12), channel_id=1, source_target_pairs={{0,1},{1,0},{2,3},{3,2},{4,5},{5,4},{6,7},{7,6},{8,9},{9,8},{10,11... | collective-permute-start | bytes 6291464 | tf_op jit(solution)/shard_map/ppermute | solution.py:445
  1.1 8.6 %collective-permute-start = (bf16[128,512]{1,0:T(8,128)(2,1)}, bf16[128,512]{1,0:T(8,128)(2,1)S(1)}, u32[]{:S(2)}, u32[]{:S(2)}) collective-permute-start(bf16[128,512]{1,0:T(8,128)(2,1)} %bitcast.20), channel_id=1, source_target_pairs={{0,4},{1,5},{2,6},{3,7},{4,0},{5,1},{6,2},{7,3},{8,12},{9,13},{10,... | collective-permute-start | bytes 393224 | tf_op jit(solution)/shard_map/ppermute | solution.py:445
  3.7 8.6 %collective-permute-start.1 = (bf16[128,512]{1,0:T(8,128)(2,1)}, bf16[128,512]{1,0:T(8,128)(2,1)S(1)}, u32[]{:S(2)}, u32[]{:S(2)}) collective-permute-start(bf16[128,512]{1,0:T(8,128)(2,1)} %bitcast.21), channel_id=1, source_target_pairs={{0,2},{1,3},{2,0},{3,1},{4,6},{5,7},{6,4},{7,5},{8,10},{9,11},{10,... | collective-permute-start | bytes 393224 | tf_op jit(solution)/shard_map/ppermute | solution.py:445
  5.2 7.1 %collective-permute-start.2 = (bf16[128,512]{1,0:T(8,128)(2,1)}, bf16[128,512]{1,0:T(8,128)(2,1)S(1)}, u32[]{:S(2)}, u32[]{:S(2)}) collective-permute-start(bf16[128,512]{1,0:T(8,128)(2,1)} %bitcast.22), channel_id=1, source_target_pairs={{0,6},{1,7},{2,4},{3,5},{4,2},{5,3},{6,0},{7,1},{8,14},{9,15},{10,... | collective-permute-start | bytes 393224 | tf_op jit(solution)/shard_map/ppermute | solution.py:445
  6.2 6.1 %copy-start.5 = (bf16[1,128,512]{2,1,0:T(8,128)(2,1)S(1)}, bf16[1,128,512]{2,1,0:T(8,128)(2,1)}, u32[]{:S(2)}) copy-start(bf16[1,128,512]{2,1,0:T(8,128)(2,1)} %param.11) | copy-start | bytes 393220
  9.7 23.8 %copy-start.6 = (s32[512]{0:T(512)S(1)}, s32[512]{0:T(512)}, u32[]{:S(2)}) copy-start(s32[512]{0:T(512)} %param.12) | copy-start | bytes 6148
  12.4 6.4 %collective-permute-start.8 = (bf16[512,512]{1,0:T(8,128)(2,1)S(1)}, bf16[512,512]{1,0:T(8,128)(2,1)S(1)}, u32[]{:S(2)}, u32[]{:S(2)}) collective-permute-start(bf16[512,512]{1,0:T(8,128)(2,1)S(1)} %get-tuple-element.47), channel_id=1, source_target_pairs={{0,1},{1,0},{2,3},{3,2},{4,5},{5,4},{6,7},{7,6},{8,9},{9,8},{10,11... | collective-permute-start | bytes 1572872 | tf_op jit(solution)/shard_map/ppermute | solution.py:445
  12.5 6.4 %collective-permute-start.7 = (bf16[64,1024]{1,0:T(8,128)(2,1)S(1)}, bf16[64,1024]{1,0:T(8,128)(2,1)S(1)}, u32[]{:S(2)}, u32[]{:S(2)}) collective-permute-start(bf16[64,1024]{1,0:T(8,128)(2,1)S(1)} %get-tuple-element.46), channel_id=1, source_target_pairs={{0,4},{1,5},{2,6},{3,7},{4,0},{5,1},{6,2},{7,3},{8,12},{9,13},{10,... | collective-permute-start | bytes 393224 | tf_op jit(solution)/shard_map/ppermute | solution.py:445
  13.8 20.2 %collective-permute-start.4 = (bf16[2,128,1024]{2,1,0:T(8,128)(2,1)S(1)}, bf16[2,128,1024]{2,1,0:T(8,128)(2,1)S(1)}, u32[]{:S(2)}, u32[]{:S(2)}) collective-permute-start(bf16[2,128,1024]{2,1,0:T(8,128)(2,1)S(1)} %get-tuple-element.43), channel_id=1, source_target_pairs={{0,4},{1,5},{2,6},{3,7},{4,0},{5,1},{6,2},{7,3},{8,12},{9,13},{10,... | collective-permute-start | bytes 1572872 | tf_op jit(solution)/shard_map/ppermute | solution.py:445
  14.6 19.5 %collective-permute-start.5 = (bf16[2,128,1024]{2,1,0:T(8,128)(2,1)S(1)}, bf16[2,128,1024]{2,1,0:T(8,128)(2,1)S(1)}, u32[]{:S(2)}, u32[]{:S(2)}) collective-permute-start(bf16[2,128,1024]{2,1,0:T(8,128)(2,1)S(1)} %get-tuple-element.44), channel_id=1, source_target_pairs={{0,2},{1,3},{2,0},{3,1},{4,6},{5,7},{6,4},{7,5},{8,10},{9,11},{10,... | collective-permute-start | bytes 1572872 | tf_op jit(solution)/shard_map/ppermute | solution.py:445
  16.1 25.7 %collective-permute-start.6 = (bf16[2,128,1024]{2,1,0:T(8,128)(2,1)S(1)}, bf16[2,128,1024]{2,1,0:T(8,128)(2,1)S(1)}, u32[]{:S(2)}, u32[]{:S(2)}) collective-permute-start(bf16[2,128,1024]{2,1,0:T(8,128)(2,1)S(1)} %get-tuple-element.45), channel_id=1, source_target_pairs={{0,6},{1,7},{2,4},{3,5},{4,2},{5,3},{6,0},{7,1},{8,14},{9,15},{10,... | collective-permute-start | bytes 1572872 | tf_op jit(solution)/shard_map/ppermute | solution.py:445
  18.8 14.1 %collective-permute-start.10 = (bf16[128,1024]{1,0:T(8,128)(2,1)S(1)}, bf16[128,1024]{1,0:T(8,128)(2,1)S(1)}, u32[]{:S(2)}, u32[]{:S(2)}) collective-permute-start(bf16[128,1024]{1,0:T(8,128)(2,1)S(1)} %stack.3.refs_8_.refs_4_.refs_0_), channel_id=1, source_target_pairs={{0,16},{1,17},{2,18},{3,19},{4,20},{5,21},{6,22},{7,23},{8,24},{9,... | collective-permute-start | bytes 786440 | tf_op jit(solution)/shard_map/ppermute | solution.py:445
  21.5 13.1 %collective-permute-start.9 = (bf16[128,1024]{1,0:T(8,128)(2,1)S(1)}, bf16[128,1024]{1,0:T(8,128)(2,1)S(1)}, u32[]{:S(2)}, u32[]{:S(2)}) collective-permute-start(bf16[128,1024]{1,0:T(8,128)(2,1)S(1)} %stack.3.refs_8_.refs_4_.refs_0_), channel_id=1, source_target_pairs={{0,8},{1,9},{2,10},{3,11},{4,12},{5,13},{6,14},{7,15},{8,0},{9,1},... | collective-permute-start | bytes 786440 | tf_op jit(solution)/shard_map/ppermute | solution.py:445
  33.0 8.8 %collective-permute-start.11 = (bf16[128,1024]{1,0:T(8,128)(2,1)S(1)}, bf16[128,1024]{1,0:T(8,128)(2,1)S(1)}, u32[]{:S(2)}, u32[]{:S(2)}) collective-permute-start(bf16[128,1024]{1,0:T(8,128)(2,1)S(1)} %collective-permute-done.10.refs_10_.refs_6_.refs_2_), channel_id=1, source_target_pairs={{0,8},{1,9},{2,10},{3,11},{4,12},{5,13},{6,14},{7,15},{8,0},{9,1},... | collective-permute-start | bytes 786440 | tf_op jit(solution)/shard_map/ppermute | solution.py:445
  34.0 17.1 %collective-permute-start.14 = (bf16[128,1024]{1,0:T(8,128)(2,1)S(1)}, bf16[128,1024]{1,0:T(8,128)(2,1)S(1)}, u32[]{:S(2)}, u32[]{:S(2)}) collective-permute-start(bf16[128,1024]{1,0:T(8,128)(2,1)S(1)} %stack.3.refs_8_.refs_4_.refs_0_), channel_id=1, source_target_pairs={{0,1},{1,0},{2,3},{3,2},{4,5},{5,4},{6,7},{7,6},{8,9},{9,8},{10,11... | collective-permute-start | bytes 786440 | tf_op jit(solution)/shard_map/ppermute | solution.py:445
  34.1 17.1 %collective-permute-start.16 = (bf16[128,1024]{1,0:T(8,128)(2,1)S(1)}, bf16[128,1024]{1,0:T(8,128)(2,1)S(1)}, u32[]{:S(2)}, u32[]{:S(2)}) collective-permute-start(bf16[128,1024]{1,0:T(8,128)(2,1)S(1)} %collective-permute-done.10.refs_10_.refs_6_.refs_2_), channel_id=1, source_target_pairs={{0,1},{1,0},{2,3},{3,2},{4,5},{5,4},{6,7},{7,6},{8,9},{9,8},{10,11... | collective-permute-start | bytes 786440 | tf_op jit(solution)/shard_map/ppermute | solution.py:445
  34.6 17.1 %collective-permute-start.15 = (bf16[128,1024]{1,0:T(8,128)(2,1)S(1)}, bf16[128,1024]{1,0:T(8,128)(2,1)S(1)}, u32[]{:S(2)}, u32[]{:S(2)}) collective-permute-start(bf16[128,1024]{1,0:T(8,128)(2,1)S(1)} %collective-permute-done.9.refs_9_.refs_5_.refs_1_), channel_id=1, source_target_pairs={{0,1},{1,0},{2,3},{3,2},{4,5},{5,4},{6,7},{7,6},{8,9},{9,8},{10,11... | collective-permute-start | bytes 786440 | tf_op jit(solution)/shard_map/ppermute | solution.py:445
  44.8 15.8 %collective-permute-start.21 = (bf16[256,1024]{1,0:T(8,128)(2,1)S(1)}, bf16[256,1024]{1,0:T(8,128)(2,1)S(1)}, u32[]{:S(2)}, u32[]{:S(2)}) collective-permute-start(bf16[256,1024]{1,0:T(8,128)(2,1)S(1)} %get-tuple-element.48.refs_8_), channel_id=1, source_target_pairs={{0,8},{1,9},{2,10},{3,11},{4,12},{5,13},{6,14},{7,15},{24,16},{25,... | collective-permute-start | bytes 1572872 | tf_op jit(solution)/shard_map/ppermute | solution.py:445
  48.4 22.2 %collective-permute-start.23 = (bf16[256,1024]{1,0:T(8,128)(2,1)S(1)}, bf16[256,1024]{1,0:T(8,128)(2,1)S(1)}, u32[]{:S(2)}, u32[]{:S(2)}) collective-permute-start(bf16[256,1024]{1,0:T(8,128)(2,1)S(1)} %get-tuple-element.64), channel_id=1, source_target_pairs={{0,8},{1,9},{2,10},{3,11},{4,12},{5,13},{6,14},{7,15},{24,16},{25,... | collective-permute-start | bytes 1572872 | tf_op jit(solution)/shard_map/ppermute | solution.py:445
  51.1 1.6 %collective-permute-start.12 = (bf16[256,512]{1,0:T(8,128)(2,1)S(1)}, bf16[256,512]{1,0:T(8,128)(2,1)S(1)}, u32[]{:S(2)}, u32[]{:S(2)}) collective-permute-start(bf16[256,512]{1,0:T(8,128)(2,1)S(1)} %get-tuple-element.50), channel_id=1, source_target_pairs={{0,1},{1,0},{2,3},{3,2},{4,5},{5,4},{6,7},{7,6},{8,9},{9,8},{10,11... | collective-permute-start | bytes 786440 | tf_op jit(solution)/shard_map/ppermute | solution.py:445
  51.2 1.9 %collective-permute-start.13 = (bf16[256,512]{1,0:T(8,128)(2,1)S(1)}, bf16[256,512]{1,0:T(8,128)(2,1)S(1)}, u32[]{:S(2)}, u32[]{:S(2)}) collective-permute-start(bf16[256,512]{1,0:T(8,128)(2,1)S(1)} %get-tuple-element.51), channel_id=1, source_target_pairs={{0,1},{1,0},{2,3},{3,2},{4,5},{5,4},{6,7},{7,6},{8,9},{9,8},{10,11... | collective-permute-start | bytes 786440 | tf_op jit(solution)/shard_map/ppermute | solution.py:445
  51.7 1.8 %collective-permute-start.17 = (bf16[128,1024]{1,0:T(8,128)(2,1)S(1)}, bf16[128,1024]{1,0:T(8,128)(2,1)S(1)}, u32[]{:S(2)}, u32[]{:S(2)}) collective-permute-start(bf16[128,1024]{1,0:T(8,128)(2,1)S(1)} %collective-permute-done.11.refs_11_.refs_7_.refs_3_), channel_id=1, source_target_pairs={{0,1},{1,0},{2,3},{3,2},{4,5},{5,4},{6,7},{7,6},{8,9},{9,8},{10,11... | collective-permute-start | bytes 786440 | tf_op jit(solution)/shard_map/ppermute | solution.py:445
  54.9 20.3 %collective-permute-start.20 = (bf16[128,2560]{1,0:T(8,128)(2,1)S(1)}, bf16[128,2560]{1,0:T(8,128)(2,1)S(1)}, u32[]{:S(2)}, u32[]{:S(2)}) collective-permute-start(bf16[128,2560]{1,0:T(8,128)(2,1)S(1)} %get-tuple-element.56), channel_id=1, source_target_pairs={{0,6},{1,7},{2,4},{3,5},{4,2},{5,3},{6,0},{7,1},{8,14},{9,15},{10,... | collective-permute-start | bytes 1966088 | tf_op jit(solution)/shard_map/ppermute | solution.py:445
  60.8 10.3 %collective-permute-start.26 = (bf16[128,1024]{1,0:T(8,128)(2,1)S(1)}, bf16[128,1024]{1,0:T(8,128)(2,1)S(1)}, u32[]{:S(2)}, u32[]{:S(2)}) collective-permute-start(bf16[128,1024]{1,0:T(8,128)(2,1)S(1)} %get-tuple-element.67), channel_id=1, source_target_pairs={{8,16},{9,17},{10,18},{11,19},{12,20},{13,21},{14,22},{15,23},{16,... | collective-permute-start | bytes 786440 | tf_op jit(solution)/shard_map/ppermute | solution.py:445
  61.5 12.7 %collective-permute-start.22 = (bf16[128,1024]{1,0:T(8,128)(2,1)S(1)}, bf16[128,1024]{1,0:T(8,128)(2,1)S(1)}, u32[]{:S(2)}, u32[]{:S(2)}) collective-permute-start(bf16[128,1024]{1,0:T(8,128)(2,1)S(1)} %get-tuple-element.62), channel_id=1, source_target_pairs={{8,16},{9,17},{10,18},{11,19},{12,20},{13,21},{14,22},{15,23},{16,... | collective-permute-start | bytes 786440 | tf_op jit(solution)/shard_map/ppermute | solution.py:445
  62.2 24.3 %collective-permute-start.18 = (bf16[128,2560]{1,0:T(8,128)(2,1)S(1)}, bf16[128,2560]{1,0:T(8,128)(2,1)S(1)}, u32[]{:S(2)}, u32[]{:S(2)}) collective-permute-start(bf16[128,2560]{1,0:T(8,128)(2,1)S(1)} %get-tuple-element.54), channel_id=1, source_target_pairs={{0,4},{1,5},{2,6},{3,7},{4,0},{5,1},{6,2},{7,3},{8,12},{9,13},{10,... | collective-permute-start | bytes 1966088 | tf_op jit(solution)/shard_map/ppermute | solution.py:445
  70.6 16.2 %collective-permute-start.19 = (bf16[128,2560]{1,0:T(8,128)(2,1)S(1)}, bf16[128,2560]{1,0:T(8,128)(2,1)S(1)}, u32[]{:S(2)}, u32[]{:S(2)}) collective-permute-start(bf16[128,2560]{1,0:T(8,128)(2,1)S(1)} %get-tuple-element.55), channel_id=1, source_target_pairs={{0,2},{1,3},{2,0},{3,1},{4,6},{5,7},{6,4},{7,5},{8,10},{9,11},{10,... | collective-permute-start | bytes 1966088 | tf_op jit(solution)/shard_map/ppermute | solution.py:445
  71.2 9.0 %collective-permute-start.27 = (bf16[128,1024]{1,0:T(8,128)(2,1)S(1)}, bf16[128,1024]{1,0:T(8,128)(2,1)S(1)}, u32[]{:S(2)}, u32[]{:S(2)}) collective-permute-start(bf16[128,1024]{1,0:T(8,128)(2,1)S(1)} %get-tuple-element.68), channel_id=1, source_target_pairs={{0,8},{1,9},{2,10},{3,11},{4,12},{5,13},{6,14},{7,15},{8,0},{9,1},... | collective-permute-start | bytes 786440 | tf_op jit(solution)/shard_map/ppermute | solution.py:445
  74.2 12.5 %copy-start = (bf16[1,128,8192]{2,1,0:T(8,128)(2,1)S(1)}, bf16[1,128,8192]{2,1,0:T(8,128)(2,1)}, u32[]{:S(2)}) copy-start(bf16[1,128,8192]{2,1,0:T(8,128)(2,1)} %param.8) | copy-start | bytes 6291460
  74.2 12.5 %copy-start.4 = (f32[8192]{0:T(1024)S(1)}, f32[8192]{0:T(1024)}, u32[]{:S(2)}) copy-start(f32[8192]{0:T(1024)} %param.9) | copy-start | bytes 98308
  74.2 6.7 %collective-permute-start.28 = (bf16[128,1024]{1,0:T(8,128)(2,1)S(1)}, bf16[128,1024]{1,0:T(8,128)(2,1)S(1)}, u32[]{:S(2)}, u32[]{:S(2)}) collective-permute-start(bf16[128,1024]{1,0:T(8,128)(2,1)S(1)} %get-tuple-element.69), channel_id=1, source_target_pairs={{8,16},{9,17},{10,18},{11,19},{12,20},{13,21},{14,22},{15,23},{16,... | collective-permute-start | bytes 786440 | tf_op jit(solution)/shard_map/ppermute | solution.py:445
  75.2 15.2 %collective-permute-start.24 = (bf16[128,1024]{1,0:T(8,128)(2,1)S(1)}, bf16[128,1024]{1,0:T(8,128)(2,1)S(1)}, u32[]{:S(2)}, u32[]{:S(2)}) collective-permute-start(bf16[128,1024]{1,0:T(8,128)(2,1)S(1)} %get-tuple-element.65), channel_id=1, source_target_pairs={{0,8},{1,9},{2,10},{3,11},{4,12},{5,13},{6,14},{7,15},{8,0},{9,1},... | collective-permute-start | bytes 786440 | tf_op jit(solution)/shard_map/ppermute | solution.py:445
  80.2 10.1 %collective-permute-start.25 = (bf16[128,1024]{1,0:T(8,128)(2,1)S(1)}, bf16[128,1024]{1,0:T(8,128)(2,1)S(1)}, u32[]{:S(2)}, u32[]{:S(2)}) collective-permute-start(bf16[128,1024]{1,0:T(8,128)(2,1)S(1)} %get-tuple-element.66), channel_id=1, source_target_pairs={{8,16},{9,17},{10,18},{11,19},{12,20},{13,21},{14,22},{15,23},{16,... | collective-permute-start | bytes 786440 | tf_op jit(solution)/shard_map/ppermute | solution.py:445
  81.0 10.3 %collective-permute-start.29 = (bf16[128,1024]{1,0:T(8,128)(2,1)S(1)}, bf16[128,1024]{1,0:T(8,128)(2,1)S(1)}, u32[]{:S(2)}, u32[]{:S(2)}) collective-permute-start(bf16[128,1024]{1,0:T(8,128)(2,1)S(1)} %relay.7), channel_id=1, source_target_pairs={{0,4},{1,5},{2,6},{3,7},{4,0},{5,1},{6,2},{7,3},{8,12},{9,13},{10,... | collective-permute-start | bytes 786440 | tf_op jit(solution)/shard_map/ppermute | solution.py:445
  86.7 4.6 %copy-start.1 = (f32[1,128,2048]{2,1,0:T(8,128)S(1)}, f32[1,128,2048]{2,1,0:T(8,128)}, u32[]{:S(2)}) copy-start(f32[1,128,2048]{2,1,0:T(8,128)} %param.13) | copy-start | bytes 3145732
  86.7 4.6 %copy-start.2 = (f32[1,128,2048]{2,1,0:T(8,128)S(1)}, f32[1,128,2048]{2,1,0:T(8,128)}, u32[]{:S(2)}) copy-start(f32[1,128,2048]{2,1,0:T(8,128)} %param.14) | copy-start | bytes 3145732
  86.7 4.6 %copy-start.3 = (f32[1,128,2048]{2,1,0:T(8,128)S(1)}, f32[1,128,2048]{2,1,0:T(8,128)}, u32[]{:S(2)}) copy-start(f32[1,128,2048]{2,1,0:T(8,128)} %param.15) | copy-start | bytes 3145732

commit v10 on v9

--- a/solution.py
+++ b/solution.py
@@ -34,7 +34,7 @@
     return pl.ds(pl.multiple_of(((seq * 2 + x) * parts + part) * width, width), width)
 
 
-def norm_kernel(parts, tok_ref, far_ref, gain_ref, *refs):
+def norm_kernel(parts, tok_ref, far_ref, gain_ref, after_ref, *refs):
     out_refs = [refs[i : i + parts] for i in range(0, len(refs), parts)]
     chips = len(out_refs)
     width = out_refs[0][0].shape[-1]
@@ -48,7 +48,7 @@
                 out_refs[k][part][i] = (scaled * gain_ref[:, cols]).astype(bf16)
 
 
-def norm_blocks(tokens, far, gain, chips, width, parts):
+def norm_blocks(tokens, far, gain, chips, width, parts, after):
     rows, model = tokens.shape
     step = min(rows, 32)
     outs = pl.pallas_call(
@@ -58,6 +58,7 @@
             pl.BlockSpec((step, model), lambda i: (i, 0)),
             pl.BlockSpec((step, model), lambda i: (i, 0)),
             pl.BlockSpec((1, model), lambda i: (0, 0)),
+            pl.BlockSpec(memory_space=pl.ANY),
         ],
         out_specs=[pl.BlockSpec((2, step, width // parts), lambda i: (0, i, 0))] * (chips * parts),
         out_shape=[jax.ShapeDtypeStruct((2, rows, width // parts), bf16)] * (chips * parts),
@@ -68,6 +69,7 @@
         pltpu.with_memory_space_constraint(tokens, pltpu.HBM),
         far,
         pltpu.with_memory_space_constraint(gain, pltpu.HBM),
+        after,
     )
     return [outs[i : i + parts] for i in range(0, len(outs), parts)]
 
@@ -146,31 +148,50 @@
     )(owner, *after)
 
 
-def weight_kernel(planes, chips, plan, *refs):
-    sel_ref, refs = refs[0], refs[1:]
-    grad_refs, refs = [*refs[:2], refs[2].at[: refs[0].shape[0]], refs[2].at[refs[0].shape[0] :]], refs[3:]
-    pieces, refs = refs[:chips], refs[chips:]
-    out_refs, (held, base) = refs[-len(plan) - 3 : -2], refs[-2:]
-    rows = pieces[0].shape[1]
-    feats = sel_ref.shape[1]
+def chip_term(k, chips, grad_refs, piece_ref, joined, at):
+    _, rows, width = piece_ref.shape
+    near = grad_refs[k * 2 // chips]
+    first = k % (chips // 2) * rows
+    joined[:rows, :] = near[first : first + rows, at : at + 256]
+    joined[rows:, :] = grad_refs[2][k * rows : (k + 1) * rows, at : at + 256]
+    return lax.dot_general(
+        joined[...],
+        piece_ref[...].reshape(2 * rows, width),
+        (((0,), (0,)), ((), ())),
+        preferred_element_type=f32,
+    )
+
+
+def early_kernel(chips, *refs):
+    grad_refs, piece_refs, (base_ref, joined) = refs[:3], refs[3:-2], refs[-2:]
+    for at in range(0, base_ref.shape[0], 256):
+        total = None
+        for k, piece_ref in enumerate(piece_refs):
+            term = chip_term(k, chips, grad_refs, piece_ref, joined, at)
+            total = term if total is None else total + term
+        base_ref[at : at + 256, :] = total
+
+
+def early_weight(grads, pieces):
+    _, rows, width = pieces[0].shape
+    feats = grads[0].shape[1]
+    return pl.pallas_call(
+        functools.partial(early_kernel, len(pieces) + 1),
+        out_shape=jax.ShapeDtypeStruct((feats, width), f32),
+        scratch_shapes=[pltpu.VMEM((2 * rows, 256), bf16)],
+        compiler_params=limit(24),
+        name="early_weight",
+    )(*grads, *pieces)
+
+
+def weight_kernel(planes, chips, plan, sel_ref, base_ref, *refs):
+    grad_refs, piece_ref = refs[:3], refs[3]
+    out_refs, (base, joined) = refs[-len(plan) - 3 : -2], refs[-2:]
     block = sel_ref.shape[0] // planes
-    half = chips // 2
     z = lax.axis_index("dp") // 2
-    for k in range(chips):
-        for i in range(2):
-            at = k % half * rows
-            held[2 * i + k // half, at : at + rows, :] = pieces[k][i]
-    for at in range(0, feats, 256):
-        total = None
-        for i in range(4):
-            term = lax.dot_general(
-                grad_refs[i][:, at : at + 256],
-                held[i],
-                (((0,), (0,)), ((), ())),
-                preferred_element_type=f32,
-            )
-            total = term if total is None else total + term
-        base[at : at + 256, :] = total.astype(bf16)
+    for at in range(0, base.shape[0], 256):
+        term = chip_term(chips - 1, chips, grad_refs, piece_ref, joined, at)
+        base[at : at + 256, :] = (base_ref[at : at + 256, :] + term).astype(bf16)
 
     def chosen(plane):
         at = pl.multiple_of(plane * block, block)
@@ -187,25 +208,19 @@
     out_refs[-1][...] = chosen(z).astype(bf16)
 
 
-def weight_blocks(selected, grads, pieces, planes, plan, after):
-    chips = len(pieces)
+def weight_blocks(selected, early, grads, piece, chips, planes, plan, after):
     slots_all, feats = selected.shape
-    _, rows, width = pieces[0].shape
-    total = 2 * chips * rows
+    _, rows, width = piece.shape
     block = slots_all // planes
     return pl.pallas_call(
         functools.partial(weight_kernel, planes, chips, plan),
-        in_specs=[pl.BlockSpec(memory_space=pltpu.VMEM)] * (4 + chips)
+        in_specs=[pl.BlockSpec(memory_space=pltpu.VMEM)] * 6
         + [pl.BlockSpec(memory_space=pl.ANY)] * len(after),
         out_shape=[jax.ShapeDtypeStruct((block, width), bf16)] * (len(plan) + 1),
-        scratch_shapes=[
-            pltpu.VMEM((4, total // 4, width), bf16),
-            pltpu.VMEM((feats, width), bf16),
-        ],
-        compiler_params=limit(40),
-        cost_estimate=cost(2 * (slots_all + total) * feats * width, 4 * total * width),
+        scratch_shapes=[pltpu.VMEM((feats, width), bf16), pltpu.VMEM((2 * rows, 256), bf16)],
+        compiler_params=limit(24),
         name="weight_blocks",
-    )(selected, *grads, *pieces, *after)
+    )(selected, early, *grads, piece, *after)
 
 
 def gather_weight(piece_refs, held):
@@ -475,7 +490,7 @@
     w_got = to_x(w_send)
 
     gain_row, owner_row = gain[None, :], owner[None, :]
-    sent = norm_blocks(tokens, tokens_far, gain_row, chips, width, parts)
+    sent = norm_blocks(tokens, tokens_far, gain_row, chips, width, parts, w_keep)
     grads = stack(grads, 2, [sent[0][0], w_keep])
     pieces = [sent[0]] + [[to_chip(p, k) for p in sent[k]] for k in range(1, chips)]
     grads_far = [to_core(grads[-1])]
@@ -495,9 +510,9 @@
         for even in (True, False)
         if any(busy(z, step, even) for z in range(planes))
     ]
-    outs = weight_blocks(
-        selected, [*grads, *grads_far], [piece[0] for piece in pieces], planes, plan, weights
-    )
+    every = [*grads, *grads_far]
+    early = early_weight(every, [piece[0] for piece in pieces[:-1]])
+    outs = weight_blocks(selected, early, every, pieces[-1][0], chips, planes, plan, weights)
     ready = dict(zip(plan, outs))
     got = {even: across(ready[1, even], 1, even) for even in (True, False) if (1, even) in ready}
     held = [{even: (value, chunk) for even, value in got.items()} for chunk in range(2)]

time: 94.3 us -> 93.5 us (level)
    pallas_call x0 -> x1, Pallas kernels: none -> 1 us  [early_weight(): pl.pallas_call(functools.partial(early_kernel, len(pieces) + 1), out_shap...]
where the time goes in v10:
time: 93.5 us; the launch traced here: 93.1 us
  waiting for transfers between devices  39.2 us (42%)
  starting transfers between devices  35.3 us (38%)
  Pallas kernels  17.7 us (19%)
    ppermute x30, waiting for transfers between devices, permute(): return lax.ppermute(value, ('dp', 'seq'), pairs)  39.2 us
    ppermute x30, starting transfers between devices, permute(): return lax.ppermute(value, ('dp', 'seq'), pairs)  35.3 us
    pallas_call x1, Pallas kernels, grad_x_blocks(): pl.pallas_call(grad_x_kernel, grid=(rows // step,), in_specs=[pl.BlockSpe...  3.62 us
    pallas_call x1, Pallas kernels, norm_blocks(): pl.pallas_call(functools.partial(norm_kernel, parts), grid=(rows // step,...  3.42 us
    pallas_call x1, Pallas kernels, adam(): pl.pallas_call(functools.partial(adam_kernel, token_total, len(parts)), g...  2.62 us
    pallas_call x1, Pallas kernels, weight_blocks(): pl.pallas_call(functools.partial(weight_kernel, planes, chips, plan), in_...  2.22 us
  transfers between devices with their start and end apart: 30, of which 12 were waited for; matrix products, arithmetic and copies ran while one was open for 0% of the time, Pallas kernels for 16%

profile of v10, /device:TPU:0, one launch (start us, length us, event | category | flops | bytes accessed | tf_op | source)
XLA Modules:
  0.0 93.1 jit_solution(1380969876638193813)
XLA Ops:
  0.6 0.5 collective-permute-start.3
  1.1 2.6 %collective-permute-start = (bf16[128,512]{1,0:T(8,128)(2,1)}, bf16[128,512]{1,0:T(8,128)(2,1)S(1)}, u32[]{:S(2)}, u32[]{:S(2)}) collective-permute-start(bf16[128,512]{1,0:T(8,128)(2,1)} %bitcast.20), channel_id=1, source_target_pairs={{0,4},{1,5},{2,6},{3,7},{4,0},{5,1},{6,2},{7,3},{8,12},{9,13},{10,... | collective-permute-start | bytes 393224 | tf_op jit(solution)/shard_map/ppermute | solution.py:460
  3.7 1.5 %collective-permute-start.1 = (bf16[128,512]{1,0:T(8,128)(2,1)}, bf16[128,512]{1,0:T(8,128)(2,1)S(1)}, u32[]{:S(2)}, u32[]{:S(2)}) collective-permute-start(bf16[128,512]{1,0:T(8,128)(2,1)} %bitcast.21), channel_id=1, source_target_pairs={{0,2},{1,3},{2,0},{3,1},{4,6},{5,7},{6,4},{7,5},{8,10},{9,11},{10,... | collective-permute-start | bytes 393224 | tf_op jit(solution)/shard_map/ppermute | solution.py:460
  5.3 1.0 %halves.1 = (bf16[64,1024]{1,0:T(8,128)(2,1)S(1)}, bf16[64,1024]{1,0:T(8,128)(2,1)S(1)}) custom-call(bf16[64,2048]{1,0:T(8,128)(2,1)} %w_ref.1), custom_call_target="tpu_custom_call" | custom-call | tf_op jit(solution)/shard_map/halves/pallas_call | solution.py:85
  6.3 3.4 %norm_blocks.1 = (bf16[2,128,1024]{2,1,0:T(8,128)(2,1)S(1)}, bf16[2,128,1024]{2,1,0:T(8,128)(2,1)S(1)}, bf16[2,128,1024]{2,1,0:T(8,128)(2,1)S(1)}, bf16[2,128,1024]{2,1,0:T(8,128)(2,1)S(1)}) custom-call(bf16[128,8192]{1,0:T(8,128)(2,1)} %bitcast.13, bf16[128,8192]{1,0:T(8,128)(2,1)S(1)} %collective-permute-done.3.far_ref, f32[1,8192]{1,0:T(1,128)} %bitcast.18, ...), custom_call_target="tpu_custom_call" | custom-call | flops 8388608 | bytes 6291456 | tf_op jit(solution)/shard_map/norm_blocks/pallas_call | solution.py:54
  9.7 2.6 %collective-permute-done.1.refs_2_ = bf16[128,512]{1,0:T(8,128)(2,1)S(1)} collective-permute-done((bf16[128,512]{1,0:T(8,128)(2,1)}, bf16[128,512]{1,0:T(8,128)(2,1)S(1)}, u32[]{:S(2)}, u32[]{:S(2)}) %collective-permute-start.1) | collective-permute-done | bytes 131104 | tf_op jit(solution)/shard_map/ppermute | solution.py:460
  12.5 1.3 %collective-permute-start.7 = (bf16[64,1024]{1,0:T(8,128)(2,1)S(1)}, bf16[64,1024]{1,0:T(8,128)(2,1)S(1)}, u32[]{:S(2)}, u32[]{:S(2)}) collective-permute-start(bf16[64,1024]{1,0:T(8,128)(2,1)S(1)} %get-tuple-element.46), channel_id=1, source_target_pairs={{0,4},{1,5},{2,6},{3,7},{4,0},{5,1},{6,2},{7,3},{8,12},{9,13},{10,... | collective-permute-start | bytes 393224 | tf_op jit(solution)/shard_map/ppermute | solution.py:460
  13.8 0.8 collective-permute-start.4
  14.6 1.5 %collective-permute-start.5 = (bf16[2,128,1024]{2,1,0:T(8,128)(2,1)S(1)}, bf16[2,128,1024]{2,1,0:T(8,128)(2,1)S(1)}, u32[]{:S(2)}, u32[]{:S(2)}) collective-permute-start(bf16[2,128,1024]{2,1,0:T(8,128)(2,1)S(1)} %get-tuple-element.44), channel_id=1, source_target_pairs={{0,2},{1,3},{2,0},{3,1},{4,6},{5,7},{6,4},{7,5},{8,10},{9,11},{10,... | collective-permute-start | bytes 1572872 | tf_op jit(solution)/shard_map/ppermute | solution.py:460
  16.1 1.2 %collective-permute-start.6 = (bf16[2,128,1024]{2,1,0:T(8,128)(2,1)S(1)}, bf16[2,128,1024]{2,1,0:T(8,128)(2,1)S(1)}, u32[]{:S(2)}, u32[]{:S(2)}) collective-permute-start(bf16[2,128,1024]{2,1,0:T(8,128)(2,1)S(1)} %get-tuple-element.45), channel_id=1, source_target_pairs={{0,6},{1,7},{2,4},{3,5},{4,2},{5,3},{6,0},{7,1},{8,14},{9,15},{10,... | collective-permute-start | bytes 1572872 | tf_op jit(solution)/shard_map/ppermute | solution.py:460
  17.2 1.6 %collective-permute-done.7.refs_1_ = bf16[64,1024]{1,0:T(8,128)(2,1)S(1)} collective-permute-done((bf16[64,1024]{1,0:T(8,128)(2,1)S(1)}, bf16[64,1024]{1,0:T(8,128)(2,1)S(1)}, u32[]{:S(2)}, u32[]{:S(2)}) %collective-permute-start.7) | collective-permute-done | bytes 131104 | tf_op jit(solution)/shard_map/ppermute | solution.py:460
  18.8 2.7 %collective-permute-start.10 = (bf16[128,1024]{1,0:T(8,128)(2,1)S(1)}, bf16[128,1024]{1,0:T(8,128)(2,1)S(1)}, u32[]{:S(2)}, u32[]{:S(2)}) collective-permute-start(bf16[128,1024]{1,0:T(8,128)(2,1)S(1)} %stack.3.refs_4_.refs_0_), channel_id=1, source_target_pairs={{0,16},{1,17},{2,18},{3,19},{4,20},{5,21},{6,22},{7,23},{8,24},{9,... | collective-permute-start | bytes 786440 | tf_op jit(solution)/shard_map/ppermute | solution.py:460
  21.5 1.6 %collective-permute-start.9 = (bf16[128,1024]{1,0:T(8,128)(2,1)S(1)}, bf16[128,1024]{1,0:T(8,128)(2,1)S(1)}, u32[]{:S(2)}, u32[]{:S(2)}) collective-permute-start(bf16[128,1024]{1,0:T(8,128)(2,1)S(1)} %stack.3.refs_4_.refs_0_), channel_id=1, source_target_pairs={{0,8},{1,9},{2,10},{3,11},{4,12},{5,13},{6,14},{7,15},{8,0},{9,1},... | collective-permute-start | bytes 786440 | tf_op jit(solution)/shard_map/ppermute | solution.py:460
  23.1 9.9 %collective-permute-done.10.refs_6_.refs_2_ = bf16[128,1024]{1,0:T(8,128)(2,1)S(1)} collective-permute-done((bf16[128,1024]{1,0:T(8,128)(2,1)S(1)}, bf16[128,1024]{1,0:T(8,128)(2,1)S(1)}, u32[]{:S(2)}, u32[]{:S(2)}) %collective-permute-start.10) | collective-permute-done | bytes 262176 | tf_op jit(solution)/shard_map/ppermute | solution.py:460
  33.0 0.6 collective-permute-start.11
  33.5 0.5 collective-permute-start.16
  34.1 0.5 select_rows.1.sel_ref
  34.6 1.0 %early_weight.1.base_ref = f32[512,1024]{1,0:T(8,128)S(1)} custom-call(bf16[256,512]{1,0:T(8,128)(2,1)S(1)} %get-tuple-element.41.refs_0_.grads_a_ref, bf16[256,512]{1,0:T(8,128)(2,1)S(1)} %get-tuple-element.42.refs_1_.grads_b_ref, bf16[512,512]{1,0:T(8,128)(2,1)S(1)} %collective-permute-done.8.refs_2_, ...), custom_call_target="tpu_custom_call" | custom-call | tf_op jit(solution)/shard_map/early_weight/pallas_call | solution.py:178
  35.6 6.2 %collective-permute-done.6.refs_3_ = bf16[2,128,1024]{2,1,0:T(8,128)(2,1)S(1)} collective-permute-done((bf16[2,128,1024]{2,1,0:T(8,128)(2,1)S(1)}, bf16[2,128,1024]{2,1,0:T(8,128)(2,1)S(1)}, u32[]{:S(2)}, u32[]{:S(2)}) %collective-permute-start.6) | collective-permute-done | bytes 524320 | tf_op jit(solution)/shard_map/ppermute | solution.py:460
  41.8 2.2 %weight_blocks.1 = (bf16[256,1024]{1,0:T(8,128)(2,1)S(1)}, bf16[256,1024]{1,0:T(8,128)(2,1)S(1)}, bf16[256,1024]{1,0:T(8,128)(2,1)S(1)}, bf16[256,1024]{1,0:T(8,...) custom-call(bf16[1024,512]{1,0:T(8,128)(2,1)S(1)} %select_rows.1.sel_ref, ...), custom_call_target="tpu_custom_call" | custom-call | tf_op jit(solution)/shard_map/weight_blocks/pallas_call | solution.py:215
  44.0 3.5 %collective-permute-start.21 = (bf16[256,1024]{1,0:T(8,128)(2,1)S(1)}, bf16[256,1024]{1,0:T(8,128)(2,1)S(1)}, u32[]{:S(2)}, u32[]{:S(2)}) collective-permute-start(bf16[256,1024]{1,0:T(8,128)(2,1)S(1)} %get-tuple-element.48.refs_8_), channel_id=1, source_target_pairs={{0,8},{1,9},{2,10},{3,11},{4,12},{5,13},{6,14},{7,15},{24,16},{25,... | collective-permute-start | bytes 1572872 | tf_op jit(solution)/shard_map/ppermute | solution.py:460
  47.6 1.3 %collective-permute-start.23 = (bf16[256,1024]{1,0:T(8,128)(2,1)S(1)}, bf16[256,1024]{1,0:T(8,128)(2,1)S(1)}, u32[]{:S(2)}, u32[]{:S(2)}) collective-permute-start(bf16[256,1024]{1,0:T(8,128)(2,1)S(1)} %get-tuple-element.64), channel_id=1, source_target_pairs={{0,8},{1,9},{2,10},{3,11},{4,12},{5,13},{6,14},{7,15},{24,16},{25,... | collective-permute-start | bytes 1572872 | tf_op jit(solution)/shard_map/ppermute | solution.py:460
  48.9 1.4 %value_parts.1 = (bf16[256,512]{1,0:T(8,128)(2,1)S(1)}, bf16[256,512]{1,0:T(8,128)(2,1)S(1)}, f32[512,512]{1,0:T(8,128)S(1)}) custom-call(bf16[2,128,1024]{2,1,0:T(8,128)(2,1)S(1)} %get-tuple-element.40.refs_4_.refs_0_.refs_3_, bf16[2,128,1024]{2,1,0:T(8,128)(2,1)S(1)} %collective-permute-done.4.refs_4_.refs_1_, ...), custom_call_target="tpu_custom_call" | custom-call | tf_op jit(solution)/shard_map/value_parts/pallas_call | solution.py:263
  50.4 0.5 collective-permute-start.13
  50.9 0.9 %collective-permute-done.12.got_a_ref = bf16[256,512]{1,0:T(8,128)(2,1)S(1)} collective-permute-done((bf16[256,512]{1,0:T(8,128)(2,1)S(1)}, bf16[256,512]{1,0:T(8,128)(2,1)S(1)}, u32[]{:S(2)}, u32[]{:S(2)}) %collective-permute-start.12) | collective-permute-done | bytes 262176 | tf_op jit(solution)/shard_map/ppermute | solution.py:460
  51.9 0.4 collective-permute-done.13.got_b_ref
  52.2 0.4 collective-permute-done.17.refs_7_
  52.6 1.4 %back_blocks.1 = (bf16[128,2048]{1,0:T(8,128)(2,1)S(1)}, bf16[128,2560]{1,0:T(8,128)(2,1)S(1)}, bf16[128,2560]{1,0:T(8,128)(2,1)S(1)}, bf16[128,2560]{1,0:T(8,128)(2,1)S(1)}, f32[128,512]{1,0:T(8,128)S(1)}) custom-call(bf16[256,512]{1,0:T(8,128)(2,1)S(1)} %get-tuple-element.41.refs_0_.grads_a_ref, ...), custom_call_target="tpu_custom_call" | custom-call | tf_op jit(solution)/shard_map/back_blocks/pallas_call | solution.py:302
  54.1 1.2 %collective-permute-start.20 = (bf16[128,2560]{1,0:T(8,128)(2,1)S(1)}, bf16[128,2560]{1,0:T(8,128)(2,1)S(1)}, u32[]{:S(2)}, u32[]{:S(2)}) collective-permute-start(bf16[128,2560]{1,0:T(8,128)(2,1)S(1)} %get-tuple-element.56), channel_id=1, source_target_pairs={{0,6},{1,7},{2,4},{3,5},{4,2},{5,3},{6,0},{7,1},{8,14},{9,15},{10,... | collective-permute-start | bytes 1966088 | tf_op jit(solution)/shard_map/ppermute | solution.py:460
  55.3 4.5 %collective-permute-done.21.refs_1_.refs_3_ = bf16[256,1024]{1,0:T(8,128)(2,1)S(1)} collective-permute-done((bf16[256,1024]{1,0:T(8,128)(2,1)S(1)}, bf16[256,1024]{1,0:T(8,128)(2,1)S(1)}, u32[]{:S(2)}, u32[]{:S(2)}) %collective-permute-start.21) | collective-permute-done | bytes 524320 | tf_op jit(solution)/shard_map/ppermute | solution.py:460
  59.9 0.1 relay.4
  60.0 0.7 collective-permute-start.26
  60.7 0.7 collective-permute-start.22
  61.3 0.6 collective-permute-start.18
  62.0 7.8 %collective-permute-done.23.refs_3_ = bf16[256,1024]{1,0:T(8,128)(2,1)S(1)} collective-permute-done((bf16[256,1024]{1,0:T(8,128)(2,1)S(1)}, bf16[256,1024]{1,0:T(8,128)(2,1)S(1)}, u32[]{:S(2)}, u32[]{:S(2)}) %collective-permute-start.23) | collective-permute-done | bytes 524320 | tf_op jit(solution)/shard_map/ppermute | solution.py:460
  69.7 0.5 collective-permute-start.19
  70.3 0.1 relay.6
  70.4 3.0 %collective-permute-start.27 = (bf16[128,1024]{1,0:T(8,128)(2,1)S(1)}, bf16[128,1024]{1,0:T(8,128)(2,1)S(1)}, u32[]{:S(2)}, u32[]{:S(2)}) collective-permute-start(bf16[128,1024]{1,0:T(8,128)(2,1)S(1)} %get-tuple-element.68), channel_id=1, source_target_pairs={{0,8},{1,9},{2,10},{3,11},{4,12},{5,13},{6,14},{7,15},{8,0},{9,1},... | collective-permute-start | bytes 786440 | tf_op jit(solution)/shard_map/ppermute | solution.py:460
  73.4 0.8 collective-permute-start.28
  74.2 0.1 relay.5
  74.3 5.1 %collective-permute-start.24 = (bf16[128,1024]{1,0:T(8,128)(2,1)S(1)}, bf16[128,1024]{1,0:T(8,128)(2,1)S(1)}, u32[]{:S(2)}, u32[]{:S(2)}) collective-permute-start(bf16[128,1024]{1,0:T(8,128)(2,1)S(1)} %get-tuple-element.65), channel_id=1, source_target_pairs={{0,8},{1,9},{2,10},{3,11},{4,12},{5,13},{6,14},{7,15},{8,0},{9,1},... | collective-permute-start | bytes 786440 | tf_op jit(solution)/shard_map/ppermute | solution.py:460
  79.4 0.7 collective-permute-start.25
  80.2 1.7 %collective-permute-start.29 = (bf16[128,1024]{1,0:T(8,128)(2,1)S(1)}, bf16[128,1024]{1,0:T(8,128)(2,1)S(1)}, u32[]{:S(2)}, u32[]{:S(2)}) collective-permute-start(bf16[128,1024]{1,0:T(8,128)(2,1)S(1)} %relay.7), channel_id=1, source_target_pairs={{0,4},{1,5},{2,6},{3,7},{4,0},{5,1},{6,2},{7,3},{8,12},{9,13},{10,... | collective-permute-start | bytes 786440 | tf_op jit(solution)/shard_map/ppermute | solution.py:460
  82.0 3.7 %collective-permute-done.18.refs_1_ = bf16[128,2560]{1,0:T(8,128)(2,1)S(1)} collective-permute-done((bf16[128,2560]{1,0:T(8,128)(2,1)S(1)}, bf16[128,2560]{1,0:T(8,128)(2,1)S(1)}, u32[]{:S(2)}, u32[]{:S(2)}) %collective-permute-start.18) | collective-permute-done | bytes 655392 | tf_op jit(solution)/shard_map/ppermute | solution.py:460
  85.7 0.2 collective-permute-done.19.refs_2_
  85.9 3.6 %grad_x_blocks.1 = (bf16[128,8192]{1,0:T(8,128)(2,1)}, bf16[128,512]{1,0:T(8,128)(2,1)}) custom-call(bf16[128,8192]{1,0:T(8,128)(2,1)S(1)} %bitcast.14, f32[1,8192]{1,0:T(1,128)S(1)} %bitcast.19, f32[128,512]{1,0:T(8,128)S(1)} %get-tuple-element.52.part_ref, bf16[128,2048]{1,0:T(8,128)(2,1)S(1)} %get-tuple-element.53.refs_0_, ...), custom_call_target="tpu_custom_call" | custom-call | flops 16777216 | bytes 6291456 | tf_op jit(solution)/shard_map/grad_x_blocks/pallas_call | solution.py:347
  89.6 1.0 %collective-permute-done.29.refs_3_ = bf16[128,1024]{1,0:T(8,128)(2,1)S(1)} collective-permute-done((bf16[128,1024]{1,0:T(8,128)(2,1)S(1)}, bf16[128,1024]{1,0:T(8,128)(2,1)S(1)}, u32[]{:S(2)}, u32[]{:S(2)}) %collective-permute-start.29) | collective-permute-done | bytes 262176 | tf_op jit(solution)/shard_map/ppermute | solution.py:460
  90.5 2.6 %adam.1 = (f32[128,2048]{1,0:T(8,128)}, f32[128,2048]{1,0:T(8,128)}, f32[128,2048]{1,0:T(8,128)}) custom-call(s32[1,512]{1,0:T(1,128)S(1)} %bitcast.25, bf16[128,1024]{1,0:T(8,128)(2,1)S(1)} %slice.3.refs_0_, bf16[128,1024]{1,0:T(8,128)(2,1)S(1)} %collective-permute-done.24.refs_1_, bf16[128,1024]{1,0:T(8,128)(2,1)S(1)} %collective-permute-done.25.refs_2_, ...), custom_call_target="tpu_custom_call" | custom-call | flops 5242880 | bytes 7864320 | tf_op jit(solution)/shard_map/adam/pallas_call | solution.py:428
  (42 shorter events, 0.6 us)
Async XLA Ops:
  0.6 5.6 %collective-permute-start.3 = (bf16[128,8192]{1,0:T(8,128)(2,1)}, bf16[128,8192]{1,0:T(8,128)(2,1)S(1)}, u32[]{:S(2)}, u32[]{:S(2)}) collective-permute-start(bf16[128,8192]{1,0:T(8,128)(2,1)} %bitcast.12), channel_id=1, source_target_pairs={{0,1},{1,0},{2,3},{3,2},{4,5},{5,4},{6,7},{7,6},{8,9},{9,8},{10,11... | collective-permute-start | bytes 6291464 | tf_op jit(solution)/shard_map/ppermute | solution.py:460
  1.1 8.6 %collective-permute-start = (bf16[128,512]{1,0:T(8,128)(2,1)}, bf16[128,512]{1,0:T(8,128)(2,1)S(1)}, u32[]{:S(2)}, u32[]{:S(2)}) collective-permute-start(bf16[128,512]{1,0:T(8,128)(2,1)} %bitcast.20), channel_id=1, source_target_pairs={{0,4},{1,5},{2,6},{3,7},{4,0},{5,1},{6,2},{7,3},{8,12},{9,13},{10,... | collective-permute-start | bytes 393224 | tf_op jit(solution)/shard_map/ppermute | solution.py:460
  3.7 8.6 %collective-permute-start.1 = (bf16[128,512]{1,0:T(8,128)(2,1)}, bf16[128,512]{1,0:T(8,128)(2,1)S(1)}, u32[]{:S(2)}, u32[]{:S(2)}) collective-permute-start(bf16[128,512]{1,0:T(8,128)(2,1)} %bitcast.21), channel_id=1, source_target_pairs={{0,2},{1,3},{2,0},{3,1},{4,6},{5,7},{6,4},{7,5},{8,10},{9,11},{10,... | collective-permute-start | bytes 393224 | tf_op jit(solution)/shard_map/ppermute | solution.py:460
  5.2 7.1 %collective-permute-start.2 = (bf16[128,512]{1,0:T(8,128)(2,1)}, bf16[128,512]{1,0:T(8,128)(2,1)S(1)}, u32[]{:S(2)}, u32[]{:S(2)}) collective-permute-start(bf16[128,512]{1,0:T(8,128)(2,1)} %bitcast.22), channel_id=1, source_target_pairs={{0,6},{1,7},{2,4},{3,5},{4,2},{5,3},{6,0},{7,1},{8,14},{9,15},{10,... | collective-permute-start | bytes 393224 | tf_op jit(solution)/shard_map/ppermute | solution.py:460
  6.2 6.1 %copy-start.5 = (bf16[1,128,512]{2,1,0:T(8,128)(2,1)S(1)}, bf16[1,128,512]{2,1,0:T(8,128)(2,1)}, u32[]{:S(2)}) copy-start(bf16[1,128,512]{2,1,0:T(8,128)(2,1)} %param.11) | copy-start | bytes 393220
  9.7 24.4 %copy-start.6 = (s32[512]{0:T(512)S(1)}, s32[512]{0:T(512)}, u32[]{:S(2)}) copy-start(s32[512]{0:T(512)} %param.12) | copy-start | bytes 6148
  12.4 6.4 %collective-permute-start.8 = (bf16[512,512]{1,0:T(8,128)(2,1)S(1)}, bf16[512,512]{1,0:T(8,128)(2,1)S(1)}, u32[]{:S(2)}, u32[]{:S(2)}) collective-permute-start(bf16[512,512]{1,0:T(8,128)(2,1)S(1)} %get-tuple-element.47), channel_id=1, source_target_pairs={{0,1},{1,0},{2,3},{3,2},{4,5},{5,4},{6,7},{7,6},{8,9},{9,8},{10,11... | collective-permute-start | bytes 1572872 | tf_op jit(solution)/shard_map/ppermute | solution.py:460
  12.5 6.4 %collective-permute-start.7 = (bf16[64,1024]{1,0:T(8,128)(2,1)S(1)}, bf16[64,1024]{1,0:T(8,128)(2,1)S(1)}, u32[]{:S(2)}, u32[]{:S(2)}) collective-permute-start(bf16[64,1024]{1,0:T(8,128)(2,1)S(1)} %get-tuple-element.46), channel_id=1, source_target_pairs={{0,4},{1,5},{2,6},{3,7},{4,0},{5,1},{6,2},{7,3},{8,12},{9,13},{10,... | collective-permute-start | bytes 393224 | tf_op jit(solution)/shard_map/ppermute | solution.py:460
  13.8 19.8 %collective-permute-start.4 = (bf16[2,128,1024]{2,1,0:T(8,128)(2,1)S(1)}, bf16[2,128,1024]{2,1,0:T(8,128)(2,1)S(1)}, u32[]{:S(2)}, u32[]{:S(2)}) collective-permute-start(bf16[2,128,1024]{2,1,0:T(8,128)(2,1)S(1)} %get-tuple-element.43), channel_id=1, source_target_pairs={{0,4},{1,5},{2,6},{3,7},{4,0},{5,1},{6,2},{7,3},{8,12},{9,13},{10,... | collective-permute-start | bytes 1572872 | tf_op jit(solution)/shard_map/ppermute | solution.py:460
  14.6 19.0 %collective-permute-start.5 = (bf16[2,128,1024]{2,1,0:T(8,128)(2,1)S(1)}, bf16[2,128,1024]{2,1,0:T(8,128)(2,1)S(1)}, u32[]{:S(2)}, u32[]{:S(2)}) collective-permute-start(bf16[2,128,1024]{2,1,0:T(8,128)(2,1)S(1)} %get-tuple-element.44), channel_id=1, source_target_pairs={{0,2},{1,3},{2,0},{3,1},{4,6},{5,7},{6,4},{7,5},{8,10},{9,11},{10,... | collective-permute-start | bytes 1572872 | tf_op jit(solution)/shard_map/ppermute | solution.py:460
  16.1 25.7 %collective-permute-start.6 = (bf16[2,128,1024]{2,1,0:T(8,128)(2,1)S(1)}, bf16[2,128,1024]{2,1,0:T(8,128)(2,1)S(1)}, u32[]{:S(2)}, u32[]{:S(2)}) collective-permute-start(bf16[2,128,1024]{2,1,0:T(8,128)(2,1)S(1)} %get-tuple-element.45), channel_id=1, source_target_pairs={{0,6},{1,7},{2,4},{3,5},{4,2},{5,3},{6,0},{7,1},{8,14},{9,15},{10,... | collective-permute-start | bytes 1572872 | tf_op jit(solution)/shard_map/ppermute | solution.py:460
  18.8 14.1 %collective-permute-start.10 = (bf16[128,1024]{1,0:T(8,128)(2,1)S(1)}, bf16[128,1024]{1,0:T(8,128)(2,1)S(1)}, u32[]{:S(2)}, u32[]{:S(2)}) collective-permute-start(bf16[128,1024]{1,0:T(8,128)(2,1)S(1)} %stack.3.refs_4_.refs_0_), channel_id=1, source_target_pairs={{0,16},{1,17},{2,18},{3,19},{4,20},{5,21},{6,22},{7,23},{8,24},{9,... | collective-permute-start | bytes 786440 | tf_op jit(solution)/shard_map/ppermute | solution.py:460
  21.5 12.5 %collective-permute-start.9 = (bf16[128,1024]{1,0:T(8,128)(2,1)S(1)}, bf16[128,1024]{1,0:T(8,128)(2,1)S(1)}, u32[]{:S(2)}, u32[]{:S(2)}) collective-permute-start(bf16[128,1024]{1,0:T(8,128)(2,1)S(1)} %stack.3.refs_4_.refs_0_), channel_id=1, source_target_pairs={{0,8},{1,9},{2,10},{3,11},{4,12},{5,13},{6,14},{7,15},{8,0},{9,1},... | collective-permute-start | bytes 786440 | tf_op jit(solution)/shard_map/ppermute | solution.py:460
  33.0 8.8 %collective-permute-start.11 = (bf16[128,1024]{1,0:T(8,128)(2,1)S(1)}, bf16[128,1024]{1,0:T(8,128)(2,1)S(1)}, u32[]{:S(2)}, u32[]{:S(2)}) collective-permute-start(bf16[128,1024]{1,0:T(8,128)(2,1)S(1)} %collective-permute-done.10.refs_6_.refs_2_), channel_id=1, source_target_pairs={{0,8},{1,9},{2,10},{3,11},{4,12},{5,13},{6,14},{7,15},{8,0},{9,1},... | collective-permute-start | bytes 786440 | tf_op jit(solution)/shard_map/ppermute | solution.py:460
  33.5 16.7 %collective-permute-start.14 = (bf16[128,1024]{1,0:T(8,128)(2,1)S(1)}, bf16[128,1024]{1,0:T(8,128)(2,1)S(1)}, u32[]{:S(2)}, u32[]{:S(2)}) collective-permute-start(bf16[128,1024]{1,0:T(8,128)(2,1)S(1)} %stack.3.refs_4_.refs_0_), channel_id=1, source_target_pairs={{0,1},{1,0},{2,3},{3,2},{4,5},{5,4},{6,7},{7,6},{8,9},{9,8},{10,11... | collective-permute-start | bytes 786440 | tf_op jit(solution)/shard_map/ppermute | solution.py:460
  33.5 16.8 %collective-permute-start.16 = (bf16[128,1024]{1,0:T(8,128)(2,1)S(1)}, bf16[128,1024]{1,0:T(8,128)(2,1)S(1)}, u32[]{:S(2)}, u32[]{:S(2)}) collective-permute-start(bf16[128,1024]{1,0:T(8,128)(2,1)S(1)} %collective-permute-done.10.refs_6_.refs_2_), channel_id=1, source_target_pairs={{0,1},{1,0},{2,3},{3,2},{4,5},{5,4},{6,7},{7,6},{8,9},{9,8},{10,11... | collective-permute-start | bytes 786440 | tf_op jit(solution)/shard_map/ppermute | solution.py:460
  34.0 16.8 %collective-permute-start.15 = (bf16[128,1024]{1,0:T(8,128)(2,1)S(1)}, bf16[128,1024]{1,0:T(8,128)(2,1)S(1)}, u32[]{:S(2)}, u32[]{:S(2)}) collective-permute-start(bf16[128,1024]{1,0:T(8,128)(2,1)S(1)} %collective-permute-done.9.refs_5_.refs_1_), channel_id=1, source_target_pairs={{0,1},{1,0},{2,3},{3,2},{4,5},{5,4},{6,7},{7,6},{8,9},{9,8},{10,11... | collective-permute-start | bytes 786440 | tf_op jit(solution)/shard_map/ppermute | solution.py:460
  44.0 15.8 %collective-permute-start.21 = (bf16[256,1024]{1,0:T(8,128)(2,1)S(1)}, bf16[256,1024]{1,0:T(8,128)(2,1)S(1)}, u32[]{:S(2)}, u32[]{:S(2)}) collective-permute-start(bf16[256,1024]{1,0:T(8,128)(2,1)S(1)} %get-tuple-element.48.refs_8_), channel_id=1, source_target_pairs={{0,8},{1,9},{2,10},{3,11},{4,12},{5,13},{6,14},{7,15},{24,16},{25,... | collective-permute-start | bytes 1572872 | tf_op jit(solution)/shard_map/ppermute | solution.py:460
  47.6 22.2 %collective-permute-start.23 = (bf16[256,1024]{1,0:T(8,128)(2,1)S(1)}, bf16[256,1024]{1,0:T(8,128)(2,1)S(1)}, u32[]{:S(2)}, u32[]{:S(2)}) collective-permute-start(bf16[256,1024]{1,0:T(8,128)(2,1)S(1)} %get-tuple-element.64), channel_id=1, source_target_pairs={{0,8},{1,9},{2,10},{3,11},{4,12},{5,13},{6,14},{7,15},{24,16},{25,... | collective-permute-start | bytes 1572872 | tf_op jit(solution)/shard_map/ppermute | solution.py:460
  50.3 1.6 %collective-permute-start.12 = (bf16[256,512]{1,0:T(8,128)(2,1)S(1)}, bf16[256,512]{1,0:T(8,128)(2,1)S(1)}, u32[]{:S(2)}, u32[]{:S(2)}) collective-permute-start(bf16[256,512]{1,0:T(8,128)(2,1)S(1)} %get-tuple-element.50), channel_id=1, source_target_pairs={{0,1},{1,0},{2,3},{3,2},{4,5},{5,4},{6,7},{7,6},{8,9},{9,8},{10,11... | collective-permute-start | bytes 786440 | tf_op jit(solution)/shard_map/ppermute | solution.py:460
  50.4 1.9 %collective-permute-start.13 = (bf16[256,512]{1,0:T(8,128)(2,1)S(1)}, bf16[256,512]{1,0:T(8,128)(2,1)S(1)}, u32[]{:S(2)}, u32[]{:S(2)}) collective-permute-start(bf16[256,512]{1,0:T(8,128)(2,1)S(1)} %get-tuple-element.51), channel_id=1, source_target_pairs={{0,1},{1,0},{2,3},{3,2},{4,5},{5,4},{6,7},{7,6},{8,9},{9,8},{10,11... | collective-permute-start | bytes 786440 | tf_op jit(solution)/shard_map/ppermute | solution.py:460
  50.9 1.8 %collective-permute-start.17 = (bf16[128,1024]{1,0:T(8,128)(2,1)S(1)}, bf16[128,1024]{1,0:T(8,128)(2,1)S(1)}, u32[]{:S(2)}, u32[]{:S(2)}) collective-permute-start(bf16[128,1024]{1,0:T(8,128)(2,1)S(1)} %collective-permute-done.11.refs_7_.refs_3_), channel_id=1, source_target_pairs={{0,1},{1,0},{2,3},{3,2},{4,5},{5,4},{6,7},{7,6},{8,9},{9,8},{10,11... | collective-permute-start | bytes 786440 | tf_op jit(solution)/shard_map/ppermute | solution.py:460
  54.1 20.3 %collective-permute-start.20 = (bf16[128,2560]{1,0:T(8,128)(2,1)S(1)}, bf16[128,2560]{1,0:T(8,128)(2,1)S(1)}, u32[]{:S(2)}, u32[]{:S(2)}) collective-permute-start(bf16[128,2560]{1,0:T(8,128)(2,1)S(1)} %get-tuple-element.56), channel_id=1, source_target_pairs={{0,6},{1,7},{2,4},{3,5},{4,2},{5,3},{6,0},{7,1},{8,14},{9,15},{10,... | collective-permute-start | bytes 1966088 | tf_op jit(solution)/shard_map/ppermute | solution.py:460
  60.0 10.3 %collective-permute-start.26 = (bf16[128,1024]{1,0:T(8,128)(2,1)S(1)}, bf16[128,1024]{1,0:T(8,128)(2,1)S(1)}, u32[]{:S(2)}, u32[]{:S(2)}) collective-permute-start(bf16[128,1024]{1,0:T(8,128)(2,1)S(1)} %get-tuple-element.67), channel_id=1, source_target_pairs={{8,16},{9,17},{10,18},{11,19},{12,20},{13,21},{14,22},{15,23},{16,... | collective-permute-start | bytes 786440 | tf_op jit(solution)/shard_map/ppermute | solution.py:460
  60.7 12.7 %collective-permute-start.22 = (bf16[128,1024]{1,0:T(8,128)(2,1)S(1)}, bf16[128,1024]{1,0:T(8,128)(2,1)S(1)}, u32[]{:S(2)}, u32[]{:S(2)}) collective-permute-start(bf16[128,1024]{1,0:T(8,128)(2,1)S(1)} %get-tuple-element.62), channel_id=1, source_target_pairs={{8,16},{9,17},{10,18},{11,19},{12,20},{13,21},{14,22},{15,23},{16,... | collective-permute-start | bytes 786440 | tf_op jit(solution)/shard_map/ppermute | solution.py:460
  61.3 24.3 %collective-permute-start.18 = (bf16[128,2560]{1,0:T(8,128)(2,1)S(1)}, bf16[128,2560]{1,0:T(8,128)(2,1)S(1)}, u32[]{:S(2)}, u32[]{:S(2)}) collective-permute-start(bf16[128,2560]{1,0:T(8,128)(2,1)S(1)} %get-tuple-element.54), channel_id=1, source_target_pairs={{0,4},{1,5},{2,6},{3,7},{4,0},{5,1},{6,2},{7,3},{8,12},{9,13},{10,... | collective-permute-start | bytes 1966088 | tf_op jit(solution)/shard_map/ppermute | solution.py:460
  69.7 16.2 %collective-permute-start.19 = (bf16[128,2560]{1,0:T(8,128)(2,1)S(1)}, bf16[128,2560]{1,0:T(8,128)(2,1)S(1)}, u32[]{:S(2)}, u32[]{:S(2)}) collective-permute-start(bf16[128,2560]{1,0:T(8,128)(2,1)S(1)} %get-tuple-element.55), channel_id=1, source_target_pairs={{0,2},{1,3},{2,0},{3,1},{4,6},{5,7},{6,4},{7,5},{8,10},{9,11},{10,... | collective-permute-start | bytes 1966088 | tf_op jit(solution)/shard_map/ppermute | solution.py:460
  70.4 9.1 %collective-permute-start.27 = (bf16[128,1024]{1,0:T(8,128)(2,1)S(1)}, bf16[128,1024]{1,0:T(8,128)(2,1)S(1)}, u32[]{:S(2)}, u32[]{:S(2)}) collective-permute-start(bf16[128,1024]{1,0:T(8,128)(2,1)S(1)} %get-tuple-element.68), channel_id=1, source_target_pairs={{0,8},{1,9},{2,10},{3,11},{4,12},{5,13},{6,14},{7,15},{8,0},{9,1},... | collective-permute-start | bytes 786440 | tf_op jit(solution)/shard_map/ppermute | solution.py:460
  73.4 12.5 %copy-start = (bf16[1,128,8192]{2,1,0:T(8,128)(2,1)S(1)}, bf16[1,128,8192]{2,1,0:T(8,128)(2,1)}, u32[]{:S(2)}) copy-start(bf16[1,128,8192]{2,1,0:T(8,128)(2,1)} %param.8) | copy-start | bytes 6291460
  73.4 12.5 %copy-start.4 = (f32[8192]{0:T(1024)S(1)}, f32[8192]{0:T(1024)}, u32[]{:S(2)}) copy-start(f32[8192]{0:T(1024)} %param.9) | copy-start | bytes 98308
  73.4 6.7 %collective-permute-start.28 = (bf16[128,1024]{1,0:T(8,128)(2,1)S(1)}, bf16[128,1024]{1,0:T(8,128)(2,1)S(1)}, u32[]{:S(2)}, u32[]{:S(2)}) collective-permute-start(bf16[128,1024]{1,0:T(8,128)(2,1)S(1)} %get-tuple-element.69), channel_id=1, source_target_pairs={{8,16},{9,17},{10,18},{11,19},{12,20},{13,21},{14,22},{15,23},{16,... | collective-permute-start | bytes 786440 | tf_op jit(solution)/shard_map/ppermute | solution.py:460
  74.3 15.2 %collective-permute-start.24 = (bf16[128,1024]{1,0:T(8,128)(2,1)S(1)}, bf16[128,1024]{1,0:T(8,128)(2,1)S(1)}, u32[]{:S(2)}, u32[]{:S(2)}) collective-permute-start(bf16[128,1024]{1,0:T(8,128)(2,1)S(1)} %get-tuple-element.65), channel_id=1, source_target_pairs={{0,8},{1,9},{2,10},{3,11},{4,12},{5,13},{6,14},{7,15},{8,0},{9,1},... | collective-permute-start | bytes 786440 | tf_op jit(solution)/shard_map/ppermute | solution.py:460
  79.4 10.1 %collective-permute-start.25 = (bf16[128,1024]{1,0:T(8,128)(2,1)S(1)}, bf16[128,1024]{1,0:T(8,128)(2,1)S(1)}, u32[]{:S(2)}, u32[]{:S(2)}) collective-permute-start(bf16[128,1024]{1,0:T(8,128)(2,1)S(1)} %get-tuple-element.66), channel_id=1, source_target_pairs={{8,16},{9,17},{10,18},{11,19},{12,20},{13,21},{14,22},{15,23},{16,... | collective-permute-start | bytes 786440 | tf_op jit(solution)/shard_map/ppermute | solution.py:460
  80.2 10.3 %collective-permute-start.29 = (bf16[128,1024]{1,0:T(8,128)(2,1)S(1)}, bf16[128,1024]{1,0:T(8,128)(2,1)S(1)}, u32[]{:S(2)}, u32[]{:S(2)}) collective-permute-start(bf16[128,1024]{1,0:T(8,128)(2,1)S(1)} %relay.7), channel_id=1, source_target_pairs={{0,4},{1,5},{2,6},{3,7},{4,0},{5,1},{6,2},{7,3},{8,12},{9,13},{10,... | collective-permute-start | bytes 786440 | tf_op jit(solution)/shard_map/ppermute | solution.py:460
  85.9 4.6 %copy-start.1 = (f32[1,128,2048]{2,1,0:T(8,128)S(1)}, f32[1,128,2048]{2,1,0:T(8,128)}, u32[]{:S(2)}) copy-start(f32[1,128,2048]{2,1,0:T(8,128)} %param.13) | copy-start | bytes 3145732
  85.9 4.6 %copy-start.2 = (f32[1,128,2048]{2,1,0:T(8,128)S(1)}, f32[1,128,2048]{2,1,0:T(8,128)}, u32[]{:S(2)}) copy-start(f32[1,128,2048]{2,1,0:T(8,128)} %param.14) | copy-start | bytes 3145732
  85.9 4.6 %copy-start.3 = (f32[1,128,2048]{2,1,0:T(8,128)S(1)}, f32[1,128,2048]{2,1,0:T(8,128)}, u32[]{:S(2)}) copy-start(f32[1,128,2048]{2,1,0:T(8,128)} %param.15) | copy-start | bytes 3145732

commit v11 on v10

--- a/solution.py
+++ b/solution.py
@@ -184,18 +184,14 @@
     )(*grads, *pieces)
 
 
-def weight_kernel(planes, chips, plan, sel_ref, base_ref, *refs):
-    grad_refs, piece_ref = refs[:3], refs[3]
-    out_refs, (base, joined) = refs[-len(plan) - 3 : -2], refs[-2:]
+def slot_blocks(planes, plan, sel_ref, base_ref, out_refs):
     block = sel_ref.shape[0] // planes
     z = lax.axis_index("dp") // 2
-    for at in range(0, base.shape[0], 256):
-        term = chip_term(chips - 1, chips, grad_refs, piece_ref, joined, at)
-        base[at : at + 256, :] = (base_ref[at : at + 256, :] + term).astype(bf16)
 
     def chosen(plane):
         at = pl.multiple_of(plane * block, block)
-        return jnp.dot(sel_ref[pl.ds(at, block), :], base[...], preferred_element_type=f32)
+        rows = jnp.dot(sel_ref[pl.ds(at, block), :], base_ref[...], preferred_element_type=f32)
+        return rows.astype(bf16)
 
     for (step, even), out_ref in zip(plan, out_refs):
         ahead = planes - step
@@ -203,9 +199,19 @@
 
         @pl.when((plane >= 0) & (plane < planes))
         def _():
-            out_ref[...] = chosen(plane).astype(bf16)
-
-    out_refs[-1][...] = chosen(z).astype(bf16)
+            out_ref[...] = chosen(plane)
+
+    if len(out_refs) > len(plan):
+        out_refs[-1][...] = chosen(z)
+
+
+def weight_kernel(planes, chips, plan, sel_ref, early_ref, *refs):
+    grad_refs, piece_ref = refs[:3], refs[3]
+    base_ref, out_refs, joined = refs[-len(plan) - 2], refs[-len(plan) - 1 : -1], refs[-1]
+    for at in range(0, base_ref.shape[0], 256):
+        term = chip_term(chips - 1, chips, grad_refs, piece_ref, joined, at)
+        base_ref[at : at + 256, :] = (early_ref[at : at + 256, :] + term).astype(bf16)
+    slot_blocks(planes, plan, sel_ref, base_ref, out_refs)
 
 
 def weight_blocks(selected, early, grads, piece, chips, planes, plan, after):
@@ -216,11 +222,28 @@
         functools.partial(weight_kernel, planes, chips, plan),
         in_specs=[pl.BlockSpec(memory_space=pltpu.VMEM)] * 6
         + [pl.BlockSpec(memory_space=pl.ANY)] * len(after),
-        out_shape=[jax.ShapeDtypeStruct((block, width), bf16)] * (len(plan) + 1),
-        scratch_shapes=[pltpu.VMEM((feats, width), bf16), pltpu.VMEM((2 * rows, 256), bf16)],
+        out_shape=[jax.ShapeDtypeStruct((feats, width), bf16)]
+        + [jax.ShapeDtypeStruct((block, width), bf16)] * len(plan),
+        scratch_shapes=[pltpu.VMEM((2 * rows, 256), bf16)],
         compiler_params=limit(24),
         name="weight_blocks",
     )(selected, early, *grads, piece, *after)
+
+
+def later_kernel(planes, plan, sel_ref, base_ref, *refs):
+    slot_blocks(planes, plan, sel_ref, base_ref, refs[-len(plan) - 1 :])
+
+
+def later_blocks(selected, base, planes, plan, after):
+    block, width = selected.shape[0] // planes, base.shape[1]
+    return pl.pallas_call(
+        functools.partial(later_kernel, planes, plan),
+        in_specs=[pl.BlockSpec(memory_space=pltpu.VMEM)] * 2
+        + [pl.BlockSpec(memory_space=pl.ANY)] * len(after),
+        out_shape=[jax.ShapeDtypeStruct((block, width), bf16)] * (len(plan) + 1),
+        compiler_params=limit(24),
+        name="later_blocks",
+    )(selected, base, *after)
 
 
 def gather_weight(piece_refs, held):
@@ -512,7 +535,10 @@
     ]
     every = [*grads, *grads_far]
     early = early_weight(every, [piece[0] for piece in pieces[:-1]])
-    outs = weight_blocks(selected, early, every, pieces[-1][0], chips, planes, plan, weights)
+    base, *outs = weight_blocks(
+        selected, early, every, pieces[-1][0], chips, planes, plan[:2], weights
+    )
+    outs += later_blocks(selected, base, planes, plan[2:], outs[:1])
     ready = dict(zip(plan, outs))
     got = {even: across(ready[1, even], 1, even) for even in (True, False) if (1, even) in ready}
     held = [{even: (value, chunk) for even, value in got.items()} for chunk in range(2)]

time: 93.5 us -> 91.9 us (0.983)
  starting transfers between devices: 35.3 us -> 34.1 us
    ppermute x30, starting transfers between devices: 35.3 us -> 34.1 us  [permute(): return lax.ppermute(value, ('dp', 'seq'), pairs)]
where the time goes in v11:
time: 91.9 us; the launch traced here: 91.4 us
  waiting for transfers between devices  38.7 us (42%)
  starting transfers between devices  34.1 us (37%)
  Pallas kernels  17.7 us (19%)
    ppermute x30, waiting for transfers between devices, permute(): return lax.ppermute(value, ('dp', 'seq'), pairs)  38.7 us
    ppermute x30, starting transfers between devices, permute(): return lax.ppermute(value, ('dp', 'seq'), pairs)  34.1 us
    pallas_call x1, Pallas kernels, grad_x_blocks(): pl.pallas_call(grad_x_kernel, grid=(rows // step,), in_specs=[pl.BlockSpe...  3.62 us
    pallas_call x1, Pallas kernels, norm_blocks(): pl.pallas_call(functools.partial(norm_kernel, parts), grid=(rows // step,...  3.42 us
    pallas_call x1, Pallas kernels, adam(): pl.pallas_call(functools.partial(adam_kernel, token_total, len(parts)), g...  2.62 us
  transfers between devices with their start and end apart: 30, of which 12 were waited for; matrix products, arithmetic and copies ran while one was open for 0% of the time, Pallas kernels for 16%

profile of v11, /device:TPU:0, one launch (start us, length us, event | category | flops | bytes accessed | tf_op | source)
XLA Modules:
  0.0 91.4 jit_solution(3418319817711795734)
XLA Ops:
  0.6 0.5 collective-permute-start.3
  1.1 2.6 %collective-permute-start = (bf16[128,512]{1,0:T(8,128)(2,1)}, bf16[128,512]{1,0:T(8,128)(2,1)S(1)}, u32[]{:S(2)}, u32[]{:S(2)}) collective-permute-start(bf16[128,512]{1,0:T(8,128)(2,1)} %bitcast.20), channel_id=1, source_target_pairs={{0,4},{1,5},{2,6},{3,7},{4,0},{5,1},{6,2},{7,3},{8,12},{9,13},{10,... | collective-permute-start | bytes 393224 | tf_op jit(solution)/shard_map/ppermute | solution.py:483
  3.7 1.5 %collective-permute-start.1 = (bf16[128,512]{1,0:T(8,128)(2,1)}, bf16[128,512]{1,0:T(8,128)(2,1)S(1)}, u32[]{:S(2)}, u32[]{:S(2)}) collective-permute-start(bf16[128,512]{1,0:T(8,128)(2,1)} %bitcast.21), channel_id=1, source_target_pairs={{0,2},{1,3},{2,0},{3,1},{4,6},{5,7},{6,4},{7,5},{8,10},{9,11},{10,... | collective-permute-start | bytes 393224 | tf_op jit(solution)/shard_map/ppermute | solution.py:483
  5.3 1.0 %halves.1 = (bf16[64,1024]{1,0:T(8,128)(2,1)S(1)}, bf16[64,1024]{1,0:T(8,128)(2,1)S(1)}) custom-call(bf16[64,2048]{1,0:T(8,128)(2,1)} %w_ref.1), custom_call_target="tpu_custom_call" | custom-call | tf_op jit(solution)/shard_map/halves/pallas_call | solution.py:85
  6.3 3.4 %norm_blocks.1 = (bf16[2,128,1024]{2,1,0:T(8,128)(2,1)S(1)}, bf16[2,128,1024]{2,1,0:T(8,128)(2,1)S(1)}, bf16[2,128,1024]{2,1,0:T(8,128)(2,1)S(1)}, bf16[2,128,1024]{2,1,0:T(8,128)(2,1)S(1)}) custom-call(bf16[128,8192]{1,0:T(8,128)(2,1)} %bitcast.13, bf16[128,8192]{1,0:T(8,128)(2,1)S(1)} %collective-permute-done.3.far_ref, f32[1,8192]{1,0:T(1,128)} %bitcast.18, ...), custom_call_target="tpu_custom_call" | custom-call | flops 8388608 | bytes 6291456 | tf_op jit(solution)/shard_map/norm_blocks/pallas_call | solution.py:54
  9.7 2.6 %collective-permute-done.1.refs_2_ = bf16[128,512]{1,0:T(8,128)(2,1)S(1)} collective-permute-done((bf16[128,512]{1,0:T(8,128)(2,1)}, bf16[128,512]{1,0:T(8,128)(2,1)S(1)}, u32[]{:S(2)}, u32[]{:S(2)}) %collective-permute-start.1) | collective-permute-done | bytes 131104 | tf_op jit(solution)/shard_map/ppermute | solution.py:483
  12.5 1.3 %collective-permute-start.7 = (bf16[64,1024]{1,0:T(8,128)(2,1)S(1)}, bf16[64,1024]{1,0:T(8,128)(2,1)S(1)}, u32[]{:S(2)}, u32[]{:S(2)}) collective-permute-start(bf16[64,1024]{1,0:T(8,128)(2,1)S(1)} %get-tuple-element.47), channel_id=1, source_target_pairs={{0,4},{1,5},{2,6},{3,7},{4,0},{5,1},{6,2},{7,3},{8,12},{9,13},{10,... | collective-permute-start | bytes 393224 | tf_op jit(solution)/shard_map/ppermute | solution.py:483
  13.8 0.8 collective-permute-start.4
  14.6 1.5 %collective-permute-start.5 = (bf16[2,128,1024]{2,1,0:T(8,128)(2,1)S(1)}, bf16[2,128,1024]{2,1,0:T(8,128)(2,1)S(1)}, u32[]{:S(2)}, u32[]{:S(2)}) collective-permute-start(bf16[2,128,1024]{2,1,0:T(8,128)(2,1)S(1)} %get-tuple-element.45), channel_id=1, source_target_pairs={{0,2},{1,3},{2,0},{3,1},{4,6},{5,7},{6,4},{7,5},{8,10},{9,11},{10,... | collective-permute-start | bytes 1572872 | tf_op jit(solution)/shard_map/ppermute | solution.py:483
  16.1 1.2 %collective-permute-start.6 = (bf16[2,128,1024]{2,1,0:T(8,128)(2,1)S(1)}, bf16[2,128,1024]{2,1,0:T(8,128)(2,1)S(1)}, u32[]{:S(2)}, u32[]{:S(2)}) collective-permute-start(bf16[2,128,1024]{2,1,0:T(8,128)(2,1)S(1)} %get-tuple-element.46), channel_id=1, source_target_pairs={{0,6},{1,7},{2,4},{3,5},{4,2},{5,3},{6,0},{7,1},{8,14},{9,15},{10,... | collective-permute-start | bytes 1572872 | tf_op jit(solution)/shard_map/ppermute | solution.py:483
  17.2 1.6 %collective-permute-done.7.refs_1_ = bf16[64,1024]{1,0:T(8,128)(2,1)S(1)} collective-permute-done((bf16[64,1024]{1,0:T(8,128)(2,1)S(1)}, bf16[64,1024]{1,0:T(8,128)(2,1)S(1)}, u32[]{:S(2)}, u32[]{:S(2)}) %collective-permute-start.7) | collective-permute-done | bytes 131104 | tf_op jit(solution)/shard_map/ppermute | solution.py:483
  18.8 2.7 %collective-permute-start.10 = (bf16[128,1024]{1,0:T(8,128)(2,1)S(1)}, bf16[128,1024]{1,0:T(8,128)(2,1)S(1)}, u32[]{:S(2)}, u32[]{:S(2)}) collective-permute-start(bf16[128,1024]{1,0:T(8,128)(2,1)S(1)} %stack.3.refs_4_.refs_0_), channel_id=1, source_target_pairs={{0,16},{1,17},{2,18},{3,19},{4,20},{5,21},{6,22},{7,23},{8,24},{9,... | collective-permute-start | bytes 786440 | tf_op jit(solution)/shard_map/ppermute | solution.py:483
  21.5 1.6 %collective-permute-start.9 = (bf16[128,1024]{1,0:T(8,128)(2,1)S(1)}, bf16[128,1024]{1,0:T(8,128)(2,1)S(1)}, u32[]{:S(2)}, u32[]{:S(2)}) collective-permute-start(bf16[128,1024]{1,0:T(8,128)(2,1)S(1)} %stack.3.refs_4_.refs_0_), channel_id=1, source_target_pairs={{0,8},{1,9},{2,10},{3,11},{4,12},{5,13},{6,14},{7,15},{8,0},{9,1},... | collective-permute-start | bytes 786440 | tf_op jit(solution)/shard_map/ppermute | solution.py:483
  23.1 9.9 %collective-permute-done.10.refs_6_.refs_2_ = bf16[128,1024]{1,0:T(8,128)(2,1)S(1)} collective-permute-done((bf16[128,1024]{1,0:T(8,128)(2,1)S(1)}, bf16[128,1024]{1,0:T(8,128)(2,1)S(1)}, u32[]{:S(2)}, u32[]{:S(2)}) %collective-permute-start.10) | collective-permute-done | bytes 262176 | tf_op jit(solution)/shard_map/ppermute | solution.py:483
  33.0 0.6 collective-permute-start.11
  33.5 0.5 collective-permute-start.16
  34.1 0.5 select_rows.1.sel_ref
  34.6 1.0 %early_weight.1.early_ref = f32[512,1024]{1,0:T(8,128)S(1)} custom-call(bf16[256,512]{1,0:T(8,128)(2,1)S(1)} %get-tuple-element.42.refs_0_.grads_a_ref, bf16[256,512]{1,0:T(8,128)(2,1)S(1)} %get-tuple-element.43.refs_1_.grads_b_ref, bf16[512,512]{1,0:T(8,128)(2,1)S(1)} %collective-permute-done.8.refs_2_, ...), custom_call_target="tpu_custom_call" | custom-call | tf_op jit(solution)/shard_map/early_weight/pallas_call | solution.py:178
  35.6 6.2 %collective-permute-done.6.refs_3_ = bf16[2,128,1024]{2,1,0:T(8,128)(2,1)S(1)} collective-permute-done((bf16[2,128,1024]{2,1,0:T(8,128)(2,1)S(1)}, bf16[2,128,1024]{2,1,0:T(8,128)(2,1)S(1)}, u32[]{:S(2)}, u32[]{:S(2)}) %collective-permute-start.6) | collective-permute-done | bytes 524320 | tf_op jit(solution)/shard_map/ppermute | solution.py:483
  41.8 1.3 %weight_blocks.1 = (bf16[512,1024]{1,0:T(8,128)(2,1)S(1)}, bf16[256,1024]{1,0:T(8,128)(2,1)S(1)}, bf16[256,1024]{1,0:T(8,128)(2,1)S(1)}) custom-call(bf16[1024,512]{1,0:T(8,128)(2,1)S(1)} %select_rows.1.sel_ref, f32[512,1024]{1,0:T(8,128)S(1)} %early_weight.1.early_ref, bf16[256,512]{1,0:T(8,128)(2,1)S(1)} %get-tuple-element.42.refs_0_.grads_a_ref, ...), custom_call_target="tpu_custom_call" | custom-call | tf_op jit(solution)/shard_map/weight_blocks/pallas_call | solution.py:221
  43.1 2.6 %collective-permute-start.21 = (bf16[256,1024]{1,0:T(8,128)(2,1)S(1)}, bf16[256,1024]{1,0:T(8,128)(2,1)S(1)}, u32[]{:S(2)}, u32[]{:S(2)}) collective-permute-start(bf16[256,1024]{1,0:T(8,128)(2,1)S(1)} %get-tuple-element.49.refs_8_.refs_0_), channel_id=1, source_target_pairs={{0,8},{1,9},{2,10},{3,11},{4,12},{5,13},{6,14},{7,15},{24,16},{25,... | collective-permute-start | bytes 1572872 | tf_op jit(solution)/shard_map/ppermute | solution.py:483
  45.8 1.3 %collective-permute-start.23 = (bf16[256,1024]{1,0:T(8,128)(2,1)S(1)}, bf16[256,1024]{1,0:T(8,128)(2,1)S(1)}, u32[]{:S(2)}, u32[]{:S(2)}) collective-permute-start(bf16[256,1024]{1,0:T(8,128)(2,1)S(1)} %get-tuple-element.66), channel_id=1, source_target_pairs={{0,8},{1,9},{2,10},{3,11},{4,12},{5,13},{6,14},{7,15},{24,16},{25,... | collective-permute-start | bytes 1572872 | tf_op jit(solution)/shard_map/ppermute | solution.py:483
  47.1 1.4 %value_parts.1 = (bf16[256,512]{1,0:T(8,128)(2,1)S(1)}, bf16[256,512]{1,0:T(8,128)(2,1)S(1)}, f32[512,512]{1,0:T(8,128)S(1)}) custom-call(bf16[2,128,1024]{2,1,0:T(8,128)(2,1)S(1)} %get-tuple-element.41.refs_4_.refs_0_.refs_3_, bf16[2,128,1024]{2,1,0:T(8,128)(2,1)S(1)} %collective-permute-done.4.refs_4_.refs_1_, ...), custom_call_target="tpu_custom_call" | custom-call | tf_op jit(solution)/shard_map/value_parts/pallas_call | solution.py:286
  48.6 0.5 collective-permute-start.13
  49.2 0.9 %collective-permute-done.12.got_a_ref = bf16[256,512]{1,0:T(8,128)(2,1)S(1)} collective-permute-done((bf16[256,512]{1,0:T(8,128)(2,1)S(1)}, bf16[256,512]{1,0:T(8,128)(2,1)S(1)}, u32[]{:S(2)}, u32[]{:S(2)}) %collective-permute-start.12) | collective-permute-done | bytes 262176 | tf_op jit(solution)/shard_map/ppermute | solution.py:483
  50.1 0.4 collective-permute-done.13.got_b_ref
  50.5 0.4 collective-permute-done.17.refs_7_
  50.9 1.4 %back_blocks.1 = (bf16[128,2048]{1,0:T(8,128)(2,1)S(1)}, bf16[128,2560]{1,0:T(8,128)(2,1)S(1)}, bf16[128,2560]{1,0:T(8,128)(2,1)S(1)}, bf16[128,2560]{1,0:T(8,128)(2,1)S(1)}, f32[128,512]{1,0:T(8,128)S(1)}) custom-call(bf16[256,512]{1,0:T(8,128)(2,1)S(1)} %get-tuple-element.42.refs_0_.grads_a_ref, ...), custom_call_target="tpu_custom_call" | custom-call | tf_op jit(solution)/shard_map/back_blocks/pallas_call | solution.py:325
  52.3 1.2 %collective-permute-start.20 = (bf16[128,2560]{1,0:T(8,128)(2,1)S(1)}, bf16[128,2560]{1,0:T(8,128)(2,1)S(1)}, u32[]{:S(2)}, u32[]{:S(2)}) collective-permute-start(bf16[128,2560]{1,0:T(8,128)(2,1)S(1)} %get-tuple-element.57), channel_id=1, source_target_pairs={{0,6},{1,7},{2,4},{3,5},{4,2},{5,3},{6,0},{7,1},{8,14},{9,15},{10,... | collective-permute-start | bytes 1966088 | tf_op jit(solution)/shard_map/ppermute | solution.py:483
  53.5 0.9 later_blocks.1
  54.4 3.7 %collective-permute-done.21.refs_1_.refs_3_ = bf16[256,1024]{1,0:T(8,128)(2,1)S(1)} collective-permute-done((bf16[256,1024]{1,0:T(8,128)(2,1)S(1)}, bf16[256,1024]{1,0:T(8,128)(2,1)S(1)}, u32[]{:S(2)}, u32[]{:S(2)}) %collective-permute-start.21) | collective-permute-done | bytes 524320 | tf_op jit(solution)/shard_map/ppermute | solution.py:483
  58.1 0.1 relay.4
  58.2 0.7 collective-permute-start.26
  58.9 0.7 collective-permute-start.22
  59.6 0.6 collective-permute-start.18
  60.2 7.8 %collective-permute-done.23.refs_3_ = bf16[256,1024]{1,0:T(8,128)(2,1)S(1)} collective-permute-done((bf16[256,1024]{1,0:T(8,128)(2,1)S(1)}, bf16[256,1024]{1,0:T(8,128)(2,1)S(1)}, u32[]{:S(2)}, u32[]{:S(2)}) %collective-permute-start.23) | collective-permute-done | bytes 524320 | tf_op jit(solution)/shard_map/ppermute | solution.py:483
  68.0 0.5 collective-permute-start.19
  68.6 3.2 %collective-permute-start.27 = (bf16[128,1024]{1,0:T(8,128)(2,1)S(1)}, bf16[128,1024]{1,0:T(8,128)(2,1)S(1)}, u32[]{:S(2)}, u32[]{:S(2)}) collective-permute-start(bf16[128,1024]{1,0:T(8,128)(2,1)S(1)} %get-tuple-element.70), channel_id=1, source_target_pairs={{0,8},{1,9},{2,10},{3,11},{4,12},{5,13},{6,14},{7,15},{8,0},{9,1},... | collective-permute-start | bytes 786440 | tf_op jit(solution)/shard_map/ppermute | solution.py:483
  71.8 0.8 collective-permute-start.28
  72.6 0.1 relay.5
  72.7 5.1 %collective-permute-start.24 = (bf16[128,1024]{1,0:T(8,128)(2,1)S(1)}, bf16[128,1024]{1,0:T(8,128)(2,1)S(1)}, u32[]{:S(2)}, u32[]{:S(2)}) collective-permute-start(bf16[128,1024]{1,0:T(8,128)(2,1)S(1)} %get-tuple-element.67), channel_id=1, source_target_pairs={{0,8},{1,9},{2,10},{3,11},{4,12},{5,13},{6,14},{7,15},{8,0},{9,1},... | collective-permute-start | bytes 786440 | tf_op jit(solution)/shard_map/ppermute | solution.py:483
  77.8 0.7 collective-permute-start.25
  78.6 1.2 %collective-permute-start.29 = (bf16[128,1024]{1,0:T(8,128)(2,1)S(1)}, bf16[128,1024]{1,0:T(8,128)(2,1)S(1)}, u32[]{:S(2)}, u32[]{:S(2)}) collective-permute-start(bf16[128,1024]{1,0:T(8,128)(2,1)S(1)} %relay.7), channel_id=1, source_target_pairs={{0,4},{1,5},{2,6},{3,7},{4,0},{5,1},{6,2},{7,3},{8,12},{9,13},{10,... | collective-permute-start | bytes 786440 | tf_op jit(solution)/shard_map/ppermute | solution.py:483
  79.9 4.1 %collective-permute-done.18.refs_1_ = bf16[128,2560]{1,0:T(8,128)(2,1)S(1)} collective-permute-done((bf16[128,2560]{1,0:T(8,128)(2,1)S(1)}, bf16[128,2560]{1,0:T(8,128)(2,1)S(1)}, u32[]{:S(2)}, u32[]{:S(2)}) %collective-permute-start.18) | collective-permute-done | bytes 655392 | tf_op jit(solution)/shard_map/ppermute | solution.py:483
  83.9 0.2 collective-permute-done.19.refs_2_
  84.2 3.6 %grad_x_blocks.1 = (bf16[128,8192]{1,0:T(8,128)(2,1)}, bf16[128,512]{1,0:T(8,128)(2,1)}) custom-call(bf16[128,8192]{1,0:T(8,128)(2,1)S(1)} %bitcast.14, f32[1,8192]{1,0:T(1,128)S(1)} %bitcast.19, f32[128,512]{1,0:T(8,128)S(1)} %get-tuple-element.53.part_ref, bf16[128,2048]{1,0:T(8,128)(2,1)S(1)} %get-tuple-element.54.refs_0_, ...), custom_call_target="tpu_custom_call" | custom-call | flops 16777216 | bytes 6291456 | tf_op jit(solution)/shard_map/grad_x_blocks/pallas_call | solution.py:370
  87.8 1.0 %collective-permute-done.29.refs_3_ = bf16[128,1024]{1,0:T(8,128)(2,1)S(1)} collective-permute-done((bf16[128,1024]{1,0:T(8,128)(2,1)S(1)}, bf16[128,1024]{1,0:T(8,128)(2,1)S(1)}, u32[]{:S(2)}, u32[]{:S(2)}) %collective-permute-start.29) | collective-permute-done | bytes 262176 | tf_op jit(solution)/shard_map/ppermute | solution.py:483
  88.8 2.6 %adam.1 = (f32[128,2048]{1,0:T(8,128)}, f32[128,2048]{1,0:T(8,128)}, f32[128,2048]{1,0:T(8,128)}) custom-call(s32[1,512]{1,0:T(1,128)S(1)} %bitcast.25, bf16[128,1024]{1,0:T(8,128)(2,1)S(1)} %slice.3.refs_0_, bf16[128,1024]{1,0:T(8,128)(2,1)S(1)} %collective-permute-done.24.refs_1_, bf16[128,1024]{1,0:T(8,128)(2,1)S(1)} %collective-permute-done.25.refs_2_, ...), custom_call_target="tpu_custom_call" | custom-call | flops 5242880 | bytes 7864320 | tf_op jit(solution)/shard_map/adam/pallas_call | solution.py:451
  (43 shorter events, 0.7 us)
Async XLA Ops:
  0.6 5.6 %collective-permute-start.3 = (bf16[128,8192]{1,0:T(8,128)(2,1)}, bf16[128,8192]{1,0:T(8,128)(2,1)S(1)}, u32[]{:S(2)}, u32[]{:S(2)}) collective-permute-start(bf16[128,8192]{1,0:T(8,128)(2,1)} %bitcast.12), channel_id=1, source_target_pairs={{0,1},{1,0},{2,3},{3,2},{4,5},{5,4},{6,7},{7,6},{8,9},{9,8},{10,11... | collective-permute-start | bytes 6291464 | tf_op jit(solution)/shard_map/ppermute | solution.py:483
  1.1 8.6 %collective-permute-start = (bf16[128,512]{1,0:T(8,128)(2,1)}, bf16[128,512]{1,0:T(8,128)(2,1)S(1)}, u32[]{:S(2)}, u32[]{:S(2)}) collective-permute-start(bf16[128,512]{1,0:T(8,128)(2,1)} %bitcast.20), channel_id=1, source_target_pairs={{0,4},{1,5},{2,6},{3,7},{4,0},{5,1},{6,2},{7,3},{8,12},{9,13},{10,... | collective-permute-start | bytes 393224 | tf_op jit(solution)/shard_map/ppermute | solution.py:483
  3.7 8.6 %collective-permute-start.1 = (bf16[128,512]{1,0:T(8,128)(2,1)}, bf16[128,512]{1,0:T(8,128)(2,1)S(1)}, u32[]{:S(2)}, u32[]{:S(2)}) collective-permute-start(bf16[128,512]{1,0:T(8,128)(2,1)} %bitcast.21), channel_id=1, source_target_pairs={{0,2},{1,3},{2,0},{3,1},{4,6},{5,7},{6,4},{7,5},{8,10},{9,11},{10,... | collective-permute-start | bytes 393224 | tf_op jit(solution)/shard_map/ppermute | solution.py:483
  5.2 7.1 %collective-permute-start.2 = (bf16[128,512]{1,0:T(8,128)(2,1)}, bf16[128,512]{1,0:T(8,128)(2,1)S(1)}, u32[]{:S(2)}, u32[]{:S(2)}) collective-permute-start(bf16[128,512]{1,0:T(8,128)(2,1)} %bitcast.22), channel_id=1, source_target_pairs={{0,6},{1,7},{2,4},{3,5},{4,2},{5,3},{6,0},{7,1},{8,14},{9,15},{10,... | collective-permute-start | bytes 393224 | tf_op jit(solution)/shard_map/ppermute | solution.py:483
  6.2 6.1 %copy-start.5 = (bf16[1,128,512]{2,1,0:T(8,128)(2,1)S(1)}, bf16[1,128,512]{2,1,0:T(8,128)(2,1)}, u32[]{:S(2)}) copy-start(bf16[1,128,512]{2,1,0:T(8,128)(2,1)} %param.11) | copy-start | bytes 393220
  9.7 24.4 %copy-start.6 = (s32[512]{0:T(512)S(1)}, s32[512]{0:T(512)}, u32[]{:S(2)}) copy-start(s32[512]{0:T(512)} %param.12) | copy-start | bytes 6148
  12.4 6.4 %collective-permute-start.8 = (bf16[512,512]{1,0:T(8,128)(2,1)S(1)}, bf16[512,512]{1,0:T(8,128)(2,1)S(1)}, u32[]{:S(2)}, u32[]{:S(2)}) collective-permute-start(bf16[512,512]{1,0:T(8,128)(2,1)S(1)} %get-tuple-element.48), channel_id=1, source_target_pairs={{0,1},{1,0},{2,3},{3,2},{4,5},{5,4},{6,7},{7,6},{8,9},{9,8},{10,11... | collective-permute-start | bytes 1572872 | tf_op jit(solution)/shard_map/ppermute | solution.py:483
  12.5 6.4 %collective-permute-start.7 = (bf16[64,1024]{1,0:T(8,128)(2,1)S(1)}, bf16[64,1024]{1,0:T(8,128)(2,1)S(1)}, u32[]{:S(2)}, u32[]{:S(2)}) collective-permute-start(bf16[64,1024]{1,0:T(8,128)(2,1)S(1)} %get-tuple-element.47), channel_id=1, source_target_pairs={{0,4},{1,5},{2,6},{3,7},{4,0},{5,1},{6,2},{7,3},{8,12},{9,13},{10,... | collective-permute-start | bytes 393224 | tf_op jit(solution)/shard_map/ppermute | solution.py:483
  13.8 19.8 %collective-permute-start.4 = (bf16[2,128,1024]{2,1,0:T(8,128)(2,1)S(1)}, bf16[2,128,1024]{2,1,0:T(8,128)(2,1)S(1)}, u32[]{:S(2)}, u32[]{:S(2)}) collective-permute-start(bf16[2,128,1024]{2,1,0:T(8,128)(2,1)S(1)} %get-tuple-element.44), channel_id=1, source_target_pairs={{0,4},{1,5},{2,6},{3,7},{4,0},{5,1},{6,2},{7,3},{8,12},{9,13},{10,... | collective-permute-start | bytes 1572872 | tf_op jit(solution)/shard_map/ppermute | solution.py:483
  14.6 19.0 %collective-permute-start.5 = (bf16[2,128,1024]{2,1,0:T(8,128)(2,1)S(1)}, bf16[2,128,1024]{2,1,0:T(8,128)(2,1)S(1)}, u32[]{:S(2)}, u32[]{:S(2)}) collective-permute-start(bf16[2,128,1024]{2,1,0:T(8,128)(2,1)S(1)} %get-tuple-element.45), channel_id=1, source_target_pairs={{0,2},{1,3},{2,0},{3,1},{4,6},{5,7},{6,4},{7,5},{8,10},{9,11},{10,... | collective-permute-start | bytes 1572872 | tf_op jit(solution)/shard_map/ppermute | solution.py:483
  16.1 25.7 %collective-permute-start.6 = (bf16[2,128,1024]{2,1,0:T(8,128)(2,1)S(1)}, bf16[2,128,1024]{2,1,0:T(8,128)(2,1)S(1)}, u32[]{:S(2)}, u32[]{:S(2)}) collective-permute-start(bf16[2,128,1024]{2,1,0:T(8,128)(2,1)S(1)} %get-tuple-element.46), channel_id=1, source_target_pairs={{0,6},{1,7},{2,4},{3,5},{4,2},{5,3},{6,0},{7,1},{8,14},{9,15},{10,... | collective-permute-start | bytes 1572872 | tf_op jit(solution)/shard_map/ppermute | solution.py:483
  18.8 14.1 %collective-permute-start.10 = (bf16[128,1024]{1,0:T(8,128)(2,1)S(1)}, bf16[128,1024]{1,0:T(8,128)(2,1)S(1)}, u32[]{:S(2)}, u32[]{:S(2)}) collective-permute-start(bf16[128,1024]{1,0:T(8,128)(2,1)S(1)} %stack.3.refs_4_.refs_0_), channel_id=1, source_target_pairs={{0,16},{1,17},{2,18},{3,19},{4,20},{5,21},{6,22},{7,23},{8,24},{9,... | collective-permute-start | bytes 786440 | tf_op jit(solution)/shard_map/ppermute | solution.py:483
  21.5 12.5 %collective-permute-start.9 = (bf16[128,1024]{1,0:T(8,128)(2,1)S(1)}, bf16[128,1024]{1,0:T(8,128)(2,1)S(1)}, u32[]{:S(2)}, u32[]{:S(2)}) collective-permute-start(bf16[128,1024]{1,0:T(8,128)(2,1)S(1)} %stack.3.refs_4_.refs_0_), channel_id=1, source_target_pairs={{0,8},{1,9},{2,10},{3,11},{4,12},{5,13},{6,14},{7,15},{8,0},{9,1},... | collective-permute-start | bytes 786440 | tf_op jit(solution)/shard_map/ppermute | solution.py:483
  33.0 8.8 %collective-permute-start.11 = (bf16[128,1024]{1,0:T(8,128)(2,1)S(1)}, bf16[128,1024]{1,0:T(8,128)(2,1)S(1)}, u32[]{:S(2)}, u32[]{:S(2)}) collective-permute-start(bf16[128,1024]{1,0:T(8,128)(2,1)S(1)} %collective-permute-done.10.refs_6_.refs_2_), channel_id=1, source_target_pairs={{0,8},{1,9},{2,10},{3,11},{4,12},{5,13},{6,14},{7,15},{8,0},{9,1},... | collective-permute-start | bytes 786440 | tf_op jit(solution)/shard_map/ppermute | solution.py:483
  33.5 15.0 %collective-permute-start.14 = (bf16[128,1024]{1,0:T(8,128)(2,1)S(1)}, bf16[128,1024]{1,0:T(8,128)(2,1)S(1)}, u32[]{:S(2)}, u32[]{:S(2)}) collective-permute-start(bf16[128,1024]{1,0:T(8,128)(2,1)S(1)} %stack.3.refs_4_.refs_0_), channel_id=1, source_target_pairs={{0,1},{1,0},{2,3},{3,2},{4,5},{5,4},{6,7},{7,6},{8,9},{9,8},{10,11... | collective-permute-start | bytes 786440 | tf_op jit(solution)/shard_map/ppermute | solution.py:483
  33.5 15.1 %collective-permute-start.16 = (bf16[128,1024]{1,0:T(8,128)(2,1)S(1)}, bf16[128,1024]{1,0:T(8,128)(2,1)S(1)}, u32[]{:S(2)}, u32[]{:S(2)}) collective-permute-start(bf16[128,1024]{1,0:T(8,128)(2,1)S(1)} %collective-permute-done.10.refs_6_.refs_2_), channel_id=1, source_target_pairs={{0,1},{1,0},{2,3},{3,2},{4,5},{5,4},{6,7},{7,6},{8,9},{9,8},{10,11... | collective-permute-start | bytes 786440 | tf_op jit(solution)/shard_map/ppermute | solution.py:483
  34.0 15.0 %collective-permute-start.15 = (bf16[128,1024]{1,0:T(8,128)(2,1)S(1)}, bf16[128,1024]{1,0:T(8,128)(2,1)S(1)}, u32[]{:S(2)}, u32[]{:S(2)}) collective-permute-start(bf16[128,1024]{1,0:T(8,128)(2,1)S(1)} %collective-permute-done.9.refs_5_.refs_1_), channel_id=1, source_target_pairs={{0,1},{1,0},{2,3},{3,2},{4,5},{5,4},{6,7},{7,6},{8,9},{9,8},{10,11... | collective-permute-start | bytes 786440 | tf_op jit(solution)/shard_map/ppermute | solution.py:483
  43.1 15.0 %collective-permute-start.21 = (bf16[256,1024]{1,0:T(8,128)(2,1)S(1)}, bf16[256,1024]{1,0:T(8,128)(2,1)S(1)}, u32[]{:S(2)}, u32[]{:S(2)}) collective-permute-start(bf16[256,1024]{1,0:T(8,128)(2,1)S(1)} %get-tuple-element.49.refs_8_.refs_0_), channel_id=1, source_target_pairs={{0,8},{1,9},{2,10},{3,11},{4,12},{5,13},{6,14},{7,15},{24,16},{25,... | collective-permute-start | bytes 1572872 | tf_op jit(solution)/shard_map/ppermute | solution.py:483
  45.8 22.2 %collective-permute-start.23 = (bf16[256,1024]{1,0:T(8,128)(2,1)S(1)}, bf16[256,1024]{1,0:T(8,128)(2,1)S(1)}, u32[]{:S(2)}, u32[]{:S(2)}) collective-permute-start(bf16[256,1024]{1,0:T(8,128)(2,1)S(1)} %get-tuple-element.66), channel_id=1, source_target_pairs={{0,8},{1,9},{2,10},{3,11},{4,12},{5,13},{6,14},{7,15},{24,16},{25,... | collective-permute-start | bytes 1572872 | tf_op jit(solution)/shard_map/ppermute | solution.py:483
  48.5 1.6 %collective-permute-start.12 = (bf16[256,512]{1,0:T(8,128)(2,1)S(1)}, bf16[256,512]{1,0:T(8,128)(2,1)S(1)}, u32[]{:S(2)}, u32[]{:S(2)}) collective-permute-start(bf16[256,512]{1,0:T(8,128)(2,1)S(1)} %get-tuple-element.51), channel_id=1, source_target_pairs={{0,1},{1,0},{2,3},{3,2},{4,5},{5,4},{6,7},{7,6},{8,9},{9,8},{10,11... | collective-permute-start | bytes 786440 | tf_op jit(solution)/shard_map/ppermute | solution.py:483
  48.6 1.9 %collective-permute-start.13 = (bf16[256,512]{1,0:T(8,128)(2,1)S(1)}, bf16[256,512]{1,0:T(8,128)(2,1)S(1)}, u32[]{:S(2)}, u32[]{:S(2)}) collective-permute-start(bf16[256,512]{1,0:T(8,128)(2,1)S(1)} %get-tuple-element.52), channel_id=1, source_target_pairs={{0,1},{1,0},{2,3},{3,2},{4,5},{5,4},{6,7},{7,6},{8,9},{9,8},{10,11... | collective-permute-start | bytes 786440 | tf_op jit(solution)/shard_map/ppermute | solution.py:483
  49.1 1.8 %collective-permute-start.17 = (bf16[128,1024]{1,0:T(8,128)(2,1)S(1)}, bf16[128,1024]{1,0:T(8,128)(2,1)S(1)}, u32[]{:S(2)}, u32[]{:S(2)}) collective-permute-start(bf16[128,1024]{1,0:T(8,128)(2,1)S(1)} %collective-permute-done.11.refs_7_.refs_3_), channel_id=1, source_target_pairs={{0,1},{1,0},{2,3},{3,2},{4,5},{5,4},{6,7},{7,6},{8,9},{9,8},{10,11... | collective-permute-start | bytes 786440 | tf_op jit(solution)/shard_map/ppermute | solution.py:483
  52.3 20.4 %collective-permute-start.20 = (bf16[128,2560]{1,0:T(8,128)(2,1)S(1)}, bf16[128,2560]{1,0:T(8,128)(2,1)S(1)}, u32[]{:S(2)}, u32[]{:S(2)}) collective-permute-start(bf16[128,2560]{1,0:T(8,128)(2,1)S(1)} %get-tuple-element.57), channel_id=1, source_target_pairs={{0,6},{1,7},{2,4},{3,5},{4,2},{5,3},{6,0},{7,1},{8,14},{9,15},{10,... | collective-permute-start | bytes 1966088 | tf_op jit(solution)/shard_map/ppermute | solution.py:483
  58.2 10.3 %collective-permute-start.26 = (bf16[128,1024]{1,0:T(8,128)(2,1)S(1)}, bf16[128,1024]{1,0:T(8,128)(2,1)S(1)}, u32[]{:S(2)}, u32[]{:S(2)}) collective-permute-start(bf16[128,1024]{1,0:T(8,128)(2,1)S(1)} %get-tuple-element.69), channel_id=1, source_target_pairs={{8,16},{9,17},{10,18},{11,19},{12,20},{13,21},{14,22},{15,23},{16,... | collective-permute-start | bytes 786440 | tf_op jit(solution)/shard_map/ppermute | solution.py:483
  58.9 12.9 %collective-permute-start.22 = (bf16[128,1024]{1,0:T(8,128)(2,1)S(1)}, bf16[128,1024]{1,0:T(8,128)(2,1)S(1)}, u32[]{:S(2)}, u32[]{:S(2)}) collective-permute-start(bf16[128,1024]{1,0:T(8,128)(2,1)S(1)} %get-tuple-element.64), channel_id=1, source_target_pairs={{8,16},{9,17},{10,18},{11,19},{12,20},{13,21},{14,22},{15,23},{16,... | collective-permute-start | bytes 786440 | tf_op jit(solution)/shard_map/ppermute | solution.py:483
  59.6 24.3 %collective-permute-start.18 = (bf16[128,2560]{1,0:T(8,128)(2,1)S(1)}, bf16[128,2560]{1,0:T(8,128)(2,1)S(1)}, u32[]{:S(2)}, u32[]{:S(2)}) collective-permute-start(bf16[128,2560]{1,0:T(8,128)(2,1)S(1)} %get-tuple-element.55), channel_id=1, source_target_pairs={{0,4},{1,5},{2,6},{3,7},{4,0},{5,1},{6,2},{7,3},{8,12},{9,13},{10,... | collective-permute-start | bytes 1966088 | tf_op jit(solution)/shard_map/ppermute | solution.py:483
  68.0 16.2 %collective-permute-start.19 = (bf16[128,2560]{1,0:T(8,128)(2,1)S(1)}, bf16[128,2560]{1,0:T(8,128)(2,1)S(1)}, u32[]{:S(2)}, u32[]{:S(2)}) collective-permute-start(bf16[128,2560]{1,0:T(8,128)(2,1)S(1)} %get-tuple-element.56), channel_id=1, source_target_pairs={{0,2},{1,3},{2,0},{3,1},{4,6},{5,7},{6,4},{7,5},{8,10},{9,11},{10,... | collective-permute-start | bytes 1966088 | tf_op jit(solution)/shard_map/ppermute | solution.py:483
  68.6 9.2 %collective-permute-start.27 = (bf16[128,1024]{1,0:T(8,128)(2,1)S(1)}, bf16[128,1024]{1,0:T(8,128)(2,1)S(1)}, u32[]{:S(2)}, u32[]{:S(2)}) collective-permute-start(bf16[128,1024]{1,0:T(8,128)(2,1)S(1)} %get-tuple-element.70), channel_id=1, source_target_pairs={{0,8},{1,9},{2,10},{3,11},{4,12},{5,13},{6,14},{7,15},{8,0},{9,1},... | collective-permute-start | bytes 786440 | tf_op jit(solution)/shard_map/ppermute | solution.py:483
  71.8 12.4 %copy-start = (bf16[1,128,8192]{2,1,0:T(8,128)(2,1)S(1)}, bf16[1,128,8192]{2,1,0:T(8,128)(2,1)}, u32[]{:S(2)}) copy-start(bf16[1,128,8192]{2,1,0:T(8,128)(2,1)} %param.8) | copy-start | bytes 6291460
  71.8 12.4 %copy-start.4 = (f32[8192]{0:T(1024)S(1)}, f32[8192]{0:T(1024)}, u32[]{:S(2)}) copy-start(f32[8192]{0:T(1024)} %param.9) | copy-start | bytes 98308
  71.8 6.7 %collective-permute-start.28 = (bf16[128,1024]{1,0:T(8,128)(2,1)S(1)}, bf16[128,1024]{1,0:T(8,128)(2,1)S(1)}, u32[]{:S(2)}, u32[]{:S(2)}) collective-permute-start(bf16[128,1024]{1,0:T(8,128)(2,1)S(1)} %get-tuple-element.71), channel_id=1, source_target_pairs={{8,16},{9,17},{10,18},{11,19},{12,20},{13,21},{14,22},{15,23},{16,... | collective-permute-start | bytes 786440 | tf_op jit(solution)/shard_map/ppermute | solution.py:483
  72.7 15.0 %collective-permute-start.24 = (bf16[128,1024]{1,0:T(8,128)(2,1)S(1)}, bf16[128,1024]{1,0:T(8,128)(2,1)S(1)}, u32[]{:S(2)}, u32[]{:S(2)}) collective-permute-start(bf16[128,1024]{1,0:T(8,128)(2,1)S(1)} %get-tuple-element.67), channel_id=1, source_target_pairs={{0,8},{1,9},{2,10},{3,11},{4,12},{5,13},{6,14},{7,15},{8,0},{9,1},... | collective-permute-start | bytes 786440 | tf_op jit(solution)/shard_map/ppermute | solution.py:483
  77.8 10.0 %collective-permute-start.25 = (bf16[128,1024]{1,0:T(8,128)(2,1)S(1)}, bf16[128,1024]{1,0:T(8,128)(2,1)S(1)}, u32[]{:S(2)}, u32[]{:S(2)}) collective-permute-start(bf16[128,1024]{1,0:T(8,128)(2,1)S(1)} %get-tuple-element.68), channel_id=1, source_target_pairs={{8,16},{9,17},{10,18},{11,19},{12,20},{13,21},{14,22},{15,23},{16,... | collective-permute-start | bytes 786440 | tf_op jit(solution)/shard_map/ppermute | solution.py:483
  78.6 10.1 %collective-permute-start.29 = (bf16[128,1024]{1,0:T(8,128)(2,1)S(1)}, bf16[128,1024]{1,0:T(8,128)(2,1)S(1)}, u32[]{:S(2)}, u32[]{:S(2)}) collective-permute-start(bf16[128,1024]{1,0:T(8,128)(2,1)S(1)} %relay.7), channel_id=1, source_target_pairs={{0,4},{1,5},{2,6},{3,7},{4,0},{5,1},{6,2},{7,3},{8,12},{9,13},{10,... | collective-permute-start | bytes 786440 | tf_op jit(solution)/shard_map/ppermute | solution.py:483
  84.2 4.6 %copy-start.1 = (f32[1,128,2048]{2,1,0:T(8,128)S(1)}, f32[1,128,2048]{2,1,0:T(8,128)}, u32[]{:S(2)}) copy-start(f32[1,128,2048]{2,1,0:T(8,128)} %param.13) | copy-start | bytes 3145732
  84.2 4.6 %copy-start.2 = (f32[1,128,2048]{2,1,0:T(8,128)S(1)}, f32[1,128,2048]{2,1,0:T(8,128)}, u32[]{:S(2)}) copy-start(f32[1,128,2048]{2,1,0:T(8,128)} %param.14) | copy-start | bytes 3145732
  84.2 4.6 %copy-start.3 = (f32[1,128,2048]{2,1,0:T(8,128)S(1)}, f32[1,128,2048]{2,1,0:T(8,128)}, u32[]{:S(2)}) copy-start(f32[1,128,2048]{2,1,0:T(8,128)} %param.15) | copy-start | bytes 3145732
